TPU v7x, 128 devices: a whole 4x4x4 slice. The times are simulated.
128 devices in a mesh: slab: 32 (over x, y, core), wsh: 4 (over z).
Axes of the slice: x: 4, y: 4, z: 4, core: 2. Of those that a mesh axis runs over, the one named last changes fastest.
Arguments:
- node_feat: bfloat16 [524288, 128], P(('slab', 'wsh')), may hold values from -6 to 6
- cotangent: bfloat16 [524288, 128], P(('slab', 'wsh')), may hold values from -6 to 6
- w_msg: bfloat16 [128, 128], P('wsh'), may hold values from -0.5 to 0.5
- w_in: bfloat16 [256, 128], P('wsh'), may hold values from -0.375 to 0.375
- w_out: bfloat16 [128, 128], P('wsh'), may hold values from -0.5 to 0.5
- ln_gain: bfloat16 [128], P('wsh'), may hold values from 0.25 to 1.75
- tile_values: bfloat16 [16384, 4, 128], P(('slab', 'wsh')), may hold values from -2 to 2
- tile_cols: int32 [16384, 4, 128], P(('slab', 'wsh')), may hold values from 0 to 127
- tile_dst: int32 [16384], P(('slab', 'wsh')), may hold values from 0 to 31
- tile_src: int32 [16384], P(('slab', 'wsh')), may hold values from 0 to 191
- tile_count: int32 [128], P(('slab', 'wsh')), may hold values from 16 to 128, as said below
- halo_rows: int32 [128, 2, 1024], P(('slab', 'wsh')), may hold values from 0 to 4095, as said below
- halo_count: int32 [128, 2], P(('slab', 'wsh')), may hold values from 512 to 1024, as said below
Outputs:
- node_out: bfloat16 [524288, 128], P(('slab', 'wsh'))
- d_node: bfloat16 [524288, 128], P(('slab', 'wsh'))
- d_w_msg: float32 [128, 128], P('wsh')
- d_w_in: float32 [256, 128], P('wsh')
- d_w_out: float32 [128, 128], P('wsh')
- d_gain: float32 [128], P('wsh')
Inputs may be any that keep to these rules, and one draw needn't show every extreme that they name: In every slab one device uses all 128 slots; the used slots are the first tile_count ones. `halo_rows`: each list holds distinct rows of the sending device. `halo_count`: some device uses all 1024 slots of both lists.
All inputs are finite; a program needn't handle non-finite values.
Results may differ from a plain program's by a relative error of at most 0.019.
Values may be sent and summed in bfloat16 or wider, within the bound.
No kernel may reach another device: no remote copies, remote signals or barrier semaphores. Data moves between devices by JAX's collectives and lax.ppermute only.
A program may use at most 128 MiB of HBM per device.

v0:
```python
import jax
import jax.numpy as jnp
from jax import lax
from jax.sharding import PartitionSpec as P


def padded(cells, sides, width):
    for axis, dim in sides:
        count = lax.axis_size(axis)
        ends = count - 1
        head = lax.slice_in_dim(cells, 0, width, axis=dim)
        tail = lax.slice_in_dim(cells, cells.shape[dim] - width, cells.shape[dim], axis=dim)
        cells = jnp.concatenate(
            [
                lax.ppermute(tail, axis, [(i, (i + 1) % count) for i in range(ends)]),
                cells,
                lax.ppermute(head, axis, [((i + 1) % count, i) for i in range(ends)]),
            ],
            axis=dim,
        )
    return cells


def silu_slope(argument):
    logistic = jax.nn.sigmoid(argument)
    return logistic * (1.0 + argument * (1.0 - logistic))


def contract_rows(left, right):
    return lax.dot_general(
        left, right, (((0,), (0,)), ((), ())), preferred_element_type=jnp.float32
    )


def contract_cols(left, right):
    return lax.dot_general(
        left, right, (((1,), (1,)), ((), ())), preferred_element_type=jnp.float32
    )


def pass_rims(buffer):
    return padded(buffer, (("slab", 0),), buffer.shape[0] // 2)


def dense_tiles(tile_part, cols, in_use, tile_side):
    matches = (
        cols[..., None] == jnp.arange(tile_side, dtype=jnp.int32)[None, None, None, :]
    ).astype(jnp.float32)
    weights = jnp.where(in_use[:, None, None], tile_part.astype(jnp.float32), 0.0)
    return jnp.sum(weights[..., None] * matches, axis=1)


def own_fetch(tile_values, tile_cols, tile_dst, tile_src, used_count, group_size):

    def fetcher(step_index):
        start_at = step_index * group_size
        tile_part = lax.dynamic_slice_in_dim(tile_values, start_at, group_size, 0)
        cols = lax.dynamic_slice_in_dim(tile_cols, start_at, group_size, 0)
        target = lax.dynamic_slice_in_dim(tile_dst, start_at, group_size, 0)
        anchor = lax.dynamic_slice_in_dim(tile_src, start_at, group_size, 0)
        in_use = start_at + jnp.arange(group_size) < used_count
        return (tile_part, cols, target, anchor, in_use)

    turns = (used_count + group_size - 1) // group_size
    return (fetcher, turns)


def on_device(
    node_feat,
    cotangent,
    w_msg,
    w_in,
    w_out,
    ln_gain,
    tile_values,
    tile_cols,
    tile_dst,
    tile_src,
    tile_count,
    halo_rows,
    halo_count,
):
    node_rows, feature_width = node_feat.shape
    tile_side = tile_values.shape[2]
    slot_count = tile_values.shape[0]
    halo_side = halo_rows.shape[2]
    block_count = node_rows // tile_side
    parties = lax.axis_size("wsh")
    position = lax.axis_index("wsh")
    group_size = slot_count // 16
    highest = lax.Precision.HIGHEST
    full_msg, full_in, full_out, full_gain = (
        lax.all_gather(w_msg, "wsh", axis=0, tiled=True),
        lax.all_gather(w_in, "wsh", axis=0, tiled=True),
        lax.all_gather(w_out, "wsh", axis=0, tiled=True),
        lax.all_gather(ln_gain, "wsh", axis=0, tiled=True),
    )
    pre_act = jnp.dot(node_feat, full_msg, preferred_element_type=jnp.float32)
    message = jax.nn.silu(pre_act).astype(jnp.bfloat16)
    listed = halo_rows.reshape(2 * halo_side)
    kept_slot = (jnp.arange(halo_side)[None, :] < halo_count.reshape(2, 1)).reshape(2 * halo_side)
    outgoing = jnp.where(kept_slot[:, None], message[listed], jnp.zeros((), jnp.bfloat16))
    arrived = pass_rims(outgoing)
    local_sources = jnp.concatenate(
        [message, arrived[:halo_side], arrived[3 * halo_side :]], axis=0
    )
    slab_sources = lax.all_gather(local_sources, "wsh", axis=0, tiled=True)
    source_count = slab_sources.shape[0] // tile_side
    source_blocks = slab_sources.reshape(source_count, tile_side, feature_width)
    fetcher, turns = own_fetch(
        tile_values, tile_cols, tile_dst, tile_src, tile_count[0], group_size
    )

    def selectors(target, anchor):
        selector = anchor[:, None] == jnp.arange(source_count, dtype=jnp.int32)[None, :]
        placer = target[:, None] == jnp.arange(block_count, dtype=jnp.int32)[None, :]
        return (selector, placer)

    def forward_step(step_index, carried):
        tile_part, cols, target, anchor, in_use = fetcher(step_index)
        dense = dense_tiles(tile_part, cols, in_use, tile_side)
        selector, placer = selectors(target, anchor)
        blocks_in = jnp.einsum(
            "gs,sbd->gbd",
            selector.astype(jnp.bfloat16),
            source_blocks,
            preferred_element_type=jnp.float32,
        )
        product = jnp.einsum("gic,gcd->gid", dense, blocks_in, precision=highest)
        return carried + jnp.einsum(
            "gt,gid->tid", placer.astype(jnp.float32), product, precision=highest
        )

    aggregate = lax.fori_loop(
        0, turns, forward_step, jnp.zeros((block_count, tile_side, feature_width), jnp.float32)
    )
    aggregate = aggregate.reshape(-1, feature_width)
    agg_rounded = aggregate.astype(jnp.bfloat16)
    hidden_pre = jnp.dot(
        node_feat, full_in[:feature_width], preferred_element_type=jnp.float32
    ) + jnp.dot(agg_rounded, full_in[feature_width:], preferred_element_type=jnp.float32)
    hidden = jax.nn.silu(hidden_pre).astype(jnp.bfloat16)
    update = jnp.dot(hidden, full_out, preferred_element_type=jnp.float32)
    centre = update - jnp.mean(update, axis=-1, keepdims=True)
    inverse = lax.rsqrt(jnp.mean(centre * centre, axis=-1, keepdims=True) + 1e-05)
    normed = centre * inverse
    gain = full_gain.astype(jnp.float32)
    node_out = (node_feat.astype(jnp.float32) + gain * normed).astype(jnp.bfloat16)
    upstream = cotangent.astype(jnp.float32)
    d_normed = upstream * gain
    d_gain = jnp.sum(upstream * normed, axis=0)
    d_update = (
        (
            d_normed
            - jnp.mean(d_normed, axis=-1, keepdims=True)
            - normed * jnp.mean(d_normed * normed, axis=-1, keepdims=True)
        )
        * inverse
    ).astype(jnp.bfloat16)
    d_w_out = contract_rows(hidden, d_update)
    d_hidden_pre = (contract_cols(d_update, full_out) * silu_slope(hidden_pre)).astype(jnp.bfloat16)
    d_w_in = jnp.concatenate(
        [contract_rows(node_feat, d_hidden_pre), contract_rows(agg_rounded, d_hidden_pre)], axis=0
    )
    d_direct = contract_cols(d_hidden_pre, full_in[:feature_width])
    d_agg = contract_cols(d_hidden_pre, full_in[feature_width:]).astype(jnp.bfloat16)
    agg_upstream = d_agg
    agg_upstream = agg_upstream.reshape(-1, tile_side, feature_width)

    def backward_step(step_index, carried):
        tile_part, cols, target, anchor, in_use = fetcher(step_index)
        dense = dense_tiles(tile_part, cols, in_use, tile_side)
        selector, placer = selectors(target, anchor)
        picked = jnp.einsum(
            "gt,tbd->gbd",
            placer.astype(jnp.bfloat16),
            agg_upstream,
            preferred_element_type=jnp.float32,
        )
        terms = jnp.einsum("gic,gid->gcd", dense, picked, precision=highest)
        return carried + jnp.einsum(
            "gs,gcd->scd", selector.astype(jnp.float32), terms, precision=highest
        )

    d_sources = lax.fori_loop(
        0, turns, backward_step, jnp.zeros((source_count, tile_side, feature_width), jnp.float32)
    )
    d_sources = d_sources.reshape(-1, feature_width)
    d_local = lax.psum_scatter(
        d_sources.astype(jnp.bfloat16), "wsh", scatter_dimension=0, tiled=True
    ).astype(jnp.float32)
    rim_grads = d_local[node_rows:].astype(jnp.bfloat16)
    returned_rims = pass_rims(rim_grads)
    returned = jnp.concatenate(
        [returned_rims[:halo_side], returned_rims[3 * halo_side :]], axis=0
    ).astype(jnp.float32)
    returned = jnp.where(kept_slot[:, None], returned, 0.0)
    d_message = d_local[:node_rows].at[listed].add(returned)
    d_pre = (d_message * silu_slope(pre_act)).astype(jnp.bfloat16)
    d_w_msg = contract_rows(node_feat, d_pre)
    d_node = (upstream + d_direct + contract_cols(d_pre, full_msg)).astype(jnp.bfloat16)
    terms = (d_w_msg, d_w_in, d_w_out, d_gain)
    summed = lax.psum((terms[0], terms[1], terms[2], terms[3]), ("slab", "wsh"))
    shares = tuple(
        (
            lax.dynamic_slice_in_dim(
                member, position * (member.shape[0] // parties), member.shape[0] // parties, 0
            )
            for member in summed
        )
    )
    return (node_out, d_node, shares[0], shares[1], shares[2], shares[3])


def solution(mesh):
    placed = (
        P(("slab", "wsh"), None),
        P(("slab", "wsh"), None),
        P("wsh", None),
        P("wsh", None),
        P("wsh", None),
        P("wsh"),
        P(("slab", "wsh"), None, None),
        P(("slab", "wsh"), None, None),
        P(("slab", "wsh")),
        P(("slab", "wsh")),
        P(("slab", "wsh")),
        P(("slab", "wsh"), None, None),
        P(("slab", "wsh"), None),
    )
    return jax.shard_map(
        on_device,
        mesh=mesh,
        in_specs=placed,
        out_specs=(
            P(("slab", "wsh"), None),
            P(("slab", "wsh"), None),
            P("wsh", None),
            P("wsh", None),
            P("wsh", None),
            P("wsh"),
        ),
        check_vma=False,
    )
```

profile of v0, /device:TPU:1, one launch (start us, length us, event | category | flops | bytes accessed | tf_op | source)
XLA Modules:
  0.0 829.5 jit_solution(10140119880566574467)
XLA Ops:
  8.7 11.5 %all_gather.17 = bf16[128,128]{1,0:T(8,128)(2,1)S(1)} all-gather(bf16[32,128]{1,0:T(8,128)(2,1)} %param.19), channel_id=1, replica_groups=mesh['slab'=32,'wsh'=4] {'wsh'}, dimensions={0}, use_global_device_ids=true | all-gather | bytes 40960 | tf_op jit(solution)/shard_map/all_gather | solution.py:93
  23.4 6.2 gather_fusion
  30.0 6.4 collective-permute-start
  39.7 4.5 collective-permute-done.1
  49.1 8.6 %all-reduce = bf16[128]{0:T(256)(128)(2,1)S(1)} all-reduce(bf16[128]{0:T(256)(128)(2,1)S(1)} %dynamic-update-slice), channel_id=1, replica_groups=mesh['slab'=32,'wsh'=4] {'wsh'}, use_global_device_ids=true, to_apply=%add | all-reduce | flops 128 | bytes 512
  58.3 9.9 %all_gather.19 = bf16[128,128]{1,0:T(8,128)(2,1)S(1)} all-gather(bf16[32,128]{1,0:T(8,128)(2,1)S(1)} %copy-done.17), channel_id=1, replica_groups=mesh['slab'=32,'wsh'=4] {'wsh'}, dimensions={0}, use_global_device_ids=true | all-gather | bytes 40960 | tf_op jit(solution)/shard_map/all_gather | solution.py:95
  68.2 10.3 %all_gather.16 = bf16[256,128]{1,0:T(8,128)(2,1)S(1)} all-gather(bf16[64,128]{1,0:T(8,128)(2,1)S(1)} %copy-done.16), channel_id=1, replica_groups=mesh['slab'=32,'wsh'=4] {'wsh'}, dimensions={0}, use_global_device_ids=true | all-gather | bytes 81920 | tf_op jit(solution)/shard_map/all_gather | solution.py:94
  80.2 33.9 %all-gather.2.cloned.1.call-done = bf16[24576,128]{1,0:T(8,128)(2,1)} async-done(((bf16[6144,128]{1,0:T(8,128)(2,1)}), bf16[24576,128]{1,0:T(8,128)(2,1)}) %all-gather.2.cloned.1.call-update) | async-done | bytes 6291472 | tf_op jit(solution)/shard_map/all_gather | solution.py:107
  114.2 9.5 %copy.42 = bf16[192,128,128]{2,0,1:T(8,128)(2,1)} copy(bf16[192,128,128]{2,1,0:T(8,128)(2,1)} %bitcast.69) | data formatting | bytes 12582912 | tf_op jit(solution)/shard_map/while | solution.py:134
  124.3 70.1 %while.20 = (s32[]{:T(128)}, f32[32,128,128]{2,0,1:T(8,128)S(1)}, s32[]{:T(128)}, s32[128]{0:T(128)S(1)}, s32[128,4,128]{2,1,0:T(4,128)}, /*index=5*/s32[]{:T(12...) while((s32[]{:T(128)}, f32[32,128,128]{2,0,1:T(8,128)S(1)}, ...), condition=%wide.region_2.3_spmd, body=%wide.region_0.2_spmd.sunk | while | flops 303965952 | bytes 13722003 | solution.py:134
  203.6 6.1 broadcast_in_dim.61
  209.7 112.1 %while.21 = (s32[]{:T(128)}, f32[192,128,128]{2,0,1:T(8,128)}, s32[]{:T(128)}, s32[128]{0:T(128)S(1)}, s32[128,4,128]{2,1,0:T(4,128)}, /*index=5*/s32[]{:T(128)}...) while((s32[]{:T(128)}, f32[192,128,128]{2,0,1:T(8,128)}, ...), condition=%wide.region_9.10_spmd, body=%wide.region_7.9_spmd.sunk | while | flops 516302592 | bytes 29450644 | solution.py:185
  214.7 10.9 %convolution_add_fusion.8 = f32[192,128,128]{2,0,1:T(8,128)} fusion(f32[192,128,128]{2,0,1:T(8,128)} %get-tuple-element.361, f32[8,128,128]{2,1,0:T(8,128)S(1)} %fusion.103, s32[8]{0:T(128)S(1)} %dynamic_slice.62), kind=kOutput, calls=%fused_computation.18.clone.1 | convolution fusion | flops 305137152 | bytes 25690144 | tf_op jit(solution)/shard_map/while/body/gs,gcd->scd/dot_general | solution.py:181
  230.7 10.9 %convolution_add_fusion.8 = f32[192,128,128]{2,0,1:T(8,128)} fusion(f32[192,128,128]{2,0,1:T(8,128)} %get-tuple-element.361, f32[8,128,128]{2,1,0:T(8,128)S(1)} %fusion.103, s32[8]{0:T(128)S(1)} %dynamic_slice.62), kind=kOutput, calls=%fused_computation.18.clone.1 | convolution fusion | flops 305137152 | bytes 25690144 | tf_op jit(solution)/shard_map/while/body/gs,gcd->scd/dot_general | solution.py:181
  246.7 10.9 %convolution_add_fusion.8 = f32[192,128,128]{2,0,1:T(8,128)} fusion(f32[192,128,128]{2,0,1:T(8,128)} %get-tuple-element.361, f32[8,128,128]{2,1,0:T(8,128)S(1)} %fusion.103, s32[8]{0:T(128)S(1)} %dynamic_slice.62), kind=kOutput, calls=%fused_computation.18.clone.1 | convolution fusion | flops 305137152 | bytes 25690144 | tf_op jit(solution)/shard_map/while/body/gs,gcd->scd/dot_general | solution.py:181
  262.7 10.9 %convolution_add_fusion.8 = f32[192,128,128]{2,0,1:T(8,128)} fusion(f32[192,128,128]{2,0,1:T(8,128)} %get-tuple-element.361, f32[8,128,128]{2,1,0:T(8,128)S(1)} %fusion.103, s32[8]{0:T(128)S(1)} %dynamic_slice.62), kind=kOutput, calls=%fused_computation.18.clone.1 | convolution fusion | flops 305137152 | bytes 25690144 | tf_op jit(solution)/shard_map/while/body/gs,gcd->scd/dot_general | solution.py:181
  278.7 10.9 %convolution_add_fusion.8 = f32[192,128,128]{2,0,1:T(8,128)} fusion(f32[192,128,128]{2,0,1:T(8,128)} %get-tuple-element.361, f32[8,128,128]{2,1,0:T(8,128)S(1)} %fusion.103, s32[8]{0:T(128)S(1)} %dynamic_slice.62), kind=kOutput, calls=%fused_computation.18.clone.1 | convolution fusion | flops 305137152 | bytes 25690144 | tf_op jit(solution)/shard_map/while/body/gs,gcd->scd/dot_general | solution.py:181
  294.7 10.9 %convolution_add_fusion.8 = f32[192,128,128]{2,0,1:T(8,128)} fusion(f32[192,128,128]{2,0,1:T(8,128)} %get-tuple-element.361, f32[8,128,128]{2,1,0:T(8,128)S(1)} %fusion.103, s32[8]{0:T(128)S(1)} %dynamic_slice.62), kind=kOutput, calls=%fused_computation.18.clone.1 | convolution fusion | flops 305137152 | bytes 25690144 | tf_op jit(solution)/shard_map/while/body/gs,gcd->scd/dot_general | solution.py:181
  310.7 10.9 %convolution_add_fusion.8 = f32[192,128,128]{2,0,1:T(8,128)} fusion(f32[192,128,128]{2,0,1:T(8,128)} %get-tuple-element.361, f32[8,128,128]{2,1,0:T(8,128)S(1)} %fusion.103, s32[8]{0:T(128)S(1)} %dynamic_slice.62), kind=kOutput, calls=%fused_computation.18.clone.1 | convolution fusion | flops 305137152 | bytes 25690144 | tf_op jit(solution)/shard_map/while/body/gs,gcd->scd/dot_general | solution.py:181
  321.8 6.0 convert_element_type.73
  327.9 6.7 copy.47
  337.1 301.5 %psum.31 = f32[128]{0:T(128)S(1)} all-reduce(f32[128]{0:T(128)S(1)} %get-tuple-element.140), channel_id=1, replica_groups=mesh['slab'=32,'wsh'=4] {'slab','wsh'}, use_global_device_ids=true, to_apply=%region_16.17 | all-reduce | flops 128 | bytes 1024 | tf_op jit(solution)/shard_map/psum | solution.py:203
  656.0 14.2 %scatter_custom_fusion = f32[4096,128]{1,0:T(8,128)S(1)} fusion(f32[4096,128]{1,0:T(8,128)S(1)} %slice_convert_fusion, s32[2048]{0:T(1024)S(1)} %bitcast.74, bf16[1024,128]{1,0:T(8,128)(2,1)} %collective-permute-done.3, bf16[]{:T(256)} %constant.86, bf16[1024,128]{1,0:T(8,128)(2,1)S(1)} %collective-permute-done.2, f32[]{:T(128)} %constant.38.clone.1, ...), kind=kCustom, calls=%fused_computation.64 | custom fusion | flops 1572864 | bytes 2623494 | tf_op jit(solution)/shard_map/scatter-add | solution.py:198
  679.0 139.2 %all-reduce.4.cloned.1.call-done = (f32[128,128]{0,1:T(8,128)}, f32[256,128]{1,0:T(8,128)}, f32[128,128]{1,0:T(8,128)}) async-done(((f32[128,128]{0,1:T(8,128)}, f32[256,128]{1,0:T(8,128)}, f32[128,128]{1,0:T(8,128)}), (f32[128,128]{0,1:T(8,128)}, f32[256,128]{1,0:T(8,128)}, f32[128,128]{1,0:T(8,128)})) %all-reduce.4.cloned.1.call-update) | async-done | bytes 262160 | tf_op jit(solution)/shard_map/psum | solution.py:203
  (222 shorter events, 161.5 us)
Async XLA Ops:
  7.2 107.0 %all-gather.2.cloned.1.call-start = ((), (), s32[]{:S(2)}) async-start(), calls=%async_computation.1 | async-start | bytes 7864320 | tf_op jit(solution)/shard_map/all_gather | solution.py:107
  30.0 9.7 %collective-permute-start = (bf16[1024,128]{1,0:T(8,128)(2,1)S(1)}, bf16[1024,128]{1,0:T(8,128)(2,1)S(1)}, u32[]{:S(2)}, u32[]{:S(2)}) collective-permute-start(bf16[1024,128]{1,0:T(8,128)(2,1)S(1)} %get-tuple-element.186), channel_id=1, source_target_pairs={{0,4},{4,8},{8,12},{12,16},{16,20},{20,24},{24,28},{28,32},{32,36}... | collective-permute-start | bytes 786440 | tf_op jit(solution)/shard_map/ppermute | solution.py:15
  36.4 9.9 %copy-start = (bf16[4096,128]{1,0:T(8,128)(2,1)S(1)}, bf16[4096,128]{1,0:T(8,128)(2,1)}, u32[]{:S(2)}) copy-start(bf16[4096,128]{1,0:T(8,128)(2,1)} %param.17) | copy-start | bytes 3145732
  36.4 7.8 collective-permute-start.1
  45.5 2.2 copy-start.21
  45.5 3.4 copy-start.18
  45.5 12.2 %copy-start.15 = (bf16[4096,128]{1,0:T(8,128)(2,1)S(1)}, bf16[4096,128]{1,0:T(8,128)(2,1)}, u32[]{:S(2)}) copy-start(bf16[4096,128]{1,0:T(8,128)(2,1)} %param.18) | copy-start | bytes 3145732
  45.5 598.2 %reduce-scatter.2.cloned.1.call-start = ((), (), s32[]{:S(2)}) async-start(), calls=%async_computation.2 | async-start | bytes 7864320 | tf_op jit(solution)/shard_map/reduce_scatter | solution.py:189
  46.3 12.0 %copy-start.17 = (bf16[32,128]{1,0:T(8,128)(2,1)S(1)}, bf16[32,128]{1,0:T(8,128)(2,1)}, u32[]{:S(2)}) copy-start(bf16[32,128]{1,0:T(8,128)(2,1)} %param.21) | copy-start | bytes 24580
  46.3 21.9 %copy-start.16 = (bf16[64,128]{1,0:T(8,128)(2,1)S(1)}, bf16[64,128]{1,0:T(8,128)(2,1)}, u32[]{:S(2)}) copy-start(bf16[64,128]{1,0:T(8,128)(2,1)} %param.20) | copy-start | bytes 49156
  58.2 140.5 %copy-start.2 = (bf16[4096,128]{0,1:T(8,128)(2,1)}, bf16[4096,128]{0,1:T(8,128)(2,1)S(1)}, u32[]{:S(2)}) copy-start(bf16[4096,128]{0,1:T(8,128)(2,1)S(1)} %copy.44) | copy-start | bytes 3145732
  194.5 1.6 copy-start.14
  195.7 1.1 copy-start.9
  197.8 1.2 copy-start.11
  334.6 304.6 %copy-start.5 = (bf16[4096,128]{1,0:T(8,128)(2,1)S(1)}, bf16[4096,128]{1,0:T(8,128)(2,1)}, u32[]{:S(2)}) copy-start(bf16[4096,128]{1,0:T(8,128)(2,1)} %copy-done.4) | copy-start | bytes 3145732
  334.6 304.6 %copy-start.10 = (bf16[32,128,128]{2,1,0:T(8,128)(2,1)S(1)}, bf16[32,128,128]{2,1,0:T(8,128)(2,1)}, u32[]{:S(2)}) copy-start(bf16[32,128,128]{2,1,0:T(8,128)(2,1)} %copy-done.9) | copy-start | bytes 3145732
  334.6 483.6 %all-reduce.4.cloned.1.call-start = ((), (), s32[]{:S(2)}) async-start(), calls=%async_computation.3 | async-start | bytes 524288 | tf_op jit(solution)/shard_map/psum | solution.py:203
  334.7 305.0 %copy-start.1 = (bf16[4096,128]{1,0:T(8,128)(2,1)S(1)}, bf16[4096,128]{1,0:T(8,128)(2,1)}, u32[]{:S(2)}) copy-start(bf16[4096,128]{1,0:T(8,128)(2,1)} %param.17) | copy-start | bytes 3145732
  639.2 1.7 copy-start.8
  639.2 1.7 copy-start.13
  639.7 2.2 copy-start.3
  644.8 6.7 collective-permute-start.2
  648.2 7.8 collective-permute-start.3
  670.2 1.4 copy-start.6
  (5 other events, 4.3 us)
Sparse Core Ops, SparseCore 0:
  45.6 68.5 all-gather.1
  334.7 298.8 reduce-scatter.1
  675.8 142.3 all-reduce.3
where the time goes:
time: 844 us; the launch traced here: 829 us
  blocking collectives  342 us (41%)
  waiting for transfers between devices  183 us (22%)
  matrix products  144 us (17%)
  other arithmetic  70.1 us (8%)
  local copies, waits for them, and re-layouts  59.2 us (7%)
  between operations  16 us (2%)
  starting transfers between devices  13.9 us (2%)
    psum x1, blocking collectives, on_device(): summed = lax.psum((terms[0], terms[1], terms[2], terms[3]), ('slab', 'wsh'))  302 us
    psum x1, waiting for transfers between devices, on_device(): summed = lax.psum((terms[0], terms[1], terms[2], terms[3]), ('slab', 'wsh'))  139 us
    dot_general x7, matrix products, backward_step(): jnp.einsum('gs,gcd->scd', selector.astype(jnp.float32), terms, precision=...  76.5 us
    all_gather x1, waiting for transfers between devices, on_device(): slab_sources = lax.all_gather(local_sources, 'wsh', axis=0, tiled=True)  33.9 us
    dot_general x7, matrix products, forward_step(): jnp.einsum('gs,sbd->gbd', selector.astype(jnp.bfloat16), source_blocks, p...  26.3 us
    reduce_sum x14, other arithmetic, dense_tiles(): return jnp.sum(weights[..., None] * matches, axis=1)  19.5 us
  transfers between devices with their start and end apart: 7, of which 5 were waited for; matrix products, arithmetic and copies ran while one was open for 2% of the time, Pallas kernels for 0%

commit v1 on v0

v1 whole, which is shorter than its diff:
```python
import functools

import jax
import jax.numpy as jnp
from jax import lax
from jax.experimental import pallas as pl
from jax.experimental.pallas import tpu as pltpu
from jax.sharding import PartitionSpec as P

F32 = jnp.float32
BF16 = jnp.bfloat16
SIDE = 128
UNROLL = 4
PARAMS = pltpu.CompilerParams(vmem_limit_bytes=48 * 2**20)
VMEM = pl.BlockSpec(memory_space=pltpu.VMEM)
SMEM = pl.BlockSpec(memory_space=pltpu.SMEM)


def dot(left, right, dims):
    return lax.dot_general(left, right, (dims, ((), ())), preferred_element_type=F32)


def rows_by_cols(left, right):
    return dot(left, right, ((1,), (0,)))


def contract_rows(left, right):
    return dot(left, right, ((0,), (0,)))


def contract_cols(left, right):
    return dot(left, right, ((1,), (1,)))


def sigmoid(v):
    return 1.0 / (1.0 + jnp.exp(-v))


def silu_slope(v):
    g = sigmoid(v)
    return g * (1.0 + v * (1.0 - g))


def pick_kernel(rows_ref, count_ref, feat_ref, out_ref, wide, picked):
    halo = rows_ref.shape[1]
    wide[...] = feat_ref[...].astype(F32)
    group = 16
    for k in range(2):
        count = count_ref[k]

        def body(step, carry):
            for u in range(group):
                slot = step * group + u
                row = rows_ref[k, slot]
                picked[pl.ds(slot, 1), :] = wide[pl.ds(row, 1), :]
            return carry

        lax.fori_loop(0, (count + group - 1) // group, body, 0)
        slots = lax.broadcasted_iota(jnp.int32, (halo, SIDE), 0)
        kept = jnp.where(slots < count, picked[...], 0.0)
        out_ref[pl.ds(k * halo, halo), :] = kept.astype(BF16)


def pick_rows(halo_rows, halo_count, node_feat):
    halo = halo_rows.shape[1]
    return pl.pallas_call(
        pick_kernel,
        out_shape=jax.ShapeDtypeStruct((2 * halo, SIDE), BF16),
        in_specs=[SMEM, SMEM, VMEM],
        out_specs=VMEM,
        scratch_shapes=[pltpu.VMEM(node_feat.shape, F32), pltpu.VMEM((halo, SIDE), F32)],
        compiler_params=PARAMS,
        name="pick_rows",
    )(halo_rows, halo_count, node_feat)


def list_kernel(parties, own_blocks, here_blocks, pos_ref, dst_ref, src_ref, count_ref, list_ref, total_ref):
    slots = dst_ref.shape[1]
    me = pos_ref[0]
    group = 8
    for k in range(parties):
        device = lax.rem(me + k, parties)
        count = count_ref[k]

        def body(step, carry):
            own, rim = carry
            for u in range(group):
                slot = step * group + u
                block = src_ref[k, slot] - me * here_blocks
                used = (slot < count) & (block >= 0) & (block < here_blocks)
                is_own = block < own_blocks
                base = device * slots + slot + (dst_ref[k, slot] << 16)
                list_ref[2 * k, own] = base + (block << 10)
                list_ref[2 * k + 1, rim] = base + ((block - own_blocks) << 10)
                own = own + jnp.where(used & is_own, 1, 0)
                rim = rim + jnp.where(used & jnp.logical_not(is_own), 1, 0)
            return (own, rim)

        own, rim = lax.fori_loop(0, slots // group, body, (jnp.int32(0), jnp.int32(0)))
        total_ref[2 * k] = own
        total_ref[2 * k + 1] = rim


def build_lists(position, dst, src, count, own_blocks, here_blocks):
    parties, slots = dst.shape
    return pl.pallas_call(
        functools.partial(list_kernel, parties, own_blocks, here_blocks),
        out_shape=(
            jax.ShapeDtypeStruct((2 * parties, slots + 16), jnp.int32),
            jax.ShapeDtypeStruct((2 * parties,), jnp.int32),
        ),
        in_specs=[SMEM] * 4,
        out_specs=(SMEM, SMEM),
        name="tile_lists",
    )(position, dst, src, count)


def dense_tile(tile, keep):
    column = lax.broadcasted_iota(jnp.int32, (SIDE, SIDE), 0).astype(F32)
    entries = tile.shape[0] // 2
    total = None
    for e in range(entries):
        weight = tile[e : e + 1, :] * keep
        term = jnp.where(column == tile[entries + e : entries + e + 1, :], weight, 0.0)
        total = term if total is None else total + term
    return total.astype(BF16)


def walk_list(list_ref, total_ref, which, tiles_ref, product, acc):
    count = total_ref[which]

    def body(step, carry):
        found = []
        for u in range(UNROLL):
            index = step * UNROLL + u
            used = index < count
            entry = jnp.where(used, list_ref[which, index], 0)
            dense = dense_tile(tiles_ref[entry & 1023], jnp.where(used, 1.0, 0.0))
            found.append(product(dense, (entry >> 10) & 63, entry >> 16))
        for target, value in found:
            acc[target] += value
        return carry

    lax.fori_loop(0, (count + UNROLL - 1) // UNROLL, body, 0)


def forward_kernel(ks, list_ref, total_ref, tiles_ref, own_ref, lower_ref, upper_ref, *rest):
    outs, (acc, rims) = rest[: len(ks)], rest[len(ks) :]
    half = lower_ref.shape[0]
    rims[pl.ds(0, half)] = lower_ref[...]
    rims[pl.ds(half, half)] = upper_ref[...]
    for k, out_ref in zip(ks, outs):
        acc[...] = jnp.zeros_like(acc)
        for part, ref in enumerate((own_ref, rims)):

            def product(dense, block, target, ref=ref):
                return (target, contract_rows(dense, ref[block]))

            walk_list(list_ref, total_ref, 2 * k + part, tiles_ref, product, acc)
        out_ref[...] = acc[...].astype(out_ref.dtype)


def forward_tiles(ks, lists, totals, tiles, own, lower, upper, kinds):
    return pl.pallas_call(
        functools.partial(forward_kernel, ks),
        out_shape=tuple(jax.ShapeDtypeStruct(own.shape, kind) for kind in kinds),
        in_specs=[SMEM, SMEM] + [VMEM] * 4,
        out_specs=tuple(VMEM for _ in ks),
        scratch_shapes=[
            pltpu.VMEM(own.shape, F32),
            pltpu.VMEM((2 * lower.shape[0],) + lower.shape[1:], BF16),
        ],
        compiler_params=PARAMS,
        cost_estimate=pl.CostEstimate(
            flops=60_000_000 * len(ks), bytes_accessed=4_000_000 * len(ks), transcendentals=0
        ),
        name="forward_tiles",
    )(lists, totals, tiles, own, lower, upper)


def node_kernel(
    feat_ref, cot_ref, a0_ref, a1_ref, a2_ref, a3_ref, in_ref, out_w_ref, gain_ref,
    node_ref, dagg_ref, dhid_ref, dwin_ref, dwout_ref, dgain_ref,
):
    @pl.when(pl.program_id(0) == 0)
    def _():
        dwin_ref[...] = jnp.zeros_like(dwin_ref)
        dwout_ref[...] = jnp.zeros_like(dwout_ref)
        dgain_ref[...] = jnp.zeros_like(dgain_ref)

    feat = feat_ref[...]
    agg = a0_ref[...] + a1_ref[...].astype(F32) + a2_ref[...].astype(F32) + a3_ref[...].astype(F32)
    agg = agg.astype(BF16)
    w_feat, w_agg, w_out = in_ref[:SIDE, :], in_ref[SIDE:, :], out_w_ref[...]
    gain = gain_ref[...].astype(F32)
    pre = rows_by_cols(feat, w_feat) + rows_by_cols(agg, w_agg)
    logistic = sigmoid(pre)
    hidden = (pre * logistic).astype(BF16)
    slope = logistic * (1.0 + pre * (1.0 - logistic))
    update = rows_by_cols(hidden, w_out)
    centre = update - jnp.mean(update, axis=-1, keepdims=True)
    inverse = lax.rsqrt(jnp.mean(centre * centre, axis=-1, keepdims=True) + 1e-05)
    normed = centre * inverse
    node_ref[...] = (feat.astype(F32) + gain * normed).astype(BF16)
    upstream = cot_ref[...].astype(F32)
    d_normed = upstream * gain
    dgain_ref[...] += jnp.sum(upstream * normed, axis=0, keepdims=True)
    d_update = (
        d_normed
        - jnp.mean(d_normed, axis=-1, keepdims=True)
        - normed * jnp.mean(d_normed * normed, axis=-1, keepdims=True)
    ) * inverse
    d_update = d_update.astype(BF16)
    d_hidden = (contract_cols(d_update, w_out) * slope).astype(BF16)
    dhid_ref[...] = d_hidden
    dagg_ref[...] = contract_cols(d_hidden, w_agg).astype(BF16)
    dwout_ref[...] += contract_rows(hidden, d_update)
    dwin_ref[:SIDE, :] += contract_rows(feat, d_hidden)
    dwin_ref[SIDE:, :] += contract_rows(agg, d_hidden)


def node_update(node_feat, cotangent, parts, w_in, w_out, gain):
    rows = node_feat.shape[0]
    steps = 8
    tall = pl.BlockSpec((rows // steps, SIDE), lambda i: (i, 0))

    def whole(shape):
        return pl.BlockSpec(shape, lambda i: (0, 0))

    wide = jax.ShapeDtypeStruct((rows, SIDE), BF16)
    return pl.pallas_call(
        node_kernel,
        grid=(steps,),
        out_shape=(
            wide,
            wide,
            wide,
            jax.ShapeDtypeStruct((2 * SIDE, SIDE), F32),
            jax.ShapeDtypeStruct((SIDE, SIDE), F32),
            jax.ShapeDtypeStruct((1, SIDE), F32),
        ),
        in_specs=[tall] * 6 + [whole((2 * SIDE, SIDE)), whole((SIDE, SIDE)), whole((1, SIDE))],
        out_specs=(tall, tall, tall, whole((2 * SIDE, SIDE)), whole((SIDE, SIDE)), whole((1, SIDE))),
        compiler_params=PARAMS,
        name="node_update",
    )(node_feat, cotangent, *parts, w_in, w_out, gain)


def backward_kernel(part, list_ref, total_ref, tiles_ref, g0_ref, g1_ref, g2_ref, g3_ref, out_ref, acc):
    acc[...] = jnp.zeros_like(acc)
    for k, ref in enumerate((g0_ref, g1_ref, g2_ref, g3_ref)):

        def product(dense, block, target, ref=ref):
            return (block, rows_by_cols(dense, ref[target]))

        walk_list(list_ref, total_ref, 2 * k + part, tiles_ref, product, acc)
    out_ref[...] = acc[...].astype(out_ref.dtype)


def backward_tiles(part, blocks, kind, lists, totals, tiles, grads):
    shape = (blocks, SIDE, SIDE)
    return pl.pallas_call(
        functools.partial(backward_kernel, part),
        out_shape=jax.ShapeDtypeStruct(shape, kind),
        in_specs=[SMEM, SMEM] + [VMEM] * 5,
        out_specs=VMEM,
        scratch_shapes=[pltpu.VMEM(shape, F32)],
        compiler_params=PARAMS,
        cost_estimate=pl.CostEstimate(flops=100_000_000, bytes_accessed=8_000_000, transcendentals=0),
        name="backward_tiles",
    )(lists, totals, tiles, *grads)


def last_kernel(
    pos_ref, rows_ref, count_ref, feat_ref, cot_ref, dhid_ref, own_ref, lower_ref, upper_ref, msg_ref, in_ref,
    dwin_ref, dwout_ref, dgain_ref,
    dnode_ref, r0_ref, r1_ref, r2_ref, r3_ref, acc, back, dw,
):
    halo = rows_ref.shape[1]
    acc[...] = own_ref[...]
    group = 8
    for k, ref in enumerate((lower_ref, upper_ref)):
        count = count_ref[k]
        slots = lax.broadcasted_iota(jnp.int32, (halo, SIDE), 0)
        back[...] = jnp.where(slots < count, ref[...].astype(F32), 0.0)

        def body(step, carry):
            rows = [rows_ref[k, step * group + u] for u in range(group)]
            added = [
                acc[pl.ds(row, 1), :] + back[pl.ds(step * group + u, 1), :] for u, row in enumerate(rows)
            ]
            for row, value in zip(rows, added):
                acc[pl.ds(row, 1), :] = value
            return carry

        lax.fori_loop(0, (count + group - 1) // group, body, 0)
    w_msg, w_feat = msg_ref[...], in_ref[:SIDE, :]
    dw[...] = jnp.zeros_like(dw)
    chunk = 512

    def step_rows(step, carry):
        at = pl.ds(pl.multiple_of(step * chunk, chunk), chunk)
        feat = feat_ref[at, :]
        d_pre = (acc[at, :] * silu_slope(rows_by_cols(feat, w_msg))).astype(BF16)
        dw[...] += contract_rows(feat, d_pre)
        total = cot_ref[at, :].astype(F32) + contract_cols(dhid_ref[at, :], w_feat)
        dnode_ref[at, :] = (total + contract_cols(d_pre, w_msg)).astype(BF16)
        return carry

    lax.fori_loop(0, acc.shape[0] // chunk, step_rows, 0)
    outs = (r0_ref, r1_ref, r2_ref, r3_ref)
    share = SIDE // len(outs)
    for k, out in enumerate(outs):
        device = lax.rem(pos_ref[0] + k, len(outs))
        start = pl.multiple_of(device * share, share)
        out[pl.ds(0, share), :] = dw[pl.ds(start, share), :]
        out[pl.ds(share, 2 * share), :] = dwin_ref[pl.ds(2 * start, 2 * share), :]
        out[pl.ds(3 * share, share), :] = dwout_ref[pl.ds(start, share), :]
        out[pl.ds(4 * share, 8), :] = jnp.broadcast_to(dgain_ref[...], (8, SIDE))


def last_products(position, halo_rows, halo_count, feat, cot, dhid, own, lower, upper, w_msg, w_in, dwin, dwout, dgain):
    rows = feat.shape[0]
    piece = jax.ShapeDtypeStruct((SIDE + 8, SIDE), F32)
    return pl.pallas_call(
        last_kernel,
        out_shape=(jax.ShapeDtypeStruct((rows, SIDE), BF16), piece, piece, piece, piece),
        in_specs=[SMEM] * 3 + [VMEM] * 11,
        out_specs=(VMEM,) * 5,
        scratch_shapes=[
            pltpu.VMEM((rows, SIDE), F32),
            pltpu.VMEM((halo_rows.shape[1], SIDE), F32),
            pltpu.VMEM((SIDE, SIDE), F32),
        ],
        compiler_params=PARAMS,
        name="last_products",
    )(position, halo_rows, halo_count, feat, cot, dhid, own, lower, upper, w_msg, w_in, dwin, dwout, dgain)


def shift_wsh(value, step):
    parties = lax.axis_size("wsh")
    return lax.ppermute(value, "wsh", [(i, (i + step) % parties) for i in range(parties)])


def shift_slab(value, step):
    count = lax.axis_size("slab")
    pairs = [(i, i + step) for i in range(count) if 0 <= i + step < count]
    return lax.ppermute(value, "slab", pairs)


def sum_slab(value):
    count = lax.axis_size("slab")
    for stride, size in ((8, 4), (2, 4), (1, 2)):
        total = value
        for k in range(1, size):
            span = stride * size
            pairs = [(i, (i // span) * span + (i + stride * k) % span) for i in range(count)]
            total = total + lax.ppermute(value, "slab", pairs)
        value = total
    return value


def on_device(
    node_feat, cotangent, w_msg, w_in, w_out, ln_gain,
    tile_values, tile_cols, tile_dst, tile_src, tile_count, halo_rows, halo_count,
):
    node_rows = node_feat.shape[0]
    slots, entries, side = tile_values.shape
    halo = halo_rows.shape[2]
    parties = lax.axis_size("wsh")
    me = lax.axis_index("wsh").astype(jnp.int32)
    position = me.reshape(1)
    share = w_msg.shape[0]
    own_blocks = node_rows // side
    rim_blocks = 2 * halo // side

    packed_tiles = jnp.concatenate([tile_values, tile_cols.astype(BF16)], axis=1)
    all_tiles = lax.all_gather(packed_tiles, "wsh", axis=0, tiled=True)

    gain_row = jnp.pad(ln_gain.reshape(1, share), ((0, 0), (0, side - share)))
    extras = jnp.concatenate(
        [
            gain_row,
            tile_dst.astype(BF16).reshape(1, side),
            tile_src.astype(BF16).reshape(1, side),
            jnp.broadcast_to(tile_count.astype(BF16).reshape(1, 1), (1, side)),
            jnp.zeros((12, side), BF16),
        ],
        axis=0,
    )
    small = jnp.concatenate([w_msg, w_in, w_out, extras], axis=0)
    arrived = [small] + [shift_wsh(small, -k) for k in range(1, parties)]
    relative = jnp.stack(arrived)
    absolute = lax.dynamic_slice_in_dim(
        jnp.concatenate([relative, relative], axis=0), lax.rem(parties - me, parties), parties, 0
    )
    full_msg = absolute[:, :share].reshape(4 * share, side)
    full_in = absolute[:, share : 3 * share].reshape(8 * share, side)
    full_out = absolute[:, 3 * share : 4 * share].reshape(4 * share, side)
    full_gain = absolute[:, 4 * share, :share].reshape(1, side)
    meta = relative[:, 4 * share + 1 : 4 * share + 4].astype(jnp.int32)
    dst, src, count = meta[:, 0], meta[:, 1], meta[:, 2, 0]

    rows = halo_rows.reshape(2, halo)
    counts = halo_count.reshape(2)
    picked = pick_rows(rows, counts, node_feat)
    outgoing = jax.nn.silu(rows_by_cols(picked, full_msg)).astype(BF16)
    lower = shift_slab(outgoing[halo:], 1)
    upper = shift_slab(outgoing[:halo], -1)
    message = jax.nn.silu(rows_by_cols(node_feat, full_msg)).astype(BF16)
    lists, totals = build_lists(position, dst, src, count, own_blocks, own_blocks + rim_blocks)
    tiles = all_tiles.astype(F32)

    blocks = message.reshape(own_blocks, side, side)
    lower = lower.reshape(rim_blocks // 2, side, side)
    upper = upper.reshape(rim_blocks // 2, side, side)
    (p2,) = forward_tiles((2,), lists, totals, tiles, blocks, lower, upper, (BF16,))
    a2 = shift_wsh(p2, 2)
    p1, p3 = forward_tiles((1, 3), lists, totals, tiles, blocks, lower, upper, (BF16, BF16))
    a1 = shift_wsh(p1, 1)
    a3 = shift_wsh(p3, 3)
    (p0,) = forward_tiles((0,), lists, totals, tiles, blocks, lower, upper, (F32,))
    parts = [part.reshape(node_rows, side) for part in (p0, a1, a2, a3)]

    node_out, d_agg, d_hidden, d_w_in, d_w_out, d_gain = node_update(
        node_feat, cotangent, parts, full_in, full_out, full_gain
    )
    grads = [d_agg] + [shift_wsh(d_agg, -k) for k in range(1, parties)]
    grads = [grad.reshape(own_blocks, side, side) for grad in grads]
    d_rims = backward_tiles(1, rim_blocks, BF16, lists, totals, tiles, grads).reshape(2 * halo, side)
    back_upper = shift_slab(d_rims[:halo], -1)
    back_lower = shift_slab(d_rims[halo:], 1)
    d_own = backward_tiles(0, own_blocks, F32, lists, totals, tiles, grads).reshape(node_rows, side)
    d_node, *pieces = last_products(
        position, rows, counts, node_feat, cotangent, d_hidden, d_own, back_lower, back_upper, full_msg, full_in,
        d_w_in, d_w_out, d_gain,
    )
    total = pieces[0]
    for k in range(1, parties):
        total = total + shift_wsh(pieces[k], k)
    total = sum_slab(total)
    gain_share = lax.dynamic_slice_in_dim(total[4 * share], me * share, share, 0)
    return (
        node_out, d_node, total[:share], total[share : 3 * share], total[3 * share : 4 * share], gain_share,
    )


def solution(mesh):
    both = ("slab", "wsh")
    tall, split, line = P(both, None), P("wsh", None), P(both)
    cube = P(both, None, None)
    return jax.shard_map(
        on_device,
        mesh=mesh,
        in_specs=(
            tall, tall, split, split, split, P("wsh"), cube, cube, line, line, line, cube, tall,
        ),
        out_specs=(tall, tall, split, split, split, P("wsh")),
        check_vma=False,
    )
```

time: 844 us -> 234 us (0.28); the launches traced: 829 us -> 233 us
  blocking collectives: 342 us -> 0 us
  matrix products: 144 us -> 1.18 us
  waiting for transfers between devices: 183 us -> 91.2 us
  other arithmetic: 70.1 us -> 4.88 us
  Pallas kernels: 0 us -> 52.5 us
  local copies, waits for them, and re-layouts: 59.2 us -> 17.9 us
  starting transfers between devices: 13.9 us -> 50.4 us
    psum x1 -> x0, blocking collectives: 302 us -> none  [on_device(): summed = lax.psum((terms[0], terms[1], terms[2], terms[3]), ('slab', 'wsh'))]
    dot_general x54 -> x2, matrix products: 144 us -> 1.18 us  [dot(): lax.dot_general(left, right, (dims, ((), ())), preferred_element_type=F32)]
    psum x1 -> x0, waiting for transfers between devices: 139 us -> none  [on_device(): summed = lax.psum((terms[0], terms[1], terms[2], terms[3]), ('slab', 'wsh'))]
    ppermute x4 -> x23, waiting for transfers between devices: 10.3 us -> 91.1 us  [the longest x12 87.2 us: shift_wsh(): lax.ppermute(value, 'wsh', [(i, (i + step) % parties) for i in range(part...]
    pallas_call x0 -> x9, Pallas kernels: none -> 52.5 us  [the longest x1 10.9 us: last_products(): pl.pallas_call(last_kernel, out_shape=(jax.ShapeDtypeStruct((rows, SIDE),...]
    ppermute x4 -> x23, starting transfers between devices: 13.8 us -> 50.4 us  [the longest x12 18.1 us: shift_wsh(): lax.ppermute(value, 'wsh', [(i, (i + step) % parties) for i in range(part...]
    all_gather x1, waiting for transfers between devices: 33.9 us -> 0.02 us  [on_device(): all_tiles = lax.all_gather(packed_tiles, 'wsh', axis=0, tiled=True)]
    all_gather x3 -> x0, blocking collectives: 31.8 us -> none  [the longest x1 11.5 us: on_device(): lax.all_gather(w_msg, 'wsh', axis=0, tiled=True)]
  transfers between devices with their start and end apart: 7 -> 24, of which waited for: 5 -> 13; matrix products, arithmetic and copies ran while one was open for 2% -> 7% of each run, Pallas kernels for 0% -> 9%
where the time goes in v1:
time: 234 us; the launch traced here: 233 us
  waiting for transfers between devices  91.2 us (39%)
  Pallas kernels  52.5 us (22%)
  starting transfers between devices  50.4 us (22%)
  local copies, waits for them, and re-layouts  17.9 us (8%)
  between operations  15.1 us (6%)
  other arithmetic  4.88 us (2%)
    ppermute x12, waiting for transfers between devices, shift_wsh(): lax.ppermute(value, 'wsh', [(i, (i + step) % parties) for i in range(part...  87.2 us
    ppermute x12, starting transfers between devices, shift_wsh(): lax.ppermute(value, 'wsh', [(i, (i + step) % parties) for i in range(part...  18.1 us
    ppermute x7, starting transfers between devices, sum_slab(): total = total + lax.ppermute(value, 'slab', pairs)  17.7 us
    ppermute x4, starting transfers between devices, shift_slab(): return lax.ppermute(value, 'slab', pairs)  14.6 us
    pallas_call x1, Pallas kernels, last_products(): pl.pallas_call(last_kernel, out_shape=(jax.ShapeDtypeStruct((rows, SIDE),...  10.9 us
    pallas_call x3, Pallas kernels, forward_tiles(): pl.pallas_call(functools.partial(forward_kernel, ks), out_shape=tuple((ja...  10.8 us
    pallas_call x1, Pallas kernels, node_update(): pl.pallas_call(node_kernel, grid=(steps,), out_shape=(wide, wide, wide, j...  9.89 us
    pallas_call x2, Pallas kernels, backward_tiles(): pl.pallas_call(functools.partial(backward_kernel, part), out_shape=jax.Sh...  8.56 us
  transfers between devices with their start and end apart: 24, of which 13 were waited for; matrix products, arithmetic and copies ran while one was open for 7% of the time, Pallas kernels for 9%

profile of v1, /device:TPU:1, one launch (start us, length us, event | category | flops | bytes accessed | tf_op | source)
XLA Modules:
  0.0 233.1 jit_solution(7680805237638225370)
XLA Ops:
  9.3 2.3 concatenate.10
  11.6 4.7 %collective-permute-start = (bf16[144,128]{1,0:T(8,128)(2,1)S(1)}, bf16[144,128]{1,0:T(8,128)(2,1)S(1)}, u32[]{:S(2)}, u32[]{:S(2)}) collective-permute-start(bf16[144,128]{1,0:T(8,128)(2,1)S(1)} %concatenate.10), channel_id=1, source_target_pairs={{0,3},{1,0},{2,1},{3,2},{4,7},{5,4},{6,5},{7,6},{8,11},{9,8},{10,9... | collective-permute-start | bytes 110600 | tf_op jit(solution)/shard_map/ppermute | solution.py:342
  21.8 4.4 %pick_rows.1 = bf16[2048,128]{1,0:T(8,128)(2,1)S(1)} custom-call(s32[2,1024]{1,0:T(2,128)S(1)} %bitcast.73, s32[2]{0:T(128)S(1)} %bitcast.75, bf16[4096,128]{1,0:T(8,128)(2,1)S(1)} %copy-done.1), custom_call_target="tpu_custom_call" | custom-call | tf_op jit(solution)/shard_map/pick_rows/pallas_call | solution.py:66
  32.5 4.8 %collective-permute-start.3 = (bf16[1024,128]{1,0:T(8,128)(2,1)}, bf16[1024,128]{1,0:T(8,128)(2,1)S(1)}, u32[]{:S(2)}, u32[]{:S(2)}) collective-permute-start(bf16[1024,128]{1,0:T(8,128)(2,1)} %get-tuple-element.39), channel_id=1, source_target_pairs={{0,4},{4,8},{8,12},{12,16},{16,20},{20,24},{24,28},{28,32},{32,36}... | collective-permute-start | bytes 786440 | tf_op jit(solution)/shard_map/ppermute | solution.py:348
  42.2 7.9 %tile_lists.1 = (s32[8,144]{1,0:T(8,128)}, s32[8]{0:T(128)}) custom-call(s32[1]{0:T(128)} %bitcast.pos_ref, s32[4,128]{1,0:T(4,128)} %get-tuple-element.45.dst_ref, s32[4,128]{1,0:T(4,128)} %get-tuple-element.44.src_ref, s32[4]{0:T(128)} %slice_reduce_fusion.count_ref), custom_call_target="tpu_custom_call" | custom-call | tf_op jit(solution)/shard_map/tile_lists/pallas_call | solution.py:106
  51.6 3.6 %forward_tiles.5 = bf16[32,128,128]{2,1,0:T(8,128)(2,1)} custom-call(s32[8,144]{1,0:T(8,128)S(1)} %copy-done.5, s32[8]{0:T(128)S(1)} %copy-done.8, f32[512,8,128]{2,1,0:T(8,128)S(1)} %convert_element_type.31.tiles_ref, bf16[32,128,128]{2,1,0:T(8,128)(2,1)S(1)} %bitcast.52, bf16[8,128,128]{2,1,0:T(8,128)(2,1)S(1)} %bitcast.64, ...), custom_call_target="tpu_custom_call" | custom-call | flops 60000000 | bytes 4000000 | tf_op jit(solution)/shard_map/forward_tiles/pallas_call | solution.py:164
  55.2 4.9 %forward_tiles.4 = (bf16[32,128,128]{2,1,0:T(8,128)(2,1)}, bf16[32,128,128]{2,1,0:T(8,128)(2,1)}) custom-call(s32[8,144]{1,0:T(8,128)S(1)} %copy-done.5, s32[8]{0:T(128)S(1)} %copy-done.8, f32[512,8,128]{2,1,0:T(8,128)S(1)} %convert_element_type.31.tiles_ref, bf16[32,128,128]{2,1,0:T(8,128)(2,1)S(1)} %bitcast.53, bf16[8,128,128]{2,1,0:T(8,128)(2,1)S(1)} %bitcast.65, ...), custom_call_target="tpu_custom_call" | custom-call | flops 120000000 | bytes 8000000 | tf_op jit(solution)/shard_map/forward_tiles/pallas_call | solution.py:164
  60.1 2.8 %collective-permute-start.6 = (bf16[32,128,128]{2,1,0:T(8,128)(2,1)}, bf16[32,128,128]{2,1,0:T(8,128)(2,1)}, u32[]{:S(2)}, u32[]{:S(2)}) collective-permute-start(bf16[32,128,128]{2,1,0:T(8,128)(2,1)} %forward_tiles.5), channel_id=1, source_target_pairs={{0,2},{1,3},{2,0},{3,1},{4,6},{5,7},{6,4},{7,5},{8,10},{9,11},{10,... | collective-permute-start | bytes 3145736 | tf_op jit(solution)/shard_map/ppermute | solution.py:342
  63.6 2.4 %collective-permute-start.7 = (bf16[32,128,128]{2,1,0:T(8,128)(2,1)}, bf16[32,128,128]{2,1,0:T(8,128)(2,1)}, u32[]{:S(2)}, u32[]{:S(2)}) collective-permute-start(bf16[32,128,128]{2,1,0:T(8,128)(2,1)} %get-tuple-element.24), channel_id=1, source_target_pairs={{0,3},{1,0},{2,1},{3,2},{4,7},{5,4},{6,5},{7,6},{8,11},{9,8},{10,9... | collective-permute-start | bytes 3145736 | tf_op jit(solution)/shard_map/ppermute | solution.py:342
  67.6 2.3 forward_tiles.3
  71.3 15.6 %collective-permute-done.6 = bf16[32,128,128]{2,1,0:T(8,128)(2,1)} collective-permute-done((bf16[32,128,128]{2,1,0:T(8,128)(2,1)}, bf16[32,128,128]{2,1,0:T(8,128)(2,1)}, u32[]{:S(2)}, u32[]{:S(2)}) %collective-permute-start.6) | collective-permute-done | bytes 1048608 | tf_op jit(solution)/shard_map/ppermute | solution.py:342
  86.9 22.5 %collective-permute-done.5 = bf16[32,128,128]{2,1,0:T(8,128)(2,1)} collective-permute-done((bf16[32,128,128]{2,1,0:T(8,128)(2,1)}, bf16[32,128,128]{2,1,0:T(8,128)(2,1)}, u32[]{:S(2)}, u32[]{:S(2)}) %collective-permute-start.5) | collective-permute-done | bytes 1048608 | tf_op jit(solution)/shard_map/ppermute | solution.py:342
  109.4 9.9 %node_update.1 = (bf16[4096,128]{1,0:T(8,128)(2,1)}, bf16[4096,128]{1,0:T(8,128)(2,1)S(1)}, bf16[4096,128]{1,0:T(8,128)(2,1)S(1)}, f32[256,128]{1,0:T(8,128)S(1)...) custom-call(bf16[4096,128]{1,0:T(8,128)(2,1)S(1)} %copy-done.2, bf16[4096,128]{1,0:T(8,128)(2,1)S(1)} %copy-done.4, ...), custom_call_target="tpu_custom_call" | custom-call | tf_op jit(solution)/shard_map/node_update/pallas_call | solution.py:231
  119.6 2.3 collective-permute-start.9
  121.8 21.8 %collective-permute-done.8 = bf16[4096,128]{1,0:T(8,128)(2,1)S(1)} collective-permute-done((bf16[4096,128]{1,0:T(8,128)(2,1)S(1)}, bf16[4096,128]{1,0:T(8,128)(2,1)S(1)}, u32[]{:S(2)}, u32[]{:S(2)}) %collective-permute-start.8) | collective-permute-done | bytes 1048608 | tf_op jit(solution)/shard_map/ppermute | solution.py:342
  145.1 23.5 %collective-permute-done.10 = bf16[4096,128]{1,0:T(8,128)(2,1)S(1)} collective-permute-done((bf16[4096,128]{1,0:T(8,128)(2,1)S(1)}, bf16[4096,128]{1,0:T(8,128)(2,1)S(1)}, u32[]{:S(2)}, u32[]{:S(2)}) %collective-permute-start.10) | collective-permute-done | bytes 1048608 | tf_op jit(solution)/shard_map/ppermute | solution.py:342
  168.6 3.1 %backward_tiles.3 = bf16[16,128,128]{2,1,0:T(8,128)(2,1)S(1)} custom-call(s32[8,144]{1,0:T(8,128)S(1)} %copy-done.5, s32[8]{0:T(128)S(1)} %copy-done.8, f32[512,8,128]{2,1,0:T(8,128)} %copy-done, bf16[32,128,128]{2,1,0:T(8,128)(2,1)S(1)} %bitcast.56, bf16[32,128,128]{2,1,0:T(8,128)(2,1)S(1)} %bitcast.58, bf16[32,128,128]{2,1,0:T(8,128)(2,1)S(1)} %bitcast.60, ...), custom_call_target="tpu_custom_call" | custom-call | flops 100000000 | bytes 8000000 | tf_op jit(solution)/shard_map/backward_tiles/pallas_call | solution.py:262
  171.8 6.0 %collective-permute-start.11 = (bf16[1024,128]{1,0:T(8,128)(2,1)S(1)}, bf16[1024,128]{1,0:T(8,128)(2,1)S(1)}, u32[]{:S(2)}, u32[]{:S(2)}) collective-permute-start(bf16[1024,128]{1,0:T(8,128)(2,1)S(1)} %bitcast.83), channel_id=1, source_target_pairs={{0,4},{4,8},{8,12},{12,16},{16,20},{20,24},{24,28},{28,32},{32,36}... | collective-permute-start | bytes 786440 | tf_op jit(solution)/shard_map/ppermute | solution.py:348
  179.7 5.5 %backward_tiles.2 = f32[32,128,128]{2,1,0:T(8,128)} custom-call(s32[8,144]{1,0:T(8,128)S(1)} %copy-done.5, s32[8]{0:T(128)S(1)} %copy-done.8, f32[512,8,128]{2,1,0:T(8,128)} %copy-done, bf16[32,128,128]{2,1,0:T(8,128)(2,1)S(1)} %bitcast.57, bf16[32,128,128]{2,1,0:T(8,128)(2,1)S(1)} %bitcast.59, bf16[32,128,128]{2,1,0:T(8,128)(2,1)S(1)} %bitcast.61, ...), custom_call_target="tpu_custom_call" | custom-call | flops 100000000 | bytes 8000000 | tf_op jit(solution)/shard_map/backward_tiles/pallas_call | solution.py:262
  185.5 10.9 %last_products.1 = (bf16[4096,128]{1,0:T(8,128)(2,1)}, f32[136,128]{1,0:T(8,128)S(1)}, f32[136,128]{1,0:T(8,128)S(1)}, f32[136,128]{1,0:T(8,128)S(1)}, f32[136,128]{1,0:T(8,128)S(1)}) custom-call(s32[1]{0:T(128)} %bitcast.pos_ref, s32[2,1024]{1,0:T(2,128)S(1)} %bitcast.74, s32[2]{0:T(128)S(1)} %bitcast.76, bf16[4096,128]{1,0:T(8,128)(2,1)S(1)} %copy-done.2, ...), custom_call_target="tpu_custom_call" | custom-call | tf_op jit(solution)/shard_map/last_products/pallas_call | solution.py:325
  200.8 2.2 collective-permute-done.14
  203.7 2.3 collective-permute-start.17
  211.1 4.5 %collective-permute-start.20 = (f32[136,128]{1,0:T(8,128)S(1)}, f32[136,128]{1,0:T(8,128)S(1)}, u32[]{:S(2)}, u32[]{:S(2)}) collective-permute-start(f32[136,128]{1,0:T(8,128)S(1)} %add_add_fusion.1), channel_id=1, source_target_pairs={{0,16},{4,20},{8,24},{12,28},{16,0},{20,4},{24,8},{28,12},{32,48},... | collective-permute-start | bytes 208904 | tf_op jit(solution)/shard_map/ppermute | solution.py:358
  219.0 4.4 %collective-permute-start.22 = (f32[136,128]{1,0:T(8,128)S(1)}, f32[136,128]{1,0:T(8,128)S(1)}, u32[]{:S(2)}, u32[]{:S(2)}) collective-permute-start(f32[136,128]{1,0:T(8,128)S(1)} %add_add_fusion), channel_id=1, source_target_pairs={{0,4},{4,0},{8,12},{12,8},{16,20},{20,16},{24,28},{28,24},{32,36},... | collective-permute-start | bytes 208904 | tf_op jit(solution)/shard_map/ppermute | solution.py:358
  (96 shorter events, 43.6 us)
Async XLA Ops:
  7.2 43.0 %all-gather.2.cloned.1.call-start = ((), (), s32[]{:S(2)}) async-start(), calls=%async_computation | async-start | bytes 1310720 | tf_op jit(solution)/shard_map/all_gather | solution.py:378
  11.6 14.6 %collective-permute-start = (bf16[144,128]{1,0:T(8,128)(2,1)S(1)}, bf16[144,128]{1,0:T(8,128)(2,1)S(1)}, u32[]{:S(2)}, u32[]{:S(2)}) collective-permute-start(bf16[144,128]{1,0:T(8,128)(2,1)S(1)} %concatenate.10), channel_id=1, source_target_pairs={{0,3},{1,0},{2,1},{3,2},{4,7},{5,4},{6,5},{7,6},{8,11},{9,8},{10,9... | collective-permute-start | bytes 110600 | tf_op jit(solution)/shard_map/ppermute | solution.py:342
  16.2 10.6 %collective-permute-start.1 = (bf16[144,128]{1,0:T(8,128)(2,1)S(1)}, bf16[144,128]{1,0:T(8,128)(2,1)S(1)}, u32[]{:S(2)}, u32[]{:S(2)}) collective-permute-start(bf16[144,128]{1,0:T(8,128)(2,1)S(1)} %concatenate.10), channel_id=1, source_target_pairs={{0,2},{1,3},{2,0},{3,1},{4,6},{5,7},{6,4},{7,5},{8,10},{9,11},{10,... | collective-permute-start | bytes 110600 | tf_op jit(solution)/shard_map/ppermute | solution.py:342
  16.2 11.2 %collective-permute-start.2 = (bf16[144,128]{1,0:T(8,128)(2,1)S(1)}, bf16[144,128]{1,0:T(8,128)(2,1)S(1)}, u32[]{:S(2)}, u32[]{:S(2)}) collective-permute-start(bf16[144,128]{1,0:T(8,128)(2,1)S(1)} %concatenate.10), channel_id=1, source_target_pairs={{0,1},{1,2},{2,3},{3,0},{4,5},{5,6},{6,7},{7,4},{8,9},{9,10},{10,1... | collective-permute-start | bytes 110600 | tf_op jit(solution)/shard_map/ppermute | solution.py:342
  32.5 19.0 %collective-permute-start.3 = (bf16[1024,128]{1,0:T(8,128)(2,1)}, bf16[1024,128]{1,0:T(8,128)(2,1)S(1)}, u32[]{:S(2)}, u32[]{:S(2)}) collective-permute-start(bf16[1024,128]{1,0:T(8,128)(2,1)} %get-tuple-element.39), channel_id=1, source_target_pairs={{0,4},{4,8},{8,12},{12,16},{16,20},{20,24},{24,28},{28,32},{32,36}... | collective-permute-start | bytes 786440 | tf_op jit(solution)/shard_map/ppermute | solution.py:348
  37.3 14.2 %collective-permute-start.4 = (bf16[1024,128]{1,0:T(8,128)(2,1)}, bf16[1024,128]{1,0:T(8,128)(2,1)}, u32[]{:S(2)}, u32[]{:S(2)}) collective-permute-start(bf16[1024,128]{1,0:T(8,128)(2,1)} %get-tuple-element.38), channel_id=1, source_target_pairs={{4,0},{8,4},{12,8},{16,12},{20,16},{24,20},{28,24},{32,28},{36,32}... | collective-permute-start | bytes 786440 | tf_op jit(solution)/shard_map/ppermute | solution.py:348
  60.1 26.8 %collective-permute-start.6 = (bf16[32,128,128]{2,1,0:T(8,128)(2,1)}, bf16[32,128,128]{2,1,0:T(8,128)(2,1)}, u32[]{:S(2)}, u32[]{:S(2)}) collective-permute-start(bf16[32,128,128]{2,1,0:T(8,128)(2,1)} %forward_tiles.5), channel_id=1, source_target_pairs={{0,2},{1,3},{2,0},{3,1},{4,6},{5,7},{6,4},{7,5},{8,10},{9,11},{10,... | collective-permute-start | bytes 3145736 | tf_op jit(solution)/shard_map/ppermute | solution.py:342
  62.9 46.5 %collective-permute-start.5 = (bf16[32,128,128]{2,1,0:T(8,128)(2,1)}, bf16[32,128,128]{2,1,0:T(8,128)(2,1)}, u32[]{:S(2)}, u32[]{:S(2)}) collective-permute-start(bf16[32,128,128]{2,1,0:T(8,128)(2,1)} %get-tuple-element.23), channel_id=1, source_target_pairs={{0,1},{1,2},{2,3},{3,0},{4,5},{5,6},{6,7},{7,4},{8,9},{9,10},{10,1... | collective-permute-start | bytes 3145736 | tf_op jit(solution)/shard_map/ppermute | solution.py:342
  63.6 45.8 %collective-permute-start.7 = (bf16[32,128,128]{2,1,0:T(8,128)(2,1)}, bf16[32,128,128]{2,1,0:T(8,128)(2,1)}, u32[]{:S(2)}, u32[]{:S(2)}) collective-permute-start(bf16[32,128,128]{2,1,0:T(8,128)(2,1)} %get-tuple-element.24), channel_id=1, source_target_pairs={{0,3},{1,0},{2,1},{3,2},{4,7},{5,4},{6,5},{7,6},{8,11},{9,8},{10,9... | collective-permute-start | bytes 3145736 | tf_op jit(solution)/shard_map/ppermute | solution.py:342
  119.3 24.3 %collective-permute-start.8 = (bf16[4096,128]{1,0:T(8,128)(2,1)S(1)}, bf16[4096,128]{1,0:T(8,128)(2,1)S(1)}, u32[]{:S(2)}, u32[]{:S(2)}) collective-permute-start(bf16[4096,128]{1,0:T(8,128)(2,1)S(1)} %get-tuple-element.27), channel_id=1, source_target_pairs={{0,3},{1,0},{2,1},{3,2},{4,7},{5,4},{6,5},{7,6},{8,11},{9,8},{10,9... | collective-permute-start | bytes 3145736 | tf_op jit(solution)/shard_map/ppermute | solution.py:342
  119.6 25.6 %collective-permute-start.9 = (bf16[4096,128]{1,0:T(8,128)(2,1)S(1)}, bf16[4096,128]{1,0:T(8,128)(2,1)S(1)}, u32[]{:S(2)}, u32[]{:S(2)}) collective-permute-start(bf16[4096,128]{1,0:T(8,128)(2,1)S(1)} %get-tuple-element.27), channel_id=1, source_target_pairs={{0,2},{1,3},{2,0},{3,1},{4,6},{5,7},{6,4},{7,5},{8,10},{9,11},{10,... | collective-permute-start | bytes 3145736 | tf_op jit(solution)/shard_map/ppermute | solution.py:342
  121.8 46.8 %collective-permute-start.10 = (bf16[4096,128]{1,0:T(8,128)(2,1)S(1)}, bf16[4096,128]{1,0:T(8,128)(2,1)S(1)}, u32[]{:S(2)}, u32[]{:S(2)}) collective-permute-start(bf16[4096,128]{1,0:T(8,128)(2,1)S(1)} %get-tuple-element.27), channel_id=1, source_target_pairs={{0,1},{1,2},{2,3},{3,0},{4,5},{5,6},{6,7},{7,4},{8,9},{9,10},{10,1... | collective-permute-start | bytes 3145736 | tf_op jit(solution)/shard_map/ppermute | solution.py:342
  171.8 13.4 %collective-permute-start.11 = (bf16[1024,128]{1,0:T(8,128)(2,1)S(1)}, bf16[1024,128]{1,0:T(8,128)(2,1)S(1)}, u32[]{:S(2)}, u32[]{:S(2)}) collective-permute-start(bf16[1024,128]{1,0:T(8,128)(2,1)S(1)} %bitcast.83), channel_id=1, source_target_pairs={{0,4},{4,8},{8,12},{12,16},{16,20},{20,24},{24,28},{28,32},{32,36}... | collective-permute-start | bytes 786440 | tf_op jit(solution)/shard_map/ppermute | solution.py:348
  177.8 7.7 %collective-permute-start.12 = (bf16[1024,128]{1,0:T(8,128)(2,1)S(1)}, bf16[1024,128]{1,0:T(8,128)(2,1)S(1)}, u32[]{:S(2)}, u32[]{:S(2)}) collective-permute-start(bf16[1024,128]{1,0:T(8,128)(2,1)S(1)} %bitcast.82), channel_id=1, source_target_pairs={{4,0},{8,4},{12,8},{16,12},{20,16},{24,20},{28,24},{32,28},{36,32}... | collective-permute-start | bytes 786440 | tf_op jit(solution)/shard_map/ppermute | solution.py:348
  196.4 4.4 %collective-permute-start.13 = (f32[136,128]{1,0:T(8,128)S(1)}, f32[136,128]{1,0:T(8,128)S(1)}, u32[]{:S(2)}, u32[]{:S(2)}) collective-permute-start(f32[136,128]{1,0:T(8,128)S(1)} %get-tuple-element.33), channel_id=1, source_target_pairs={{0,1},{1,2},{2,3},{3,0},{4,5},{5,6},{6,7},{7,4},{8,9},{9,10},{10,1... | collective-permute-start | bytes 208904 | tf_op jit(solution)/shard_map/ppermute | solution.py:342
  198.3 4.7 %collective-permute-start.14 = (f32[136,128]{1,0:T(8,128)S(1)}, f32[136,128]{1,0:T(8,128)S(1)}, u32[]{:S(2)}, u32[]{:S(2)}) collective-permute-start(f32[136,128]{1,0:T(8,128)S(1)} %get-tuple-element.34), channel_id=1, source_target_pairs={{0,2},{1,3},{2,0},{3,1},{4,6},{5,7},{6,4},{7,5},{8,10},{9,11},{10,... | collective-permute-start | bytes 208904 | tf_op jit(solution)/shard_map/ppermute | solution.py:342
  198.8 4.1 %collective-permute-start.15 = (f32[136,128]{1,0:T(8,128)S(1)}, f32[136,128]{1,0:T(8,128)S(1)}, u32[]{:S(2)}, u32[]{:S(2)}) collective-permute-start(f32[136,128]{1,0:T(8,128)S(1)} %get-tuple-element.35), channel_id=1, source_target_pairs={{0,3},{1,0},{2,1},{3,2},{4,7},{5,4},{6,5},{7,6},{8,11},{9,8},{10,9... | collective-permute-start | bytes 208904 | tf_op jit(solution)/shard_map/ppermute | solution.py:342
  203.0 5.0 %collective-permute-start.16 = (f32[136,128]{1,0:T(8,128)S(1)}, f32[136,128]{1,0:T(8,128)S(1)}, u32[]{:S(2)}, u32[]{:S(2)}) collective-permute-start(f32[136,128]{1,0:T(8,128)S(1)} %add_add_fusion.2), channel_id=1, source_target_pairs={{0,32},{4,36},{8,40},{12,44},{16,48},{20,52},{24,56},{28,60},{32,6... | collective-permute-start | bytes 208904 | tf_op jit(solution)/shard_map/ppermute | solution.py:358
  203.7 4.8 %collective-permute-start.17 = (f32[136,128]{1,0:T(8,128)S(1)}, f32[136,128]{1,0:T(8,128)S(1)}, u32[]{:S(2)}, u32[]{:S(2)}) collective-permute-start(f32[136,128]{1,0:T(8,128)S(1)} %add_add_fusion.2), channel_id=1, source_target_pairs={{0,64},{4,68},{8,72},{12,76},{16,80},{20,84},{24,88},{28,92},{32,9... | collective-permute-start | bytes 208904 | tf_op jit(solution)/shard_map/ppermute | solution.py:358
  206.0 3.3 %collective-permute-start.18 = (f32[136,128]{1,0:T(8,128)S(1)}, f32[136,128]{1,0:T(8,128)S(1)}, u32[]{:S(2)}, u32[]{:S(2)}) collective-permute-start(f32[136,128]{1,0:T(8,128)S(1)} %add_add_fusion.2), channel_id=1, source_target_pairs={{0,96},{4,100},{8,104},{12,108},{16,112},{20,116},{24,120},{28,124... | collective-permute-start | bytes 208904 | tf_op jit(solution)/shard_map/ppermute | solution.py:358
  209.3 8.3 %collective-permute-start.19 = (f32[136,128]{1,0:T(8,128)S(1)}, f32[136,128]{1,0:T(8,128)S(1)}, u32[]{:S(2)}, u32[]{:S(2)}) collective-permute-start(f32[136,128]{1,0:T(8,128)S(1)} %add_add_fusion.1), channel_id=1, source_target_pairs={{0,8},{4,12},{8,16},{12,20},{16,24},{20,28},{24,0},{28,4},{32,40},... | collective-permute-start | bytes 208904 | tf_op jit(solution)/shard_map/ppermute | solution.py:358
  211.1 6.9 %collective-permute-start.20 = (f32[136,128]{1,0:T(8,128)S(1)}, f32[136,128]{1,0:T(8,128)S(1)}, u32[]{:S(2)}, u32[]{:S(2)}) collective-permute-start(f32[136,128]{1,0:T(8,128)S(1)} %add_add_fusion.1), channel_id=1, source_target_pairs={{0,16},{4,20},{8,24},{12,28},{16,0},{20,4},{24,8},{28,12},{32,48},... | collective-permute-start | bytes 208904 | tf_op jit(solution)/shard_map/ppermute | solution.py:358
  215.6 3.3 %collective-permute-start.21 = (f32[136,128]{1,0:T(8,128)S(1)}, f32[136,128]{1,0:T(8,128)S(1)}, u32[]{:S(2)}, u32[]{:S(2)}) collective-permute-start(f32[136,128]{1,0:T(8,128)S(1)} %add_add_fusion.1), channel_id=1, source_target_pairs={{0,24},{4,28},{8,0},{12,4},{16,8},{20,12},{24,16},{28,20},{32,56},... | collective-permute-start | bytes 208904 | tf_op jit(solution)/shard_map/ppermute | solution.py:358
  219.0 5.4 %collective-permute-start.22 = (f32[136,128]{1,0:T(8,128)S(1)}, f32[136,128]{1,0:T(8,128)S(1)}, u32[]{:S(2)}, u32[]{:S(2)}) collective-permute-start(f32[136,128]{1,0:T(8,128)S(1)} %add_add_fusion), channel_id=1, source_target_pairs={{0,4},{4,0},{8,12},{12,8},{16,20},{20,16},{24,28},{28,24},{32,36},... | collective-permute-start | bytes 208904 | tf_op jit(solution)/shard_map/ppermute | solution.py:358
  (11 other events, 133.8 us)
Sparse Core Ops, SparseCore 0:
  19.8 24.7 all-gather.1

commit v2 on v1

v2 whole, which is shorter than its diff:
```python
import functools

import jax
import jax.numpy as jnp
from jax import lax
from jax.experimental import pallas as pl
from jax.experimental.pallas import tpu as pltpu
from jax.sharding import PartitionSpec as P

F32 = jnp.float32
BF16 = jnp.bfloat16
SIDE = 128
UNROLL = 4
PARAMS = pltpu.CompilerParams(vmem_limit_bytes=48 * 2**20)
VMEM = pl.BlockSpec(memory_space=pltpu.VMEM)
SMEM = pl.BlockSpec(memory_space=pltpu.SMEM)


def dot(left, right, dims):
    return lax.dot_general(left, right, (dims, ((), ())), preferred_element_type=F32)


def rows_by_cols(left, right):
    return dot(left, right, ((1,), (0,)))


def contract_rows(left, right):
    return dot(left, right, ((0,), (0,)))


def contract_cols(left, right):
    return dot(left, right, ((1,), (1,)))


def sigmoid(v):
    return 1.0 / (1.0 + jnp.exp(-v))


def silu_slope(v):
    g = sigmoid(v)
    return g * (1.0 + v * (1.0 - g))


def pick_kernel(rows_ref, count_ref, feat_ref, out_ref, wide, picked):
    halo = rows_ref.shape[1]
    wide[...] = feat_ref[...].astype(F32)
    group = 16
    for k in range(2):
        count = count_ref[k]

        def body(step, carry):
            for u in range(group):
                slot = step * group + u
                row = rows_ref[k, slot]
                picked[pl.ds(slot, 1), :] = wide[pl.ds(row, 1), :]
            return carry

        lax.fori_loop(0, (count + group - 1) // group, body, 0)
        slots = lax.broadcasted_iota(jnp.int32, (halo, SIDE), 0)
        kept = jnp.where(slots < count, picked[...], 0.0)
        out_ref[pl.ds(k * halo, halo), :] = kept.astype(BF16)


def pick_rows(halo_rows, halo_count, node_feat):
    halo = halo_rows.shape[1]
    return pl.pallas_call(
        pick_kernel,
        out_shape=jax.ShapeDtypeStruct((2 * halo, SIDE), BF16),
        in_specs=[SMEM, SMEM, VMEM],
        out_specs=VMEM,
        scratch_shapes=[pltpu.VMEM(node_feat.shape, F32), pltpu.VMEM((halo, SIDE), F32)],
        compiler_params=PARAMS,
        name="pick_rows",
    )(halo_rows, halo_count, node_feat)


def pack_kernel(count_ref, msg_ref, in_ref, out_w_ref, gain_ref, dst_ref, src_ref, pack_ref, lines):
    share = msg_ref.shape[0]
    pack_ref[pl.ds(0, share), :] = msg_ref[...]
    pack_ref[pl.ds(share, 2 * share), :] = in_ref[...]
    pack_ref[pl.ds(3 * share, share), :] = out_w_ref[...]
    lines[...] = jnp.zeros_like(lines)
    gain = gain_ref[...].astype(F32)
    for j in range(SIDE // share):
        lines[0:1, j * share : (j + 1) * share] = gain
    lines[1:2, :] = dst_ref[...].astype(F32)
    lines[2:3, :] = src_ref[...].astype(F32)
    lines[3:4, :] = jnp.full((1, SIDE), count_ref[0]).astype(F32)
    pack_ref[pl.ds(4 * share, 16), :] = lines[...].astype(BF16)


def pack_small(tile_count, w_msg, w_in, w_out, ln_gain, tile_dst, tile_src):
    share = w_msg.shape[0]
    return pl.pallas_call(
        pack_kernel,
        out_shape=jax.ShapeDtypeStruct((4 * share + 16, SIDE), BF16),
        in_specs=[SMEM] + [VMEM] * 6,
        out_specs=VMEM,
        scratch_shapes=[pltpu.VMEM((16, SIDE), F32)],
        name="pack_small",
    )(tile_count, w_msg, w_in, w_out, ln_gain.reshape(1, share), tile_dst.reshape(1, SIDE), tile_src.reshape(1, SIDE))


def prepare_kernel(
    own_blocks, here_blocks, pos_ref, s0_ref, s1_ref, s2_ref, s3_ref, picked_ref,
    low_ref, high_ref, msg_ref, in_ref, out_w_ref, gain_ref, code_ref,
):
    me = pos_ref[0]
    smalls = (s0_ref, s1_ref, s2_ref, s3_ref)
    parties = len(smalls)
    share = SIDE // parties
    lane = lax.broadcasted_iota(jnp.int32, (1, SIDE), 1)
    gain = jnp.zeros((1, SIDE), F32)
    for k, ref in enumerate(smalls):
        device = lax.rem(me + k, parties)
        at = pl.multiple_of(device * share, share)
        msg_ref[pl.ds(at, share), :] = ref[pl.ds(0, share), :]
        in_ref[pl.ds(pl.multiple_of(2 * at, 2 * share), 2 * share), :] = ref[pl.ds(share, 2 * share), :]
        out_w_ref[pl.ds(at, share), :] = ref[pl.ds(3 * share, share), :]
        lines = ref[pl.ds(4 * share, 16), :].astype(F32)
        gain = jnp.where((lane >= at) & (lane < at + share), lines[0:1, :], gain)
        dst, src, count = (lines[i : i + 1, :].astype(jnp.int32) for i in (1, 2, 3))
        block = src - me * here_blocks
        used = (lane < count) & (block >= 0) & (block < here_blocks)
        is_rim = block >= own_blocks
        place = jnp.where(is_rim, block - own_blocks, block)
        code = lane + (place << 7) + (dst << 13) + jnp.where(is_rim, 2 << 20, 1 << 20)
        code_ref[k : k + 1, :] = jnp.where(used, code, 0)
        code_ref[parties + k : parties + k + 1, :] = count
    gain_ref[...] = gain
    half = low_ref.shape[0]
    w_msg = msg_ref[...]
    for k, ref in enumerate((low_ref, high_ref)):
        pre = rows_by_cols(picked_ref[pl.ds(k * half, half), :], w_msg)
        ref[...] = (pre * sigmoid(pre)).astype(BF16)


def prepare(position, smalls, picked, own_blocks, here_blocks):
    half = picked.shape[0] // 2
    return pl.pallas_call(
        functools.partial(prepare_kernel, own_blocks, here_blocks),
        out_shape=(
            jax.ShapeDtypeStruct((half, SIDE), BF16),
            jax.ShapeDtypeStruct((half, SIDE), BF16),
            jax.ShapeDtypeStruct((SIDE, SIDE), BF16),
            jax.ShapeDtypeStruct((2 * SIDE, SIDE), BF16),
            jax.ShapeDtypeStruct((SIDE, SIDE), BF16),
            jax.ShapeDtypeStruct((1, SIDE), F32),
            jax.ShapeDtypeStruct((8, SIDE), jnp.int32),
        ),
        in_specs=[SMEM] + [VMEM] * 5,
        out_specs=(VMEM,) * 7,
        compiler_params=PARAMS,
        name="prepare",
    )(position, *smalls, picked)


def list_kernel(code_ref, list_ref, total_ref):
    parties = code_ref.shape[0] // 2
    group = 8
    for k in range(parties):

        def body(step, carry):
            own, rim = carry
            for u in range(group):
                code = code_ref[k, step * group + u]
                list_ref[2 * k, own] = code
                list_ref[2 * k + 1, rim] = code
                own = own + ((code >> 20) & 1)
                rim = rim + (code >> 21)
            return (own, rim)

        steps = (code_ref[parties + k, 0] + group - 1) // group
        own, rim = lax.fori_loop(0, steps, body, (jnp.int32(0), jnp.int32(0)))
        total_ref[2 * k] = own
        total_ref[2 * k + 1] = rim


def build_lists(codes):
    parties, slots = codes.shape[0] // 2, codes.shape[1]
    return pl.pallas_call(
        list_kernel,
        out_shape=(
            jax.ShapeDtypeStruct((2 * parties, slots + 16), jnp.int32),
            jax.ShapeDtypeStruct((2 * parties,), jnp.int32),
        ),
        in_specs=[SMEM],
        out_specs=(SMEM, SMEM),
        name="tile_lists",
    )(codes)


def dense_tile(tile, keep):
    column = lax.broadcasted_iota(jnp.int32, (SIDE, SIDE), 0).astype(F32)
    entries = tile.shape[0] // 2
    total = None
    for e in range(entries):
        weight = tile[e : e + 1, :] * keep
        term = jnp.where(column == tile[entries + e : entries + e + 1, :], weight, 0.0)
        total = term if total is None else total + term
    return total.astype(BF16)


def walk_list(list_ref, total_ref, which, tiles_ref, product, acc):
    count = total_ref[which]

    def body(step, carry):
        found = []
        for u in range(UNROLL):
            index = step * UNROLL + u
            used = index < count
            entry = jnp.where(used, list_ref[which, index], 0)
            rows = pl.ds(pl.multiple_of((entry & 127) * 8, 8), 8)
            dense = dense_tile(tiles_ref[rows, :], jnp.where(used, 1.0, 0.0))
            found.append(product(dense, (entry >> 7) & 63, (entry >> 13) & 31))
        for target, value in found:
            acc[target] += value
        return carry

    lax.fori_loop(0, (count + UNROLL - 1) // UNROLL, body, 0)


def forward_kernel(ks, list_ref, total_ref, own_ref, lower_ref, upper_ref, *rest):
    tile_refs, rest = rest[: len(ks)], rest[len(ks) :]
    outs, (acc, rims, tiles) = rest[: 4 * len(ks)], rest[4 * len(ks) :]
    half = lower_ref.shape[0]
    rims[pl.ds(0, half)] = lower_ref[...]
    rims[pl.ds(half, half)] = upper_ref[...]
    for at, (k, tile_ref) in enumerate(zip(ks, tile_refs)):
        acc[...] = jnp.zeros_like(acc)
        tiles[...] = tile_ref[...].astype(F32)
        for part, ref in enumerate((own_ref, rims)):

            def product(dense, block, target, ref=ref):
                return (target, contract_rows(dense, ref[block]))

            walk_list(list_ref, total_ref, 2 * k + part, tiles, product, acc)
        for q in range(4):
            out_ref = outs[4 * at + q]
            span = out_ref.shape[0]
            out_ref[...] = acc[pl.ds(q * span, span)].astype(out_ref.dtype)


def forward_tiles(ks, lists, totals, own, lower, upper, tiles, kind):
    quarter = jax.ShapeDtypeStruct((own.shape[0] // 4,) + own.shape[1:], kind)
    return pl.pallas_call(
        functools.partial(forward_kernel, ks),
        out_shape=(quarter,) * (4 * len(ks)),
        in_specs=[SMEM, SMEM] + [VMEM] * (3 + len(ks)),
        out_specs=(VMEM,) * (4 * len(ks)),
        scratch_shapes=[
            pltpu.VMEM(own.shape, F32),
            pltpu.VMEM((2 * lower.shape[0],) + lower.shape[1:], BF16),
            pltpu.VMEM(tiles[0].shape, F32),
        ],
        compiler_params=PARAMS,
        cost_estimate=pl.CostEstimate(
            flops=1_000_000_000 * len(ks), bytes_accessed=4_000_000 * len(ks), transcendentals=0
        ),
        name="forward_tiles",
    )(lists, totals, own, lower, upper, *[tiles[k] for k in ks])


def node_kernel(
    feat_ref, cot_ref, own_ref, la_ref, ra_ref, lb_ref, rb_ref, in_ref, out_w_ref, gain_ref, *rest,
):
    node_ref, dhid_ref, dagg_ref, dwin_ref, dwout_ref, dgain_ref = rest[-6:]
    before = rest[:-6]
    sums = (dwin_ref, dwout_ref, dgain_ref)
    step = pl.program_id(0)

    @pl.when(step == 0)
    def _():
        for at, ref in enumerate(sums):
            ref[...] = before[2 + at][...] if before else jnp.zeros_like(ref)

    feat = feat_ref[...]
    first = step < pl.num_programs(0) // 2
    left = jnp.where(first, la_ref[...].astype(F32), lb_ref[...].astype(F32))
    right = jnp.where(first, ra_ref[...].astype(F32), rb_ref[...].astype(F32))
    agg = (own_ref[...] + (left + right)).astype(BF16)
    w_feat, w_agg, w_out = in_ref[:SIDE, :], in_ref[SIDE:, :], out_w_ref[...]
    gain = gain_ref[...]
    pre = rows_by_cols(feat, w_feat) + rows_by_cols(agg, w_agg)
    logistic = sigmoid(pre)
    hidden = (pre * logistic).astype(BF16)
    slope = logistic * (1.0 + pre * (1.0 - logistic))
    update = rows_by_cols(hidden, w_out)
    centre = update - jnp.mean(update, axis=-1, keepdims=True)
    inverse = lax.rsqrt(jnp.mean(centre * centre, axis=-1, keepdims=True) + 1e-05)
    normed = centre * inverse
    node_ref[...] = (feat.astype(F32) + gain * normed).astype(BF16)
    upstream = cot_ref[...].astype(F32)
    d_normed = upstream * gain
    dgain_ref[...] += jnp.sum(upstream * normed, axis=0, keepdims=True)
    d_update = (
        d_normed
        - jnp.mean(d_normed, axis=-1, keepdims=True)
        - normed * jnp.mean(d_normed * normed, axis=-1, keepdims=True)
    ) * inverse
    d_update = d_update.astype(BF16)
    d_hidden = (contract_cols(d_update, w_out) * slope).astype(BF16)
    dhid_ref[...] = d_hidden
    dagg_ref[...] = contract_cols(d_hidden, w_agg).astype(BF16)
    dwout_ref[...] += contract_rows(hidden, d_update)
    dwin_ref[:SIDE, :] += contract_rows(feat, d_hidden)
    dwin_ref[SIDE:, :] += contract_rows(agg, d_hidden)


def node_update(half, node_feat, cotangent, own, left_a, right_a, left_b, right_b, w_in, w_out, gain, before):
    rows = node_feat.shape[0]
    chunk = 512
    per = rows // 4 // chunk
    steps = 2 * per

    def whole(shape):
        return pl.BlockSpec(shape, lambda i: (0, 0))

    tall = pl.BlockSpec((chunk, SIDE), lambda i: (half * per + i + per * (i // per), 0))
    part_a = pl.BlockSpec((chunk, SIDE), lambda i: (jnp.minimum(i, per - 1), 0))
    part_b = pl.BlockSpec((chunk, SIDE), lambda i: (jnp.maximum(i - per, 0), 0))
    wide = jax.ShapeDtypeStruct((rows, SIDE), BF16)
    anywhere = pl.BlockSpec(memory_space=pl.ANY)
    sums = [(2 * SIDE, SIDE), (SIDE, SIDE), (1, SIDE)]
    return pl.pallas_call(
        node_kernel,
        grid=(steps,),
        out_shape=(
            wide,
            wide,
            jax.ShapeDtypeStruct((rows // 2, SIDE), BF16),
        ) + tuple(jax.ShapeDtypeStruct(shape, F32) for shape in sums),
        in_specs=[tall, tall, pl.BlockSpec((chunk, SIDE), lambda i: (i, 0)), part_a, part_a, part_b, part_b]
        + [whole((2 * SIDE, SIDE)), whole((SIDE, SIDE)), whole((1, SIDE))]
        + ([anywhere, anywhere] + [whole(shape) for shape in sums] if before else []),
        out_specs=(tall, tall, pl.BlockSpec((chunk, SIDE), lambda i: (i, 0)))
        + tuple(whole(shape) for shape in sums),
        input_output_aliases={10: 0, 11: 1} if before else {},
        compiler_params=PARAMS,
        cost_estimate=pl.CostEstimate(flops=5_000_000_000, bytes_accessed=10_000_000, transcendentals=0),
        name="node_update",
    )(node_feat, cotangent, own, left_a, right_a, left_b, right_b, w_in, w_out, gain, *before)


def share_kernel(pos_ref, dwin_ref, dwout_ref, dgain_ref, *outs):
    share = SIDE // len(outs)
    for k, out in enumerate(outs):
        device = lax.rem(pos_ref[0] + k, len(outs))
        start = pl.multiple_of(device * share, share)
        out[pl.ds(0, 2 * share), :] = dwin_ref[pl.ds(2 * start, 2 * share), :]
        out[pl.ds(2 * share, share), :] = dwout_ref[pl.ds(start, share), :]
        out[pl.ds(3 * share, 8), :] = jnp.broadcast_to(dgain_ref[...], (8, SIDE))


def split_shares(position, dwin, dwout, dgain):
    piece = jax.ShapeDtypeStruct((3 * SIDE // 4 + 8, SIDE), F32)
    return pl.pallas_call(
        share_kernel,
        out_shape=(piece,) * 4,
        in_specs=[SMEM] + [VMEM] * 3,
        out_specs=(VMEM,) * 4,
        name="split_shares",
    )(position, dwin, dwout, dgain)


def ahead_kernel(feat_ref, cot_ref, dhid_ref, msg_ref, in_ref, slope_ref, base_ref):
    slope_ref[...] = silu_slope(rows_by_cols(feat_ref[...], msg_ref[...]))
    base_ref[...] = cot_ref[...].astype(F32) + contract_cols(dhid_ref[...], in_ref[:SIDE, :])


def ahead(feat, cot, dhid, w_msg, w_in):
    rows = feat.shape[0]
    steps = 4
    tall = pl.BlockSpec((rows // steps, SIDE), lambda i: (i, 0))
    wide = jax.ShapeDtypeStruct((rows, SIDE), F32)
    return pl.pallas_call(
        ahead_kernel,
        grid=(steps,),
        out_shape=(wide, wide),
        in_specs=[tall] * 3 + [pl.BlockSpec(w.shape, lambda i: (0, 0)) for w in (w_msg, w_in)],
        out_specs=(tall, tall),
        compiler_params=PARAMS,
        cost_estimate=pl.CostEstimate(flops=3_000_000_000, bytes_accessed=7_000_000, transcendentals=0),
        name="ahead",
    )(feat, cot, dhid, w_msg, w_in)


def backward_kernel(part, list_ref, total_ref, *rest):
    tile_refs, quarters, (out_ref, acc, tiles, grads) = rest[:4], rest[4:-4], rest[-4:]
    acc[...] = jnp.zeros_like(acc)
    span = grads.shape[0] // 4
    for k, tile_ref in enumerate(tile_refs):
        tiles[...] = tile_ref[...].astype(F32)
        if k == 2:
            for q in range(4):
                grads[pl.ds(q * span, span)] = quarters[4 + q][...]
        else:
            for h in range(2):
                ref = quarters[{0: 0, 1: 2, 3: 8}[k] + h]
                grads[pl.ds(h * span, span)] = ref[pl.ds(0, span)]
                grads[pl.ds((2 + h) * span, span)] = ref[pl.ds(span, span)]

        def product(dense, block, target):
            return (block, rows_by_cols(dense, grads[target]))

        walk_list(list_ref, total_ref, 2 * k + part, tiles, product, acc)
    out_ref[...] = acc[...].astype(out_ref.dtype)


def backward_tiles(part, blocks, kind, lists, totals, tiles, grads):
    shape = (blocks, SIDE, SIDE)
    cubes = [grad.reshape(-1, SIDE, SIDE) for grad in grads]
    return pl.pallas_call(
        functools.partial(backward_kernel, part),
        out_shape=jax.ShapeDtypeStruct(shape, kind),
        in_specs=[SMEM, SMEM] + [VMEM] * (len(tiles) + len(cubes)),
        out_specs=VMEM,
        scratch_shapes=[
            pltpu.VMEM(shape, F32),
            pltpu.VMEM(tiles[0].shape, F32),
            pltpu.VMEM((2 * cubes[0].shape[0], SIDE, SIDE), BF16),
        ],
        compiler_params=PARAMS,
        cost_estimate=pl.CostEstimate(flops=3_000_000_000, bytes_accessed=8_000_000, transcendentals=0),
        name="backward_tiles",
    )(lists, totals, *tiles, *cubes)


def last_kernel(
    pos_ref, rows_ref, count_ref, own_ref, lower_ref, upper_ref, msg_ref, feat_any, slope_any, base_any,
    dnode_ref, r0_ref, r1_ref, r2_ref, r3_ref, back, dw, feat_ref, slope_ref, base_ref, acc, sems,
):
    copies = [
        pltpu.make_async_copy(source, target, sems.at[i])
        for i, (source, target) in enumerate(
            ((feat_any, feat_ref), (slope_any, slope_ref), (base_any, base_ref))
        )
    ]
    for copy in copies:
        copy.start()
    halo = rows_ref.shape[1]
    acc[...] = own_ref[...]
    group = 16
    for k, ref in enumerate((lower_ref, upper_ref)):
        count = count_ref[k]
        slots = lax.broadcasted_iota(jnp.int32, (halo, SIDE), 0)
        back[...] = jnp.where(slots < count, ref[...].astype(F32), 0.0)

        def body(step, carry):
            rows = [rows_ref[k, step * group + u] for u in range(group)]
            added = [
                acc[pl.ds(row, 1), :] + back[pl.ds(step * group + u, 1), :] for u, row in enumerate(rows)
            ]
            for row, value in zip(rows, added):
                acc[pl.ds(row, 1), :] = value
            return carry

        lax.fori_loop(0, (count + group - 1) // group, body, 0)
    for copy in copies:
        copy.wait()
    w_msg = msg_ref[...]
    dw[...] = jnp.zeros_like(dw)
    chunk = 512

    def step_rows(step, carry):
        at = pl.ds(pl.multiple_of(step * chunk, chunk), chunk)
        d_pre = (acc[at, :] * slope_ref[at, :]).astype(BF16)
        dw[...] += contract_rows(feat_ref[at, :], d_pre)
        dnode_ref[at, :] = (base_ref[at, :] + contract_cols(d_pre, w_msg)).astype(BF16)
        return carry

    lax.fori_loop(0, acc.shape[0] // chunk, step_rows, 0)
    outs = (r0_ref, r1_ref, r2_ref, r3_ref)
    share = SIDE // len(outs)
    for k, out in enumerate(outs):
        device = lax.rem(pos_ref[0] + k, len(outs))
        out[...] = dw[pl.ds(pl.multiple_of(device * share, share), share), :]


def last_products(position, halo_rows, halo_count, own, lower, upper, w_msg, feat, slope, base):
    rows = feat.shape[0]
    piece = jax.ShapeDtypeStruct((SIDE // 4, SIDE), F32)
    return pl.pallas_call(
        last_kernel,
        out_shape=(jax.ShapeDtypeStruct((rows, SIDE), BF16), piece, piece, piece, piece),
        in_specs=[SMEM] * 3 + [VMEM] * 4 + [pl.BlockSpec(memory_space=pl.ANY)] * 3,
        out_specs=(VMEM,) * 5,
        scratch_shapes=[
            pltpu.VMEM((halo_rows.shape[1], SIDE), F32),
            pltpu.VMEM((SIDE, SIDE), F32),
            pltpu.VMEM((rows, SIDE), BF16),
            pltpu.VMEM((rows, SIDE), F32),
            pltpu.VMEM((rows, SIDE), F32),
            pltpu.VMEM((rows, SIDE), F32),
            pltpu.SemaphoreType.DMA((3,)),
        ],
        compiler_params=PARAMS,
        name="last_products",
    )(position, halo_rows, halo_count, own, lower, upper, w_msg, feat, slope, base)


def shift_wsh(value, step):
    parties = lax.axis_size("wsh")
    return lax.ppermute(value, "wsh", [(i, (i + step) % parties) for i in range(parties)])


def shift_slab(value, step):
    count = lax.axis_size("slab")
    pairs = [(i, i + step) for i in range(count) if 0 <= i + step < count]
    return lax.ppermute(value, "slab", pairs)


def sum_slab(value):
    count = lax.axis_size("slab")
    for stride, size in ((8, 4), (2, 4), (1, 2)):
        total = value
        for k in range(1, size):
            span = stride * size
            pairs = [(i, (i // span) * span + (i + stride * k) % span) for i in range(count)]
            total = total + lax.ppermute(value, "slab", pairs)
        value = total
    return value


def sum_wsh(pieces):
    total = pieces[0]
    for k in range(1, len(pieces)):
        total = total + shift_wsh(pieces[k], k)
    return total


def add_parts(mine, theirs):
    return (mine.astype(F32) + theirs.astype(F32)).astype(BF16)


def on_device(
    node_feat, cotangent, w_msg, w_in, w_out, ln_gain,
    tile_values, tile_cols, tile_dst, tile_src, tile_count, halo_rows, halo_count,
):
    node_rows = node_feat.shape[0]
    slots, entries, side = tile_values.shape
    halo = halo_rows.shape[2]
    parties = lax.axis_size("wsh")
    me = lax.axis_index("wsh").astype(jnp.int32)
    position = me.reshape(1)
    share = w_msg.shape[0]
    own_blocks = node_rows // side
    rim_blocks = 2 * halo // side
    quarter = node_rows // 4

    small = pack_small(tile_count, w_msg, w_in, w_out, ln_gain, tile_dst, tile_src)
    smalls = [small] + [shift_wsh(small, -k) for k in range(1, parties)]
    own_tiles = jnp.concatenate([tile_values, tile_cols.astype(BF16)], axis=1).reshape(2 * entries * slots, side)
    tiles = [own_tiles] + [shift_wsh(own_tiles, -k) for k in range(1, parties)]

    rows = halo_rows.reshape(2, halo)
    counts = halo_count.reshape(2)
    picked = pick_rows(rows, counts, node_feat)
    low, high, full_msg, full_in, full_out, gain, codes = prepare(
        position, smalls, picked, own_blocks, own_blocks + rim_blocks
    )
    lower = shift_slab(high, 1).reshape(rim_blocks // 2, side, side)
    upper = shift_slab(low, -1).reshape(rim_blocks // 2, side, side)
    lists, totals = build_lists(codes)
    message = jax.nn.silu(rows_by_cols(node_feat, full_msg)).astype(BF16)
    sources = (message.reshape(own_blocks, side, side), lower, upper)

    far = forward_tiles((2,), lists, totals, *sources, tiles, BF16)
    from_right = [shift_wsh(far[q], -1) for q in (0, 1)]
    from_left = [shift_wsh(far[2 + q], 1) for q in (0, 1)]
    near = forward_tiles((1, 3), lists, totals, *sources, tiles, BF16)
    after, prior = near[:4], near[4:]
    left_a = [shift_wsh(after[q], 1) for q in (0, 1)]
    right_b = [shift_wsh(prior[2 + q], -1) for q in (0, 1)]
    left_b = [shift_wsh(add_parts(after[2 + q], from_left[q]), 1) for q in (0, 1)]
    right_a = [shift_wsh(add_parts(prior[q], from_right[q]), -1) for q in (0, 1)]
    mine = forward_tiles((0,), lists, totals, *sources, tiles, F32)

    before = ()
    halves = []
    for h in (0, 1):
        own = jnp.concatenate([mine[h], mine[2 + h]], axis=0).reshape(2 * quarter, side)
        pieces = [part.reshape(quarter, side) for part in (left_a[h], right_a[h], left_b[h], right_b[h])]
        node_out, d_hidden, half, *sums = node_update(
            h, node_feat, cotangent, own, *pieces, full_in, full_out, gain, before
        )
        before = (node_out, d_hidden, *sums)
        halves.append(half)
    after = [shift_wsh(half, -1) for half in halves]
    prior = [shift_wsh(half, 1) for half in halves]
    far_a = [shift_wsh(half[:quarter], 1) for half in prior]
    far_b = [shift_wsh(half[quarter:], -1) for half in after]
    grads = halves + after + far_a + far_b + prior

    early = sum_slab(sum_wsh(split_shares(position, *sums)))
    slope, base = ahead(node_feat, cotangent, d_hidden, full_msg, full_in)

    d_rims = backward_tiles(1, rim_blocks, BF16, lists, totals, tiles, grads).reshape(2 * halo, side)
    back_upper = shift_slab(d_rims[:halo], -1)
    back_lower = shift_slab(d_rims[halo:], 1)
    d_own = backward_tiles(0, own_blocks, F32, lists, totals, tiles, grads).reshape(node_rows, side)
    d_node, *pieces = last_products(
        position, rows, counts, d_own, back_lower, back_upper, full_msg, node_feat, slope, base
    )
    d_w_msg = sum_slab(sum_wsh(pieces))
    gain_share = lax.dynamic_slice_in_dim(early[3 * share], me * share, share, 0)
    return (node_out, d_node, d_w_msg, early[: 2 * share], early[2 * share : 3 * share], gain_share)


def solution(mesh):
    both = ("slab", "wsh")
    tall, split, line = P(both, None), P("wsh", None), P(both)
    cube = P(both, None, None)
    return jax.shard_map(
        on_device,
        mesh=mesh,
        in_specs=(
            tall, tall, split, split, split, P("wsh"), cube, cube, line, line, line, cube, tall,
        ),
        out_specs=(tall, tall, split, split, split, P("wsh")),
        check_vma=False,
    )
```

time: 234 us -> 186 us (0.79)
  waiting for transfers between devices: 91.2 us -> 34 us
  starting transfers between devices: 50.4 us -> 76.7 us
  between operations: 15.1 us -> 1.84 us
  local copies, waits for them, and re-layouts: 17.9 us -> 11.5 us
  Pallas kernels: 52.5 us -> 56.5 us
    ppermute x12 -> x32, waiting for transfers between devices: 87.2 us -> 28.8 us  [shift_wsh(): lax.ppermute(value, 'wsh', [(i, (i + step) % parties) for i in range(part...]
    ppermute x12 -> x32, starting transfers between devices: 18.1 us -> 40.2 us  [shift_wsh(): lax.ppermute(value, 'wsh', [(i, (i + step) % parties) for i in range(part...]
    ppermute x7 -> x14, starting transfers between devices: 17.7 us -> 23.3 us  [sum_slab(): total = total + lax.ppermute(value, 'slab', pairs)]
    slice x8 -> x7, local copies, waits for them, and re-layouts: 5.1 us -> 1.3 us  [the longest x1 0.62 us: on_device(): early[:2 * share]]
    concatenate x2 -> x0, local copies, waits for them, and re-layouts: 2.9 us -> none  [the longest x1 2.28 us: on_device(): small = jnp.concatenate([w_msg, w_in, w_out, extras], axis=0)]
    pallas_call x5 -> x10, Pallas kernels: 28.6 us -> 31.3 us  [the longest x2 10.6 us: node_update(): pl.pallas_call(node_kernel, grid=(steps,), out_shape=(wide, wide, jax.Sha...]
    ppermute x7 -> x14, waiting for transfers between devices: 3.65 us -> 5.24 us  [sum_slab(): total = total + lax.ppermute(value, 'slab', pairs)]
    unnamed x29 -> x54, local copies, waits for them, and re-layouts: 7.02 us -> 7.92 us
  transfers between devices with their start and end apart: 24 -> 50, of which waited for: 13 -> 14; matrix products, arithmetic and copies ran while one was open for 7% -> 5% of each run, Pallas kernels for 9% -> 26%
where the time goes in v2:
time: 186 us
  starting transfers between devices  76.7 us (41%)
  Pallas kernels  56.5 us (30%)
  waiting for transfers between devices  34 us (18%)
  local copies, waits for them, and re-layouts  11.5 us (6%)
  other arithmetic  4.19 us (2%)
    ppermute x32, starting transfers between devices, shift_wsh(): lax.ppermute(value, 'wsh', [(i, (i + step) % parties) for i in range(part...  40.2 us
    ppermute x32, waiting for transfers between devices, shift_wsh(): lax.ppermute(value, 'wsh', [(i, (i + step) % parties) for i in range(part...  28.8 us
    ppermute x14, starting transfers between devices, sum_slab(): total = total + lax.ppermute(value, 'slab', pairs)  23.3 us
    ppermute x4, starting transfers between devices, shift_slab(): return lax.ppermute(value, 'slab', pairs)  13.1 us
    pallas_call x2, Pallas kernels, node_update(): pl.pallas_call(node_kernel, grid=(steps,), out_shape=(wide, wide, jax.Sha...  10.6 us
    pallas_call x3, Pallas kernels, forward_tiles(): pl.pallas_call(functools.partial(forward_kernel, ks), out_shape=(quarter,...  10.3 us
    pallas_call x1, Pallas kernels, last_products(): pl.pallas_call(last_kernel, out_shape=(jax.ShapeDtypeStruct((rows, SIDE),...  10 us
    pallas_call x2, Pallas kernels, backward_tiles(): pl.pallas_call(functools.partial(backward_kernel, part), out_shape=jax.Sh...  9.78 us
  transfers between devices with their start and end apart: 50, of which 14 were waited for; matrix products, arithmetic and copies ran while one was open for 5% of the time, Pallas kernels for 26%

profile of v2, /device:TPU:1, one launch (start us, length us, event | category | flops | bytes accessed | tf_op | source)
XLA Modules:
  0.0 186.4 jit_solution(15530159075245218534)
XLA Ops:
  5.2 3.3 %collective-permute-start.1 = (bf16[144,128]{1,0:T(8,128)(2,1)}, bf16[144,128]{1,0:T(8,128)(2,1)S(1)}, u32[]{:S(2)}, u32[]{:S(2)}) collective-permute-start(bf16[144,128]{1,0:T(8,128)(2,1)} %pack_small.1.s0_ref), channel_id=1, source_target_pairs={{0,2},{1,3},{2,0},{3,1},{4,6},{5,7},{6,4},{7,5},{8,10},{9,11},{10,... | collective-permute-start | bytes 110600 | tf_op jit(solution)/shard_map/ppermute | solution.py:504
  14.8 5.4 %pick_rows.1.picked_ref = bf16[2048,128]{1,0:T(8,128)(2,1)S(1)} custom-call(s32[2,1024]{1,0:T(2,128)S(1)} %bitcast.55, s32[2]{0:T(128)S(1)} %bitcast.57, bf16[4096,128]{1,0:T(8,128)(2,1)S(1)} %copy-done), custom_call_target="tpu_custom_call" | custom-call | tf_op jit(solution)/shard_map/pick_rows/pallas_call | solution.py:66
  23.7 4.5 %collective-permute-start.3 = (bf16[1024,128]{1,0:T(8,128)(2,1)}, bf16[1024,128]{1,0:T(8,128)(2,1)S(1)}, u32[]{:S(2)}, u32[]{:S(2)}) collective-permute-start(bf16[1024,128]{1,0:T(8,128)(2,1)} %get-tuple-element.58), channel_id=1, source_target_pairs={{0,4},{4,8},{8,12},{12,16},{16,20},{20,24},{24,28},{28,32},{32,36}... | collective-permute-start | bytes 786440 | tf_op jit(solution)/shard_map/ppermute | solution.py:510
  31.9 3.4 %tile_lists.1 = (s32[8,144]{1,0:T(8,128)}, s32[8]{0:T(128)}) custom-call(s32[8,128]{1,0:T(8,128)} %copy-done.8), custom_call_target="tpu_custom_call" | custom-call | tf_op jit(solution)/shard_map/tile_lists/pallas_call | solution.py:181
  37.0 4.0 %forward_tiles.5 = (bf16[8,128,128]{2,1,0:T(8,128)(2,1)S(1)}, bf16[8,128,128]{2,1,0:T(8,128)(2,1)S(1)}, bf16[8,128,128]{2,1,0:T(8,128)(2,1)S(1)}, bf16[8,128,128]{2,1,0:T(8,128)(2,1)S(1)}) custom-call(s32[8,144]{1,0:T(8,128)S(1)} %copy-done.22, s32[8]{0:T(128)S(1)} %copy-done.23, bf16[32,128,128]{2,1,0:T(8,128)(2,1)S(1)} %bitcast.44, ...), custom_call_target="tpu_custom_call" | custom-call | flops 1000000000 | bytes 4000000 | tf_op jit(solution)/shard_map/forward_tiles/pallas_call | solution.py:246
  47.4 3.9 %forward_tiles.4 = (bf16[8,128,128]{2,1,0:T(8,128)(2,1)S(1)}, bf16[8,128,128]{2,1,0:T(8,128)(2,1)S(1)}, bf16[8,128,128]{2,1,0:T(8,128)(2,1)S(1)}, bf16[8,128,128...) custom-call(s32[8,144]{1,0:T(8,128)S(1)} %copy-done.22, ...), custom_call_target="tpu_custom_call" | custom-call | flops 2000000000 | bytes 8000000 | tf_op jit(solution)/shard_map/forward_tiles/pallas_call | solution.py:246
  51.3 3.1 %collective-permute-start.14 = (bf16[8,128,128]{2,1,0:T(8,128)(2,1)S(1)}, bf16[8,128,128]{2,1,0:T(8,128)(2,1)S(1)}, u32[]{:S(2)}, u32[]{:S(2)}) collective-permute-start(bf16[8,128,128]{2,1,0:T(8,128)(2,1)S(1)} %get-tuple-element.73), channel_id=1, source_target_pairs={{0,1},{1,2},{2,3},{3,0},{4,5},{5,6},{6,7},{7,4},{8,9},{9,10},{10,1... | collective-permute-start | bytes 786440 | tf_op jit(solution)/shard_map/ppermute | solution.py:504
  61.2 2.8 %collective-permute-done.19 = bf16[8,128,128]{2,1,0:T(8,128)(2,1)S(1)} collective-permute-done((bf16[8,128,128]{2,1,0:T(8,128)(2,1)S(1)}, bf16[8,128,128]{2,1,0:T(8,128)(2,1)S(1)}, u32[]{:S(2)}, u32[]{:S(2)}) %collective-permute-start.19) | collective-permute-done | bytes 262176 | tf_op jit(solution)/shard_map/ppermute | solution.py:504
  66.0 3.6 %collective-permute-done.16 = bf16[8,128,128]{2,1,0:T(8,128)(2,1)S(1)} collective-permute-done((bf16[8,128,128]{2,1,0:T(8,128)(2,1)S(1)}, bf16[8,128,128]{2,1,0:T(8,128)(2,1)S(1)}, u32[]{:S(2)}, u32[]{:S(2)}) %collective-permute-start.16) | collective-permute-done | bytes 262176 | tf_op jit(solution)/shard_map/ppermute | solution.py:504
  69.7 4.9 %node_update.2 = (bf16[4096,128]{1,0:T(8,128)(2,1)}, bf16[4096,128]{1,0:T(8,128)(2,1)S(1)}, bf16[2048,128]{1,0:T(8,128)(2,1)}, f32[256,128]{1,0:T(8,128)S(1)}, f...) custom-call(bf16[4096,128]{1,0:T(8,128)(2,1)S(1)} %copy-done.1, bf16[4096,128]{1,0:T(8,128)(2,1)S(1)} %copy-done.12, ...), custom_call_target="tpu_custom_call" | custom-call | flops 5000000000 | bytes 10000000 | tf_op jit(solution)/shard_map/node_update/pallas_call | solution.py:325
  75.2 3.3 %collective-permute-done.10 = bf16[8,128,128]{2,1,0:T(8,128)(2,1)S(1)} collective-permute-done((bf16[8,128,128]{2,1,0:T(8,128)(2,1)S(1)}, bf16[8,128,128]{2,1,0:T(8,128)(2,1)S(1)}, u32[]{:S(2)}, u32[]{:S(2)}) %collective-permute-start.10) | collective-permute-done | bytes 262176 | tf_op jit(solution)/shard_map/ppermute | solution.py:504
  78.6 5.8 %node_update.3 = (bf16[4096,128]{1,0:T(8,128)(2,1)}, bf16[4096,128]{1,0:T(8,128)(2,1)S(1)}, bf16[2048,128]{1,0:T(8,128)(2,1)}, f32[256,128]{1,0:T(8,128)S(1)}, f...) custom-call(bf16[4096,128]{1,0:T(8,128)(2,1)S(1)} %copy-done.1, ...), custom_call_target="tpu_custom_call", output_to_operand_aliasing={{0}: (10, {}), {1}: (11, {})} | custom-call | flops 5000000000 | bytes 10000000 | tf_op jit(solution)/shard_map/node_update/pallas_call | solution.py:325
  94.1 8.3 %collective-permute-done.24 = bf16[2048,128]{1,0:T(8,128)(2,1)S(1)} collective-permute-done((bf16[2048,128]{1,0:T(8,128)(2,1)}, bf16[2048,128]{1,0:T(8,128)(2,1)S(1)}, u32[]{:S(2)}, u32[]{:S(2)}) %collective-permute-start.24) | collective-permute-done | bytes 524320 | tf_op jit(solution)/shard_map/ppermute | solution.py:504
  105.1 8.0 %collective-permute-done.22 = bf16[2048,128]{1,0:T(8,128)(2,1)S(1)} collective-permute-done((bf16[2048,128]{1,0:T(8,128)(2,1)}, bf16[2048,128]{1,0:T(8,128)(2,1)S(1)}, u32[]{:S(2)}, u32[]{:S(2)}) %collective-permute-start.22) | collective-permute-done | bytes 524320 | tf_op jit(solution)/shard_map/ppermute | solution.py:504
  113.4 3.5 %collective-permute-start.27 = (bf16[1024,128]{1,0:T(8,128)(2,1)S(1)}, bf16[1024,128]{1,0:T(8,128)(2,1)S(1)}, u32[]{:S(2)}, u32[]{:S(2)}) collective-permute-start(bf16[1024,128]{1,0:T(8,128)(2,1)S(1)} %slice.47), channel_id=1, source_target_pairs={{0,3},{1,0},{2,1},{3,2},{4,7},{5,4},{6,5},{7,6},{8,11},{9,8},{10,9... | collective-permute-start | bytes 786440 | tf_op jit(solution)/shard_map/ppermute | solution.py:504
  117.0 2.7 %collective-permute-start.26 = (bf16[1024,128]{1,0:T(8,128)(2,1)S(1)}, bf16[1024,128]{1,0:T(8,128)(2,1)S(1)}, u32[]{:S(2)}, u32[]{:S(2)}) collective-permute-start(bf16[1024,128]{1,0:T(8,128)(2,1)S(1)} %slice.46), channel_id=1, source_target_pairs={{0,3},{1,0},{2,1},{3,2},{4,7},{5,4},{6,5},{7,6},{8,11},{9,8},{10,9... | collective-permute-start | bytes 786440 | tf_op jit(solution)/shard_map/ppermute | solution.py:504
  127.9 3.3 %backward_tiles.3 = bf16[16,128,128]{2,1,0:T(8,128)(2,1)S(1)} custom-call(s32[8,144]{1,0:T(8,128)S(1)} %copy-done.22, s32[8]{0:T(128)S(1)} %copy-done.23, bf16[1024,128]{1,0:T(8,128)(2,1)S(1)} %maximum_bitcast_fusion.rest_0_, bf16[1024,128]{1,0:T(8,128)(2,1)S(1)} %copy-done.19, bf16[1024,128]{1,0:T(8,128)(2,1)S(1)} %copy-done.15, ...), custom_call_target="tpu_custom_call" | custom-call | flops 3000000000 | bytes 8000000 | tf_op jit(solution)/shard_map/backward_tiles/pallas_call | solution.py:413
  131.3 4.5 %collective-permute-start.28 = (bf16[1024,128]{1,0:T(8,128)(2,1)S(1)}, bf16[1024,128]{1,0:T(8,128)(2,1)S(1)}, u32[]{:S(2)}, u32[]{:S(2)}) collective-permute-start(bf16[1024,128]{1,0:T(8,128)(2,1)S(1)} %bitcast.80), channel_id=1, source_target_pairs={{0,4},{4,8},{8,12},{12,16},{16,20},{20,24},{24,28},{28,32},{32,36}... | collective-permute-start | bytes 786440 | tf_op jit(solution)/shard_map/ppermute | solution.py:510
  138.0 6.4 %backward_tiles.2 = f32[32,128,128]{2,1,0:T(8,128)} custom-call(s32[8,144]{1,0:T(8,128)S(1)} %copy-done.22, s32[8]{0:T(128)S(1)} %copy-done.23, bf16[1024,128]{1,0:T(8,128)(2,1)S(1)} %maximum_bitcast_fusion.rest_0_, bf16[1024,128]{1,0:T(8,128)(2,1)S(1)} %copy-done.19, bf16[1024,128]{1,0:T(8,128)(2,1)S(1)} %copy-done.15, bf16[1024,128]{1,0:T(8,128)(2,1)S(1)} %copy-done.17, ...), custom_call_target="tpu_custom_call" | custom-call | flops 3000000000 | bytes 8000000 | tf_op jit(solution)/shard_map/backward_tiles/pallas_call | solution.py:413
  146.1 10.0 %last_products.1 = (bf16[4096,128]{1,0:T(8,128)(2,1)}, f32[32,128]{1,0:T(8,128)S(1)}, f32[32,128]{1,0:T(8,128)S(1)}, f32[32,128]{1,0:T(8,128)S(1)}, f32[32,128]{1,0:T(8,128)S(1)}) custom-call(s32[1]{0:T(128)} %bitcast.pos_ref, s32[2,1024]{1,0:T(2,128)S(1)} %bitcast.56, s32[2]{0:T(128)S(1)} %bitcast.58, f32[4096,128]{1,0:T(8,128)S(1)} %bitcast.42, ...), custom_call_target="tpu_custom_call" | custom-call | tf_op jit(solution)/shard_map/last_products/pallas_call | solution.py:483
  159.3 5.1 %collective-permute-start.48 = (f32[104,128]{1,0:T(8,128)S(1)}, f32[104,128]{1,0:T(8,128)S(1)}, u32[]{:S(2)}, u32[]{:S(2)}) collective-permute-start(f32[104,128]{1,0:T(8,128)S(1)} %add_add_fusion.1), channel_id=1, source_target_pairs={{0,24},{4,28},{8,0},{12,4},{16,8},{20,12},{24,16},{28,20},{32,56},... | collective-permute-start | bytes 159752 | tf_op jit(solution)/shard_map/ppermute | solution.py:520
  171.1 2.7 %collective-permute-start.38 = (f32[32,128]{1,0:T(8,128)S(1)}, f32[32,128]{1,0:T(8,128)S(1)}, u32[]{:S(2)}, u32[]{:S(2)}) collective-permute-start(f32[32,128]{1,0:T(8,128)S(1)} %add_add_fusion.4), channel_id=1, source_target_pairs={{0,24},{4,28},{8,0},{12,4},{16,8},{20,12},{24,16},{28,20},{32,56},... | collective-permute-start | bytes 49160 | tf_op jit(solution)/shard_map/ppermute | solution.py:520
  174.8 3.0 %collective-permute-done.37 = f32[32,128]{1,0:T(8,128)S(1)} collective-permute-done((f32[32,128]{1,0:T(8,128)S(1)}, f32[32,128]{1,0:T(8,128)S(1)}, u32[]{:S(2)}, u32[]{:S(2)}) %collective-permute-start.37) | collective-permute-done | bytes 16416 | tf_op jit(solution)/shard_map/ppermute | solution.py:520
  178.5 5.5 %collective-permute-start.39 = (f32[32,128]{1,0:T(8,128)S(1)}, f32[32,128]{1,0:T(8,128)S(1)}, u32[]{:S(2)}, u32[]{:S(2)}) collective-permute-start(f32[32,128]{1,0:T(8,128)S(1)} %add_add_fusion.3), channel_id=1, source_target_pairs={{0,4},{4,0},{8,12},{12,8},{16,20},{20,16},{24,28},{28,24},{32,36},... | collective-permute-start | bytes 49160 | tf_op jit(solution)/shard_map/ppermute | solution.py:520
  (171 shorter events, 73.6 us)
Async XLA Ops:
  2.7 17.5 %collective-permute-start.2 = (bf16[144,128]{1,0:T(8,128)(2,1)}, bf16[144,128]{1,0:T(8,128)(2,1)S(1)}, u32[]{:S(2)}, u32[]{:S(2)}) collective-permute-start(bf16[144,128]{1,0:T(8,128)(2,1)} %pack_small.1.s0_ref), channel_id=1, source_target_pairs={{0,1},{1,2},{2,3},{3,0},{4,5},{5,6},{6,7},{7,4},{8,9},{9,10},{10,1... | collective-permute-start | bytes 110600 | tf_op jit(solution)/shard_map/ppermute | solution.py:504
  5.2 17.2 %collective-permute-start.1 = (bf16[144,128]{1,0:T(8,128)(2,1)}, bf16[144,128]{1,0:T(8,128)(2,1)S(1)}, u32[]{:S(2)}, u32[]{:S(2)}) collective-permute-start(bf16[144,128]{1,0:T(8,128)(2,1)} %pack_small.1.s0_ref), channel_id=1, source_target_pairs={{0,2},{1,3},{2,0},{3,1},{4,6},{5,7},{6,4},{7,5},{8,10},{9,11},{10,... | collective-permute-start | bytes 110600 | tf_op jit(solution)/shard_map/ppermute | solution.py:504
  8.5 13.9 %collective-permute-start = (bf16[144,128]{1,0:T(8,128)(2,1)}, bf16[144,128]{1,0:T(8,128)(2,1)S(1)}, u32[]{:S(2)}, u32[]{:S(2)}) collective-permute-start(bf16[144,128]{1,0:T(8,128)(2,1)} %pack_small.1.s0_ref), channel_id=1, source_target_pairs={{0,3},{1,0},{2,1},{3,2},{4,7},{5,4},{6,5},{7,6},{8,11},{9,8},{10,9... | collective-permute-start | bytes 110600 | tf_op jit(solution)/shard_map/ppermute | solution.py:504
  11.3 25.7 %collective-permute-start.8 = (bf16[1024,128]{1,0:T(8,128)(2,1)S(1)}, bf16[1024,128]{1,0:T(8,128)(2,1)S(1)}, u32[]{:S(2)}, u32[]{:S(2)}) collective-permute-start(bf16[1024,128]{1,0:T(8,128)(2,1)S(1)} %maximum_bitcast_fusion.rest_0_), channel_id=1, source_target_pairs={{0,2},{1,3},{2,0},{3,1},{4,6},{5,7},{6,4},{7,5},{8,10},{9,11},{10,... | collective-permute-start | bytes 786440 | tf_op jit(solution)/shard_map/ppermute | solution.py:504
  11.8 34.5 %collective-permute-start.6 = (bf16[1024,128]{1,0:T(8,128)(2,1)S(1)}, bf16[1024,128]{1,0:T(8,128)(2,1)S(1)}, u32[]{:S(2)}, u32[]{:S(2)}) collective-permute-start(bf16[1024,128]{1,0:T(8,128)(2,1)S(1)} %maximum_bitcast_fusion.rest_0_), channel_id=1, source_target_pairs={{0,1},{1,2},{2,3},{3,0},{4,5},{5,6},{6,7},{7,4},{8,9},{9,10},{10,1... | collective-permute-start | bytes 786440 | tf_op jit(solution)/shard_map/ppermute | solution.py:504
  20.2 26.2 %collective-permute-start.5 = (bf16[1024,128]{1,0:T(8,128)(2,1)S(1)}, bf16[1024,128]{1,0:T(8,128)(2,1)S(1)}, u32[]{:S(2)}, u32[]{:S(2)}) collective-permute-start(bf16[1024,128]{1,0:T(8,128)(2,1)S(1)} %maximum_bitcast_fusion.rest_0_), channel_id=1, source_target_pairs={{0,3},{1,0},{2,1},{3,2},{4,7},{5,4},{6,5},{7,6},{8,11},{9,8},{10,9... | collective-permute-start | bytes 786440 | tf_op jit(solution)/shard_map/ppermute | solution.py:504
  23.7 13.3 %collective-permute-start.3 = (bf16[1024,128]{1,0:T(8,128)(2,1)}, bf16[1024,128]{1,0:T(8,128)(2,1)S(1)}, u32[]{:S(2)}, u32[]{:S(2)}) collective-permute-start(bf16[1024,128]{1,0:T(8,128)(2,1)} %get-tuple-element.58), channel_id=1, source_target_pairs={{0,4},{4,8},{8,12},{12,16},{16,20},{20,24},{24,28},{28,32},{32,36}... | collective-permute-start | bytes 786440 | tf_op jit(solution)/shard_map/ppermute | solution.py:510
  41.0 17.3 %collective-permute-start.9 = (bf16[8,128,128]{2,1,0:T(8,128)(2,1)S(1)}, bf16[8,128,128]{2,1,0:T(8,128)(2,1)S(1)}, u32[]{:S(2)}, u32[]{:S(2)}) collective-permute-start(bf16[8,128,128]{2,1,0:T(8,128)(2,1)S(1)} %get-tuple-element.64), channel_id=1, source_target_pairs={{0,3},{1,0},{2,1},{3,2},{4,7},{5,4},{6,5},{7,6},{8,11},{9,8},{10,9... | collective-permute-start | bytes 786440 | tf_op jit(solution)/shard_map/ppermute | solution.py:504
  41.1 17.0 %collective-permute-start.11 = (bf16[8,128,128]{2,1,0:T(8,128)(2,1)S(1)}, bf16[8,128,128]{2,1,0:T(8,128)(2,1)S(1)}, u32[]{:S(2)}, u32[]{:S(2)}) collective-permute-start(bf16[8,128,128]{2,1,0:T(8,128)(2,1)S(1)} %get-tuple-element.66), channel_id=1, source_target_pairs={{0,1},{1,2},{2,3},{3,0},{4,5},{5,6},{6,7},{7,4},{8,9},{9,10},{10,1... | collective-permute-start | bytes 786440 | tf_op jit(solution)/shard_map/ppermute | solution.py:504
  56.5 13.1 %collective-permute-start.16 = (bf16[8,128,128]{2,1,0:T(8,128)(2,1)S(1)}, bf16[8,128,128]{2,1,0:T(8,128)(2,1)S(1)}, u32[]{:S(2)}, u32[]{:S(2)}) collective-permute-start(bf16[8,128,128]{2,1,0:T(8,128)(2,1)S(1)} %add_convert_fusion.1), channel_id=1, source_target_pairs={{0,3},{1,0},{2,1},{3,2},{4,7},{5,4},{6,5},{7,6},{8,11},{9,8},{10,9... | collective-permute-start | bytes 786440 | tf_op jit(solution)/shard_map/ppermute | solution.py:504
  58.3 16.3 %collective-permute-start.7 = (bf16[8,128,128]{2,1,0:T(8,128)(2,1)S(1)}, bf16[8,128,128]{2,1,0:T(8,128)(2,1)S(1)}, u32[]{:S(2)}, u32[]{:S(2)}) collective-permute-start(bf16[8,128,128]{2,1,0:T(8,128)(2,1)S(1)} %get-tuple-element.62), channel_id=1, source_target_pairs={{0,1},{1,2},{2,3},{3,0},{4,5},{5,6},{6,7},{7,4},{8,9},{9,10},{10,1... | collective-permute-start | bytes 786440 | tf_op jit(solution)/shard_map/ppermute | solution.py:504
  59.5 15.8 %collective-permute-start.13 = (bf16[8,128,128]{2,1,0:T(8,128)(2,1)S(1)}, bf16[8,128,128]{2,1,0:T(8,128)(2,1)S(1)}, u32[]{:S(2)}, u32[]{:S(2)}) collective-permute-start(bf16[8,128,128]{2,1,0:T(8,128)(2,1)S(1)} %get-tuple-element.67), channel_id=1, source_target_pairs={{0,3},{1,0},{2,1},{3,2},{4,7},{5,4},{6,5},{7,6},{8,11},{9,8},{10,9... | collective-permute-start | bytes 786440 | tf_op jit(solution)/shard_map/ppermute | solution.py:504
  64.0 14.6 %collective-permute-start.10 = (bf16[8,128,128]{2,1,0:T(8,128)(2,1)S(1)}, bf16[8,128,128]{2,1,0:T(8,128)(2,1)S(1)}, u32[]{:S(2)}, u32[]{:S(2)}) collective-permute-start(bf16[8,128,128]{2,1,0:T(8,128)(2,1)S(1)} %add_convert_fusion.3), channel_id=1, source_target_pairs={{0,3},{1,0},{2,1},{3,2},{4,7},{5,4},{6,5},{7,6},{8,11},{9,8},{10,9... | collective-permute-start | bytes 786440 | tf_op jit(solution)/shard_map/ppermute | solution.py:504
  87.1 15.3 %collective-permute-start.24 = (bf16[2048,128]{1,0:T(8,128)(2,1)}, bf16[2048,128]{1,0:T(8,128)(2,1)S(1)}, u32[]{:S(2)}, u32[]{:S(2)}) collective-permute-start(bf16[2048,128]{1,0:T(8,128)(2,1)} %get-tuple-element.86), channel_id=1, source_target_pairs={{0,1},{1,2},{2,3},{3,0},{4,5},{5,6},{6,7},{7,4},{8,9},{9,10},{10,1... | collective-permute-start | bytes 1572872 | tf_op jit(solution)/shard_map/ppermute | solution.py:504
  88.8 14.0 %collective-permute-start.21 = (bf16[2048,128]{1,0:T(8,128)(2,1)}, bf16[2048,128]{1,0:T(8,128)(2,1)S(1)}, u32[]{:S(2)}, u32[]{:S(2)}) collective-permute-start(bf16[2048,128]{1,0:T(8,128)(2,1)} %get-tuple-element.86), channel_id=1, source_target_pairs={{0,3},{1,0},{2,1},{3,2},{4,7},{5,4},{6,5},{7,6},{8,11},{9,8},{10,9... | collective-permute-start | bytes 1572872 | tf_op jit(solution)/shard_map/ppermute | solution.py:504
  89.7 23.4 %collective-permute-start.22 = (bf16[2048,128]{1,0:T(8,128)(2,1)}, bf16[2048,128]{1,0:T(8,128)(2,1)S(1)}, u32[]{:S(2)}, u32[]{:S(2)}) collective-permute-start(bf16[2048,128]{1,0:T(8,128)(2,1)} %get-tuple-element.85), channel_id=1, source_target_pairs={{0,1},{1,2},{2,3},{3,0},{4,5},{5,6},{6,7},{7,4},{8,9},{9,10},{10,1... | collective-permute-start | bytes 1572872 | tf_op jit(solution)/shard_map/ppermute | solution.py:504
  90.3 23.2 %collective-permute-start.20 = (bf16[2048,128]{1,0:T(8,128)(2,1)}, bf16[2048,128]{1,0:T(8,128)(2,1)S(1)}, u32[]{:S(2)}, u32[]{:S(2)}) collective-permute-start(bf16[2048,128]{1,0:T(8,128)(2,1)} %get-tuple-element.85), channel_id=1, source_target_pairs={{0,3},{1,0},{2,1},{3,2},{4,7},{5,4},{6,5},{7,6},{8,11},{9,8},{10,9... | collective-permute-start | bytes 1572872 | tf_op jit(solution)/shard_map/ppermute | solution.py:504
  94.1 22.9 %collective-permute-start.40 = (f32[104,128]{1,0:T(8,128)}, f32[104,128]{1,0:T(8,128)S(1)}, u32[]{:S(2)}, u32[]{:S(2)}) collective-permute-start(f32[104,128]{1,0:T(8,128)} %get-tuple-element.99), channel_id=1, source_target_pairs={{0,1},{1,2},{2,3},{3,0},{4,5},{5,6},{6,7},{7,4},{8,9},{9,10},{10,1... | collective-permute-start | bytes 159752 | tf_op jit(solution)/shard_map/ppermute | solution.py:504
  102.4 14.6 %collective-permute-start.41 = (f32[104,128]{1,0:T(8,128)}, f32[104,128]{1,0:T(8,128)S(1)}, u32[]{:S(2)}, u32[]{:S(2)}) collective-permute-start(f32[104,128]{1,0:T(8,128)} %get-tuple-element.100), channel_id=1, source_target_pairs={{0,2},{1,3},{2,0},{3,1},{4,6},{5,7},{6,4},{7,5},{8,10},{9,11},{10,... | collective-permute-start | bytes 159752 | tf_op jit(solution)/shard_map/ppermute | solution.py:504
  102.8 19.6 %collective-permute-start.42 = (f32[104,128]{1,0:T(8,128)}, f32[104,128]{1,0:T(8,128)S(1)}, u32[]{:S(2)}, u32[]{:S(2)}) collective-permute-start(f32[104,128]{1,0:T(8,128)} %get-tuple-element.101), channel_id=1, source_target_pairs={{0,3},{1,0},{2,1},{3,2},{4,7},{5,4},{6,5},{7,6},{8,11},{9,8},{10,9... | collective-permute-start | bytes 159752 | tf_op jit(solution)/shard_map/ppermute | solution.py:504
  122.4 35.2 %collective-permute-start.45 = (f32[104,128]{1,0:T(8,128)S(1)}, f32[104,128]{1,0:T(8,128)S(1)}, u32[]{:S(2)}, u32[]{:S(2)}) collective-permute-start(f32[104,128]{1,0:T(8,128)S(1)} %add_add_fusion.2), channel_id=1, source_target_pairs={{0,96},{4,100},{8,104},{12,108},{16,112},{20,116},{24,120},{28,124... | collective-permute-start | bytes 159752 | tf_op jit(solution)/shard_map/ppermute | solution.py:520
  124.8 34.4 %collective-permute-start.44 = (f32[104,128]{1,0:T(8,128)S(1)}, f32[104,128]{1,0:T(8,128)S(1)}, u32[]{:S(2)}, u32[]{:S(2)}) collective-permute-start(f32[104,128]{1,0:T(8,128)S(1)} %add_add_fusion.2), channel_id=1, source_target_pairs={{0,64},{4,68},{8,72},{12,76},{16,80},{20,84},{24,88},{28,92},{32,9... | collective-permute-start | bytes 159752 | tf_op jit(solution)/shard_map/ppermute | solution.py:520
  126.4 32.9 %collective-permute-start.43 = (f32[104,128]{1,0:T(8,128)S(1)}, f32[104,128]{1,0:T(8,128)S(1)}, u32[]{:S(2)}, u32[]{:S(2)}) collective-permute-start(f32[104,128]{1,0:T(8,128)S(1)} %add_add_fusion.2), channel_id=1, source_target_pairs={{0,32},{4,36},{8,40},{12,44},{16,48},{20,52},{24,56},{28,60},{32,6... | collective-permute-start | bytes 159752 | tf_op jit(solution)/shard_map/ppermute | solution.py:520
  131.3 13.2 %collective-permute-start.28 = (bf16[1024,128]{1,0:T(8,128)(2,1)S(1)}, bf16[1024,128]{1,0:T(8,128)(2,1)S(1)}, u32[]{:S(2)}, u32[]{:S(2)}) collective-permute-start(bf16[1024,128]{1,0:T(8,128)(2,1)S(1)} %bitcast.80), channel_id=1, source_target_pairs={{0,4},{4,8},{8,12},{12,16},{16,20},{20,24},{24,28},{28,32},{32,36}... | collective-permute-start | bytes 786440 | tf_op jit(solution)/shard_map/ppermute | solution.py:510
  (53 other events, 397.0 us)

commit v3 on v2

v3 whole, which is shorter than its diff:
```python
import functools

import jax
import jax.numpy as jnp
from jax import lax
from jax.experimental import pallas as pl
from jax.experimental.pallas import tpu as pltpu
from jax.sharding import PartitionSpec as P

F32 = jnp.float32
BF16 = jnp.bfloat16
SIDE = 128
UNROLL = 4
PARAMS = pltpu.CompilerParams(vmem_limit_bytes=20 * 2**20)
ROOMY = pltpu.CompilerParams(vmem_limit_bytes=60 * 2**20)
VMEM = pl.BlockSpec(memory_space=pltpu.VMEM)
SMEM = pl.BlockSpec(memory_space=pltpu.SMEM)
ANY = pl.BlockSpec(memory_space=pl.ANY)


def cost(flops, size):
    return pl.CostEstimate(flops=flops, bytes_accessed=size, transcendentals=0)


def dot(left, right, dims):
    return lax.dot_general(left, right, (dims, ((), ())), preferred_element_type=F32)


def rows_by_cols(left, right):
    return dot(left, right, ((1,), (0,)))


def contract_rows(left, right):
    return dot(left, right, ((0,), (0,)))


def contract_cols(left, right):
    return dot(left, right, ((1,), (1,)))


def sigmoid(v):
    return 1.0 / (1.0 + jnp.exp(-v))


def silu_slope(v):
    g = sigmoid(v)
    return g * (1.0 + v * (1.0 - g))


def pick_kernel(rows_ref, count_ref, feat_ref, out_ref, wide, picked):
    halo = rows_ref.shape[1]
    wide[...] = feat_ref[...].astype(F32)
    group = 16
    for k in range(2):
        count = count_ref[k]

        def body(step, carry):
            for u in range(group):
                slot = step * group + u
                row = rows_ref[k, slot]
                picked[pl.ds(slot, 1), :] = wide[pl.ds(row, 1), :]
            return carry

        lax.fori_loop(0, (count + group - 1) // group, body, 0)
        slots = lax.broadcasted_iota(jnp.int32, (halo, SIDE), 0)
        kept = jnp.where(slots < count, picked[...], 0.0)
        out_ref[pl.ds(k * halo, halo), :] = kept.astype(BF16)


def pick_rows(halo_rows, halo_count, node_feat):
    halo = halo_rows.shape[1]
    return pl.pallas_call(
        pick_kernel,
        out_shape=jax.ShapeDtypeStruct((2 * halo, SIDE), BF16),
        in_specs=[SMEM, SMEM, VMEM],
        out_specs=VMEM,
        scratch_shapes=[pltpu.VMEM(node_feat.shape, F32), pltpu.VMEM((halo, SIDE), F32)],
        compiler_params=ROOMY,
        name="pick_rows",
    )(halo_rows, halo_count, node_feat)


def pack_kernel(
    count_ref, values_ref, cols_ref, msg_ref, in_ref, out_w_ref, gain_ref, dst_ref, src_ref, pack_ref, lines
):
    share, edges = msg_ref.shape[0], values_ref.shape[0]
    pack_ref[pl.ds(0, edges), :] = values_ref[...]
    pack_ref[pl.ds(edges, edges), :] = cols_ref[...].astype(F32).astype(BF16)
    small = 2 * edges
    pack_ref[pl.ds(small, share), :] = msg_ref[...]
    pack_ref[pl.ds(small + share, 2 * share), :] = in_ref[...]
    pack_ref[pl.ds(small + 3 * share, share), :] = out_w_ref[...]
    lines[...] = jnp.zeros_like(lines)
    gain = gain_ref[...].astype(F32)
    for j in range(SIDE // share):
        lines[0:1, j * share : (j + 1) * share] = gain
    lines[1:2, :] = dst_ref[...].astype(F32)
    lines[2:3, :] = src_ref[...].astype(F32)
    lines[3:4, :] = jnp.full((1, SIDE), count_ref[0]).astype(F32)
    pack_ref[pl.ds(small + 4 * share, 16), :] = lines[...].astype(BF16)


def pack_shares(tile_count, tile_values, tile_cols, w_msg, w_in, w_out, ln_gain, tile_dst, tile_src):
    share = w_msg.shape[0]
    values, cols = (array.reshape(-1, SIDE) for array in (tile_values, tile_cols))
    return pl.pallas_call(
        pack_kernel,
        out_shape=jax.ShapeDtypeStruct((2 * values.shape[0] + 4 * share + 16, SIDE), BF16),
        in_specs=[SMEM] + [VMEM] * 8,
        out_specs=VMEM,
        scratch_shapes=[pltpu.VMEM((16, SIDE), F32)],
        compiler_params=ROOMY,
        name="pack_shares",
    )(
        tile_count, values, cols, w_msg, w_in, w_out, ln_gain.reshape(1, share), tile_dst.reshape(1, SIDE),
        tile_src.reshape(1, SIDE),
    )


def prepare_kernel(
    own_blocks, here_blocks, pos_ref, s0_ref, s1_ref, s2_ref, s3_ref, picked_ref,
    low_ref, high_ref, msg_ref, in_ref, out_w_ref, gain_ref, code_ref,
):
    me = pos_ref[0]
    smalls = (s0_ref, s1_ref, s2_ref, s3_ref)
    parties = len(smalls)
    share = SIDE // parties
    small = s0_ref.shape[0] - SIDE - 16
    lane = lax.broadcasted_iota(jnp.int32, (1, SIDE), 1)
    gain = jnp.zeros((1, SIDE), F32)
    for k, ref in enumerate(smalls):
        device = lax.rem(me + k, parties)
        at = pl.multiple_of(device * share, share)
        msg_ref[pl.ds(at, share), :] = ref[pl.ds(small, share), :]
        in_ref[pl.ds(pl.multiple_of(2 * at, 2 * share), 2 * share), :] = ref[pl.ds(small + share, 2 * share), :]
        out_w_ref[pl.ds(at, share), :] = ref[pl.ds(small + 3 * share, share), :]
        lines = ref[pl.ds(small + 4 * share, 16), :].astype(F32)
        gain = jnp.where((lane >= at) & (lane < at + share), lines[0:1, :], gain)
        dst, src, count = (lines[i : i + 1, :].astype(jnp.int32) for i in (1, 2, 3))
        block = src - me * here_blocks
        used = (lane < count) & (block >= 0) & (block < here_blocks)
        is_rim = block >= own_blocks
        place = jnp.where(is_rim, block - own_blocks, block)
        code = lane + (place << 7) + (dst << 13) + jnp.where(is_rim, 2 << 20, 1 << 20)
        code_ref[k : k + 1, :] = jnp.where(used, code, 0)
        code_ref[parties + k : parties + k + 1, :] = count
    gain_ref[...] = gain
    half = low_ref.shape[0]
    w_msg = msg_ref[...]
    for k, ref in enumerate((low_ref, high_ref)):
        pre = rows_by_cols(picked_ref[pl.ds(k * half, half), :], w_msg)
        ref[...] = (pre * sigmoid(pre)).astype(BF16)


def prepare(position, smalls, picked, own_blocks, here_blocks):
    half = picked.shape[0] // 2
    return pl.pallas_call(
        functools.partial(prepare_kernel, own_blocks, here_blocks),
        out_shape=(
            jax.ShapeDtypeStruct((half, SIDE), BF16),
            jax.ShapeDtypeStruct((half, SIDE), BF16),
            jax.ShapeDtypeStruct((SIDE, SIDE), BF16),
            jax.ShapeDtypeStruct((2 * SIDE, SIDE), BF16),
            jax.ShapeDtypeStruct((SIDE, SIDE), BF16),
            jax.ShapeDtypeStruct((1, SIDE), F32),
            jax.ShapeDtypeStruct((8, SIDE), jnp.int32),
        ),
        in_specs=[SMEM] + [VMEM] * 5,
        out_specs=(VMEM,) * 7,
        compiler_params=PARAMS,
        name="prepare",
    )(position, *smalls, picked)


def message_kernel(feat_ref, msg_ref, out_ref):
    pre = rows_by_cols(feat_ref[...], msg_ref[...])
    out_ref[...] = (pre * sigmoid(pre)).astype(BF16)


def messages(feat, w_msg):
    rows = feat.shape[0]
    steps = 2
    tall = pl.BlockSpec((rows // steps, SIDE), lambda i: (i, 0))
    return pl.pallas_call(
        message_kernel,
        grid=(steps,),
        out_shape=jax.ShapeDtypeStruct((rows, SIDE), BF16),
        in_specs=[tall, pl.BlockSpec(w_msg.shape, lambda i: (0, 0))],
        out_specs=tall,
        compiler_params=PARAMS,
        name="messages",
    )(feat, w_msg)


def list_kernel(code_ref, list_ref, total_ref):
    parties = code_ref.shape[0] // 2
    group = 8
    for k in range(parties):

        def body(step, carry):
            own, rim = carry
            for u in range(group):
                code = code_ref[k, step * group + u]
                list_ref[2 * k, own] = code
                list_ref[2 * k + 1, rim] = code
                own = own + ((code >> 20) & 1)
                rim = rim + (code >> 21)
            return (own, rim)

        steps = (code_ref[parties + k, 0] + group - 1) // group
        own, rim = lax.fori_loop(0, steps, body, (jnp.int32(0), jnp.int32(0)))
        total_ref[2 * k] = own
        total_ref[2 * k + 1] = rim


def build_lists(codes):
    parties, slots = codes.shape[0] // 2, codes.shape[1]
    return pl.pallas_call(
        list_kernel,
        out_shape=(
            jax.ShapeDtypeStruct((2 * parties, slots + 16), jnp.int32),
            jax.ShapeDtypeStruct((2 * parties,), jnp.int32),
        ),
        in_specs=[SMEM],
        out_specs=(SMEM, SMEM),
        name="tile_lists",
    )(codes)


def dense_tile(tiles_ref, slot, keep):
    column = lax.broadcasted_iota(jnp.int32, (SIDE, SIDE), 0).astype(F32)
    edges = tiles_ref.shape[0] // 2
    entries = edges // SIDE
    total = None
    for e in range(entries):
        at = slot * entries + e
        weight = tiles_ref[pl.ds(at, 1), :] * keep
        term = jnp.where(column == tiles_ref[pl.ds(edges + at, 1), :], weight, 0.0)
        total = term if total is None else total + term
    return total.astype(BF16)


def walk_list(list_ref, total_ref, which, tiles_ref, product, acc):
    count = total_ref[which]

    def body(step, carry):
        found = []
        for u in range(UNROLL):
            index = step * UNROLL + u
            used = index < count
            entry = jnp.where(used, list_ref[which, index], 0)
            dense = dense_tile(tiles_ref, entry & 127, jnp.where(used, 1.0, 0.0))
            found.append(product(dense, (entry >> 7) & 63, (entry >> 13) & 31))
        for target, value in found:
            acc[target] += value
        return carry

    lax.fori_loop(0, (count + UNROLL - 1) // UNROLL, body, 0)


def forward_kernel(ks, list_ref, total_ref, own_ref, lower_ref, upper_ref, *rest):
    slot_refs, rest = rest[: len(ks)], rest[len(ks) :]
    outs, (acc, rims, tiles) = rest[: 2 * len(ks)], rest[2 * len(ks) :]
    half = lower_ref.shape[0]
    rims[pl.ds(0, half)] = lower_ref[...]
    rims[pl.ds(half, half)] = upper_ref[...]
    for at, (k, slot_ref) in enumerate(zip(ks, slot_refs)):
        acc[...] = jnp.zeros_like(acc)
        tiles[...] = slot_ref[pl.ds(0, tiles.shape[0]), :].astype(F32)
        for part, ref in enumerate((own_ref, rims)):

            def product(dense, block, target, ref=ref):
                return (target, contract_rows(dense, ref[block]))

            walk_list(list_ref, total_ref, 2 * k + part, tiles, product, acc)
        for h in range(2):
            out_ref = outs[2 * at + h]
            span = out_ref.shape[0]
            out_ref[...] = acc[pl.ds(h * span, span)].astype(out_ref.dtype)


def forward_tiles(ks, lists, totals, own, lower, upper, tiles, kind):
    blocks = own.shape[0]
    half = jax.ShapeDtypeStruct((blocks // 2,) + own.shape[1:], kind)
    return pl.pallas_call(
        functools.partial(forward_kernel, ks),
        out_shape=(half,) * (2 * len(ks)),
        in_specs=[SMEM, SMEM] + [VMEM] * (3 + len(ks)),
        out_specs=(VMEM,) * (2 * len(ks)),
        scratch_shapes=[
            pltpu.VMEM(own.shape, F32),
            pltpu.VMEM((2 * lower.shape[0],) + lower.shape[1:], BF16),
            pltpu.VMEM((tiles[0].shape[0] - SIDE - 16, SIDE), F32),
        ],
        compiler_params=PARAMS,
        cost_estimate=cost(1_000_000_000 * len(ks), 4_000_000 * len(ks)),
        name="forward_tiles",
    )(lists, totals, own, lower, upper, *[tiles[k] for k in ks])


def join_kernel(after_ref, left_ref, prior_ref, right_ref, *outs):
    for mine, theirs, out_ref in ((after_ref, left_ref, outs[0]), (prior_ref, right_ref, outs[1])):
        out_ref[...] = (mine[...].astype(F32) + theirs[...].astype(F32)).astype(BF16)


def join(after, from_left, prior, from_right):
    kind = jax.ShapeDtypeStruct(after.shape, BF16)
    return pl.pallas_call(
        join_kernel,
        out_shape=(kind, kind),
        in_specs=[VMEM] * 4,
        out_specs=(VMEM, VMEM),
        compiler_params=PARAMS,
        name="join",
    )(after, from_left, prior, from_right)


def node_kernel(
    feat_ref, cot_ref, own_a_ref, own_b_ref, la_ref, ra_ref, lb_ref, rb_ref, in_ref, out_w_ref, gain_ref,
    node_ref, dhid_ref, dagg_ref, dwin_ref, dwout_ref, dgain_ref,
):
    step = pl.program_id(0)

    @pl.when(step == 0)
    def _():
        for ref in (dwin_ref, dwout_ref, dgain_ref):
            ref[...] = jnp.zeros_like(ref)

    feat = feat_ref[...]
    first = step < pl.num_programs(0) // 2
    left = jnp.where(first, la_ref[...].astype(F32), lb_ref[...].astype(F32))
    right = jnp.where(first, ra_ref[...].astype(F32), rb_ref[...].astype(F32))
    own = jnp.where(first, own_a_ref[...], own_b_ref[...])
    agg = (own + (left + right)).astype(BF16)
    w_feat, w_agg, w_out = in_ref[:SIDE, :], in_ref[SIDE:, :], out_w_ref[...]
    gain = gain_ref[...]
    pre = rows_by_cols(feat, w_feat) + rows_by_cols(agg, w_agg)
    logistic = sigmoid(pre)
    hidden = (pre * logistic).astype(BF16)
    slope = logistic * (1.0 + pre * (1.0 - logistic))
    update = rows_by_cols(hidden, w_out)
    centre = update - jnp.mean(update, axis=-1, keepdims=True)
    inverse = lax.rsqrt(jnp.mean(centre * centre, axis=-1, keepdims=True) + 1e-05)
    normed = centre * inverse
    node_ref[...] = (feat.astype(F32) + gain * normed).astype(BF16)
    upstream = cot_ref[...].astype(F32)
    d_normed = upstream * gain
    dgain_ref[...] += jnp.sum(upstream * normed, axis=0, keepdims=True)
    d_update = (
        d_normed
        - jnp.mean(d_normed, axis=-1, keepdims=True)
        - normed * jnp.mean(d_normed * normed, axis=-1, keepdims=True)
    ) * inverse
    d_update = d_update.astype(BF16)
    d_hidden = (contract_cols(d_update, w_out) * slope).astype(BF16)
    dhid_ref[...] = d_hidden
    dagg_ref[...] = contract_cols(d_hidden, w_agg).astype(BF16)
    dwout_ref[...] += contract_rows(hidden, d_update)
    dwin_ref[:SIDE, :] += contract_rows(feat, d_hidden)
    dwin_ref[SIDE:, :] += contract_rows(agg, d_hidden)


def node_update(node_feat, cotangent, parts, w_in, w_out, gain):
    rows = node_feat.shape[0]
    chunk = 512
    steps = rows // chunk
    per = steps // 2

    def whole(shape):
        return pl.BlockSpec(shape, lambda i: (0, 0))

    tall = pl.BlockSpec((chunk, SIDE), lambda i: (i, 0))
    part_a = pl.BlockSpec((chunk, SIDE), lambda i: (jnp.minimum(i, per - 1), 0))
    part_b = pl.BlockSpec((chunk, SIDE), lambda i: (jnp.maximum(i - per, 0), 0))
    wide = jax.ShapeDtypeStruct((rows, SIDE), BF16)
    sums = [(2 * SIDE, SIDE), (SIDE, SIDE), (1, SIDE)]
    return pl.pallas_call(
        node_kernel,
        grid=(steps,),
        out_shape=(wide, wide, wide) + tuple(jax.ShapeDtypeStruct(shape, F32) for shape in sums),
        in_specs=[tall, tall, part_a, part_b, part_a, part_a, part_b, part_b]
        + [whole((2 * SIDE, SIDE)), whole((SIDE, SIDE)), whole((1, SIDE))],
        out_specs=(tall, tall, tall) + tuple(whole(shape) for shape in sums),
        compiler_params=PARAMS,
        cost_estimate=cost(10_000_000_000, 20_000_000),
        name="node_update",
    )(node_feat, cotangent, *parts, w_in, w_out, gain)


def ahead_kernel(feat_ref, cot_ref, dhid_ref, msg_ref, in_ref, slope_ref, base_ref):
    slope_ref[...] = silu_slope(rows_by_cols(feat_ref[...], msg_ref[...]))
    base_ref[...] = cot_ref[...].astype(F32) + contract_cols(dhid_ref[...], in_ref[:SIDE, :])


def ahead(feat, cot, dhid, w_msg, w_in):
    rows = feat.shape[0]
    steps = 4
    tall = pl.BlockSpec((rows // steps, SIDE), lambda i: (i, 0))
    wide = jax.ShapeDtypeStruct((rows, SIDE), F32)
    return pl.pallas_call(
        ahead_kernel,
        grid=(steps,),
        out_shape=(wide, wide),
        in_specs=[tall] * 3 + [pl.BlockSpec(w.shape, lambda i: (0, 0)) for w in (w_msg, w_in)],
        out_specs=(tall, tall),
        compiler_params=PARAMS,
        cost_estimate=cost(3_000_000_000, 7_000_000),
        name="ahead",
    )(feat, cot, dhid, w_msg, w_in)


def backward_kernel(ks, cuts, parts, started, list_ref, total_ref, *rest):
    slot_refs, rest = rest[: len(ks)], rest[len(ks) :]
    tiles, grads, accs = rest[-2 - len(parts)], rest[-1 - len(parts)], rest[-len(parts) :]
    arrays, rest = rest[: cuts * len(ks)], rest[cuts * len(ks) : -2 - len(parts)]
    for at, acc in enumerate(accs):
        acc[...] = rest[at][...] if started else jnp.zeros_like(acc)
    for at, (k, slot_ref) in enumerate(zip(ks, slot_refs)):
        tiles[...] = slot_ref[pl.ds(0, tiles.shape[0]), :].astype(F32)
        source = arrays[at]
        if cuts > 1:
            source, span = grads, grads.shape[0] // cuts
            for c in range(cuts):
                grads[pl.ds(c * span, span)] = arrays[cuts * at + c][...]

        def product(dense, block, target, source=source):
            return (block, rows_by_cols(dense, source[target]))

        for part, acc in zip(parts, accs):
            walk_list(list_ref, total_ref, 2 * k + part, tiles, product, acc)
    if parts == (1,):
        half = accs[0].shape[0] // 2
        for at, out_ref in enumerate(rest[-2:]):
            out_ref[...] = accs[0][pl.ds(at * half, half)].astype(out_ref.dtype)
    else:
        for out_ref, acc in zip(rest[-len(parts) :], accs):
            out_ref[...] = acc[...]


def backward_tiles(ks, parts, sizes, kinds, lists, totals, tiles, arrays, started, follow=()):
    cuts = len(arrays[0])
    cubes = [array.reshape(-1, SIDE, SIDE) for group in arrays for array in group]
    accs = [sum(sizes)] if len(sizes) > len(parts) else sizes
    return pl.pallas_call(
        functools.partial(backward_kernel, ks, cuts, parts, bool(started)),
        out_shape=tuple(jax.ShapeDtypeStruct((size, SIDE, SIDE), kind) for size, kind in zip(sizes, kinds)),
        in_specs=[SMEM, SMEM] + [VMEM] * (len(ks) + len(cubes) + len(started)) + [ANY] * len(follow),
        out_specs=(VMEM,) * len(sizes),
        scratch_shapes=[pltpu.VMEM((tiles[0].shape[0] - SIDE - 16, SIDE), F32), pltpu.VMEM((cuts * cubes[0].shape[0], SIDE, SIDE), BF16)]
        + [pltpu.VMEM((size, SIDE, SIDE), F32) for size in accs],
        compiler_params=PARAMS,
        cost_estimate=cost(2_000_000_000 * len(ks), 4_000_000),
        name="backward_tiles",
    )(lists, totals, *[tiles[k] for k in ks], *cubes, *started, *follow)


def last_kernel(
    pos_ref, rows_ref, count_ref, own_ref, lower_ref, upper_ref, msg_ref, dwin_ref, dwout_ref, dgain_ref,
    feat_ref, slope_ref, base_ref,
    dnode_ref, r0_ref, r1_ref, r2_ref, r3_ref, back, dw, acc,
):
    halo = rows_ref.shape[1]
    acc[...] = own_ref[...]
    group = 16
    for k, ref in enumerate((lower_ref, upper_ref)):
        count = count_ref[k]
        slots = lax.broadcasted_iota(jnp.int32, (halo, SIDE), 0)
        back[...] = jnp.where(slots < count, ref[...].astype(F32), 0.0)

        def body(step, carry):
            rows = [rows_ref[k, step * group + u] for u in range(group)]
            added = [
                acc[pl.ds(row, 1), :] + back[pl.ds(step * group + u, 1), :] for u, row in enumerate(rows)
            ]
            for row, value in zip(rows, added):
                acc[pl.ds(row, 1), :] = value
            return carry

        lax.fori_loop(0, (count + group - 1) // group, body, 0)
    w_msg = msg_ref[...]
    dw[...] = jnp.zeros_like(dw)
    chunk = 512

    def step_rows(step, carry):
        at = pl.ds(pl.multiple_of(step * chunk, chunk), chunk)
        d_pre = (acc[at, :] * slope_ref[at, :]).astype(BF16)
        dw[...] += contract_rows(feat_ref[at, :], d_pre)
        dnode_ref[at, :] = (base_ref[at, :] + contract_cols(d_pre, w_msg)).astype(BF16)
        return carry

    lax.fori_loop(0, acc.shape[0] // chunk, step_rows, 0)
    outs = (r0_ref, r1_ref, r2_ref, r3_ref)
    share = SIDE // len(outs)
    for k, out in enumerate(outs):
        device = lax.rem(pos_ref[0] + k, len(outs))
        start = pl.multiple_of(device * share, share)
        gain = jnp.zeros((16, SIDE), F32)
        for j in range(len(outs)):
            wide = jnp.broadcast_to(dgain_ref[...], (16, SIDE))
            gain = jnp.where(device == j, pltpu.roll(wide, (SIDE - j * share) % SIDE, 1), gain)
        out[pl.ds(0, share), :] = dw[pl.ds(start, share), :].astype(out.dtype)
        at = pl.ds(pl.multiple_of(2 * start, 2 * share), 2 * share)
        out[pl.ds(share, 2 * share), :] = dwin_ref[at, :].astype(out.dtype)
        out[pl.ds(3 * share, share), :] = dwout_ref[pl.ds(start, share), :].astype(out.dtype)
        out[pl.ds(4 * share, 16), :] = gain.astype(out.dtype)


def last_products(position, halo_rows, halo_count, own, lower, upper, w_msg, sums, feat, slope, base):
    rows = feat.shape[0]
    piece = jax.ShapeDtypeStruct((SIDE + 16, SIDE), BF16)
    return pl.pallas_call(
        last_kernel,
        out_shape=(jax.ShapeDtypeStruct((rows, SIDE), BF16), piece, piece, piece, piece),
        in_specs=[SMEM] * 3 + [VMEM] * 10,
        out_specs=(VMEM,) * 5,
        scratch_shapes=[
            pltpu.VMEM((halo_rows.shape[1], SIDE), F32),
            pltpu.VMEM((SIDE, SIDE), F32),
            pltpu.VMEM((rows, SIDE), F32),
        ],
        compiler_params=PARAMS,
        name="last_products",
    )(position, halo_rows, halo_count, own, lower, upper, w_msg, *sums, feat, slope, base)


def shift_wsh(value, step):
    parties = lax.axis_size("wsh")
    return lax.ppermute(value, "wsh", [(i, (i + step) % parties) for i in range(parties)])


def shift_slab(value, step):
    count = lax.axis_size("slab")
    pairs = [(i, i + step) for i in range(count) if 0 <= i + step < count]
    return lax.ppermute(value, "slab", pairs)


def sum_group(terms):
    total = terms[0].astype(F32)
    for term in terms[1:]:
        total = total + term.astype(F32)
    return total.astype(BF16)


def sum_everywhere(pieces):
    count = lax.axis_size("slab")
    value = sum_group([pieces[0]] + [shift_wsh(pieces[k], k) for k in range(1, len(pieces))])
    for stride, size in ((8, 4), (2, 4)):
        span = stride * size
        turns = [[(i, (i // span) * span + (i + stride * k) % span) for i in range(count)] for k in range(1, size)]
        value = sum_group([value] + [lax.ppermute(value, "slab", pairs) for pairs in turns])
    return value, lax.ppermute(value, "slab", [(i, i ^ 1) for i in range(count)])


def finish_kernel(one_ref, two_ref, msg_ref, in_ref, out_w_ref, gain_ref):
    share = msg_ref.shape[0]
    total = one_ref[...].astype(F32) + two_ref[...].astype(F32)
    msg_ref[...] = total[:share]
    in_ref[...] = total[share : 3 * share]
    out_w_ref[...] = total[3 * share : 4 * share]
    gain_ref[...] = total[4 * share : 4 * share + 1, :share]


def finish(one, two):
    share = SIDE // 4
    shapes = [(share, SIDE), (2 * share, SIDE), (share, SIDE), (1, share)]
    return pl.pallas_call(
        finish_kernel,
        out_shape=tuple(jax.ShapeDtypeStruct(shape, F32) for shape in shapes),
        in_specs=[VMEM, VMEM],
        out_specs=(VMEM,) * 4,
        name="finish",
    )(one, two)


def on_device(
    node_feat, cotangent, w_msg, w_in, w_out, ln_gain,
    tile_values, tile_cols, tile_dst, tile_src, tile_count, halo_rows, halo_count,
):
    node_rows = node_feat.shape[0]
    slots, entries, side = tile_values.shape
    halo = halo_rows.shape[2]
    parties = lax.axis_size("wsh")
    me = lax.axis_index("wsh").astype(jnp.int32)
    position = me.reshape(1)
    share = w_msg.shape[0]
    own_blocks = node_rows // side
    rim_blocks = 2 * halo // side

    tile = pack_shares(tile_count, tile_values, tile_cols, w_msg, w_in, w_out, ln_gain, tile_dst, tile_src)
    tiles = [tile] + [shift_wsh(tile, -k) for k in range(1, parties)]

    rows = halo_rows.reshape(2, halo)
    counts = halo_count.reshape(2)
    picked = pick_rows(rows, counts, node_feat)
    low, high, full_msg, full_in, full_out, gain, codes = prepare(
        position, tiles, picked, own_blocks, own_blocks + rim_blocks
    )
    lower = shift_slab(high, 1).reshape(rim_blocks // 2, side, side)
    upper = shift_slab(low, -1).reshape(rim_blocks // 2, side, side)
    message = messages(node_feat, full_msg)
    lists, totals = build_lists(codes)
    forward = functools.partial(
        forward_tiles, lists=lists, totals=totals, own=message.reshape(own_blocks, side, side), lower=lower,
        upper=upper, tiles=tiles,
    )

    far_first, far_second = forward((2,), kind=BF16)
    from_right = shift_wsh(far_first, -1)
    from_left = shift_wsh(far_second, 1)
    after_first, after_second, prior_first, prior_second = forward((1, 3), kind=BF16)
    left_first = shift_wsh(after_first, 1)
    right_second = shift_wsh(prior_second, -1)
    mine_first, mine_second = forward((0,), kind=F32)
    to_after, to_prior = join(after_second, from_left, prior_first, from_right)
    left_second = shift_wsh(to_after, 1)
    right_first = shift_wsh(to_prior, -1)
    parts = (mine_first, mine_second, left_first, right_first, left_second, right_second)
    parts = [part.reshape(-1, side) for part in parts]
    node_out, d_hidden, d_agg, *sums = node_update(node_feat, cotangent, parts, full_in, full_out, gain)
    from_prior = shift_wsh(d_agg, 1)
    from_after = shift_wsh(d_agg, -1)
    half = node_rows // 2
    far_first = shift_wsh(from_prior[:half], 1)
    far_second = shift_wsh(from_after[half:], -1)
    slope, base = ahead(node_feat, cotangent, d_hidden, full_msg, full_in)

    backward = functools.partial(backward_tiles, lists=lists, totals=totals, tiles=tiles)
    own_part, rim_part = backward(
        (0, 1, 3), (0, 1), (own_blocks, rim_blocks), (F32, F32), arrays=((d_agg,), (from_after,), (from_prior,)),
        started=(),
    )
    far = ((far_first, far_second),)
    back_low, back_high = backward(
        (2,), (1,), (rim_blocks // 2,) * 2, (BF16,) * 2, arrays=far, started=(rim_part,), follow=(slope,)
    )
    back_upper = shift_slab(back_low.reshape(halo, side), -1)
    back_lower = shift_slab(back_high.reshape(halo, side), 1)
    (d_own,) = backward((2,), (0,), (own_blocks,), (F32,), arrays=far, started=(own_part,))
    d_node, *pieces = last_products(
        position, rows, counts, d_own.reshape(node_rows, side), back_lower, back_upper, full_msg, sums, node_feat,
        slope, base,
    )
    d_w_msg, d_w_in, d_w_out, d_gain = finish(*sum_everywhere(pieces))
    return (node_out, d_node, d_w_msg, d_w_in, d_w_out, d_gain.reshape(share))


def solution(mesh):
    both = ("slab", "wsh")
    tall, split, line = P(both, None), P("wsh", None), P(both)
    cube = P(both, None, None)
    return jax.shard_map(
        on_device,
        mesh=mesh,
        in_specs=(
            tall, tall, split, split, split, P("wsh"), cube, cube, line, line, line, cube, tall,
        ),
        out_specs=(tall, tall, split, split, split, P("wsh")),
        check_vma=False,
    )
```

time: 186 us -> 179 us (0.962)
  waiting for transfers between devices: 34 us -> 72.1 us
  starting transfers between devices: 76.7 us -> 52.4 us
  local copies, waits for them, and re-layouts: 11.5 us -> 3.32 us
  Pallas kernels: 56.5 us -> 49 us
  other arithmetic: 4.19 us -> 0.07 us
    ppermute x32 -> x16, waiting for transfers between devices: 28.8 us -> 61.3 us  [shift_wsh(): lax.ppermute(value, 'wsh', [(i, (i + step) % parties) for i in range(part...]
    ppermute x32 -> x16, starting transfers between devices: 40.2 us -> 24.1 us  [shift_wsh(): lax.ppermute(value, 'wsh', [(i, (i + step) % parties) for i in range(part...]
    ppermute x14 -> x7, starting transfers between devices: 23.3 us -> 14.8 us  [the longest x6 8.46 us: sum_everywhere(): lax.ppermute(value, 'slab', pairs)]
    pallas_call x9 -> x11, Pallas kernels: 33.8 us -> 27.8 us  [the longest x1 8.65 us: node_update(): pl.pallas_call(node_kernel, grid=(steps,), out_shape=(wide, wide, wide) +...]
    unnamed x54 -> x24, local copies, waits for them, and re-layouts: 7.92 us -> 3.25 us
    ppermute x14 -> x7, waiting for transfers between devices: 5.24 us -> 8.36 us  [the longest x6 7.5 us: sum_everywhere(): lax.ppermute(value, 'slab', pairs)]
    ppermute x4, waiting for transfers between devices: 0.01 us -> 2.38 us  [shift_slab(): return lax.ppermute(value, 'slab', pairs)]
  transfers between devices with their start and end apart: 50 -> 27, of which waited for: 14 -> 19; matrix products, arithmetic and copies ran while one was open for 5% -> 0% of each run, Pallas kernels for 26% -> 12%
where the time goes in v3:
time: 179 us; the launch traced here: 178 us
  waiting for transfers between devices  72.1 us (40%)
  starting transfers between devices  52.4 us (29%)
  Pallas kernels  49 us (27%)
  local copies, waits for them, and re-layouts  3.32 us (2%)
    ppermute x16, waiting for transfers between devices, shift_wsh(): lax.ppermute(value, 'wsh', [(i, (i + step) % parties) for i in range(part...  61.3 us
    ppermute x16, starting transfers between devices, shift_wsh(): lax.ppermute(value, 'wsh', [(i, (i + step) % parties) for i in range(part...  24.1 us
    ppermute x4, starting transfers between devices, shift_slab(): return lax.ppermute(value, 'slab', pairs)  13.4 us
    pallas_call x1, Pallas kernels, last_products(): pl.pallas_call(last_kernel, out_shape=(jax.ShapeDtypeStruct((rows, SIDE),...  9.5 us
    pallas_call x1, Pallas kernels, node_update(): pl.pallas_call(node_kernel, grid=(steps,), out_shape=(wide, wide, wide) +...  8.65 us
    ppermute x6, starting transfers between devices, sum_everywhere(): lax.ppermute(value, 'slab', pairs)  8.46 us
    pallas_call x3, Pallas kernels, forward_tiles(): pl.pallas_call(functools.partial(forward_kernel, ks), out_shape=(half,) *...  7.79 us
    ppermute x6, waiting for transfers between devices, sum_everywhere(): lax.ppermute(value, 'slab', pairs)  7.5 us
  transfers between devices with their start and end apart: 27, of which 19 were waited for; matrix products, arithmetic and copies ran while one was open for 0% of the time, Pallas kernels for 12%

profile of v3, /device:TPU:1, one launch (start us, length us, event | category | flops | bytes accessed | tf_op | source)
XLA Modules:
  0.0 178.4 jit_solution(14279072791875311294)
XLA Ops:
  5.7 3.3 %collective-permute-start.1 = (bf16[1168,128]{1,0:T(8,128)(2,1)}, bf16[1168,128]{1,0:T(8,128)(2,1)S(1)}, u32[]{:S(2)}, u32[]{:S(2)}) collective-permute-start(bf16[1168,128]{1,0:T(8,128)(2,1)} %pack_shares.1.s0_ref.rest_0_), channel_id=1, source_target_pairs={{0,2},{1,3},{2,0},{3,1},{4,6},{5,7},{6,4},{7,5},{8,10},{9,11},{10,... | collective-permute-start | bytes 897032 | tf_op jit(solution)/shard_map/ppermute | solution.py:528
  9.7 6.6 %pick_rows.1.picked_ref = bf16[2048,128]{1,0:T(8,128)(2,1)} custom-call(s32[2,1024]{1,0:T(2,128)} %bitcast.32, s32[2]{0:T(128)} %bitcast.34, bf16[4096,128]{1,0:T(8,128)(2,1)} %feat_ref.9), custom_call_target="tpu_custom_call" | custom-call | tf_op jit(solution)/shard_map/pick_rows/pallas_call | solution.py:72
  16.3 5.8 %collective-permute-done.1.s2_ref.rest_0_ = bf16[1168,128]{1,0:T(8,128)(2,1)S(1)} collective-permute-done((bf16[1168,128]{1,0:T(8,128)(2,1)}, bf16[1168,128]{1,0:T(8,128)(2,1)S(1)}, u32[]{:S(2)}, u32[]{:S(2)}) %collective-permute-start.1) | collective-permute-done | bytes 299040 | tf_op jit(solution)/shard_map/ppermute | solution.py:528
  25.1 4.6 %collective-permute-start.3 = (bf16[1024,128]{1,0:T(8,128)(2,1)S(1)}, bf16[1024,128]{1,0:T(8,128)(2,1)S(1)}, u32[]{:S(2)}, u32[]{:S(2)}) collective-permute-start(bf16[1024,128]{1,0:T(8,128)(2,1)S(1)} %get-tuple-element.50), channel_id=1, source_target_pairs={{0,4},{4,8},{8,12},{12,16},{16,20},{20,24},{24,28},{28,32},{32,36}... | collective-permute-start | bytes 786440 | tf_op jit(solution)/shard_map/ppermute | solution.py:534
  31.7 3.3 %tile_lists.1 = (s32[8,144]{1,0:T(8,128)}, s32[8]{0:T(128)}) custom-call(s32[8,128]{1,0:T(8,128)} %copy-done.5), custom_call_target="tpu_custom_call" | custom-call | tf_op jit(solution)/shard_map/tile_lists/pallas_call | solution.py:218
  37.5 3.8 %forward_tiles.5 = (bf16[16,128,128]{2,1,0:T(8,128)(2,1)S(1)}, bf16[16,128,128]{2,1,0:T(8,128)(2,1)S(1)}) custom-call(s32[8,144]{1,0:T(8,128)S(1)} %copy-done.8, s32[8]{0:T(128)S(1)} %copy-done.9, bf16[32,128,128]{2,1,0:T(8,128)(2,1)S(1)} %bitcast.27, bf16[8,128,128]{2,1,0:T(8,128)(2,1)S(1)} %bitcast.45, bf16[8,128,128]{2,1,0:T(8,128)(2,1)S(1)} %bitcast.48, ...), custom_call_target="tpu_custom_call" | custom-call | flops 1000000000 | bytes 4000000 | tf_op jit(solution)/shard_map/forward_tiles/pallas_call | solution.py:285
  41.4 2.7 %collective-permute-start.7 = (bf16[16,128,128]{2,1,0:T(8,128)(2,1)S(1)}, bf16[16,128,128]{2,1,0:T(8,128)(2,1)S(1)}, u32[]{:S(2)}, u32[]{:S(2)}) collective-permute-start(bf16[16,128,128]{2,1,0:T(8,128)(2,1)S(1)} %get-tuple-element.58), channel_id=1, source_target_pairs={{0,3},{1,0},{2,1},{3,2},{4,7},{5,4},{6,5},{7,6},{8,11},{9,8},{10,9... | collective-permute-start | bytes 1572872 | tf_op jit(solution)/shard_map/ppermute | solution.py:528
  48.9 6.5 %collective-permute-done.6.left_ref = bf16[16,128,128]{2,1,0:T(8,128)(2,1)S(1)} collective-permute-done((bf16[16,128,128]{2,1,0:T(8,128)(2,1)S(1)}, bf16[16,128,128]{2,1,0:T(8,128)(2,1)S(1)}, u32[]{:S(2)}, u32[]{:S(2)}) %collective-permute-start.6) | collective-permute-done | bytes 524320 | tf_op jit(solution)/shard_map/ppermute | solution.py:528
  55.7 3.2 %collective-permute-start.8 = (bf16[16,128,128]{2,1,0:T(8,128)(2,1)S(1)}, bf16[16,128,128]{2,1,0:T(8,128)(2,1)S(1)}, u32[]{:S(2)}, u32[]{:S(2)}) collective-permute-start(bf16[16,128,128]{2,1,0:T(8,128)(2,1)S(1)} %get-tuple-element.59), channel_id=1, source_target_pairs={{0,3},{1,0},{2,1},{3,2},{4,7},{5,4},{6,5},{7,6},{8,11},{9,8},{10,9... | collective-permute-start | bytes 1572872 | tf_op jit(solution)/shard_map/ppermute | solution.py:528
  60.7 5.9 %collective-permute-done.5 = bf16[16,128,128]{2,1,0:T(8,128)(2,1)S(1)} collective-permute-done((bf16[16,128,128]{2,1,0:T(8,128)(2,1)S(1)}, bf16[16,128,128]{2,1,0:T(8,128)(2,1)S(1)}, u32[]{:S(2)}, u32[]{:S(2)}) %collective-permute-start.5) | collective-permute-done | bytes 524320 | tf_op jit(solution)/shard_map/ppermute | solution.py:528
  66.6 8.0 %collective-permute-done.8 = bf16[16,128,128]{2,1,0:T(8,128)(2,1)S(1)} collective-permute-done((bf16[16,128,128]{2,1,0:T(8,128)(2,1)S(1)}, bf16[16,128,128]{2,1,0:T(8,128)(2,1)S(1)}, u32[]{:S(2)}, u32[]{:S(2)}) %collective-permute-start.8) | collective-permute-done | bytes 524320 | tf_op jit(solution)/shard_map/ppermute | solution.py:528
  74.7 8.6 %node_update.1 = (bf16[4096,128]{1,0:T(8,128)(2,1)}, bf16[4096,128]{1,0:T(8,128)(2,1)S(1)}, bf16[4096,128]{1,0:T(8,128)(2,1)S(1)}, f32[256,128]{1,0:T(8,128)S(1)...) custom-call(bf16[4096,128]{1,0:T(8,128)(2,1)S(1)} %copy-done, bf16[4096,128]{1,0:T(8,128)(2,1)S(1)} %copy-done.7, ...), custom_call_target="tpu_custom_call" | custom-call | flops 10000000000 | bytes 20000000 | tf_op jit(solution)/shard_map/node_update/pallas_call | solution.py:377
  83.4 3.0 %collective-permute-start.13 = (bf16[4096,128]{1,0:T(8,128)(2,1)S(1)}, bf16[4096,128]{1,0:T(8,128)(2,1)S(1)}, u32[]{:S(2)}, u32[]{:S(2)}) collective-permute-start(bf16[4096,128]{1,0:T(8,128)(2,1)S(1)} %get-tuple-element.66), channel_id=1, source_target_pairs={{0,3},{1,0},{2,1},{3,2},{4,7},{5,4},{6,5},{7,6},{8,11},{9,8},{10,9... | collective-permute-start | bytes 3145736 | tf_op jit(solution)/shard_map/ppermute | solution.py:528
  87.8 20.3 %collective-permute-done.13 = bf16[4096,128]{1,0:T(8,128)(2,1)S(1)} collective-permute-done((bf16[4096,128]{1,0:T(8,128)(2,1)S(1)}, bf16[4096,128]{1,0:T(8,128)(2,1)S(1)}, u32[]{:S(2)}, u32[]{:S(2)}) %collective-permute-start.13) | collective-permute-done | bytes 1048608 | tf_op jit(solution)/shard_map/ppermute | solution.py:528
  108.2 3.2 %collective-permute-start.14 = (bf16[2048,128]{1,0:T(8,128)(2,1)S(1)}, bf16[2048,128]{1,0:T(8,128)(2,1)S(1)}, u32[]{:S(2)}, u32[]{:S(2)}) collective-permute-start(bf16[2048,128]{1,0:T(8,128)(2,1)S(1)} %slice.9), channel_id=1, source_target_pairs={{0,3},{1,0},{2,1},{3,2},{4,7},{5,4},{6,5},{7,6},{8,11},{9,8},{10,9... | collective-permute-start | bytes 1572872 | tf_op jit(solution)/shard_map/ppermute | solution.py:528
  111.7 2.8 %backward_tiles.3 = (f32[32,128,128]{2,1,0:T(8,128)S(1)}, f32[16,128,128]{2,1,0:T(8,128)S(1)}) custom-call(s32[8,144]{1,0:T(8,128)S(1)} %copy-done.8, s32[8]{0:T(128)S(1)} %copy-done.9, bf16[1168,128]{1,0:T(8,128)(2,1)S(1)} %copy-done.3, bf16[1168,128]{1,0:T(8,128)(2,1)S(1)} %collective-permute-done.s1_ref.rest_0_.rest_1_, ...), custom_call_target="tpu_custom_call" | custom-call | flops 6000000000 | bytes 4000000 | tf_op jit(solution)/shard_map/backward_tiles/pallas_call | solution.py:444
  114.4 8.6 %collective-permute-done.14 = bf16[2048,128]{1,0:T(8,128)(2,1)S(1)} collective-permute-done((bf16[2048,128]{1,0:T(8,128)(2,1)S(1)}, bf16[2048,128]{1,0:T(8,128)(2,1)S(1)}, u32[]{:S(2)}, u32[]{:S(2)}) %collective-permute-start.14) | collective-permute-done | bytes 524320 | tf_op jit(solution)/shard_map/ppermute | solution.py:528
  123.0 3.6 %collective-permute-done.12 = bf16[2048,128]{1,0:T(8,128)(2,1)S(1)} collective-permute-done((bf16[2048,128]{1,0:T(8,128)(2,1)S(1)}, bf16[2048,128]{1,0:T(8,128)(2,1)S(1)}, u32[]{:S(2)}, u32[]{:S(2)}) %collective-permute-start.12) | collective-permute-done | bytes 524320 | tf_op jit(solution)/shard_map/ppermute | solution.py:528
  130.4 5.0 %collective-permute-start.15 = (bf16[1024,128]{1,0:T(8,128)(2,1)S(1)}, bf16[1024,128]{1,0:T(8,128)(2,1)S(1)}, u32[]{:S(2)}, u32[]{:S(2)}) collective-permute-start(bf16[1024,128]{1,0:T(8,128)(2,1)S(1)} %bitcast.51), channel_id=1, source_target_pairs={{0,4},{4,8},{8,12},{12,16},{16,20},{20,24},{24,28},{28,32},{32,36}... | collective-permute-start | bytes 786440 | tf_op jit(solution)/shard_map/ppermute | solution.py:534
  138.6 9.5 %last_products.1 = (bf16[4096,128]{1,0:T(8,128)(2,1)}, bf16[144,128]{1,0:T(8,128)(2,1)S(1)}, bf16[144,128]{1,0:T(8,128)(2,1)S(1)}, bf16[144,128]{1,0:T(8,128)(2,1)S(1)}, bf16[144,128]{1,0:T(8,128)(2,1)S(1)}) custom-call(s32[1]{0:T(128)} %bitcast.pos_ref, s32[2,1024]{1,0:T(2,128)S(1)} %bitcast.33, s32[2]{0:T(128)S(1)} %bitcast.35, f32[4096,128]{1,0:T(8,128)S(1)} %bitcast.26, ...), custom_call_target="tpu_custom_call" | custom-call | tf_op jit(solution)/shard_map/last_products/pallas_call | solution.py:511
  156.7 3.4 %collective-permute-done.21 = bf16[144,128]{1,0:T(8,128)(2,1)S(1)} collective-permute-done((bf16[144,128]{1,0:T(8,128)(2,1)S(1)}, bf16[144,128]{1,0:T(8,128)(2,1)S(1)}, u32[]{:S(2)}, u32[]{:S(2)}) %collective-permute-start.21) | collective-permute-done | bytes 36896 | tf_op jit(solution)/shard_map/ppermute | solution.py:550
  160.0 4.7 %collective-permute-start.25 = (bf16[144,128]{1,0:T(8,128)(2,1)S(1)}, bf16[144,128]{1,0:T(8,128)(2,1)S(1)}, u32[]{:S(2)}, u32[]{:S(2)}) collective-permute-start(bf16[144,128]{1,0:T(8,128)(2,1)S(1)} %add_convert_fusion.1), channel_id=1, source_target_pairs={{0,24},{4,28},{8,0},{12,4},{16,8},{20,12},{24,16},{28,20},{32,56},... | collective-permute-start | bytes 110600 | tf_op jit(solution)/shard_map/ppermute | solution.py:550
  165.8 3.4 %collective-permute-done.24 = bf16[144,128]{1,0:T(8,128)(2,1)S(1)} collective-permute-done((bf16[144,128]{1,0:T(8,128)(2,1)S(1)}, bf16[144,128]{1,0:T(8,128)(2,1)S(1)}, u32[]{:S(2)}, u32[]{:S(2)}) %collective-permute-start.24) | collective-permute-done | bytes 36896 | tf_op jit(solution)/shard_map/ppermute | solution.py:550
  169.2 6.3 %collective-permute-start.26 = (bf16[144,128]{1,0:T(8,128)(2,1)S(1)}, bf16[144,128]{1,0:T(8,128)(2,1)S(1)}, u32[]{:S(2)}, u32[]{:S(2)}) collective-permute-start(bf16[144,128]{1,0:T(8,128)(2,1)S(1)} %add_convert_fusion.one_ref), channel_id=1, source_target_pairs={{0,4},{4,0},{8,12},{12,8},{16,20},{20,16},{24,28},{28,24},{32,36},... | collective-permute-start | bytes 110600 | tf_op jit(solution)/shard_map/ppermute | solution.py:551
  (75 shorter events, 40.8 us)
Async XLA Ops:
  3.2 13.1 %collective-permute-start.2 = (bf16[1168,128]{1,0:T(8,128)(2,1)}, bf16[1168,128]{1,0:T(8,128)(2,1)S(1)}, u32[]{:S(2)}, u32[]{:S(2)}) collective-permute-start(bf16[1168,128]{1,0:T(8,128)(2,1)} %pack_shares.1.s0_ref.rest_0_), channel_id=1, source_target_pairs={{0,1},{1,2},{2,3},{3,0},{4,5},{5,6},{6,7},{7,4},{8,9},{9,10},{10,1... | collective-permute-start | bytes 897032 | tf_op jit(solution)/shard_map/ppermute | solution.py:528
  5.7 16.4 %collective-permute-start.1 = (bf16[1168,128]{1,0:T(8,128)(2,1)}, bf16[1168,128]{1,0:T(8,128)(2,1)S(1)}, u32[]{:S(2)}, u32[]{:S(2)}) collective-permute-start(bf16[1168,128]{1,0:T(8,128)(2,1)} %pack_shares.1.s0_ref.rest_0_), channel_id=1, source_target_pairs={{0,2},{1,3},{2,0},{3,1},{4,6},{5,7},{6,4},{7,5},{8,10},{9,11},{10,... | collective-permute-start | bytes 897032 | tf_op jit(solution)/shard_map/ppermute | solution.py:528
  9.0 13.1 %collective-permute-start = (bf16[1168,128]{1,0:T(8,128)(2,1)}, bf16[1168,128]{1,0:T(8,128)(2,1)S(1)}, u32[]{:S(2)}, u32[]{:S(2)}) collective-permute-start(bf16[1168,128]{1,0:T(8,128)(2,1)} %pack_shares.1.s0_ref.rest_0_), channel_id=1, source_target_pairs={{0,3},{1,0},{2,1},{3,2},{4,7},{5,4},{6,5},{7,6},{8,11},{9,8},{10,9... | collective-permute-start | bytes 897032 | tf_op jit(solution)/shard_map/ppermute | solution.py:528
  25.1 10.8 %collective-permute-start.3 = (bf16[1024,128]{1,0:T(8,128)(2,1)S(1)}, bf16[1024,128]{1,0:T(8,128)(2,1)S(1)}, u32[]{:S(2)}, u32[]{:S(2)}) collective-permute-start(bf16[1024,128]{1,0:T(8,128)(2,1)S(1)} %get-tuple-element.50), channel_id=1, source_target_pairs={{0,4},{4,8},{8,12},{12,16},{16,20},{20,24},{24,28},{28,32},{32,36}... | collective-permute-start | bytes 786440 | tf_op jit(solution)/shard_map/ppermute | solution.py:534
  29.8 7.7 %collective-permute-start.4 = (bf16[1024,128]{1,0:T(8,128)(2,1)S(1)}, bf16[1024,128]{1,0:T(8,128)(2,1)S(1)}, u32[]{:S(2)}, u32[]{:S(2)}) collective-permute-start(bf16[1024,128]{1,0:T(8,128)(2,1)S(1)} %get-tuple-element.51), channel_id=1, source_target_pairs={{4,0},{8,4},{12,8},{16,12},{20,16},{24,20},{28,24},{32,28},{36,32}... | collective-permute-start | bytes 786440 | tf_op jit(solution)/shard_map/ppermute | solution.py:534
  41.3 14.0 %collective-permute-start.6 = (bf16[16,128,128]{2,1,0:T(8,128)(2,1)S(1)}, bf16[16,128,128]{2,1,0:T(8,128)(2,1)S(1)}, u32[]{:S(2)}, u32[]{:S(2)}) collective-permute-start(bf16[16,128,128]{2,1,0:T(8,128)(2,1)S(1)} %get-tuple-element.56), channel_id=1, source_target_pairs={{0,1},{1,2},{2,3},{3,0},{4,5},{5,6},{6,7},{7,4},{8,9},{9,10},{10,1... | collective-permute-start | bytes 1572872 | tf_op jit(solution)/shard_map/ppermute | solution.py:528
  41.4 14.0 %collective-permute-start.7 = (bf16[16,128,128]{2,1,0:T(8,128)(2,1)S(1)}, bf16[16,128,128]{2,1,0:T(8,128)(2,1)S(1)}, u32[]{:S(2)}, u32[]{:S(2)}) collective-permute-start(bf16[16,128,128]{2,1,0:T(8,128)(2,1)S(1)} %get-tuple-element.58), channel_id=1, source_target_pairs={{0,3},{1,0},{2,1},{3,2},{4,7},{5,4},{6,5},{7,6},{8,11},{9,8},{10,9... | collective-permute-start | bytes 1572872 | tf_op jit(solution)/shard_map/ppermute | solution.py:528
  46.2 20.4 %collective-permute-start.5 = (bf16[16,128,128]{2,1,0:T(8,128)(2,1)S(1)}, bf16[16,128,128]{2,1,0:T(8,128)(2,1)S(1)}, u32[]{:S(2)}, u32[]{:S(2)}) collective-permute-start(bf16[16,128,128]{2,1,0:T(8,128)(2,1)S(1)} %get-tuple-element.54), channel_id=1, source_target_pairs={{0,1},{1,2},{2,3},{3,0},{4,5},{5,6},{6,7},{7,4},{8,9},{9,10},{10,1... | collective-permute-start | bytes 1572872 | tf_op jit(solution)/shard_map/ppermute | solution.py:528
  47.7 18.9 %collective-permute-start.10 = (bf16[16,128,128]{2,1,0:T(8,128)(2,1)S(1)}, bf16[16,128,128]{2,1,0:T(8,128)(2,1)S(1)}, u32[]{:S(2)}, u32[]{:S(2)}) collective-permute-start(bf16[16,128,128]{2,1,0:T(8,128)(2,1)S(1)} %get-tuple-element.61), channel_id=1, source_target_pairs={{0,3},{1,0},{2,1},{3,2},{4,7},{5,4},{6,5},{7,6},{8,11},{9,8},{10,9... | collective-permute-start | bytes 1572872 | tf_op jit(solution)/shard_map/ppermute | solution.py:528
  55.7 19.0 %collective-permute-start.8 = (bf16[16,128,128]{2,1,0:T(8,128)(2,1)S(1)}, bf16[16,128,128]{2,1,0:T(8,128)(2,1)S(1)}, u32[]{:S(2)}, u32[]{:S(2)}) collective-permute-start(bf16[16,128,128]{2,1,0:T(8,128)(2,1)S(1)} %get-tuple-element.59), channel_id=1, source_target_pairs={{0,3},{1,0},{2,1},{3,2},{4,7},{5,4},{6,5},{7,6},{8,11},{9,8},{10,9... | collective-permute-start | bytes 1572872 | tf_op jit(solution)/shard_map/ppermute | solution.py:528
  58.9 15.9 %collective-permute-start.9 = (bf16[16,128,128]{2,1,0:T(8,128)(2,1)S(1)}, bf16[16,128,128]{2,1,0:T(8,128)(2,1)S(1)}, u32[]{:S(2)}, u32[]{:S(2)}) collective-permute-start(bf16[16,128,128]{2,1,0:T(8,128)(2,1)S(1)} %get-tuple-element.60), channel_id=1, source_target_pairs={{0,1},{1,2},{2,3},{3,0},{4,5},{5,6},{6,7},{7,4},{8,9},{9,10},{10,1... | collective-permute-start | bytes 1572872 | tf_op jit(solution)/shard_map/ppermute | solution.py:528
  83.4 24.7 %collective-permute-start.13 = (bf16[4096,128]{1,0:T(8,128)(2,1)S(1)}, bf16[4096,128]{1,0:T(8,128)(2,1)S(1)}, u32[]{:S(2)}, u32[]{:S(2)}) collective-permute-start(bf16[4096,128]{1,0:T(8,128)(2,1)S(1)} %get-tuple-element.66), channel_id=1, source_target_pairs={{0,3},{1,0},{2,1},{3,2},{4,7},{5,4},{6,5},{7,6},{8,11},{9,8},{10,9... | collective-permute-start | bytes 3145736 | tf_op jit(solution)/shard_map/ppermute | solution.py:528
  86.4 25.1 %collective-permute-start.11 = (bf16[4096,128]{1,0:T(8,128)(2,1)S(1)}, bf16[4096,128]{1,0:T(8,128)(2,1)S(1)}, u32[]{:S(2)}, u32[]{:S(2)}) collective-permute-start(bf16[4096,128]{1,0:T(8,128)(2,1)S(1)} %get-tuple-element.66), channel_id=1, source_target_pairs={{0,1},{1,2},{2,3},{3,0},{4,5},{5,6},{6,7},{7,4},{8,9},{9,10},{10,1... | collective-permute-start | bytes 3145736 | tf_op jit(solution)/shard_map/ppermute | solution.py:528
  108.2 14.8 %collective-permute-start.14 = (bf16[2048,128]{1,0:T(8,128)(2,1)S(1)}, bf16[2048,128]{1,0:T(8,128)(2,1)S(1)}, u32[]{:S(2)}, u32[]{:S(2)}) collective-permute-start(bf16[2048,128]{1,0:T(8,128)(2,1)S(1)} %slice.9), channel_id=1, source_target_pairs={{0,3},{1,0},{2,1},{3,2},{4,7},{5,4},{6,5},{7,6},{8,11},{9,8},{10,9... | collective-permute-start | bytes 1572872 | tf_op jit(solution)/shard_map/ppermute | solution.py:528
  111.6 15.1 %collective-permute-start.12 = (bf16[2048,128]{1,0:T(8,128)(2,1)S(1)}, bf16[2048,128]{1,0:T(8,128)(2,1)S(1)}, u32[]{:S(2)}, u32[]{:S(2)}) collective-permute-start(bf16[2048,128]{1,0:T(8,128)(2,1)S(1)} %slice.8), channel_id=1, source_target_pairs={{0,1},{1,2},{2,3},{3,0},{4,5},{5,6},{6,7},{7,4},{8,9},{9,10},{10,1... | collective-permute-start | bytes 1572872 | tf_op jit(solution)/shard_map/ppermute | solution.py:528
  128.4 9.3 %collective-permute-start.16 = (bf16[1024,128]{1,0:T(8,128)(2,1)S(1)}, bf16[1024,128]{1,0:T(8,128)(2,1)S(1)}, u32[]{:S(2)}, u32[]{:S(2)}) collective-permute-start(bf16[1024,128]{1,0:T(8,128)(2,1)S(1)} %bitcast.52), channel_id=1, source_target_pairs={{4,0},{8,4},{12,8},{16,12},{20,16},{24,20},{28,24},{32,28},{36,32}... | collective-permute-start | bytes 786440 | tf_op jit(solution)/shard_map/ppermute | solution.py:534
  130.4 8.3 %collective-permute-start.15 = (bf16[1024,128]{1,0:T(8,128)(2,1)S(1)}, bf16[1024,128]{1,0:T(8,128)(2,1)S(1)}, u32[]{:S(2)}, u32[]{:S(2)}) collective-permute-start(bf16[1024,128]{1,0:T(8,128)(2,1)S(1)} %bitcast.51), channel_id=1, source_target_pairs={{0,4},{4,8},{8,12},{12,16},{16,20},{20,24},{24,28},{28,32},{32,36}... | collective-permute-start | bytes 786440 | tf_op jit(solution)/shard_map/ppermute | solution.py:534
  148.4 4.7 %collective-permute-start.19 = (bf16[144,128]{1,0:T(8,128)(2,1)S(1)}, bf16[144,128]{1,0:T(8,128)(2,1)S(1)}, u32[]{:S(2)}, u32[]{:S(2)}) collective-permute-start(bf16[144,128]{1,0:T(8,128)(2,1)S(1)} %get-tuple-element.81), channel_id=1, source_target_pairs={{0,3},{1,0},{2,1},{3,2},{4,7},{5,4},{6,5},{7,6},{8,11},{9,8},{10,9... | collective-permute-start | bytes 110600 | tf_op jit(solution)/shard_map/ppermute | solution.py:528
  155.6 4.4 %collective-permute-start.21 = (bf16[144,128]{1,0:T(8,128)(2,1)S(1)}, bf16[144,128]{1,0:T(8,128)(2,1)S(1)}, u32[]{:S(2)}, u32[]{:S(2)}) collective-permute-start(bf16[144,128]{1,0:T(8,128)(2,1)S(1)} %add_convert_fusion.2), channel_id=1, source_target_pairs={{0,64},{4,68},{8,72},{12,76},{16,80},{20,84},{24,88},{28,92},{32,9... | collective-permute-start | bytes 110600 | tf_op jit(solution)/shard_map/ppermute | solution.py:550
  155.6 4.4 %collective-permute-start.20 = (bf16[144,128]{1,0:T(8,128)(2,1)S(1)}, bf16[144,128]{1,0:T(8,128)(2,1)S(1)}, u32[]{:S(2)}, u32[]{:S(2)}) collective-permute-start(bf16[144,128]{1,0:T(8,128)(2,1)S(1)} %add_convert_fusion.2), channel_id=1, source_target_pairs={{0,32},{4,36},{8,40},{12,44},{16,48},{20,52},{24,56},{28,60},{32,6... | collective-permute-start | bytes 110600 | tf_op jit(solution)/shard_map/ppermute | solution.py:550
  160.0 5.7 %collective-permute-start.25 = (bf16[144,128]{1,0:T(8,128)(2,1)S(1)}, bf16[144,128]{1,0:T(8,128)(2,1)S(1)}, u32[]{:S(2)}, u32[]{:S(2)}) collective-permute-start(bf16[144,128]{1,0:T(8,128)(2,1)S(1)} %add_convert_fusion.1), channel_id=1, source_target_pairs={{0,24},{4,28},{8,0},{12,4},{16,8},{20,12},{24,16},{28,20},{32,56},... | collective-permute-start | bytes 110600 | tf_op jit(solution)/shard_map/ppermute | solution.py:550
  164.7 4.4 %collective-permute-start.24 = (bf16[144,128]{1,0:T(8,128)(2,1)S(1)}, bf16[144,128]{1,0:T(8,128)(2,1)S(1)}, u32[]{:S(2)}, u32[]{:S(2)}) collective-permute-start(bf16[144,128]{1,0:T(8,128)(2,1)S(1)} %add_convert_fusion.1), channel_id=1, source_target_pairs={{0,16},{4,20},{8,24},{12,28},{16,0},{20,4},{24,8},{28,12},{32,48},... | collective-permute-start | bytes 110600 | tf_op jit(solution)/shard_map/ppermute | solution.py:550
  164.7 4.4 %collective-permute-start.23 = (bf16[144,128]{1,0:T(8,128)(2,1)S(1)}, bf16[144,128]{1,0:T(8,128)(2,1)S(1)}, u32[]{:S(2)}, u32[]{:S(2)}) collective-permute-start(bf16[144,128]{1,0:T(8,128)(2,1)S(1)} %add_convert_fusion.1), channel_id=1, source_target_pairs={{0,8},{4,12},{8,16},{12,20},{16,24},{20,28},{24,0},{28,4},{32,40},... | collective-permute-start | bytes 110600 | tf_op jit(solution)/shard_map/ppermute | solution.py:550
  169.2 7.2 %collective-permute-start.26 = (bf16[144,128]{1,0:T(8,128)(2,1)S(1)}, bf16[144,128]{1,0:T(8,128)(2,1)S(1)}, u32[]{:S(2)}, u32[]{:S(2)}) collective-permute-start(bf16[144,128]{1,0:T(8,128)(2,1)S(1)} %add_convert_fusion.one_ref), channel_id=1, source_target_pairs={{0,4},{4,0},{8,12},{12,8},{16,20},{20,16},{24,28},{28,24},{32,36},... | collective-permute-start | bytes 110600 | tf_op jit(solution)/shard_map/ppermute | solution.py:551
  (15 other events, 100.0 us)

commit v4 on v3

--- a/solution.py
+++ b/solution.py
@@ -81,15 +81,14 @@
 
 
 def pack_kernel(
-    count_ref, values_ref, cols_ref, msg_ref, in_ref, out_w_ref, gain_ref, dst_ref, src_ref, pack_ref, lines
+    count_ref, values_ref, cols_ref, msg_ref, in_ref, out_w_ref, gain_ref, dst_ref, src_ref, tiles_ref, pack_ref, lines
 ):
     share, edges = msg_ref.shape[0], values_ref.shape[0]
-    pack_ref[pl.ds(0, edges), :] = values_ref[...]
-    pack_ref[pl.ds(edges, edges), :] = cols_ref[...].astype(F32).astype(BF16)
-    small = 2 * edges
-    pack_ref[pl.ds(small, share), :] = msg_ref[...]
-    pack_ref[pl.ds(small + share, 2 * share), :] = in_ref[...]
-    pack_ref[pl.ds(small + 3 * share, share), :] = out_w_ref[...]
+    tiles_ref[pl.ds(0, edges), :] = values_ref[...]
+    tiles_ref[pl.ds(edges, edges), :] = cols_ref[...].astype(F32).astype(BF16)
+    pack_ref[pl.ds(0, share), :] = msg_ref[...]
+    pack_ref[pl.ds(share, 2 * share), :] = in_ref[...]
+    pack_ref[pl.ds(3 * share, share), :] = out_w_ref[...]
     lines[...] = jnp.zeros_like(lines)
     gain = gain_ref[...].astype(F32)
     for j in range(SIDE // share):
@@ -97,7 +96,7 @@
     lines[1:2, :] = dst_ref[...].astype(F32)
     lines[2:3, :] = src_ref[...].astype(F32)
     lines[3:4, :] = jnp.full((1, SIDE), count_ref[0]).astype(F32)
-    pack_ref[pl.ds(small + 4 * share, 16), :] = lines[...].astype(BF16)
+    pack_ref[pl.ds(4 * share, 16), :] = lines[...].astype(BF16)
 
 
 def pack_shares(tile_count, tile_values, tile_cols, w_msg, w_in, w_out, ln_gain, tile_dst, tile_src):
@@ -105,9 +104,12 @@
     values, cols = (array.reshape(-1, SIDE) for array in (tile_values, tile_cols))
     return pl.pallas_call(
         pack_kernel,
-        out_shape=jax.ShapeDtypeStruct((2 * values.shape[0] + 4 * share + 16, SIDE), BF16),
+        out_shape=(
+            jax.ShapeDtypeStruct((2 * values.shape[0], SIDE), BF16),
+            jax.ShapeDtypeStruct((4 * share + 16, SIDE), BF16),
+        ),
         in_specs=[SMEM] + [VMEM] * 8,
-        out_specs=VMEM,
+        out_specs=(VMEM, VMEM),
         scratch_shapes=[pltpu.VMEM((16, SIDE), F32)],
         compiler_params=ROOMY,
         name="pack_shares",
@@ -125,16 +127,15 @@
     smalls = (s0_ref, s1_ref, s2_ref, s3_ref)
     parties = len(smalls)
     share = SIDE // parties
-    small = s0_ref.shape[0] - SIDE - 16
     lane = lax.broadcasted_iota(jnp.int32, (1, SIDE), 1)
     gain = jnp.zeros((1, SIDE), F32)
     for k, ref in enumerate(smalls):
         device = lax.rem(me + k, parties)
         at = pl.multiple_of(device * share, share)
-        msg_ref[pl.ds(at, share), :] = ref[pl.ds(small, share), :]
-        in_ref[pl.ds(pl.multiple_of(2 * at, 2 * share), 2 * share), :] = ref[pl.ds(small + share, 2 * share), :]
-        out_w_ref[pl.ds(at, share), :] = ref[pl.ds(small + 3 * share, share), :]
-        lines = ref[pl.ds(small + 4 * share, 16), :].astype(F32)
+        msg_ref[pl.ds(at, share), :] = ref[pl.ds(0, share), :]
+        in_ref[pl.ds(pl.multiple_of(2 * at, 2 * share), 2 * share), :] = ref[pl.ds(share, 2 * share), :]
+        out_w_ref[pl.ds(at, share), :] = ref[pl.ds(3 * share, share), :]
+        lines = ref[pl.ds(4 * share, 16), :].astype(F32)
         gain = jnp.where((lane >= at) & (lane < at + share), lines[0:1, :], gain)
         dst, src, count = (lines[i : i + 1, :].astype(jnp.int32) for i in (1, 2, 3))
         block = src - me * here_blocks
@@ -167,17 +168,18 @@
         ),
         in_specs=[SMEM] + [VMEM] * 5,
         out_specs=(VMEM,) * 7,
-        compiler_params=PARAMS,
+        compiler_params=ROOMY,
         name="prepare",
     )(position, *smalls, picked)
 
 
-def message_kernel(feat_ref, msg_ref, out_ref):
+def message_kernel(feat_ref, msg_ref, *rest):
+    out_ref = rest[-1]
     pre = rows_by_cols(feat_ref[...], msg_ref[...])
     out_ref[...] = (pre * sigmoid(pre)).astype(BF16)
 
 
-def messages(feat, w_msg):
+def messages(feat, w_msg, follow):
     rows = feat.shape[0]
     steps = 2
     tall = pl.BlockSpec((rows // steps, SIDE), lambda i: (i, 0))
@@ -185,11 +187,11 @@
         message_kernel,
         grid=(steps,),
         out_shape=jax.ShapeDtypeStruct((rows, SIDE), BF16),
-        in_specs=[tall, pl.BlockSpec(w_msg.shape, lambda i: (0, 0))],
+        in_specs=[tall, pl.BlockSpec(w_msg.shape, lambda i: (0, 0))] + [ANY] * len(follow),
         out_specs=tall,
         compiler_params=PARAMS,
         name="messages",
-    )(feat, w_msg)
+    )(feat, w_msg, *follow)
 
 
 def list_kernel(code_ref, list_ref, total_ref):
@@ -199,8 +201,8 @@
 
         def body(step, carry):
             own, rim = carry
-            for u in range(group):
-                code = code_ref[k, step * group + u]
+            codes = [code_ref[k, step * group + u] for u in range(group)]
+            for code in codes:
                 list_ref[2 * k, own] = code
                 list_ref[2 * k + 1, rim] = code
                 own = own + ((code >> 20) & 1)
@@ -266,7 +268,7 @@
     rims[pl.ds(half, half)] = upper_ref[...]
     for at, (k, slot_ref) in enumerate(zip(ks, slot_refs)):
         acc[...] = jnp.zeros_like(acc)
-        tiles[...] = slot_ref[pl.ds(0, tiles.shape[0]), :].astype(F32)
+        tiles[...] = slot_ref[...].astype(F32)
         for part, ref in enumerate((own_ref, rims)):
 
             def product(dense, block, target, ref=ref):
@@ -290,7 +292,7 @@
         scratch_shapes=[
             pltpu.VMEM(own.shape, F32),
             pltpu.VMEM((2 * lower.shape[0],) + lower.shape[1:], BF16),
-            pltpu.VMEM((tiles[0].shape[0] - SIDE - 16, SIDE), F32),
+            pltpu.VMEM(tiles[0].shape, F32),
         ],
         compiler_params=PARAMS,
         cost_estimate=cost(1_000_000_000 * len(ks), 4_000_000 * len(ks)),
@@ -316,22 +318,18 @@
 
 
 def node_kernel(
-    feat_ref, cot_ref, own_a_ref, own_b_ref, la_ref, ra_ref, lb_ref, rb_ref, in_ref, out_w_ref, gain_ref,
-    node_ref, dhid_ref, dagg_ref, dwin_ref, dwout_ref, dgain_ref,
+    continued, feat_ref, cot_ref, own_ref, left_ref, right_ref, in_ref, out_w_ref, gain_ref, *rest,
 ):
+    node_ref, dhid_ref, dagg_ref, dwin_ref, dwout_ref, dgain_ref = rest[-6:]
     step = pl.program_id(0)
 
     @pl.when(step == 0)
     def _():
-        for ref in (dwin_ref, dwout_ref, dgain_ref):
-            ref[...] = jnp.zeros_like(ref)
+        for at, ref in enumerate((dwin_ref, dwout_ref, dgain_ref)):
+            ref[...] = rest[2 + at][...] if continued else jnp.zeros_like(ref)
 
     feat = feat_ref[...]
-    first = step < pl.num_programs(0) // 2
-    left = jnp.where(first, la_ref[...].astype(F32), lb_ref[...].astype(F32))
-    right = jnp.where(first, ra_ref[...].astype(F32), rb_ref[...].astype(F32))
-    own = jnp.where(first, own_a_ref[...], own_b_ref[...])
-    agg = (own + (left + right)).astype(BF16)
+    agg = (own_ref[...] + (left_ref[...].astype(F32) + right_ref[...].astype(F32))).astype(BF16)
     w_feat, w_agg, w_out = in_ref[:SIDE, :], in_ref[SIDE:, :], out_w_ref[...]
     gain = gain_ref[...]
     pre = rows_by_cols(feat, w_feat) + rows_by_cols(agg, w_agg)
@@ -360,53 +358,57 @@
     dwin_ref[SIDE:, :] += contract_rows(agg, d_hidden)
 
 
-def node_update(node_feat, cotangent, parts, w_in, w_out, gain):
+def node_update(h, node_feat, cotangent, parts, w_in, w_out, gain, before):
     rows = node_feat.shape[0]
     chunk = 512
-    steps = rows // chunk
-    per = steps // 2
+    steps = rows // 2 // chunk
 
     def whole(shape):
         return pl.BlockSpec(shape, lambda i: (0, 0))
 
-    tall = pl.BlockSpec((chunk, SIDE), lambda i: (i, 0))
-    part_a = pl.BlockSpec((chunk, SIDE), lambda i: (jnp.minimum(i, per - 1), 0))
-    part_b = pl.BlockSpec((chunk, SIDE), lambda i: (jnp.maximum(i - per, 0), 0))
+    tall = pl.BlockSpec((chunk, SIDE), lambda i: (h * steps + i, 0))
+    part = pl.BlockSpec((chunk, SIDE), lambda i: (i, 0))
     wide = jax.ShapeDtypeStruct((rows, SIDE), BF16)
+    half = jax.ShapeDtypeStruct((rows // 2, SIDE), BF16)
     sums = [(2 * SIDE, SIDE), (SIDE, SIDE), (1, SIDE)]
     return pl.pallas_call(
-        node_kernel,
+        functools.partial(node_kernel, bool(before)),
         grid=(steps,),
-        out_shape=(wide, wide, wide) + tuple(jax.ShapeDtypeStruct(shape, F32) for shape in sums),
-        in_specs=[tall, tall, part_a, part_b, part_a, part_a, part_b, part_b]
-        + [whole((2 * SIDE, SIDE)), whole((SIDE, SIDE)), whole((1, SIDE))],
-        out_specs=(tall, tall, tall) + tuple(whole(shape) for shape in sums),
-        compiler_params=PARAMS,
-        cost_estimate=cost(10_000_000_000, 20_000_000),
+        out_shape=(wide, wide, half) + tuple(jax.ShapeDtypeStruct(shape, F32) for shape in sums),
+        in_specs=[tall, tall, part, part, part]
+        + [whole((2 * SIDE, SIDE)), whole((SIDE, SIDE)), whole((1, SIDE))]
+        + ([ANY, ANY] + [whole(shape) for shape in sums] if before else []),
+        out_specs=(tall, tall, part) + tuple(whole(shape) for shape in sums),
+        input_output_aliases={8: 0, 9: 1} if before else {},
+        compiler_params=PARAMS,
+        cost_estimate=cost(5_000_000_000, 10_000_000),
         name="node_update",
-    )(node_feat, cotangent, *parts, w_in, w_out, gain)
-
-
-def ahead_kernel(feat_ref, cot_ref, dhid_ref, msg_ref, in_ref, slope_ref, base_ref):
-    slope_ref[...] = silu_slope(rows_by_cols(feat_ref[...], msg_ref[...]))
+    )(node_feat, cotangent, *parts, w_in, w_out, gain, *before)
+
+
+def ahead_kernel(feat_ref, cot_ref, dhid_ref, picked_ref, msg_ref, in_ref, slope_ref, base_ref, far_ref):
+    w_msg = msg_ref[...]
+    slope_ref[...] = silu_slope(rows_by_cols(feat_ref[...], w_msg))
+    far_ref[...] = silu_slope(rows_by_cols(picked_ref[...], w_msg))
     base_ref[...] = cot_ref[...].astype(F32) + contract_cols(dhid_ref[...], in_ref[:SIDE, :])
 
 
-def ahead(feat, cot, dhid, w_msg, w_in):
+def ahead(feat, cot, dhid, picked, w_msg, w_in):
     rows = feat.shape[0]
     steps = 4
     tall = pl.BlockSpec((rows // steps, SIDE), lambda i: (i, 0))
+    short = pl.BlockSpec((picked.shape[0] // steps, SIDE), lambda i: (i, 0))
     wide = jax.ShapeDtypeStruct((rows, SIDE), F32)
     return pl.pallas_call(
         ahead_kernel,
         grid=(steps,),
-        out_shape=(wide, wide),
-        in_specs=[tall] * 3 + [pl.BlockSpec(w.shape, lambda i: (0, 0)) for w in (w_msg, w_in)],
-        out_specs=(tall, tall),
+        out_shape=(wide, wide, jax.ShapeDtypeStruct(picked.shape, F32)),
+        in_specs=[tall] * 3 + [short] + [pl.BlockSpec(w.shape, lambda i: (0, 0)) for w in (w_msg, w_in)],
+        out_specs=(tall, tall, short),
         compiler_params=PARAMS,
         cost_estimate=cost(3_000_000_000, 7_000_000),
         name="ahead",
-    )(feat, cot, dhid, w_msg, w_in)
+    )(feat, cot, dhid, picked, w_msg, w_in)
 
 
 def backward_kernel(ks, cuts, parts, started, list_ref, total_ref, *rest):
@@ -416,7 +418,7 @@
     for at, acc in enumerate(accs):
         acc[...] = rest[at][...] if started else jnp.zeros_like(acc)
     for at, (k, slot_ref) in enumerate(zip(ks, slot_refs)):
-        tiles[...] = slot_ref[pl.ds(0, tiles.shape[0]), :].astype(F32)
+        tiles[...] = slot_ref[...].astype(F32)
         source = arrays[at]
         if cuts > 1:
             source, span = grads, grads.shape[0] // cuts
@@ -446,7 +448,7 @@
         out_shape=tuple(jax.ShapeDtypeStruct((size, SIDE, SIDE), kind) for size, kind in zip(sizes, kinds)),
         in_specs=[SMEM, SMEM] + [VMEM] * (len(ks) + len(cubes) + len(started)) + [ANY] * len(follow),
         out_specs=(VMEM,) * len(sizes),
-        scratch_shapes=[pltpu.VMEM((tiles[0].shape[0] - SIDE - 16, SIDE), F32), pltpu.VMEM((cuts * cubes[0].shape[0], SIDE, SIDE), BF16)]
+        scratch_shapes=[pltpu.VMEM(tiles[0].shape, F32), pltpu.VMEM((cuts * cubes[0].shape[0], SIDE, SIDE), BF16)]
         + [pltpu.VMEM((size, SIDE, SIDE), F32) for size in accs],
         compiler_params=PARAMS,
         cost_estimate=cost(2_000_000_000 * len(ks), 4_000_000),
@@ -454,41 +456,45 @@
     )(lists, totals, *[tiles[k] for k in ks], *cubes, *started, *follow)
 
 
-def last_kernel(
-    pos_ref, rows_ref, count_ref, own_ref, lower_ref, upper_ref, msg_ref, dwin_ref, dwout_ref, dgain_ref,
-    feat_ref, slope_ref, base_ref,
-    dnode_ref, r0_ref, r1_ref, r2_ref, r3_ref, back, dw, acc,
+def own_kernel(feat_ref, slope_ref, base_ref, own_ref, msg_ref, sum_ref, dw_ref):
+    @pl.when(pl.program_id(0) == 0)
+    def _():
+        dw_ref[...] = jnp.zeros_like(dw_ref)
+
+    d_pre = (own_ref[...] * slope_ref[...]).astype(BF16)
+    dw_ref[...] += contract_rows(feat_ref[...], d_pre)
+    sum_ref[...] = base_ref[...] + contract_cols(d_pre, msg_ref[...])
+
+
+def own_products(feat, slope, base, own, w_msg):
+    rows = feat.shape[0]
+    steps = 4
+    tall = pl.BlockSpec((rows // steps, SIDE), lambda i: (i, 0))
+    square = pl.BlockSpec((SIDE, SIDE), lambda i: (0, 0))
+    return pl.pallas_call(
+        own_kernel,
+        grid=(steps,),
+        out_shape=(jax.ShapeDtypeStruct((rows, SIDE), F32), jax.ShapeDtypeStruct((SIDE, SIDE), F32)),
+        in_specs=[tall] * 4 + [square],
+        out_specs=(tall, square),
+        compiler_params=PARAMS,
+        cost_estimate=cost(3_000_000_000, 7_000_000),
+        name="own_products",
+    )(feat, slope, base, own, w_msg)
+
+
+def rim_kernel(
+    pos_ref, count_ref, lower_ref, upper_ref, picked_ref, far_ref, dw_ref, dwin_ref, dwout_ref, dgain_ref,
+    dpre_ref, r0_ref, r1_ref, r2_ref, r3_ref, dw,
 ):
-    halo = rows_ref.shape[1]
-    acc[...] = own_ref[...]
-    group = 16
+    halo = lower_ref.shape[0]
+    dw[...] = dw_ref[...]
     for k, ref in enumerate((lower_ref, upper_ref)):
-        count = count_ref[k]
+        at = pl.ds(k * halo, halo)
         slots = lax.broadcasted_iota(jnp.int32, (halo, SIDE), 0)
-        back[...] = jnp.where(slots < count, ref[...].astype(F32), 0.0)
-
-        def body(step, carry):
-            rows = [rows_ref[k, step * group + u] for u in range(group)]
-            added = [
-                acc[pl.ds(row, 1), :] + back[pl.ds(step * group + u, 1), :] for u, row in enumerate(rows)
-            ]
-            for row, value in zip(rows, added):
-                acc[pl.ds(row, 1), :] = value
-            return carry
-
-        lax.fori_loop(0, (count + group - 1) // group, body, 0)
-    w_msg = msg_ref[...]
-    dw[...] = jnp.zeros_like(dw)
-    chunk = 512
-
-    def step_rows(step, carry):
-        at = pl.ds(pl.multiple_of(step * chunk, chunk), chunk)
-        d_pre = (acc[at, :] * slope_ref[at, :]).astype(BF16)
-        dw[...] += contract_rows(feat_ref[at, :], d_pre)
-        dnode_ref[at, :] = (base_ref[at, :] + contract_cols(d_pre, w_msg)).astype(BF16)
-        return carry
-
-    lax.fori_loop(0, acc.shape[0] // chunk, step_rows, 0)
+        d_pre = jnp.where(slots < count_ref[k], ref[...].astype(F32) * far_ref[at, :], 0.0).astype(BF16)
+        dpre_ref[at, :] = d_pre
+        dw[...] += contract_rows(picked_ref[at, :], d_pre)
     outs = (r0_ref, r1_ref, r2_ref, r3_ref)
     share = SIDE // len(outs)
     for k, out in enumerate(outs):
@@ -505,22 +511,49 @@
         out[pl.ds(4 * share, 16), :] = gain.astype(out.dtype)
 
 
-def last_products(position, halo_rows, halo_count, own, lower, upper, w_msg, sums, feat, slope, base):
-    rows = feat.shape[0]
+def rim_products(position, halo_count, lower, upper, picked, far, dw, sums):
     piece = jax.ShapeDtypeStruct((SIDE + 16, SIDE), BF16)
     return pl.pallas_call(
-        last_kernel,
-        out_shape=(jax.ShapeDtypeStruct((rows, SIDE), BF16), piece, piece, piece, piece),
-        in_specs=[SMEM] * 3 + [VMEM] * 10,
+        rim_kernel,
+        out_shape=(jax.ShapeDtypeStruct(picked.shape, BF16), piece, piece, piece, piece),
+        in_specs=[SMEM] * 2 + [VMEM] * 8,
         out_specs=(VMEM,) * 5,
-        scratch_shapes=[
-            pltpu.VMEM((halo_rows.shape[1], SIDE), F32),
-            pltpu.VMEM((SIDE, SIDE), F32),
-            pltpu.VMEM((rows, SIDE), F32),
-        ],
-        compiler_params=PARAMS,
-        name="last_products",
-    )(position, halo_rows, halo_count, own, lower, upper, w_msg, *sums, feat, slope, base)
+        scratch_shapes=[pltpu.VMEM((SIDE, SIDE), F32)],
+        compiler_params=PARAMS,
+        name="rim_products",
+    )(position, halo_count, lower, upper, picked, far, dw, *sums)
+
+
+def place_kernel(k, rows_ref, count_ref, sum_ref, dpre_ref, msg_ref, *rest):
+    out_ref, token_ref, acc, added = rest[-4:]
+    token_ref[...] = jnp.zeros_like(token_ref)
+    halo = rows_ref.shape[1]
+    acc[...] = sum_ref[...]
+    added[...] = contract_cols(dpre_ref[pl.ds(k * halo, halo), :], msg_ref[...])
+    group = 16
+
+    def body(step, carry):
+        rows = [rows_ref[k, step * group + u] for u in range(group)]
+        values = [acc[pl.ds(row, 1), :] + added[pl.ds(step * group + u, 1), :] for u, row in enumerate(rows)]
+        for row, value in zip(rows, values):
+            acc[pl.ds(row, 1), :] = value
+        return carry
+
+    lax.fori_loop(0, (count_ref[k] + group - 1) // group, body, 0)
+    out_ref[...] = acc[...].astype(out_ref.dtype)
+
+
+def place_rows(k, kind, halo_rows, halo_count, total, d_pre, w_msg, follow):
+    return pl.pallas_call(
+        functools.partial(place_kernel, k),
+        out_shape=(jax.ShapeDtypeStruct(total.shape, kind), jax.ShapeDtypeStruct((8, SIDE), F32)),
+        in_specs=[SMEM] * 2 + [VMEM] * 3 + [ANY] * len(follow),
+        out_specs=(VMEM, VMEM),
+        scratch_shapes=[pltpu.VMEM(total.shape, F32), pltpu.VMEM((halo_rows.shape[1], SIDE), F32)],
+        compiler_params=PARAMS,
+        cost_estimate=cost(4_000_000_000, 7_000_000),
+        name="place_rows",
+    )(halo_rows, halo_count, total, d_pre, w_msg, *follow)
 
 
 def shift_wsh(value, step):
@@ -534,21 +567,37 @@
     return lax.ppermute(value, "slab", pairs)
 
 
-def sum_group(terms):
-    total = terms[0].astype(F32)
-    for term in terms[1:]:
-        total = total + term.astype(F32)
-    return total.astype(BF16)
-
-
-def sum_everywhere(pieces):
+def sum_kernel(count, *refs):
+    total = refs[0][...].astype(F32)
+    for ref in refs[1:count]:
+        total = total + ref[...].astype(F32)
+    refs[-1][...] = total.astype(BF16)
+
+
+def sum_group(terms, follow=()):
+    return pl.pallas_call(
+        functools.partial(sum_kernel, len(terms)),
+        out_shape=jax.ShapeDtypeStruct(terms[0].shape, BF16),
+        in_specs=[VMEM] * len(terms) + [ANY] * len(follow),
+        out_specs=VMEM,
+        compiler_params=PARAMS,
+        name="sum_group",
+    )(*terms, *follow)
+
+
+def sum_wsh(pieces, follow):
+    return sum_group([pieces[0]] + [shift_wsh(pieces[k], k) for k in range(1, len(pieces))], follow)
+
+
+def sum_slab(value, stride, size, follow=()):
     count = lax.axis_size("slab")
-    value = sum_group([pieces[0]] + [shift_wsh(pieces[k], k) for k in range(1, len(pieces))])
-    for stride, size in ((8, 4), (2, 4)):
-        span = stride * size
-        turns = [[(i, (i // span) * span + (i + stride * k) % span) for i in range(count)] for k in range(1, size)]
-        value = sum_group([value] + [lax.ppermute(value, "slab", pairs) for pairs in turns])
-    return value, lax.ppermute(value, "slab", [(i, i ^ 1) for i in range(count)])
+    span = stride * size
+    turns = [[(i, (i // span) * span + (i + stride * k) % span) for i in range(count)] for k in range(1, size)]
+    return sum_group([value] + [lax.ppermute(value, "slab", pairs) for pairs in turns], follow)
+
+
+def other_core(value):
+    return lax.ppermute(value, "slab", [(i, i ^ 1) for i in range(lax.axis_size("slab"))])
 
 
 def finish_kernel(one_ref, two_ref, msg_ref, in_ref, out_w_ref, gain_ref):
@@ -586,18 +635,19 @@
     own_blocks = node_rows // side
     rim_blocks = 2 * halo // side
 
-    tile = pack_shares(tile_count, tile_values, tile_cols, w_msg, w_in, w_out, ln_gain, tile_dst, tile_src)
+    tile, small = pack_shares(tile_count, tile_values, tile_cols, w_msg, w_in, w_out, ln_gain, tile_dst, tile_src)
+    smalls = [small] + [shift_wsh(small, -k) for k in range(1, parties)]
     tiles = [tile] + [shift_wsh(tile, -k) for k in range(1, parties)]
 
     rows = halo_rows.reshape(2, halo)
     counts = halo_count.reshape(2)
     picked = pick_rows(rows, counts, node_feat)
     low, high, full_msg, full_in, full_out, gain, codes = prepare(
-        position, tiles, picked, own_blocks, own_blocks + rim_blocks
+        position, smalls, picked, own_blocks, own_blocks + rim_blocks
     )
     lower = shift_slab(high, 1).reshape(rim_blocks // 2, side, side)
     upper = shift_slab(low, -1).reshape(rim_blocks // 2, side, side)
-    message = messages(node_feat, full_msg)
+    message = messages(node_feat, full_msg, tiles[1:])
     lists, totals = build_lists(codes)
     forward = functools.partial(
         forward_tiles, lists=lists, totals=totals, own=message.reshape(own_blocks, side, side), lower=lower,
@@ -614,33 +664,46 @@
     to_after, to_prior = join(after_second, from_left, prior_first, from_right)
     left_second = shift_wsh(to_after, 1)
     right_first = shift_wsh(to_prior, -1)
-    parts = (mine_first, mine_second, left_first, right_first, left_second, right_second)
-    parts = [part.reshape(-1, side) for part in parts]
-    node_out, d_hidden, d_agg, *sums = node_update(node_feat, cotangent, parts, full_in, full_out, gain)
-    from_prior = shift_wsh(d_agg, 1)
-    from_after = shift_wsh(d_agg, -1)
-    half = node_rows // 2
-    far_first = shift_wsh(from_prior[:half], 1)
-    far_second = shift_wsh(from_after[half:], -1)
-    slope, base = ahead(node_feat, cotangent, d_hidden, full_msg, full_in)
+    parts = ((mine_first, left_first, right_first), (mine_second, left_second, right_second))
+    before, d_agg, from_prior, from_after = (), [], [], []
+    for h in (0, 1):
+        pieces = [part.reshape(-1, side) for part in parts[h]]
+        node_out, d_hidden, half, *sums = node_update(
+            h, node_feat, cotangent, pieces, full_in, full_out, gain, before
+        )
+        before = (node_out, d_hidden, *sums)
+        d_agg.append(half)
+        from_prior.append(shift_wsh(half, 1))
+        from_after.append(shift_wsh(half, -1))
+    quarter = node_rows // 4
+    far = []
+    for h in (0, 1):
+        far.append(shift_wsh(from_prior[h][:quarter], 1))
+        far.append(shift_wsh(from_after[h][quarter:], -1))
+    slope, base, far_slope = ahead(node_feat, cotangent, d_hidden, picked, full_msg, full_in)
 
     backward = functools.partial(backward_tiles, lists=lists, totals=totals, tiles=tiles)
     own_part, rim_part = backward(
-        (0, 1, 3), (0, 1), (own_blocks, rim_blocks), (F32, F32), arrays=((d_agg,), (from_after,), (from_prior,)),
+        (0, 1, 3), (0, 1), (own_blocks, rim_blocks), (F32, F32), arrays=(d_agg, from_after, from_prior),
         started=(),
     )
-    far = ((far_first, far_second),)
     back_low, back_high = backward(
-        (2,), (1,), (rim_blocks // 2,) * 2, (BF16,) * 2, arrays=far, started=(rim_part,), follow=(slope,)
+        (2,), (1,), (rim_blocks // 2,) * 2, (BF16,) * 2, arrays=(far,), started=(rim_part,), follow=(slope,)
     )
     back_upper = shift_slab(back_low.reshape(halo, side), -1)
     back_lower = shift_slab(back_high.reshape(halo, side), 1)
-    (d_own,) = backward((2,), (0,), (own_blocks,), (F32,), arrays=far, started=(own_part,))
-    d_node, *pieces = last_products(
-        position, rows, counts, d_own.reshape(node_rows, side), back_lower, back_upper, full_msg, sums, node_feat,
-        slope, base,
+    (d_own,) = backward((2,), (0,), (own_blocks,), (F32,), arrays=(far,), started=(own_part,))
+    total, d_w_own = own_products(node_feat, slope, base, d_own.reshape(node_rows, side), full_msg)
+    d_pre, *pieces = rim_products(
+        position, counts, back_lower, back_upper, picked, far_slope, d_w_own, sums
     )
-    d_w_msg, d_w_in, d_w_out, d_gain = finish(*sum_everywhere(pieces))
+    place = functools.partial(place_rows, halo_rows=rows, halo_count=counts, d_pre=d_pre, w_msg=full_msg)
+    total, token = place(0, F32, total=total, follow=())
+    value = sum_wsh(pieces, (token,))
+    d_node, token = place(1, BF16, total=total, follow=(value,))
+    value = sum_slab(value, 8, 4, (token,))
+    value = sum_slab(value, 2, 4)
+    d_w_msg, d_w_in, d_w_out, d_gain = finish(value, other_core(value))
     return (node_out, d_node, d_w_msg, d_w_in, d_w_out, d_gain.reshape(share))
 
 

time: 179 us -> 165 us (0.922)
  waiting for transfers between devices: 72.1 us -> 48.4 us
  starting transfers between devices: 52.4 us -> 59.2 us
  Pallas kernels: 49 us -> 53.4 us
    ppermute x16 -> x23, waiting for transfers between devices: 61.3 us -> 42.7 us  [shift_wsh(): lax.ppermute(value, 'wsh', [(i, (i + step) % parties) for i in range(part...]
    ppermute x4, starting transfers between devices: 13.4 us -> 20.5 us  [shift_slab(): return lax.ppermute(value, 'slab', pairs)]
    ppermute x7, waiting for transfers between devices: 8.36 us -> 4.62 us  [the longest x6 3.76 us: sum_slab(): lax.ppermute(value, 'slab', pairs)]
    pallas_call x1, Pallas kernels: 0.45 us -> 2.38 us  [prepare(): pl.pallas_call(functools.partial(prepare_kernel, own_blocks, here_blocks)...]
    pallas_call x4 -> x11, Pallas kernels: 21.3 us -> 22.9 us  [the longest x2 8.88 us: node_update(): pl.pallas_call(functools.partial(node_kernel, bool(before)), grid=(steps,...]
    ppermute x16 -> x23, starting transfers between devices: 24.1 us -> 25.7 us  [shift_wsh(): lax.ppermute(value, 'wsh', [(i, (i + step) % parties) for i in range(part...]
  transfers between devices with their start and end apart: 27 -> 34, of which waited for: 19 -> 13; matrix products, arithmetic and copies ran while one was open for 0% -> 0% of each run, Pallas kernels for 12% -> 24%
where the time goes in v4:
time: 165 us
  starting transfers between devices  59.2 us (36%)
  Pallas kernels  53.4 us (32%)
  waiting for transfers between devices  48.4 us (29%)
  local copies, waits for them, and re-layouts  2.1 us (1%)
  between operations  1.8 us (1%)
    ppermute x23, waiting for transfers between devices, shift_wsh(): lax.ppermute(value, 'wsh', [(i, (i + step) % parties) for i in range(part...  42.7 us
    ppermute x23, starting transfers between devices, shift_wsh(): lax.ppermute(value, 'wsh', [(i, (i + step) % parties) for i in range(part...  25.7 us
    ppermute x4, starting transfers between devices, shift_slab(): return lax.ppermute(value, 'slab', pairs)  20.5 us
    pallas_call x2, Pallas kernels, node_update(): pl.pallas_call(functools.partial(node_kernel, bool(before)), grid=(steps,...  8.88 us
    pallas_call x3, Pallas kernels, forward_tiles(): pl.pallas_call(functools.partial(forward_kernel, ks), out_shape=(half,) *...  8.68 us
    pallas_call x2, Pallas kernels, place_rows(): pl.pallas_call(functools.partial(place_kernel, k), out_shape=(jax.ShapeDt...  8.03 us
    ppermute x6, starting transfers between devices, sum_slab(): lax.ppermute(value, 'slab', pairs)  8 us
    pallas_call x3, Pallas kernels, backward_tiles(): pl.pallas_call(functools.partial(backward_kernel, ks, cuts, parts, bool(s...  7.67 us
  transfers between devices with their start and end apart: 34, of which 13 were waited for; matrix products, arithmetic and copies ran while one was open for 0% of the time, Pallas kernels for 24%

profile of v4, /device:TPU:1, one launch (start us, length us, event | category | flops | bytes accessed | tf_op | source)
XLA Modules:
  0.0 164.9 jit_solution(15583942233063812340)
XLA Ops:
  3.1 2.5 %collective-permute-start.2 = (bf16[144,128]{1,0:T(8,128)(2,1)}, bf16[144,128]{1,0:T(8,128)(2,1)S(1)}, u32[]{:S(2)}, u32[]{:S(2)}) collective-permute-start(bf16[144,128]{1,0:T(8,128)(2,1)} %get-tuple-element.61.s0_ref), channel_id=1, source_target_pairs={{0,1},{1,2},{2,3},{3,0},{4,5},{5,6},{6,7},{7,4},{8,9},{9,10},{10,1... | collective-permute-start | bytes 110600 | tf_op jit(solution)/shard_map/ppermute | solution.py:561
  5.6 3.3 %collective-permute-start.1 = (bf16[144,128]{1,0:T(8,128)(2,1)}, bf16[144,128]{1,0:T(8,128)(2,1)S(1)}, u32[]{:S(2)}, u32[]{:S(2)}) collective-permute-start(bf16[144,128]{1,0:T(8,128)(2,1)} %get-tuple-element.61.s0_ref), channel_id=1, source_target_pairs={{0,2},{1,3},{2,0},{3,1},{4,6},{5,7},{6,4},{7,5},{8,10},{9,11},{10,... | collective-permute-start | bytes 110600 | tf_op jit(solution)/shard_map/ppermute | solution.py:561
  10.8 6.1 %pick_rows.1.picked_ref = bf16[2048,128]{1,0:T(8,128)(2,1)} custom-call(s32[2,1024]{1,0:T(2,128)} %bitcast.38, s32[2]{0:T(128)} %bitcast.41, bf16[4096,128]{1,0:T(8,128)(2,1)} %feat_ref.11), custom_call_target="tpu_custom_call" | custom-call | tf_op jit(solution)/shard_map/pick_rows/pallas_call | solution.py:72
  21.3 5.9 %collective-permute-start.6 = (bf16[1024,128]{1,0:T(8,128)(2,1)}, bf16[1024,128]{1,0:T(8,128)(2,1)S(1)}, u32[]{:S(2)}, u32[]{:S(2)}) collective-permute-start(bf16[1024,128]{1,0:T(8,128)(2,1)} %get-tuple-element.67), channel_id=1, source_target_pairs={{0,4},{4,8},{8,12},{12,16},{16,20},{20,24},{24,28},{28,32},{32,36}... | collective-permute-start | bytes 786440 | tf_op jit(solution)/shard_map/ppermute | solution.py:567
  29.1 3.2 %tile_lists.1 = (s32[8,144]{1,0:T(8,128)}, s32[8]{0:T(128)}) custom-call(s32[8,128]{1,0:T(8,128)} %get-tuple-element.62.code_ref), custom_call_target="tpu_custom_call" | custom-call | tf_op jit(solution)/shard_map/tile_lists/pallas_call | solution.py:220
  35.1 3.9 %forward_tiles.5 = (bf16[16,128,128]{2,1,0:T(8,128)(2,1)S(1)}, bf16[16,128,128]{2,1,0:T(8,128)(2,1)S(1)}) custom-call(s32[8,144]{1,0:T(8,128)S(1)} %copy-done.11, s32[8]{0:T(128)S(1)} %copy-done.12, bf16[32,128,128]{2,1,0:T(8,128)(2,1)S(1)} %bitcast.31, bf16[8,128,128]{2,1,0:T(8,128)(2,1)S(1)} %bitcast.51, bf16[8,128,128]{2,1,0:T(8,128)(2,1)S(1)} %bitcast.54, ...), custom_call_target="tpu_custom_call" | custom-call | flops 1000000000 | bytes 4000000 | tf_op jit(solution)/shard_map/forward_tiles/pallas_call | solution.py:287
  39.0 2.7 %collective-permute-start.9 = (bf16[16,128,128]{2,1,0:T(8,128)(2,1)S(1)}, bf16[16,128,128]{2,1,0:T(8,128)(2,1)S(1)}, u32[]{:S(2)}, u32[]{:S(2)}) collective-permute-start(bf16[16,128,128]{2,1,0:T(8,128)(2,1)S(1)} %get-tuple-element.73), channel_id=1, source_target_pairs={{0,3},{1,0},{2,1},{3,2},{4,7},{5,4},{6,5},{7,6},{8,11},{9,8},{10,9... | collective-permute-start | bytes 1572872 | tf_op jit(solution)/shard_map/ppermute | solution.py:561
  41.7 2.6 %forward_tiles.4 = (bf16[16,128,128]{2,1,0:T(8,128)(2,1)S(1)}, bf16[16,128,128]{2,1,0:T(8,128)(2,1)S(1)}, bf16[16,128,128]{2,1,0:T(8,128)(2,1)S(1)}, bf16[16,128,128]{2,1,0:T(8,128)(2,1)S(1)}) custom-call(s32[8,144]{1,0:T(8,128)S(1)} %copy-done.11, s32[8]{0:T(128)S(1)} %copy-done.12, bf16[32,128,128]{2,1,0:T(8,128)(2,1)S(1)} %bitcast.32, ...), custom_call_target="tpu_custom_call" | custom-call | flops 2000000000 | bytes 8000000 | tf_op jit(solution)/shard_map/forward_tiles/pallas_call | solution.py:287
  45.3 6.8 %collective-permute-done.8.left_ref = bf16[16,128,128]{2,1,0:T(8,128)(2,1)S(1)} collective-permute-done((bf16[16,128,128]{2,1,0:T(8,128)(2,1)S(1)}, bf16[16,128,128]{2,1,0:T(8,128)(2,1)S(1)}, u32[]{:S(2)}, u32[]{:S(2)}) %collective-permute-start.8) | collective-permute-done | bytes 524320 | tf_op jit(solution)/shard_map/ppermute | solution.py:561
  56.6 6.8 %collective-permute-done.12 = bf16[16,128,128]{2,1,0:T(8,128)(2,1)S(1)} collective-permute-done((bf16[16,128,128]{2,1,0:T(8,128)(2,1)S(1)}, bf16[16,128,128]{2,1,0:T(8,128)(2,1)S(1)}, u32[]{:S(2)}, u32[]{:S(2)}) %collective-permute-start.12) | collective-permute-done | bytes 524320 | tf_op jit(solution)/shard_map/ppermute | solution.py:561
  63.3 3.1 %collective-permute-done.13 = bf16[16,128,128]{2,1,0:T(8,128)(2,1)S(1)} collective-permute-done((bf16[16,128,128]{2,1,0:T(8,128)(2,1)S(1)}, bf16[16,128,128]{2,1,0:T(8,128)(2,1)S(1)}, u32[]{:S(2)}, u32[]{:S(2)}) %collective-permute-start.13) | collective-permute-done | bytes 524320 | tf_op jit(solution)/shard_map/ppermute | solution.py:561
  66.5 4.4 %node_update.2 = (bf16[4096,128]{1,0:T(8,128)(2,1)}, bf16[4096,128]{1,0:T(8,128)(2,1)S(1)}, bf16[2048,128]{1,0:T(8,128)(2,1)S(1)}, f32[256,128]{1,0:T(8,128)S(1)...) custom-call(bf16[4096,128]{1,0:T(8,128)(2,1)S(1)} %copy-done.1, bf16[4096,128]{1,0:T(8,128)(2,1)S(1)} %copy-done.7, ...), custom_call_target="tpu_custom_call" | custom-call | flops 5000000000 | bytes 10000000 | tf_op jit(solution)/shard_map/node_update/pallas_call | solution.py:374
  70.9 3.5 %collective-permute-done.11 = bf16[16,128,128]{2,1,0:T(8,128)(2,1)S(1)} collective-permute-done((bf16[16,128,128]{2,1,0:T(8,128)(2,1)S(1)}, bf16[16,128,128]{2,1,0:T(8,128)(2,1)S(1)}, u32[]{:S(2)}, u32[]{:S(2)}) %collective-permute-start.11) | collective-permute-done | bytes 524320 | tf_op jit(solution)/shard_map/ppermute | solution.py:561
  74.5 4.5 %node_update.3 = (bf16[4096,128]{1,0:T(8,128)(2,1)}, bf16[4096,128]{1,0:T(8,128)(2,1)S(1)}, bf16[2048,128]{1,0:T(8,128)(2,1)S(1)}, f32[256,128]{1,0:T(8,128)S(1)...) custom-call(bf16[4096,128]{1,0:T(8,128)(2,1)S(1)} %copy-done.1, ...), custom_call_target="tpu_custom_call", output_to_operand_aliasing={{0}: (8, {}), {1}: (9, {})} | custom-call | flops 5000000000 | bytes 10000000 | tf_op jit(solution)/shard_map/node_update/pallas_call | solution.py:374
  84.3 8.6 %collective-permute-done.20 = bf16[2048,128]{1,0:T(8,128)(2,1)S(1)} collective-permute-done((bf16[2048,128]{1,0:T(8,128)(2,1)S(1)}, bf16[2048,128]{1,0:T(8,128)(2,1)S(1)}, u32[]{:S(2)}, u32[]{:S(2)}) %collective-permute-start.20) | collective-permute-done | bytes 524320 | tf_op jit(solution)/shard_map/ppermute | solution.py:561
  95.3 8.9 %collective-permute-done.16 = bf16[2048,128]{1,0:T(8,128)(2,1)S(1)} collective-permute-done((bf16[2048,128]{1,0:T(8,128)(2,1)S(1)}, bf16[2048,128]{1,0:T(8,128)(2,1)S(1)}, u32[]{:S(2)}, u32[]{:S(2)}) %collective-permute-start.16) | collective-permute-done | bytes 524320 | tf_op jit(solution)/shard_map/ppermute | solution.py:561
  106.5 3.5 %backward_tiles.3 = (f32[32,128,128]{2,1,0:T(8,128)S(1)}, f32[16,128,128]{2,1,0:T(8,128)S(1)}) custom-call(s32[8,144]{1,0:T(8,128)S(1)} %copy-done.11, s32[8]{0:T(128)S(1)} %copy-done.12, bf16[1024,128]{1,0:T(8,128)(2,1)S(1)} %copy-done.8, bf16[1024,128]{1,0:T(8,128)(2,1)S(1)} %collective-permute-done.3.rest_0_.rest_1_, ...), custom_call_target="tpu_custom_call" | custom-call | flops 6000000000 | bytes 4000000 | tf_op jit(solution)/shard_map/backward_tiles/pallas_call | solution.py:446
  118.6 10.8 %collective-permute-start.22 = (bf16[1024,128]{1,0:T(8,128)(2,1)S(1)}, bf16[1024,128]{1,0:T(8,128)(2,1)S(1)}, u32[]{:S(2)}, u32[]{:S(2)}) collective-permute-start(bf16[1024,128]{1,0:T(8,128)(2,1)S(1)} %bitcast.65), channel_id=1, source_target_pairs={{0,4},{4,8},{8,12},{12,16},{16,20},{20,24},{24,28},{28,32},{32,36}... | collective-permute-start | bytes 786440 | tf_op jit(solution)/shard_map/ppermute | solution.py:567
  129.4 2.4 %backward_tiles.4 = f32[32,128,128]{2,1,0:T(8,128)S(1)} custom-call(s32[8,144]{1,0:T(8,128)S(1)} %copy-done.11, s32[8]{0:T(128)S(1)} %copy-done.12, bf16[1024,128]{1,0:T(8,128)(2,1)S(1)} %collective-permute-done.4.rest_1_.rest_0_, bf16[8,128,128]{2,1,0:T(8,128)(2,1)S(1)} %bitcast.64, bf16[8,128,128]{2,1,0:T(8,128)(2,1)S(1)} %bitcast.62, ...), custom_call_target="tpu_custom_call" | custom-call | flops 2000000000 | bytes 4000000 | tf_op jit(solution)/shard_map/backward_tiles/pallas_call | solution.py:446
  137.0 3.7 %place_rows.2 = (f32[4096,128]{1,0:T(8,128)S(1)}, f32[8,128]{1,0:T(8,128)S(1)}) custom-call(s32[2,1024]{1,0:T(2,128)S(1)} %bitcast.39, s32[2]{0:T(128)S(1)} %bitcast.43, f32[4096,128]{1,0:T(8,128)S(1)} %get-tuple-element.94.sum_ref, bf16[2048,128]{1,0:T(8,128)(2,1)S(1)} %get-tuple-element.103.dpre_ref, bf16[128,128]{1,0:T(8,128)(2,1)S(1)} %copy-done.4), custom_call_target="tpu_custom_call" | custom-call | flops 4000000000 | bytes 7000000 | tf_op jit(solution)/shard_map/place_rows/pallas_call | solution.py:547
  145.1 4.3 %place_rows.3 = (bf16[4096,128]{1,0:T(8,128)(2,1)}, f32[8,128]{1,0:T(8,128)S(1)}) custom-call(s32[2,1024]{1,0:T(2,128)S(1)} %bitcast.40, s32[2]{0:T(128)S(1)} %bitcast.44, f32[4096,128]{1,0:T(8,128)S(1)} %get-tuple-element.104.sum_ref, bf16[2048,128]{1,0:T(8,128)(2,1)S(1)} %get-tuple-element.103.dpre_ref, bf16[128,128]{1,0:T(8,128)(2,1)S(1)} %copy-done.4, ...), custom_call_target="tpu_custom_call" | custom-call | flops 4000000000 | bytes 7000000 | tf_op jit(solution)/shard_map/place_rows/pallas_call | solution.py:547
  149.4 3.1 %collective-permute-start.32 = (bf16[144,128]{1,0:T(8,128)(2,1)S(1)}, bf16[144,128]{1,0:T(8,128)(2,1)S(1)}, u32[]{:S(2)}, u32[]{:S(2)}) collective-permute-start(bf16[144,128]{1,0:T(8,128)(2,1)S(1)} %sum_group.4.refs_0_), channel_id=1, source_target_pairs={{0,24},{4,28},{8,0},{12,4},{16,8},{20,12},{24,16},{28,20},{32,56},... | collective-permute-start | bytes 110600 | tf_op jit(solution)/shard_map/ppermute | solution.py:596
  153.6 3.4 %collective-permute-done.31.refs_2_ = bf16[144,128]{1,0:T(8,128)(2,1)S(1)} collective-permute-done((bf16[144,128]{1,0:T(8,128)(2,1)S(1)}, bf16[144,128]{1,0:T(8,128)(2,1)S(1)}, u32[]{:S(2)}, u32[]{:S(2)}) %collective-permute-start.31) | collective-permute-done | bytes 36896 | tf_op jit(solution)/shard_map/ppermute | solution.py:596
  157.0 5.0 %collective-permute-start.33 = (bf16[144,128]{1,0:T(8,128)(2,1)S(1)}, bf16[144,128]{1,0:T(8,128)(2,1)S(1)}, u32[]{:S(2)}, u32[]{:S(2)}) collective-permute-start(bf16[144,128]{1,0:T(8,128)(2,1)S(1)} %sum_group.5.one_ref), channel_id=1, source_target_pairs={{0,4},{4,0},{8,12},{12,8},{16,20},{20,16},{24,28},{28,24},{32,36},... | collective-permute-start | bytes 110600 | tf_op jit(solution)/shard_map/ppermute | solution.py:600
  (107 shorter events, 50.3 us)
Async XLA Ops:
  3.1 13.8 %collective-permute-start.2 = (bf16[144,128]{1,0:T(8,128)(2,1)}, bf16[144,128]{1,0:T(8,128)(2,1)S(1)}, u32[]{:S(2)}, u32[]{:S(2)}) collective-permute-start(bf16[144,128]{1,0:T(8,128)(2,1)} %get-tuple-element.61.s0_ref), channel_id=1, source_target_pairs={{0,1},{1,2},{2,3},{3,0},{4,5},{5,6},{6,7},{7,4},{8,9},{9,10},{10,1... | collective-permute-start | bytes 110600 | tf_op jit(solution)/shard_map/ppermute | solution.py:561
  5.6 12.7 %collective-permute-start.1 = (bf16[144,128]{1,0:T(8,128)(2,1)}, bf16[144,128]{1,0:T(8,128)(2,1)S(1)}, u32[]{:S(2)}, u32[]{:S(2)}) collective-permute-start(bf16[144,128]{1,0:T(8,128)(2,1)} %get-tuple-element.61.s0_ref), channel_id=1, source_target_pairs={{0,2},{1,3},{2,0},{3,1},{4,6},{5,7},{6,4},{7,5},{8,10},{9,11},{10,... | collective-permute-start | bytes 110600 | tf_op jit(solution)/shard_map/ppermute | solution.py:561
  8.9 9.4 %collective-permute-start = (bf16[144,128]{1,0:T(8,128)(2,1)}, bf16[144,128]{1,0:T(8,128)(2,1)S(1)}, u32[]{:S(2)}, u32[]{:S(2)}) collective-permute-start(bf16[144,128]{1,0:T(8,128)(2,1)} %get-tuple-element.61.s0_ref), channel_id=1, source_target_pairs={{0,3},{1,0},{2,1},{3,2},{4,7},{5,4},{6,5},{7,6},{8,11},{9,8},{10,9... | collective-permute-start | bytes 110600 | tf_op jit(solution)/shard_map/ppermute | solution.py:561
  9.6 22.6 %collective-permute-start.5 = (bf16[1024,128]{1,0:T(8,128)(2,1)}, bf16[1024,128]{1,0:T(8,128)(2,1)S(1)}, u32[]{:S(2)}, u32[]{:S(2)}) collective-permute-start(bf16[1024,128]{1,0:T(8,128)(2,1)} %get-tuple-element.66.rest_0_), channel_id=1, source_target_pairs={{0,1},{1,2},{2,3},{3,0},{4,5},{5,6},{6,7},{7,4},{8,9},{9,10},{10,1... | collective-permute-start | bytes 786440 | tf_op jit(solution)/shard_map/ppermute | solution.py:561
  10.4 21.9 %collective-permute-start.4 = (bf16[1024,128]{1,0:T(8,128)(2,1)}, bf16[1024,128]{1,0:T(8,128)(2,1)S(1)}, u32[]{:S(2)}, u32[]{:S(2)}) collective-permute-start(bf16[1024,128]{1,0:T(8,128)(2,1)} %get-tuple-element.66.rest_0_), channel_id=1, source_target_pairs={{0,2},{1,3},{2,0},{3,1},{4,6},{5,7},{6,4},{7,5},{8,10},{9,11},{10,... | collective-permute-start | bytes 786440 | tf_op jit(solution)/shard_map/ppermute | solution.py:561
  16.9 15.4 %collective-permute-start.3 = (bf16[1024,128]{1,0:T(8,128)(2,1)}, bf16[1024,128]{1,0:T(8,128)(2,1)S(1)}, u32[]{:S(2)}, u32[]{:S(2)}) collective-permute-start(bf16[1024,128]{1,0:T(8,128)(2,1)} %get-tuple-element.66.rest_0_), channel_id=1, source_target_pairs={{0,3},{1,0},{2,1},{3,2},{4,7},{5,4},{6,5},{7,6},{8,11},{9,8},{10,9... | collective-permute-start | bytes 786440 | tf_op jit(solution)/shard_map/ppermute | solution.py:561
  21.3 12.7 %collective-permute-start.6 = (bf16[1024,128]{1,0:T(8,128)(2,1)}, bf16[1024,128]{1,0:T(8,128)(2,1)S(1)}, u32[]{:S(2)}, u32[]{:S(2)}) collective-permute-start(bf16[1024,128]{1,0:T(8,128)(2,1)} %get-tuple-element.67), channel_id=1, source_target_pairs={{0,4},{4,8},{8,12},{12,16},{16,20},{20,24},{24,28},{28,32},{32,36}... | collective-permute-start | bytes 786440 | tf_op jit(solution)/shard_map/ppermute | solution.py:567
  38.9 13.2 %collective-permute-start.8 = (bf16[16,128,128]{2,1,0:T(8,128)(2,1)S(1)}, bf16[16,128,128]{2,1,0:T(8,128)(2,1)S(1)}, u32[]{:S(2)}, u32[]{:S(2)}) collective-permute-start(bf16[16,128,128]{2,1,0:T(8,128)(2,1)S(1)} %get-tuple-element.71), channel_id=1, source_target_pairs={{0,1},{1,2},{2,3},{3,0},{4,5},{5,6},{6,7},{7,4},{8,9},{9,10},{10,1... | collective-permute-start | bytes 1572872 | tf_op jit(solution)/shard_map/ppermute | solution.py:561
  39.0 13.1 %collective-permute-start.9 = (bf16[16,128,128]{2,1,0:T(8,128)(2,1)S(1)}, bf16[16,128,128]{2,1,0:T(8,128)(2,1)S(1)}, u32[]{:S(2)}, u32[]{:S(2)}) collective-permute-start(bf16[16,128,128]{2,1,0:T(8,128)(2,1)S(1)} %get-tuple-element.73), channel_id=1, source_target_pairs={{0,3},{1,0},{2,1},{3,2},{4,7},{5,4},{6,5},{7,6},{8,11},{9,8},{10,9... | collective-permute-start | bytes 1572872 | tf_op jit(solution)/shard_map/ppermute | solution.py:561
  44.4 19.0 %collective-permute-start.12 = (bf16[16,128,128]{2,1,0:T(8,128)(2,1)S(1)}, bf16[16,128,128]{2,1,0:T(8,128)(2,1)S(1)}, u32[]{:S(2)}, u32[]{:S(2)}) collective-permute-start(bf16[16,128,128]{2,1,0:T(8,128)(2,1)S(1)} %get-tuple-element.80), channel_id=1, source_target_pairs={{0,1},{1,2},{2,3},{3,0},{4,5},{5,6},{6,7},{7,4},{8,9},{9,10},{10,1... | collective-permute-start | bytes 1572872 | tf_op jit(solution)/shard_map/ppermute | solution.py:561
  52.4 14.1 %collective-permute-start.13 = (bf16[16,128,128]{2,1,0:T(8,128)(2,1)S(1)}, bf16[16,128,128]{2,1,0:T(8,128)(2,1)S(1)}, u32[]{:S(2)}, u32[]{:S(2)}) collective-permute-start(bf16[16,128,128]{2,1,0:T(8,128)(2,1)S(1)} %get-tuple-element.81), channel_id=1, source_target_pairs={{0,3},{1,0},{2,1},{3,2},{4,7},{5,4},{6,5},{7,6},{8,11},{9,8},{10,9... | collective-permute-start | bytes 1572872 | tf_op jit(solution)/shard_map/ppermute | solution.py:561
  52.9 21.5 %collective-permute-start.11 = (bf16[16,128,128]{2,1,0:T(8,128)(2,1)S(1)}, bf16[16,128,128]{2,1,0:T(8,128)(2,1)S(1)}, u32[]{:S(2)}, u32[]{:S(2)}) collective-permute-start(bf16[16,128,128]{2,1,0:T(8,128)(2,1)S(1)} %get-tuple-element.75), channel_id=1, source_target_pairs={{0,3},{1,0},{2,1},{3,2},{4,7},{5,4},{6,5},{7,6},{8,11},{9,8},{10,9... | collective-permute-start | bytes 1572872 | tf_op jit(solution)/shard_map/ppermute | solution.py:561
  54.4 20.1 %collective-permute-start.10 = (bf16[16,128,128]{2,1,0:T(8,128)(2,1)S(1)}, bf16[16,128,128]{2,1,0:T(8,128)(2,1)S(1)}, u32[]{:S(2)}, u32[]{:S(2)}) collective-permute-start(bf16[16,128,128]{2,1,0:T(8,128)(2,1)S(1)} %get-tuple-element.74), channel_id=1, source_target_pairs={{0,1},{1,2},{2,3},{3,0},{4,5},{5,6},{6,7},{7,4},{8,9},{9,10},{10,1... | collective-permute-start | bytes 1572872 | tf_op jit(solution)/shard_map/ppermute | solution.py:561
  78.9 14.0 %collective-permute-start.20 = (bf16[2048,128]{1,0:T(8,128)(2,1)S(1)}, bf16[2048,128]{1,0:T(8,128)(2,1)S(1)}, u32[]{:S(2)}, u32[]{:S(2)}) collective-permute-start(bf16[2048,128]{1,0:T(8,128)(2,1)S(1)} %get-tuple-element.92), channel_id=1, source_target_pairs={{0,3},{1,0},{2,1},{3,2},{4,7},{5,4},{6,5},{7,6},{8,11},{9,8},{10,9... | collective-permute-start | bytes 1572872 | tf_op jit(solution)/shard_map/ppermute | solution.py:561
  79.8 15.3 %collective-permute-start.18 = (bf16[2048,128]{1,0:T(8,128)(2,1)S(1)}, bf16[2048,128]{1,0:T(8,128)(2,1)S(1)}, u32[]{:S(2)}, u32[]{:S(2)}) collective-permute-start(bf16[2048,128]{1,0:T(8,128)(2,1)S(1)} %get-tuple-element.92), channel_id=1, source_target_pairs={{0,1},{1,2},{2,3},{3,0},{4,5},{5,6},{6,7},{7,4},{8,9},{9,10},{10,1... | collective-permute-start | bytes 1572872 | tf_op jit(solution)/shard_map/ppermute | solution.py:561
  80.4 23.8 %collective-permute-start.16 = (bf16[2048,128]{1,0:T(8,128)(2,1)S(1)}, bf16[2048,128]{1,0:T(8,128)(2,1)S(1)}, u32[]{:S(2)}, u32[]{:S(2)}) collective-permute-start(bf16[2048,128]{1,0:T(8,128)(2,1)S(1)} %get-tuple-element.91), channel_id=1, source_target_pairs={{0,3},{1,0},{2,1},{3,2},{4,7},{5,4},{6,5},{7,6},{8,11},{9,8},{10,9... | collective-permute-start | bytes 1572872 | tf_op jit(solution)/shard_map/ppermute | solution.py:561
  82.5 23.9 %collective-permute-start.14 = (bf16[2048,128]{1,0:T(8,128)(2,1)S(1)}, bf16[2048,128]{1,0:T(8,128)(2,1)S(1)}, u32[]{:S(2)}, u32[]{:S(2)}) collective-permute-start(bf16[2048,128]{1,0:T(8,128)(2,1)S(1)} %get-tuple-element.91), channel_id=1, source_target_pairs={{0,1},{1,2},{2,3},{3,0},{4,5},{5,6},{6,7},{7,4},{8,9},{9,10},{10,1... | collective-permute-start | bytes 1572872 | tf_op jit(solution)/shard_map/ppermute | solution.py:561
  92.9 17.0 %collective-permute-start.21 = (bf16[1024,128]{1,0:T(8,128)(2,1)S(1)}, bf16[1024,128]{1,0:T(8,128)(2,1)S(1)}, u32[]{:S(2)}, u32[]{:S(2)}) collective-permute-start(bf16[1024,128]{1,0:T(8,128)(2,1)S(1)} %slice.19), channel_id=1, source_target_pairs={{0,3},{1,0},{2,1},{3,2},{4,7},{5,4},{6,5},{7,6},{8,11},{9,8},{10,9... | collective-permute-start | bytes 786440 | tf_op jit(solution)/shard_map/ppermute | solution.py:561
  95.2 16.7 %collective-permute-start.19 = (bf16[1024,128]{1,0:T(8,128)(2,1)S(1)}, bf16[1024,128]{1,0:T(8,128)(2,1)S(1)}, u32[]{:S(2)}, u32[]{:S(2)}) collective-permute-start(bf16[1024,128]{1,0:T(8,128)(2,1)S(1)} %slice.18), channel_id=1, source_target_pairs={{0,1},{1,2},{2,3},{3,0},{4,5},{5,6},{6,7},{7,4},{8,9},{9,10},{10,1... | collective-permute-start | bytes 786440 | tf_op jit(solution)/shard_map/ppermute | solution.py:561
  104.2 9.0 %collective-permute-start.17 = (bf16[1024,128]{1,0:T(8,128)(2,1)S(1)}, bf16[1024,128]{1,0:T(8,128)(2,1)S(1)}, u32[]{:S(2)}, u32[]{:S(2)}) collective-permute-start(bf16[1024,128]{1,0:T(8,128)(2,1)S(1)} %slice.17), channel_id=1, source_target_pairs={{0,3},{1,0},{2,1},{3,2},{4,7},{5,4},{6,5},{7,6},{8,11},{9,8},{10,9... | collective-permute-start | bytes 786440 | tf_op jit(solution)/shard_map/ppermute | solution.py:561
  106.4 8.5 %collective-permute-start.15 = (bf16[1024,128]{1,0:T(8,128)(2,1)S(1)}, bf16[1024,128]{1,0:T(8,128)(2,1)S(1)}, u32[]{:S(2)}, u32[]{:S(2)}) collective-permute-start(bf16[1024,128]{1,0:T(8,128)(2,1)S(1)} %slice.16), channel_id=1, source_target_pairs={{0,1},{1,2},{2,3},{3,0},{4,5},{5,6},{6,7},{7,4},{8,9},{9,10},{10,1... | collective-permute-start | bytes 786440 | tf_op jit(solution)/shard_map/ppermute | solution.py:561
  116.7 16.6 %collective-permute-start.23 = (bf16[1024,128]{1,0:T(8,128)(2,1)S(1)}, bf16[1024,128]{1,0:T(8,128)(2,1)S(1)}, u32[]{:S(2)}, u32[]{:S(2)}) collective-permute-start(bf16[1024,128]{1,0:T(8,128)(2,1)S(1)} %bitcast.66), channel_id=1, source_target_pairs={{4,0},{8,4},{12,8},{16,12},{20,16},{24,20},{28,24},{32,28},{36,32}... | collective-permute-start | bytes 786440 | tf_op jit(solution)/shard_map/ppermute | solution.py:567
  118.6 14.7 %collective-permute-start.22 = (bf16[1024,128]{1,0:T(8,128)(2,1)S(1)}, bf16[1024,128]{1,0:T(8,128)(2,1)S(1)}, u32[]{:S(2)}, u32[]{:S(2)}) collective-permute-start(bf16[1024,128]{1,0:T(8,128)(2,1)S(1)} %bitcast.65), channel_id=1, source_target_pairs={{0,4},{4,8},{8,12},{12,16},{16,20},{20,24},{24,28},{28,32},{32,36}... | collective-permute-start | bytes 786440 | tf_op jit(solution)/shard_map/ppermute | solution.py:567
  140.8 8.6 %collective-permute-start.29 = (bf16[144,128]{1,0:T(8,128)(2,1)S(1)}, bf16[144,128]{1,0:T(8,128)(2,1)S(1)}, u32[]{:S(2)}, u32[]{:S(2)}) collective-permute-start(bf16[144,128]{1,0:T(8,128)(2,1)S(1)} %sum_group.3.rest_0_.refs_0_), channel_id=1, source_target_pairs={{0,96},{4,100},{8,104},{12,108},{16,112},{20,116},{24,120},{28,124... | collective-permute-start | bytes 110600 | tf_op jit(solution)/shard_map/ppermute | solution.py:596
  (28 other events, 191.0 us)

commit v5 on v4

--- a/solution.py
+++ b/solution.py
@@ -12,6 +12,7 @@
 SIDE = 128
 UNROLL = 4
 PARAMS = pltpu.CompilerParams(vmem_limit_bytes=20 * 2**20)
+SMALL = pltpu.CompilerParams(vmem_limit_bytes=4 * 2**20)
 ROOMY = pltpu.CompilerParams(vmem_limit_bytes=60 * 2**20)
 VMEM = pl.BlockSpec(memory_space=pltpu.VMEM)
 SMEM = pl.BlockSpec(memory_space=pltpu.SMEM)
@@ -194,10 +195,11 @@
     )(feat, w_msg, *follow)
 
 
-def list_kernel(code_ref, list_ref, total_ref):
+def list_kernel(ks, code_ref, *rest):
+    list_ref, total_ref = rest[-2:]
     parties = code_ref.shape[0] // 2
     group = 8
-    for k in range(parties):
+    for k in ks:
 
         def body(step, carry):
             own, rim = carry
@@ -215,18 +217,19 @@
         total_ref[2 * k + 1] = rim
 
 
-def build_lists(codes):
+def build_lists(ks, codes, follow):
     parties, slots = codes.shape[0] // 2, codes.shape[1]
     return pl.pallas_call(
-        list_kernel,
+        functools.partial(list_kernel, ks),
         out_shape=(
             jax.ShapeDtypeStruct((2 * parties, slots + 16), jnp.int32),
             jax.ShapeDtypeStruct((2 * parties,), jnp.int32),
         ),
-        in_specs=[SMEM],
+        in_specs=[SMEM] + [ANY] * len(follow),
         out_specs=(SMEM, SMEM),
+        compiler_params=SMALL,
         name="tile_lists",
-    )(codes)
+    )(codes, *follow)
 
 
 def dense_tile(tiles_ref, slot, keep):
@@ -262,7 +265,8 @@
 
 def forward_kernel(ks, list_ref, total_ref, own_ref, lower_ref, upper_ref, *rest):
     slot_refs, rest = rest[: len(ks)], rest[len(ks) :]
-    outs, (acc, rims, tiles) = rest[: 2 * len(ks)], rest[2 * len(ks) :]
+    outs, (token_ref, acc, rims, tiles) = rest[:-4], rest[-4:]
+    token_ref[...] = jnp.zeros_like(token_ref)
     half = lower_ref.shape[0]
     rims[pl.ds(0, half)] = lower_ref[...]
     rims[pl.ds(half, half)] = upper_ref[...]
@@ -286,9 +290,9 @@
     half = jax.ShapeDtypeStruct((blocks // 2,) + own.shape[1:], kind)
     return pl.pallas_call(
         functools.partial(forward_kernel, ks),
-        out_shape=(half,) * (2 * len(ks)),
+        out_shape=(half,) * (2 * len(ks)) + (jax.ShapeDtypeStruct((8, SIDE), F32),),
         in_specs=[SMEM, SMEM] + [VMEM] * (3 + len(ks)),
-        out_specs=(VMEM,) * (2 * len(ks)),
+        out_specs=(VMEM,) * (2 * len(ks) + 1),
         scratch_shapes=[
             pltpu.VMEM(own.shape, F32),
             pltpu.VMEM((2 * lower.shape[0],) + lower.shape[1:], BF16),
@@ -358,7 +362,7 @@
     dwin_ref[SIDE:, :] += contract_rows(agg, d_hidden)
 
 
-def node_update(h, node_feat, cotangent, parts, w_in, w_out, gain, before):
+def node_update(h, node_feat, cotangent, parts, w_in, w_out, gain, before, follow):
     rows = node_feat.shape[0]
     chunk = 512
     steps = rows // 2 // chunk
@@ -377,13 +381,14 @@
         out_shape=(wide, wide, half) + tuple(jax.ShapeDtypeStruct(shape, F32) for shape in sums),
         in_specs=[tall, tall, part, part, part]
         + [whole((2 * SIDE, SIDE)), whole((SIDE, SIDE)), whole((1, SIDE))]
-        + ([ANY, ANY] + [whole(shape) for shape in sums] if before else []),
+        + ([ANY, ANY] + [whole(shape) for shape in sums] if before else [])
+        + [ANY] * len(follow),
         out_specs=(tall, tall, part) + tuple(whole(shape) for shape in sums),
         input_output_aliases={8: 0, 9: 1} if before else {},
         compiler_params=PARAMS,
         cost_estimate=cost(5_000_000_000, 10_000_000),
         name="node_update",
-    )(node_feat, cotangent, *parts, w_in, w_out, gain, *before)
+    )(node_feat, cotangent, *parts, w_in, w_out, gain, *before, *follow)
 
 
 def ahead_kernel(feat_ref, cot_ref, dhid_ref, picked_ref, msg_ref, in_ref, slope_ref, base_ref, far_ref):
@@ -439,7 +444,7 @@
             out_ref[...] = acc[...]
 
 
-def backward_tiles(ks, parts, sizes, kinds, lists, totals, tiles, arrays, started, follow=()):
+def backward_tiles(ks, lists, parts, sizes, kinds, tiles, arrays, started, follow=()):
     cuts = len(arrays[0])
     cubes = [array.reshape(-1, SIDE, SIDE) for group in arrays for array in group]
     accs = [sum(sizes)] if len(sizes) > len(parts) else sizes
@@ -453,7 +458,7 @@
         compiler_params=PARAMS,
         cost_estimate=cost(2_000_000_000 * len(ks), 4_000_000),
         name="backward_tiles",
-    )(lists, totals, *[tiles[k] for k in ks], *cubes, *started, *follow)
+    )(*lists, *[tiles[k] for k in ks], *cubes, *started, *follow)
 
 
 def own_kernel(feat_ref, slope_ref, base_ref, own_ref, msg_ref, sum_ref, dw_ref):
@@ -617,6 +622,7 @@
         out_shape=tuple(jax.ShapeDtypeStruct(shape, F32) for shape in shapes),
         in_specs=[VMEM, VMEM],
         out_specs=(VMEM,) * 4,
+        compiler_params=SMALL,
         name="finish",
     )(one, two)
 
@@ -648,19 +654,20 @@
     lower = shift_slab(high, 1).reshape(rim_blocks // 2, side, side)
     upper = shift_slab(low, -1).reshape(rim_blocks // 2, side, side)
     message = messages(node_feat, full_msg, tiles[1:])
-    lists, totals = build_lists(codes)
+    far_lists = build_lists((2,), codes, ())
     forward = functools.partial(
-        forward_tiles, lists=lists, totals=totals, own=message.reshape(own_blocks, side, side), lower=lower,
+        forward_tiles, own=message.reshape(own_blocks, side, side), lower=lower,
         upper=upper, tiles=tiles,
     )
 
-    far_first, far_second = forward((2,), kind=BF16)
+    far_first, far_second, token = forward((2,), *far_lists, kind=BF16)
+    lists = build_lists((0, 1, 3), codes, (token,))
     from_right = shift_wsh(far_first, -1)
     from_left = shift_wsh(far_second, 1)
-    after_first, after_second, prior_first, prior_second = forward((1, 3), kind=BF16)
+    after_first, after_second, prior_first, prior_second, _ = forward((1, 3), *lists, kind=BF16)
     left_first = shift_wsh(after_first, 1)
     right_second = shift_wsh(prior_second, -1)
-    mine_first, mine_second = forward((0,), kind=F32)
+    mine_first, mine_second, _ = forward((0,), *lists, kind=F32)
     to_after, to_prior = join(after_second, from_left, prior_first, from_right)
     left_second = shift_wsh(to_after, 1)
     right_first = shift_wsh(to_prior, -1)
@@ -669,7 +676,7 @@
     for h in (0, 1):
         pieces = [part.reshape(-1, side) for part in parts[h]]
         node_out, d_hidden, half, *sums = node_update(
-            h, node_feat, cotangent, pieces, full_in, full_out, gain, before
+            h, node_feat, cotangent, pieces, full_in, full_out, gain, before, from_prior
         )
         before = (node_out, d_hidden, *sums)
         d_agg.append(half)
@@ -682,17 +689,17 @@
         far.append(shift_wsh(from_after[h][quarter:], -1))
     slope, base, far_slope = ahead(node_feat, cotangent, d_hidden, picked, full_msg, full_in)
 
-    backward = functools.partial(backward_tiles, lists=lists, totals=totals, tiles=tiles)
+    backward = functools.partial(backward_tiles, tiles=tiles)
     own_part, rim_part = backward(
-        (0, 1, 3), (0, 1), (own_blocks, rim_blocks), (F32, F32), arrays=(d_agg, from_after, from_prior),
+        (0, 1, 3), lists, (0, 1), (own_blocks, rim_blocks), (F32, F32), arrays=(d_agg, from_after, from_prior),
         started=(),
     )
     back_low, back_high = backward(
-        (2,), (1,), (rim_blocks // 2,) * 2, (BF16,) * 2, arrays=(far,), started=(rim_part,), follow=(slope,)
+        (2,), far_lists, (1,), (rim_blocks // 2,) * 2, (BF16,) * 2, arrays=(far,), started=(rim_part,), follow=(slope,)
     )
     back_upper = shift_slab(back_low.reshape(halo, side), -1)
     back_lower = shift_slab(back_high.reshape(halo, side), 1)
-    (d_own,) = backward((2,), (0,), (own_blocks,), (F32,), arrays=(far,), started=(own_part,))
+    (d_own,) = backward((2,), far_lists, (0,), (own_blocks,), (F32,), arrays=(far,), started=(own_part,))
     total, d_w_own = own_products(node_feat, slope, base, d_own.reshape(node_rows, side), full_msg)
     d_pre, *pieces = rim_products(
         position, counts, back_lower, back_upper, picked, far_slope, d_w_own, sums

time: 165 us -> 159 us (0.964)
  waiting for transfers between devices: 48.4 us -> 41.2 us
    ppermute x23, waiting for transfers between devices: 42.7 us -> 34 us  [shift_wsh(): lax.ppermute(value, 'wsh', [(i, (i + step) % parties) for i in range(part...]
    ppermute x4, starting transfers between devices: 20.5 us -> 15 us  [shift_slab(): return lax.ppermute(value, 'slab', pairs)]
    ppermute x23, starting transfers between devices: 25.7 us -> 29.1 us  [shift_wsh(): lax.ppermute(value, 'wsh', [(i, (i + step) % parties) for i in range(part...]
    ppermute x6, starting transfers between devices: 8 us -> 10.2 us  [sum_slab(): lax.ppermute(value, 'slab', pairs)]
    pallas_call x1 -> x2, Pallas kernels: 3.18 us -> 4.51 us  [build_lists(): pl.pallas_call(functools.partial(list_kernel, ks), out_shape=(jax.ShapeDt...]
  transfers between devices with their start and end apart: 34 -> 34, of which waited for: 13 -> 15; matrix products, arithmetic and copies ran while one was open for 0% -> 0% of each run, Pallas kernels for 24% -> 30%
where the time goes in v5:
time: 159 us; the launch traced here: 158 us
  starting transfers between devices  59.8 us (38%)
  Pallas kernels  53.1 us (33%)
  waiting for transfers between devices  41.2 us (26%)
  local copies, waits for them, and re-layouts  2.19 us (1%)
  between operations  1.78 us (1%)
    ppermute x23, waiting for transfers between devices, shift_wsh(): lax.ppermute(value, 'wsh', [(i, (i + step) % parties) for i in range(part...  34 us
    ppermute x23, starting transfers between devices, shift_wsh(): lax.ppermute(value, 'wsh', [(i, (i + step) % parties) for i in range(part...  29.1 us
    ppermute x4, starting transfers between devices, shift_slab(): return lax.ppermute(value, 'slab', pairs)  15 us
    ppermute x6, starting transfers between devices, sum_slab(): lax.ppermute(value, 'slab', pairs)  10.2 us
    pallas_call x3, Pallas kernels, forward_tiles(): pl.pallas_call(functools.partial(forward_kernel, ks), out_shape=(half,) *...  9.32 us
    pallas_call x2, Pallas kernels, node_update(): pl.pallas_call(functools.partial(node_kernel, bool(before)), grid=(steps,...  9.01 us
    pallas_call x3, Pallas kernels, backward_tiles(): pl.pallas_call(functools.partial(backward_kernel, ks, cuts, parts, bool(s...  7.43 us
    pallas_call x2, Pallas kernels, place_rows(): pl.pallas_call(functools.partial(place_kernel, k), out_shape=(jax.ShapeDt...  7.25 us
  transfers between devices with their start and end apart: 34, of which 15 were waited for; matrix products, arithmetic and copies ran while one was open for 0% of the time, Pallas kernels for 30%

profile of v5, /device:TPU:1, one launch (start us, length us, event | category | flops | bytes accessed | tf_op | source)
XLA Modules:
  0.0 158.1 jit_solution(12869445271188815412)
XLA Ops:
  5.6 3.3 %collective-permute-start.1 = (bf16[144,128]{1,0:T(8,128)(2,1)}, bf16[144,128]{1,0:T(8,128)(2,1)S(1)}, u32[]{:S(2)}, u32[]{:S(2)}) collective-permute-start(bf16[144,128]{1,0:T(8,128)(2,1)} %get-tuple-element.64.s0_ref), channel_id=1, source_target_pairs={{0,2},{1,3},{2,0},{3,1},{4,6},{5,7},{6,4},{7,5},{8,10},{9,11},{10,... | collective-permute-start | bytes 110600 | tf_op jit(solution)/shard_map/ppermute | solution.py:566
  10.8 5.4 %pick_rows.1.picked_ref = bf16[2048,128]{1,0:T(8,128)(2,1)} custom-call(s32[2,1024]{1,0:T(2,128)} %bitcast.38, s32[2]{0:T(128)} %bitcast.41, bf16[4096,128]{1,0:T(8,128)(2,1)} %feat_ref.11), custom_call_target="tpu_custom_call" | custom-call | tf_op jit(solution)/shard_map/pick_rows/pallas_call | solution.py:73
  21.3 5.8 %collective-permute-start.6 = (bf16[1024,128]{1,0:T(8,128)(2,1)}, bf16[1024,128]{1,0:T(8,128)(2,1)S(1)}, u32[]{:S(2)}, u32[]{:S(2)}) collective-permute-start(bf16[1024,128]{1,0:T(8,128)(2,1)} %get-tuple-element.70), channel_id=1, source_target_pairs={{0,4},{4,8},{8,12},{12,16},{16,20},{20,24},{24,28},{28,32},{32,36}... | collective-permute-start | bytes 786440 | tf_op jit(solution)/shard_map/ppermute | solution.py:572
  39.0 3.0 %tile_lists.3 = (s32[8,144]{1,0:T(8,128)S(1)}, s32[8]{0:T(128)S(1)}) custom-call(s32[8,128]{1,0:T(8,128)S(1)} %copy-done.5, f32[8,128]{1,0:T(8,128)S(1)} %get-tuple-element.72.rest_0_), custom_call_target="tpu_custom_call" | custom-call | tf_op jit(solution)/shard_map/tile_lists/pallas_call | solution.py:222
  42.0 5.4 %forward_tiles.5 = (bf16[16,128,128]{2,1,0:T(8,128)(2,1)S(1)}, bf16[16,128,128]{2,1,0:T(8,128)(2,1)S(1)}, bf16[16,128,128]{2,1,0:T(8,128)(2,1)S(1)}, bf16[16,128,128]{2,1,0:T(8,128)(2,1)S(1)}, f32[8,128]{1,0:T(8,128)}) custom-call(s32[8,144]{1,0:T(8,128)S(1)} %get-tuple-element.73.list_ref, s32[8]{0:T(128)S(1)} %get-tuple-element.74.total_ref, ...), custom_call_target="tpu_custom_call" | custom-call | flops 2000000000 | bytes 8000000 | tf_op jit(solution)/shard_map/forward_tiles/pallas_call | solution.py:291
  51.2 2.6 %collective-permute-start.11 = (bf16[16,128,128]{2,1,0:T(8,128)(2,1)S(1)}, bf16[16,128,128]{2,1,0:T(8,128)(2,1)S(1)}, u32[]{:S(2)}, u32[]{:S(2)}) collective-permute-start(bf16[16,128,128]{2,1,0:T(8,128)(2,1)S(1)} %get-tuple-element.81), channel_id=1, source_target_pairs={{0,3},{1,0},{2,1},{3,2},{4,7},{5,4},{6,5},{7,6},{8,11},{9,8},{10,9... | collective-permute-start | bytes 1572872 | tf_op jit(solution)/shard_map/ppermute | solution.py:566
  53.8 2.6 %forward_tiles.4 = (f32[16,128,128]{2,1,0:T(8,128)S(1)}, f32[16,128,128]{2,1,0:T(8,128)S(1)}, f32[8,128]{1,0:T(8,128)}) custom-call(s32[8,144]{1,0:T(8,128)S(1)} %get-tuple-element.73.list_ref, s32[8]{0:T(128)S(1)} %get-tuple-element.74.total_ref, bf16[32,128,128]{2,1,0:T(8,128)(2,1)S(1)} %bitcast.33, bf16[8,128,128]{2,1,0:T(8,128)(2,1)S(1)} %bitcast.53, ...), custom_call_target="tpu_custom_call" | custom-call | flops 1000000000 | bytes 4000000 | tf_op jit(solution)/shard_map/forward_tiles/pallas_call | solution.py:291
  56.4 3.2 %collective-permute-done.12 = bf16[16,128,128]{2,1,0:T(8,128)(2,1)S(1)} collective-permute-done((bf16[16,128,128]{2,1,0:T(8,128)(2,1)S(1)}, bf16[16,128,128]{2,1,0:T(8,128)(2,1)S(1)}, u32[]{:S(2)}, u32[]{:S(2)}) %collective-permute-start.12) | collective-permute-done | bytes 524320 | tf_op jit(solution)/shard_map/ppermute | solution.py:566
  59.6 4.5 %collective-permute-done.13 = bf16[16,128,128]{2,1,0:T(8,128)(2,1)S(1)} collective-permute-done((bf16[16,128,128]{2,1,0:T(8,128)(2,1)S(1)}, bf16[16,128,128]{2,1,0:T(8,128)(2,1)S(1)}, u32[]{:S(2)}, u32[]{:S(2)}) %collective-permute-start.13) | collective-permute-done | bytes 524320 | tf_op jit(solution)/shard_map/ppermute | solution.py:566
  64.1 4.4 %node_update.2 = (bf16[4096,128]{1,0:T(8,128)(2,1)}, bf16[4096,128]{1,0:T(8,128)(2,1)S(1)}, bf16[2048,128]{1,0:T(8,128)(2,1)S(1)}, f32[256,128]{1,0:T(8,128)S(1)...) custom-call(bf16[4096,128]{1,0:T(8,128)(2,1)S(1)} %copy-done.1, bf16[4096,128]{1,0:T(8,128)(2,1)S(1)} %copy-done.8, ...), custom_call_target="tpu_custom_call" | custom-call | flops 5000000000 | bytes 10000000 | tf_op jit(solution)/shard_map/node_update/pallas_call | solution.py:378
  71.2 4.1 %collective-permute-done.11 = bf16[16,128,128]{2,1,0:T(8,128)(2,1)S(1)} collective-permute-done((bf16[16,128,128]{2,1,0:T(8,128)(2,1)S(1)}, bf16[16,128,128]{2,1,0:T(8,128)(2,1)S(1)}, u32[]{:S(2)}, u32[]{:S(2)}) %collective-permute-start.11) | collective-permute-done | bytes 524320 | tf_op jit(solution)/shard_map/ppermute | solution.py:566
  75.3 6.8 %collective-permute-done.14.rest_5_ = bf16[2048,128]{1,0:T(8,128)(2,1)S(1)} collective-permute-done((bf16[2048,128]{1,0:T(8,128)(2,1)S(1)}, bf16[2048,128]{1,0:T(8,128)(2,1)S(1)}, u32[]{:S(2)}, u32[]{:S(2)}) %collective-permute-start.14) | collective-permute-done | bytes 524320 | tf_op jit(solution)/shard_map/ppermute | solution.py:566
  82.2 4.6 %node_update.3 = (bf16[4096,128]{1,0:T(8,128)(2,1)}, bf16[4096,128]{1,0:T(8,128)(2,1)S(1)}, bf16[2048,128]{1,0:T(8,128)(2,1)S(1)}, f32[256,128]{1,0:T(8,128)S(1)...) custom-call(bf16[4096,128]{1,0:T(8,128)(2,1)S(1)} %copy-done.1, ...), custom_call_target="tpu_custom_call", output_to_operand_aliasing={{0}: (8, {}), {1}: (9, {})} | custom-call | flops 5000000000 | bytes 10000000 | tf_op jit(solution)/shard_map/node_update/pallas_call | solution.py:378
  88.3 2.6 %collective-permute-start.17 = (bf16[1024,128]{1,0:T(8,128)(2,1)S(1)}, bf16[1024,128]{1,0:T(8,128)(2,1)S(1)}, u32[]{:S(2)}, u32[]{:S(2)}) collective-permute-start(bf16[1024,128]{1,0:T(8,128)(2,1)S(1)} %slice.17), channel_id=1, source_target_pairs={{0,3},{1,0},{2,1},{3,2},{4,7},{5,4},{6,5},{7,6},{8,11},{9,8},{10,9... | collective-permute-start | bytes 786440 | tf_op jit(solution)/shard_map/ppermute | solution.py:566
  92.8 7.9 %collective-permute-done.20 = bf16[2048,128]{1,0:T(8,128)(2,1)S(1)} collective-permute-done((bf16[2048,128]{1,0:T(8,128)(2,1)S(1)}, bf16[2048,128]{1,0:T(8,128)(2,1)S(1)}, u32[]{:S(2)}, u32[]{:S(2)}) %collective-permute-start.20) | collective-permute-done | bytes 524320 | tf_op jit(solution)/shard_map/ppermute | solution.py:566
  100.7 2.6 %collective-permute-start.21 = (bf16[1024,128]{1,0:T(8,128)(2,1)S(1)}, bf16[1024,128]{1,0:T(8,128)(2,1)S(1)}, u32[]{:S(2)}, u32[]{:S(2)}) collective-permute-start(bf16[1024,128]{1,0:T(8,128)(2,1)S(1)} %slice.19), channel_id=1, source_target_pairs={{0,3},{1,0},{2,1},{3,2},{4,7},{5,4},{6,5},{7,6},{8,11},{9,8},{10,9... | collective-permute-start | bytes 786440 | tf_op jit(solution)/shard_map/ppermute | solution.py:566
  103.4 5.3 %backward_tiles.3 = (f32[32,128,128]{2,1,0:T(8,128)S(1)}, f32[16,128,128]{2,1,0:T(8,128)S(1)}) custom-call(s32[8,144]{1,0:T(8,128)S(1)} %get-tuple-element.73.list_ref, s32[8]{0:T(128)S(1)} %get-tuple-element.74.total_ref, bf16[1024,128]{1,0:T(8,128)(2,1)S(1)} %copy-done.9, bf16[1024,128]{1,0:T(8,128)(2,1)S(1)} %collective-permute-done.3.rest_0_.rest_1_, ...), custom_call_target="tpu_custom_call" | custom-call | flops 6000000000 | bytes 4000000 | tf_op jit(solution)/shard_map/backward_tiles/pallas_call | solution.py:451
  108.9 3.0 %collective-permute-done.21 = bf16[1024,128]{1,0:T(8,128)(2,1)S(1)} collective-permute-done((bf16[1024,128]{1,0:T(8,128)(2,1)S(1)}, bf16[1024,128]{1,0:T(8,128)(2,1)S(1)}, u32[]{:S(2)}, u32[]{:S(2)}) %collective-permute-start.21) | collective-permute-done | bytes 262176 | tf_op jit(solution)/shard_map/ppermute | solution.py:566
  117.5 4.8 %collective-permute-start.22 = (bf16[1024,128]{1,0:T(8,128)(2,1)S(1)}, bf16[1024,128]{1,0:T(8,128)(2,1)S(1)}, u32[]{:S(2)}, u32[]{:S(2)}) collective-permute-start(bf16[1024,128]{1,0:T(8,128)(2,1)S(1)} %bitcast.65), channel_id=1, source_target_pairs={{0,4},{4,8},{8,12},{12,16},{16,20},{20,24},{24,28},{28,32},{32,36}... | collective-permute-start | bytes 786440 | tf_op jit(solution)/shard_map/ppermute | solution.py:572
  129.7 3.4 %place_rows.2 = (f32[4096,128]{1,0:T(8,128)S(1)}, f32[8,128]{1,0:T(8,128)S(1)}) custom-call(s32[2,1024]{1,0:T(2,128)S(1)} %bitcast.39, s32[2]{0:T(128)S(1)} %bitcast.43, f32[4096,128]{1,0:T(8,128)S(1)} %get-tuple-element.100.sum_ref, bf16[2048,128]{1,0:T(8,128)(2,1)S(1)} %get-tuple-element.109.dpre_ref, bf16[128,128]{1,0:T(8,128)(2,1)S(1)} %copy-done.3), custom_call_target="tpu_custom_call" | custom-call | flops 4000000000 | bytes 7000000 | tf_op jit(solution)/shard_map/place_rows/pallas_call | solution.py:552
  138.9 3.8 %place_rows.3 = (bf16[4096,128]{1,0:T(8,128)(2,1)}, f32[8,128]{1,0:T(8,128)S(1)}) custom-call(s32[2,1024]{1,0:T(2,128)S(1)} %bitcast.40, s32[2]{0:T(128)S(1)} %bitcast.44, f32[4096,128]{1,0:T(8,128)S(1)} %get-tuple-element.110.sum_ref, bf16[2048,128]{1,0:T(8,128)(2,1)S(1)} %get-tuple-element.109.dpre_ref, bf16[128,128]{1,0:T(8,128)(2,1)S(1)} %copy-done.3, ...), custom_call_target="tpu_custom_call" | custom-call | flops 4000000000 | bytes 7000000 | tf_op jit(solution)/shard_map/place_rows/pallas_call | solution.py:552
  142.7 3.9 %collective-permute-start.32 = (bf16[144,128]{1,0:T(8,128)(2,1)S(1)}, bf16[144,128]{1,0:T(8,128)(2,1)S(1)}, u32[]{:S(2)}, u32[]{:S(2)}) collective-permute-start(bf16[144,128]{1,0:T(8,128)(2,1)S(1)} %sum_group.4.refs_0_), channel_id=1, source_target_pairs={{0,24},{4,28},{8,0},{12,4},{16,8},{20,12},{24,16},{28,20},{32,56},... | collective-permute-start | bytes 110600 | tf_op jit(solution)/shard_map/ppermute | solution.py:601
  147.7 3.4 %collective-permute-done.31.refs_2_ = bf16[144,128]{1,0:T(8,128)(2,1)S(1)} collective-permute-done((bf16[144,128]{1,0:T(8,128)(2,1)S(1)}, bf16[144,128]{1,0:T(8,128)(2,1)S(1)}, u32[]{:S(2)}, u32[]{:S(2)}) %collective-permute-start.31) | collective-permute-done | bytes 36896 | tf_op jit(solution)/shard_map/ppermute | solution.py:601
  151.1 5.5 %collective-permute-start.33 = (bf16[144,128]{1,0:T(8,128)(2,1)S(1)}, bf16[144,128]{1,0:T(8,128)(2,1)S(1)}, u32[]{:S(2)}, u32[]{:S(2)}) collective-permute-start(bf16[144,128]{1,0:T(8,128)(2,1)S(1)} %sum_group.5.one_ref), channel_id=1, source_target_pairs={{0,4},{4,0},{8,12},{12,8},{16,20},{20,16},{24,28},{28,24},{32,36},... | collective-permute-start | bytes 110600 | tf_op jit(solution)/shard_map/ppermute | solution.py:605
  (104 shorter events, 54.3 us)
Async XLA Ops:
  3.1 13.1 %collective-permute-start.2 = (bf16[144,128]{1,0:T(8,128)(2,1)}, bf16[144,128]{1,0:T(8,128)(2,1)S(1)}, u32[]{:S(2)}, u32[]{:S(2)}) collective-permute-start(bf16[144,128]{1,0:T(8,128)(2,1)} %get-tuple-element.64.s0_ref), channel_id=1, source_target_pairs={{0,1},{1,2},{2,3},{3,0},{4,5},{5,6},{6,7},{7,4},{8,9},{9,10},{10,1... | collective-permute-start | bytes 110600 | tf_op jit(solution)/shard_map/ppermute | solution.py:566
  5.6 12.6 %collective-permute-start.1 = (bf16[144,128]{1,0:T(8,128)(2,1)}, bf16[144,128]{1,0:T(8,128)(2,1)S(1)}, u32[]{:S(2)}, u32[]{:S(2)}) collective-permute-start(bf16[144,128]{1,0:T(8,128)(2,1)} %get-tuple-element.64.s0_ref), channel_id=1, source_target_pairs={{0,2},{1,3},{2,0},{3,1},{4,6},{5,7},{6,4},{7,5},{8,10},{9,11},{10,... | collective-permute-start | bytes 110600 | tf_op jit(solution)/shard_map/ppermute | solution.py:566
  8.9 9.3 %collective-permute-start = (bf16[144,128]{1,0:T(8,128)(2,1)}, bf16[144,128]{1,0:T(8,128)(2,1)S(1)}, u32[]{:S(2)}, u32[]{:S(2)}) collective-permute-start(bf16[144,128]{1,0:T(8,128)(2,1)} %get-tuple-element.64.s0_ref), channel_id=1, source_target_pairs={{0,3},{1,0},{2,1},{3,2},{4,7},{5,4},{6,5},{7,6},{8,11},{9,8},{10,9... | collective-permute-start | bytes 110600 | tf_op jit(solution)/shard_map/ppermute | solution.py:566
  9.6 21.5 %collective-permute-start.5 = (bf16[1024,128]{1,0:T(8,128)(2,1)}, bf16[1024,128]{1,0:T(8,128)(2,1)S(1)}, u32[]{:S(2)}, u32[]{:S(2)}) collective-permute-start(bf16[1024,128]{1,0:T(8,128)(2,1)} %get-tuple-element.69.rest_0_), channel_id=1, source_target_pairs={{0,1},{1,2},{2,3},{3,0},{4,5},{5,6},{6,7},{7,4},{8,9},{9,10},{10,1... | collective-permute-start | bytes 786440 | tf_op jit(solution)/shard_map/ppermute | solution.py:566
  10.4 20.8 %collective-permute-start.4 = (bf16[1024,128]{1,0:T(8,128)(2,1)}, bf16[1024,128]{1,0:T(8,128)(2,1)S(1)}, u32[]{:S(2)}, u32[]{:S(2)}) collective-permute-start(bf16[1024,128]{1,0:T(8,128)(2,1)} %get-tuple-element.69.rest_0_), channel_id=1, source_target_pairs={{0,2},{1,3},{2,0},{3,1},{4,6},{5,7},{6,4},{7,5},{8,10},{9,11},{10,... | collective-permute-start | bytes 786440 | tf_op jit(solution)/shard_map/ppermute | solution.py:566
  16.3 14.9 %collective-permute-start.3 = (bf16[1024,128]{1,0:T(8,128)(2,1)}, bf16[1024,128]{1,0:T(8,128)(2,1)S(1)}, u32[]{:S(2)}, u32[]{:S(2)}) collective-permute-start(bf16[1024,128]{1,0:T(8,128)(2,1)} %get-tuple-element.69.rest_0_), channel_id=1, source_target_pairs={{0,3},{1,0},{2,1},{3,2},{4,7},{5,4},{6,5},{7,6},{8,11},{9,8},{10,9... | collective-permute-start | bytes 786440 | tf_op jit(solution)/shard_map/ppermute | solution.py:566
  21.3 11.6 %collective-permute-start.6 = (bf16[1024,128]{1,0:T(8,128)(2,1)}, bf16[1024,128]{1,0:T(8,128)(2,1)S(1)}, u32[]{:S(2)}, u32[]{:S(2)}) collective-permute-start(bf16[1024,128]{1,0:T(8,128)(2,1)} %get-tuple-element.70), channel_id=1, source_target_pairs={{0,4},{4,8},{8,12},{12,16},{16,20},{20,24},{24,28},{28,32},{32,36}... | collective-permute-start | bytes 786440 | tf_op jit(solution)/shard_map/ppermute | solution.py:572
  36.2 12.6 %collective-permute-start.8 = (bf16[16,128,128]{2,1,0:T(8,128)(2,1)S(1)}, bf16[16,128,128]{2,1,0:T(8,128)(2,1)S(1)}, u32[]{:S(2)}, u32[]{:S(2)}) collective-permute-start(bf16[16,128,128]{2,1,0:T(8,128)(2,1)S(1)} %get-tuple-element.77), channel_id=1, source_target_pairs={{0,1},{1,2},{2,3},{3,0},{4,5},{5,6},{6,7},{7,4},{8,9},{9,10},{10,1... | collective-permute-start | bytes 1572872 | tf_op jit(solution)/shard_map/ppermute | solution.py:566
  38.5 11.0 %collective-permute-start.9 = (bf16[16,128,128]{2,1,0:T(8,128)(2,1)S(1)}, bf16[16,128,128]{2,1,0:T(8,128)(2,1)S(1)}, u32[]{:S(2)}, u32[]{:S(2)}) collective-permute-start(bf16[16,128,128]{2,1,0:T(8,128)(2,1)S(1)} %get-tuple-element.79), channel_id=1, source_target_pairs={{0,3},{1,0},{2,1},{3,2},{4,7},{5,4},{6,5},{7,6},{8,11},{9,8},{10,9... | collective-permute-start | bytes 1572872 | tf_op jit(solution)/shard_map/ppermute | solution.py:566
  47.4 12.2 %collective-permute-start.12 = (bf16[16,128,128]{2,1,0:T(8,128)(2,1)S(1)}, bf16[16,128,128]{2,1,0:T(8,128)(2,1)S(1)}, u32[]{:S(2)}, u32[]{:S(2)}) collective-permute-start(bf16[16,128,128]{2,1,0:T(8,128)(2,1)S(1)} %get-tuple-element.86), channel_id=1, source_target_pairs={{0,1},{1,2},{2,3},{3,0},{4,5},{5,6},{6,7},{7,4},{8,9},{9,10},{10,1... | collective-permute-start | bytes 1572872 | tf_op jit(solution)/shard_map/ppermute | solution.py:566
  49.8 14.3 %collective-permute-start.13 = (bf16[16,128,128]{2,1,0:T(8,128)(2,1)S(1)}, bf16[16,128,128]{2,1,0:T(8,128)(2,1)S(1)}, u32[]{:S(2)}, u32[]{:S(2)}) collective-permute-start(bf16[16,128,128]{2,1,0:T(8,128)(2,1)S(1)} %get-tuple-element.87), channel_id=1, source_target_pairs={{0,3},{1,0},{2,1},{3,2},{4,7},{5,4},{6,5},{7,6},{8,11},{9,8},{10,9... | collective-permute-start | bytes 1572872 | tf_op jit(solution)/shard_map/ppermute | solution.py:566
  51.2 24.1 %collective-permute-start.11 = (bf16[16,128,128]{2,1,0:T(8,128)(2,1)S(1)}, bf16[16,128,128]{2,1,0:T(8,128)(2,1)S(1)}, u32[]{:S(2)}, u32[]{:S(2)}) collective-permute-start(bf16[16,128,128]{2,1,0:T(8,128)(2,1)S(1)} %get-tuple-element.81), channel_id=1, source_target_pairs={{0,3},{1,0},{2,1},{3,2},{4,7},{5,4},{6,5},{7,6},{8,11},{9,8},{10,9... | collective-permute-start | bytes 1572872 | tf_op jit(solution)/shard_map/ppermute | solution.py:566
  56.4 18.9 %collective-permute-start.10 = (bf16[16,128,128]{2,1,0:T(8,128)(2,1)S(1)}, bf16[16,128,128]{2,1,0:T(8,128)(2,1)S(1)}, u32[]{:S(2)}, u32[]{:S(2)}) collective-permute-start(bf16[16,128,128]{2,1,0:T(8,128)(2,1)S(1)} %get-tuple-element.80), channel_id=1, source_target_pairs={{0,1},{1,2},{2,3},{3,0},{4,5},{5,6},{6,7},{7,4},{8,9},{9,10},{10,1... | collective-permute-start | bytes 1572872 | tf_op jit(solution)/shard_map/ppermute | solution.py:566
  68.5 13.7 %collective-permute-start.14 = (bf16[2048,128]{1,0:T(8,128)(2,1)S(1)}, bf16[2048,128]{1,0:T(8,128)(2,1)S(1)}, u32[]{:S(2)}, u32[]{:S(2)}) collective-permute-start(bf16[2048,128]{1,0:T(8,128)(2,1)S(1)} %get-tuple-element.93), channel_id=1, source_target_pairs={{0,1},{1,2},{2,3},{3,0},{4,5},{5,6},{6,7},{7,4},{8,9},{9,10},{10,1... | collective-permute-start | bytes 1572872 | tf_op jit(solution)/shard_map/ppermute | solution.py:566
  70.1 18.2 %collective-permute-start.16 = (bf16[2048,128]{1,0:T(8,128)(2,1)S(1)}, bf16[2048,128]{1,0:T(8,128)(2,1)S(1)}, u32[]{:S(2)}, u32[]{:S(2)}) collective-permute-start(bf16[2048,128]{1,0:T(8,128)(2,1)S(1)} %get-tuple-element.93), channel_id=1, source_target_pairs={{0,3},{1,0},{2,1},{3,2},{4,7},{5,4},{6,5},{7,6},{8,11},{9,8},{10,9... | collective-permute-start | bytes 1572872 | tf_op jit(solution)/shard_map/ppermute | solution.py:566
  86.8 13.9 %collective-permute-start.20 = (bf16[2048,128]{1,0:T(8,128)(2,1)S(1)}, bf16[2048,128]{1,0:T(8,128)(2,1)S(1)}, u32[]{:S(2)}, u32[]{:S(2)}) collective-permute-start(bf16[2048,128]{1,0:T(8,128)(2,1)S(1)} %get-tuple-element.98), channel_id=1, source_target_pairs={{0,3},{1,0},{2,1},{3,2},{4,7},{5,4},{6,5},{7,6},{8,11},{9,8},{10,9... | collective-permute-start | bytes 1572872 | tf_op jit(solution)/shard_map/ppermute | solution.py:566
  88.1 15.2 %collective-permute-start.18 = (bf16[2048,128]{1,0:T(8,128)(2,1)S(1)}, bf16[2048,128]{1,0:T(8,128)(2,1)S(1)}, u32[]{:S(2)}, u32[]{:S(2)}) collective-permute-start(bf16[2048,128]{1,0:T(8,128)(2,1)S(1)} %get-tuple-element.98), channel_id=1, source_target_pairs={{0,1},{1,2},{2,3},{3,0},{4,5},{5,6},{6,7},{7,4},{8,9},{9,10},{10,1... | collective-permute-start | bytes 1572872 | tf_op jit(solution)/shard_map/ppermute | solution.py:566
  88.3 20.4 %collective-permute-start.17 = (bf16[1024,128]{1,0:T(8,128)(2,1)S(1)}, bf16[1024,128]{1,0:T(8,128)(2,1)S(1)}, u32[]{:S(2)}, u32[]{:S(2)}) collective-permute-start(bf16[1024,128]{1,0:T(8,128)(2,1)S(1)} %slice.17), channel_id=1, source_target_pairs={{0,3},{1,0},{2,1},{3,2},{4,7},{5,4},{6,5},{7,6},{8,11},{9,8},{10,9... | collective-permute-start | bytes 786440 | tf_op jit(solution)/shard_map/ppermute | solution.py:566
  90.9 18.0 %collective-permute-start.15 = (bf16[1024,128]{1,0:T(8,128)(2,1)S(1)}, bf16[1024,128]{1,0:T(8,128)(2,1)S(1)}, u32[]{:S(2)}, u32[]{:S(2)}) collective-permute-start(bf16[1024,128]{1,0:T(8,128)(2,1)S(1)} %slice.16), channel_id=1, source_target_pairs={{0,1},{1,2},{2,3},{3,0},{4,5},{5,6},{6,7},{7,4},{8,9},{9,10},{10,1... | collective-permute-start | bytes 786440 | tf_op jit(solution)/shard_map/ppermute | solution.py:566
  100.7 11.1 %collective-permute-start.21 = (bf16[1024,128]{1,0:T(8,128)(2,1)S(1)}, bf16[1024,128]{1,0:T(8,128)(2,1)S(1)}, u32[]{:S(2)}, u32[]{:S(2)}) collective-permute-start(bf16[1024,128]{1,0:T(8,128)(2,1)S(1)} %slice.19), channel_id=1, source_target_pairs={{0,3},{1,0},{2,1},{3,2},{4,7},{5,4},{6,5},{7,6},{8,11},{9,8},{10,9... | collective-permute-start | bytes 786440 | tf_op jit(solution)/shard_map/ppermute | solution.py:566
  103.3 10.7 %collective-permute-start.19 = (bf16[1024,128]{1,0:T(8,128)(2,1)S(1)}, bf16[1024,128]{1,0:T(8,128)(2,1)S(1)}, u32[]{:S(2)}, u32[]{:S(2)}) collective-permute-start(bf16[1024,128]{1,0:T(8,128)(2,1)S(1)} %slice.18), channel_id=1, source_target_pairs={{0,1},{1,2},{2,3},{3,0},{4,5},{5,6},{6,7},{7,4},{8,9},{9,10},{10,1... | collective-permute-start | bytes 786440 | tf_op jit(solution)/shard_map/ppermute | solution.py:566
  115.0 10.2 %collective-permute-start.23 = (bf16[1024,128]{1,0:T(8,128)(2,1)S(1)}, bf16[1024,128]{1,0:T(8,128)(2,1)S(1)}, u32[]{:S(2)}, u32[]{:S(2)}) collective-permute-start(bf16[1024,128]{1,0:T(8,128)(2,1)S(1)} %bitcast.66), channel_id=1, source_target_pairs={{4,0},{8,4},{12,8},{16,12},{20,16},{24,20},{28,24},{32,28},{36,32}... | collective-permute-start | bytes 786440 | tf_op jit(solution)/shard_map/ppermute | solution.py:572
  117.5 8.2 %collective-permute-start.22 = (bf16[1024,128]{1,0:T(8,128)(2,1)S(1)}, bf16[1024,128]{1,0:T(8,128)(2,1)S(1)}, u32[]{:S(2)}, u32[]{:S(2)}) collective-permute-start(bf16[1024,128]{1,0:T(8,128)(2,1)S(1)} %bitcast.65), channel_id=1, source_target_pairs={{0,4},{4,8},{8,12},{12,16},{16,20},{20,24},{24,28},{28,32},{32,36}... | collective-permute-start | bytes 786440 | tf_op jit(solution)/shard_map/ppermute | solution.py:572
  133.2 9.4 %collective-permute-start.29 = (bf16[144,128]{1,0:T(8,128)(2,1)S(1)}, bf16[144,128]{1,0:T(8,128)(2,1)S(1)}, u32[]{:S(2)}, u32[]{:S(2)}) collective-permute-start(bf16[144,128]{1,0:T(8,128)(2,1)S(1)} %sum_group.3.rest_0_.refs_0_), channel_id=1, source_target_pairs={{0,96},{4,100},{8,104},{12,108},{16,112},{20,116},{24,120},{28,124... | collective-permute-start | bytes 110600 | tf_op jit(solution)/shard_map/ppermute | solution.py:601
  (26 other events, 186.6 us)

commit v6 on v5

--- a/solution.py
+++ b/solution.py
@@ -10,8 +10,8 @@
 F32 = jnp.float32
 BF16 = jnp.bfloat16
 SIDE = 128
-UNROLL = 4
-PARAMS = pltpu.CompilerParams(vmem_limit_bytes=20 * 2**20)
+UNROLL = 8
+PARAMS = pltpu.CompilerParams(vmem_limit_bytes=16 * 2**20)
 SMALL = pltpu.CompilerParams(vmem_limit_bytes=4 * 2**20)
 ROOMY = pltpu.CompilerParams(vmem_limit_bytes=60 * 2**20)
 VMEM = pl.BlockSpec(memory_space=pltpu.VMEM)
@@ -585,7 +585,7 @@
         out_shape=jax.ShapeDtypeStruct(terms[0].shape, BF16),
         in_specs=[VMEM] * len(terms) + [ANY] * len(follow),
         out_specs=VMEM,
-        compiler_params=PARAMS,
+        compiler_params=SMALL,
         name="sum_group",
     )(*terms, *follow)
 

time: 159 us -> 160 us (level)
  Pallas kernels: 53.1 us -> 55.3 us
    ppermute x23, starting transfers between devices: 29.1 us -> 26.7 us  [shift_wsh(): lax.ppermute(value, 'wsh', [(i, (i + step) % parties) for i in range(part...]
  transfers between devices with their start and end apart: 34 -> 34, of which waited for: 15 -> 14; matrix products, arithmetic and copies ran while one was open for 0% -> 0% of each run, Pallas kernels for 30% -> 31%
where the time goes in v6:
time: 160 us; the launch traced here: 159 us
  starting transfers between devices  58.4 us (36%)
  Pallas kernels  55.3 us (35%)
  waiting for transfers between devices  41 us (26%)
  local copies, waits for them, and re-layouts  2.19 us (1%)
  between operations  1.79 us (1%)
    ppermute x23, waiting for transfers between devices, shift_wsh(): lax.ppermute(value, 'wsh', [(i, (i + step) % parties) for i in range(part...  34.5 us
    ppermute x23, starting transfers between devices, shift_wsh(): lax.ppermute(value, 'wsh', [(i, (i + step) % parties) for i in range(part...  26.7 us
    ppermute x4, starting transfers between devices, shift_slab(): return lax.ppermute(value, 'slab', pairs)  14.7 us
    ppermute x6, starting transfers between devices, sum_slab(): lax.ppermute(value, 'slab', pairs)  10.9 us
    pallas_call x2, Pallas kernels, node_update(): pl.pallas_call(functools.partial(node_kernel, bool(before)), grid=(steps,...  9.01 us
    pallas_call x3, Pallas kernels, forward_tiles(): pl.pallas_call(functools.partial(forward_kernel, ks), out_shape=(half,) *...  8.93 us
    pallas_call x2, Pallas kernels, place_rows(): pl.pallas_call(functools.partial(place_kernel, k), out_shape=(jax.ShapeDt...  8.66 us
    pallas_call x3, Pallas kernels, backward_tiles(): pl.pallas_call(functools.partial(backward_kernel, ks, cuts, parts, bool(s...  7.31 us
  transfers between devices with their start and end apart: 34, of which 14 were waited for; matrix products, arithmetic and copies ran while one was open for 0% of the time, Pallas kernels for 31%

profile of v6, /device:TPU:1, one launch (start us, length us, event | category | flops | bytes accessed | tf_op | source)
XLA Modules:
  0.0 158.7 jit_solution(11221975396647444822)
XLA Ops:
  5.6 3.3 %collective-permute-start.1 = (bf16[144,128]{1,0:T(8,128)(2,1)}, bf16[144,128]{1,0:T(8,128)(2,1)S(1)}, u32[]{:S(2)}, u32[]{:S(2)}) collective-permute-start(bf16[144,128]{1,0:T(8,128)(2,1)} %get-tuple-element.64.s0_ref), channel_id=1, source_target_pairs={{0,2},{1,3},{2,0},{3,1},{4,6},{5,7},{6,4},{7,5},{8,10},{9,11},{10,... | collective-permute-start | bytes 110600 | tf_op jit(solution)/shard_map/ppermute | solution.py:566
  10.8 6.6 %pick_rows.1.picked_ref = bf16[2048,128]{1,0:T(8,128)(2,1)} custom-call(s32[2,1024]{1,0:T(2,128)} %bitcast.38, s32[2]{0:T(128)} %bitcast.41, bf16[4096,128]{1,0:T(8,128)(2,1)} %feat_ref.11), custom_call_target="tpu_custom_call" | custom-call | tf_op jit(solution)/shard_map/pick_rows/pallas_call | solution.py:73
  21.6 5.8 %collective-permute-start.6 = (bf16[1024,128]{1,0:T(8,128)(2,1)}, bf16[1024,128]{1,0:T(8,128)(2,1)S(1)}, u32[]{:S(2)}, u32[]{:S(2)}) collective-permute-start(bf16[1024,128]{1,0:T(8,128)(2,1)} %get-tuple-element.70), channel_id=1, source_target_pairs={{0,4},{4,8},{8,12},{12,16},{16,20},{20,24},{24,28},{28,32},{32,36}... | collective-permute-start | bytes 786440 | tf_op jit(solution)/shard_map/ppermute | solution.py:572
  37.6 2.7 %collective-permute-start.9 = (bf16[16,128,128]{2,1,0:T(8,128)(2,1)S(1)}, bf16[16,128,128]{2,1,0:T(8,128)(2,1)S(1)}, u32[]{:S(2)}, u32[]{:S(2)}) collective-permute-start(bf16[16,128,128]{2,1,0:T(8,128)(2,1)S(1)} %get-tuple-element.79), channel_id=1, source_target_pairs={{0,3},{1,0},{2,1},{3,2},{4,7},{5,4},{6,5},{7,6},{8,11},{9,8},{10,9... | collective-permute-start | bytes 1572872 | tf_op jit(solution)/shard_map/ppermute | solution.py:566
  40.3 2.9 %tile_lists.3 = (s32[8,144]{1,0:T(8,128)S(1)}, s32[8]{0:T(128)S(1)}) custom-call(s32[8,128]{1,0:T(8,128)S(1)} %copy-done.5, f32[8,128]{1,0:T(8,128)S(1)} %get-tuple-element.72.rest_0_), custom_call_target="tpu_custom_call" | custom-call | tf_op jit(solution)/shard_map/tile_lists/pallas_call | solution.py:222
  43.2 4.5 %forward_tiles.5 = (bf16[16,128,128]{2,1,0:T(8,128)(2,1)S(1)}, bf16[16,128,128]{2,1,0:T(8,128)(2,1)S(1)}, bf16[16,128,128]{2,1,0:T(8,128)(2,1)S(1)}, bf16[16,128,128]{2,1,0:T(8,128)(2,1)S(1)}, f32[8,128]{1,0:T(8,128)}) custom-call(s32[8,144]{1,0:T(8,128)S(1)} %get-tuple-element.73.list_ref, s32[8]{0:T(128)S(1)} %get-tuple-element.74.total_ref, ...), custom_call_target="tpu_custom_call" | custom-call | flops 2000000000 | bytes 8000000 | tf_op jit(solution)/shard_map/forward_tiles/pallas_call | solution.py:291
  56.7 4.3 %collective-permute-done.12 = bf16[16,128,128]{2,1,0:T(8,128)(2,1)S(1)} collective-permute-done((bf16[16,128,128]{2,1,0:T(8,128)(2,1)S(1)}, bf16[16,128,128]{2,1,0:T(8,128)(2,1)S(1)}, u32[]{:S(2)}, u32[]{:S(2)}) %collective-permute-start.12) | collective-permute-done | bytes 524320 | tf_op jit(solution)/shard_map/ppermute | solution.py:566
  61.0 3.5 %collective-permute-done.13 = bf16[16,128,128]{2,1,0:T(8,128)(2,1)S(1)} collective-permute-done((bf16[16,128,128]{2,1,0:T(8,128)(2,1)S(1)}, bf16[16,128,128]{2,1,0:T(8,128)(2,1)S(1)}, u32[]{:S(2)}, u32[]{:S(2)}) %collective-permute-start.13) | collective-permute-done | bytes 524320 | tf_op jit(solution)/shard_map/ppermute | solution.py:566
  64.5 4.4 %node_update.2 = (bf16[4096,128]{1,0:T(8,128)(2,1)}, bf16[4096,128]{1,0:T(8,128)(2,1)S(1)}, bf16[2048,128]{1,0:T(8,128)(2,1)S(1)}, f32[256,128]{1,0:T(8,128)S(1)...) custom-call(bf16[4096,128]{1,0:T(8,128)(2,1)S(1)} %copy-done.1, bf16[4096,128]{1,0:T(8,128)(2,1)S(1)} %copy-done.8, ...), custom_call_target="tpu_custom_call" | custom-call | flops 5000000000 | bytes 10000000 | tf_op jit(solution)/shard_map/node_update/pallas_call | solution.py:378
  71.6 4.0 %collective-permute-done.11 = bf16[16,128,128]{2,1,0:T(8,128)(2,1)S(1)} collective-permute-done((bf16[16,128,128]{2,1,0:T(8,128)(2,1)S(1)}, bf16[16,128,128]{2,1,0:T(8,128)(2,1)S(1)}, u32[]{:S(2)}, u32[]{:S(2)}) %collective-permute-start.11) | collective-permute-done | bytes 524320 | tf_op jit(solution)/shard_map/ppermute | solution.py:566
  75.6 6.6 %collective-permute-done.14.rest_5_ = bf16[2048,128]{1,0:T(8,128)(2,1)S(1)} collective-permute-done((bf16[2048,128]{1,0:T(8,128)(2,1)S(1)}, bf16[2048,128]{1,0:T(8,128)(2,1)S(1)}, u32[]{:S(2)}, u32[]{:S(2)}) %collective-permute-start.14) | collective-permute-done | bytes 524320 | tf_op jit(solution)/shard_map/ppermute | solution.py:566
  82.2 4.6 %node_update.3 = (bf16[4096,128]{1,0:T(8,128)(2,1)}, bf16[4096,128]{1,0:T(8,128)(2,1)S(1)}, bf16[2048,128]{1,0:T(8,128)(2,1)S(1)}, f32[256,128]{1,0:T(8,128)S(1)...) custom-call(bf16[4096,128]{1,0:T(8,128)(2,1)S(1)} %copy-done.1, ...), custom_call_target="tpu_custom_call", output_to_operand_aliasing={{0}: (8, {}), {1}: (9, {})} | custom-call | flops 5000000000 | bytes 10000000 | tf_op jit(solution)/shard_map/node_update/pallas_call | solution.py:378
  92.1 8.6 %collective-permute-done.20 = bf16[2048,128]{1,0:T(8,128)(2,1)S(1)} collective-permute-done((bf16[2048,128]{1,0:T(8,128)(2,1)S(1)}, bf16[2048,128]{1,0:T(8,128)(2,1)S(1)}, u32[]{:S(2)}, u32[]{:S(2)}) %collective-permute-start.20) | collective-permute-done | bytes 524320 | tf_op jit(solution)/shard_map/ppermute | solution.py:566
  102.9 4.4 %backward_tiles.3 = (f32[32,128,128]{2,1,0:T(8,128)S(1)}, f32[16,128,128]{2,1,0:T(8,128)S(1)}) custom-call(s32[8,144]{1,0:T(8,128)S(1)} %get-tuple-element.73.list_ref, s32[8]{0:T(128)S(1)} %get-tuple-element.74.total_ref, bf16[1024,128]{1,0:T(8,128)(2,1)S(1)} %copy-done.9, bf16[1024,128]{1,0:T(8,128)(2,1)S(1)} %collective-permute-done.3.rest_0_.rest_1_, ...), custom_call_target="tpu_custom_call" | custom-call | flops 6000000000 | bytes 4000000 | tf_op jit(solution)/shard_map/backward_tiles/pallas_call | solution.py:451
  108.2 3.3 %collective-permute-done.21 = bf16[1024,128]{1,0:T(8,128)(2,1)S(1)} collective-permute-done((bf16[1024,128]{1,0:T(8,128)(2,1)S(1)}, bf16[1024,128]{1,0:T(8,128)(2,1)S(1)}, u32[]{:S(2)}, u32[]{:S(2)}) %collective-permute-start.21) | collective-permute-done | bytes 262176 | tf_op jit(solution)/shard_map/ppermute | solution.py:566
  115.6 5.0 %collective-permute-start.22 = (bf16[1024,128]{1,0:T(8,128)(2,1)S(1)}, bf16[1024,128]{1,0:T(8,128)(2,1)S(1)}, u32[]{:S(2)}, u32[]{:S(2)}) collective-permute-start(bf16[1024,128]{1,0:T(8,128)(2,1)S(1)} %bitcast.65), channel_id=1, source_target_pairs={{0,4},{4,8},{8,12},{12,16},{16,20},{20,24},{24,28},{28,32},{32,36}... | collective-permute-start | bytes 786440 | tf_op jit(solution)/shard_map/ppermute | solution.py:572
  125.0 2.6 %collective-permute-start.25 = (bf16[144,128]{1,0:T(8,128)(2,1)S(1)}, bf16[144,128]{1,0:T(8,128)(2,1)S(1)}, u32[]{:S(2)}, u32[]{:S(2)}) collective-permute-start(bf16[144,128]{1,0:T(8,128)(2,1)S(1)} %get-tuple-element.113), channel_id=1, source_target_pairs={{0,2},{1,3},{2,0},{3,1},{4,6},{5,7},{6,4},{7,5},{8,10},{9,11},{10,... | collective-permute-start | bytes 110600 | tf_op jit(solution)/shard_map/ppermute | solution.py:566
  127.6 3.7 %place_rows.2 = (f32[4096,128]{1,0:T(8,128)S(1)}, f32[8,128]{1,0:T(8,128)S(1)}) custom-call(s32[2,1024]{1,0:T(2,128)S(1)} %bitcast.39, s32[2]{0:T(128)S(1)} %bitcast.43, f32[4096,128]{1,0:T(8,128)S(1)} %get-tuple-element.100.sum_ref, bf16[2048,128]{1,0:T(8,128)(2,1)S(1)} %get-tuple-element.109.dpre_ref, bf16[128,128]{1,0:T(8,128)(2,1)S(1)} %copy-done.3), custom_call_target="tpu_custom_call" | custom-call | flops 4000000000 | bytes 7000000 | tf_op jit(solution)/shard_map/place_rows/pallas_call | solution.py:552
  131.4 2.8 %collective-permute-start.29 = (bf16[144,128]{1,0:T(8,128)(2,1)S(1)}, bf16[144,128]{1,0:T(8,128)(2,1)S(1)}, u32[]{:S(2)}, u32[]{:S(2)}) collective-permute-start(bf16[144,128]{1,0:T(8,128)(2,1)S(1)} %sum_group.3.rest_0_.refs_0_), channel_id=1, source_target_pairs={{0,96},{4,100},{8,104},{12,108},{16,112},{20,116},{24,120},{28,124... | collective-permute-start | bytes 110600 | tf_op jit(solution)/shard_map/ppermute | solution.py:601
  134.2 2.7 %collective-permute-start.28 = (bf16[144,128]{1,0:T(8,128)(2,1)S(1)}, bf16[144,128]{1,0:T(8,128)(2,1)S(1)}, u32[]{:S(2)}, u32[]{:S(2)}) collective-permute-start(bf16[144,128]{1,0:T(8,128)(2,1)S(1)} %sum_group.3.rest_0_.refs_0_), channel_id=1, source_target_pairs={{0,64},{4,68},{8,72},{12,76},{16,80},{20,84},{24,88},{28,92},{32,9... | collective-permute-start | bytes 110600 | tf_op jit(solution)/shard_map/ppermute | solution.py:601
  137.7 4.9 %place_rows.3 = (bf16[4096,128]{1,0:T(8,128)(2,1)}, f32[8,128]{1,0:T(8,128)S(1)}) custom-call(s32[2,1024]{1,0:T(2,128)S(1)} %bitcast.40, s32[2]{0:T(128)S(1)} %bitcast.44, f32[4096,128]{1,0:T(8,128)S(1)} %get-tuple-element.110.sum_ref, bf16[2048,128]{1,0:T(8,128)(2,1)S(1)} %get-tuple-element.109.dpre_ref, bf16[128,128]{1,0:T(8,128)(2,1)S(1)} %copy-done.3, ...), custom_call_target="tpu_custom_call" | custom-call | flops 4000000000 | bytes 7000000 | tf_op jit(solution)/shard_map/place_rows/pallas_call | solution.py:552
  142.7 3.9 %collective-permute-start.32 = (bf16[144,128]{1,0:T(8,128)(2,1)S(1)}, bf16[144,128]{1,0:T(8,128)(2,1)S(1)}, u32[]{:S(2)}, u32[]{:S(2)}) collective-permute-start(bf16[144,128]{1,0:T(8,128)(2,1)S(1)} %sum_group.4.refs_0_), channel_id=1, source_target_pairs={{0,24},{4,28},{8,0},{12,4},{16,8},{20,12},{24,16},{28,20},{32,56},... | collective-permute-start | bytes 110600 | tf_op jit(solution)/shard_map/ppermute | solution.py:601
  147.7 3.4 %collective-permute-done.31.refs_2_ = bf16[144,128]{1,0:T(8,128)(2,1)S(1)} collective-permute-done((bf16[144,128]{1,0:T(8,128)(2,1)S(1)}, bf16[144,128]{1,0:T(8,128)(2,1)S(1)}, u32[]{:S(2)}, u32[]{:S(2)}) %collective-permute-start.31) | collective-permute-done | bytes 36896 | tf_op jit(solution)/shard_map/ppermute | solution.py:601
  151.1 6.2 %collective-permute-start.33 = (bf16[144,128]{1,0:T(8,128)(2,1)S(1)}, bf16[144,128]{1,0:T(8,128)(2,1)S(1)}, u32[]{:S(2)}, u32[]{:S(2)}) collective-permute-start(bf16[144,128]{1,0:T(8,128)(2,1)S(1)} %sum_group.5.one_ref), channel_id=1, source_target_pairs={{0,4},{4,0},{8,12},{12,8},{16,20},{20,16},{24,28},{28,24},{32,36},... | collective-permute-start | bytes 110600 | tf_op jit(solution)/shard_map/ppermute | solution.py:605
  (104 shorter events, 52.3 us)
Async XLA Ops:
  3.1 14.3 %collective-permute-start.2 = (bf16[144,128]{1,0:T(8,128)(2,1)}, bf16[144,128]{1,0:T(8,128)(2,1)S(1)}, u32[]{:S(2)}, u32[]{:S(2)}) collective-permute-start(bf16[144,128]{1,0:T(8,128)(2,1)} %get-tuple-element.64.s0_ref), channel_id=1, source_target_pairs={{0,1},{1,2},{2,3},{3,0},{4,5},{5,6},{6,7},{7,4},{8,9},{9,10},{10,1... | collective-permute-start | bytes 110600 | tf_op jit(solution)/shard_map/ppermute | solution.py:566
  5.6 13.0 %collective-permute-start.1 = (bf16[144,128]{1,0:T(8,128)(2,1)}, bf16[144,128]{1,0:T(8,128)(2,1)S(1)}, u32[]{:S(2)}, u32[]{:S(2)}) collective-permute-start(bf16[144,128]{1,0:T(8,128)(2,1)} %get-tuple-element.64.s0_ref), channel_id=1, source_target_pairs={{0,2},{1,3},{2,0},{3,1},{4,6},{5,7},{6,4},{7,5},{8,10},{9,11},{10,... | collective-permute-start | bytes 110600 | tf_op jit(solution)/shard_map/ppermute | solution.py:566
  8.9 9.7 %collective-permute-start = (bf16[144,128]{1,0:T(8,128)(2,1)}, bf16[144,128]{1,0:T(8,128)(2,1)S(1)}, u32[]{:S(2)}, u32[]{:S(2)}) collective-permute-start(bf16[144,128]{1,0:T(8,128)(2,1)} %get-tuple-element.64.s0_ref), channel_id=1, source_target_pairs={{0,3},{1,0},{2,1},{3,2},{4,7},{5,4},{6,5},{7,6},{8,11},{9,8},{10,9... | collective-permute-start | bytes 110600 | tf_op jit(solution)/shard_map/ppermute | solution.py:566
  9.6 22.2 %collective-permute-start.5 = (bf16[1024,128]{1,0:T(8,128)(2,1)}, bf16[1024,128]{1,0:T(8,128)(2,1)S(1)}, u32[]{:S(2)}, u32[]{:S(2)}) collective-permute-start(bf16[1024,128]{1,0:T(8,128)(2,1)} %get-tuple-element.69.rest_0_), channel_id=1, source_target_pairs={{0,1},{1,2},{2,3},{3,0},{4,5},{5,6},{6,7},{7,4},{8,9},{9,10},{10,1... | collective-permute-start | bytes 786440 | tf_op jit(solution)/shard_map/ppermute | solution.py:566
  10.4 21.5 %collective-permute-start.4 = (bf16[1024,128]{1,0:T(8,128)(2,1)}, bf16[1024,128]{1,0:T(8,128)(2,1)S(1)}, u32[]{:S(2)}, u32[]{:S(2)}) collective-permute-start(bf16[1024,128]{1,0:T(8,128)(2,1)} %get-tuple-element.69.rest_0_), channel_id=1, source_target_pairs={{0,2},{1,3},{2,0},{3,1},{4,6},{5,7},{6,4},{7,5},{8,10},{9,11},{10,... | collective-permute-start | bytes 786440 | tf_op jit(solution)/shard_map/ppermute | solution.py:566
  17.4 14.5 %collective-permute-start.3 = (bf16[1024,128]{1,0:T(8,128)(2,1)}, bf16[1024,128]{1,0:T(8,128)(2,1)S(1)}, u32[]{:S(2)}, u32[]{:S(2)}) collective-permute-start(bf16[1024,128]{1,0:T(8,128)(2,1)} %get-tuple-element.69.rest_0_), channel_id=1, source_target_pairs={{0,3},{1,0},{2,1},{3,2},{4,7},{5,4},{6,5},{7,6},{8,11},{9,8},{10,9... | collective-permute-start | bytes 786440 | tf_op jit(solution)/shard_map/ppermute | solution.py:566
  21.6 11.9 %collective-permute-start.6 = (bf16[1024,128]{1,0:T(8,128)(2,1)}, bf16[1024,128]{1,0:T(8,128)(2,1)S(1)}, u32[]{:S(2)}, u32[]{:S(2)}) collective-permute-start(bf16[1024,128]{1,0:T(8,128)(2,1)} %get-tuple-element.70), channel_id=1, source_target_pairs={{0,4},{4,8},{8,12},{12,16},{16,20},{20,24},{24,28},{28,32},{32,36}... | collective-permute-start | bytes 786440 | tf_op jit(solution)/shard_map/ppermute | solution.py:572
  37.5 12.6 %collective-permute-start.8 = (bf16[16,128,128]{2,1,0:T(8,128)(2,1)S(1)}, bf16[16,128,128]{2,1,0:T(8,128)(2,1)S(1)}, u32[]{:S(2)}, u32[]{:S(2)}) collective-permute-start(bf16[16,128,128]{2,1,0:T(8,128)(2,1)S(1)} %get-tuple-element.77), channel_id=1, source_target_pairs={{0,1},{1,2},{2,3},{3,0},{4,5},{5,6},{6,7},{7,4},{8,9},{9,10},{10,1... | collective-permute-start | bytes 1572872 | tf_op jit(solution)/shard_map/ppermute | solution.py:566
  37.6 12.5 %collective-permute-start.9 = (bf16[16,128,128]{2,1,0:T(8,128)(2,1)S(1)}, bf16[16,128,128]{2,1,0:T(8,128)(2,1)S(1)}, u32[]{:S(2)}, u32[]{:S(2)}) collective-permute-start(bf16[16,128,128]{2,1,0:T(8,128)(2,1)S(1)} %get-tuple-element.79), channel_id=1, source_target_pairs={{0,3},{1,0},{2,1},{3,2},{4,7},{5,4},{6,5},{7,6},{8,11},{9,8},{10,9... | collective-permute-start | bytes 1572872 | tf_op jit(solution)/shard_map/ppermute | solution.py:566
  47.7 13.3 %collective-permute-start.12 = (bf16[16,128,128]{2,1,0:T(8,128)(2,1)S(1)}, bf16[16,128,128]{2,1,0:T(8,128)(2,1)S(1)}, u32[]{:S(2)}, u32[]{:S(2)}) collective-permute-start(bf16[16,128,128]{2,1,0:T(8,128)(2,1)S(1)} %get-tuple-element.86), channel_id=1, source_target_pairs={{0,1},{1,2},{2,3},{3,0},{4,5},{5,6},{6,7},{7,4},{8,9},{9,10},{10,1... | collective-permute-start | bytes 1572872 | tf_op jit(solution)/shard_map/ppermute | solution.py:566
  50.4 14.1 %collective-permute-start.13 = (bf16[16,128,128]{2,1,0:T(8,128)(2,1)S(1)}, bf16[16,128,128]{2,1,0:T(8,128)(2,1)S(1)}, u32[]{:S(2)}, u32[]{:S(2)}) collective-permute-start(bf16[16,128,128]{2,1,0:T(8,128)(2,1)S(1)} %get-tuple-element.87), channel_id=1, source_target_pairs={{0,3},{1,0},{2,1},{3,2},{4,7},{5,4},{6,5},{7,6},{8,11},{9,8},{10,9... | collective-permute-start | bytes 1572872 | tf_op jit(solution)/shard_map/ppermute | solution.py:566
  51.8 23.8 %collective-permute-start.11 = (bf16[16,128,128]{2,1,0:T(8,128)(2,1)S(1)}, bf16[16,128,128]{2,1,0:T(8,128)(2,1)S(1)}, u32[]{:S(2)}, u32[]{:S(2)}) collective-permute-start(bf16[16,128,128]{2,1,0:T(8,128)(2,1)S(1)} %get-tuple-element.81), channel_id=1, source_target_pairs={{0,3},{1,0},{2,1},{3,2},{4,7},{5,4},{6,5},{7,6},{8,11},{9,8},{10,9... | collective-permute-start | bytes 1572872 | tf_op jit(solution)/shard_map/ppermute | solution.py:566
  54.5 21.0 %collective-permute-start.10 = (bf16[16,128,128]{2,1,0:T(8,128)(2,1)S(1)}, bf16[16,128,128]{2,1,0:T(8,128)(2,1)S(1)}, u32[]{:S(2)}, u32[]{:S(2)}) collective-permute-start(bf16[16,128,128]{2,1,0:T(8,128)(2,1)S(1)} %get-tuple-element.80), channel_id=1, source_target_pairs={{0,1},{1,2},{2,3},{3,0},{4,5},{5,6},{6,7},{7,4},{8,9},{9,10},{10,1... | collective-permute-start | bytes 1572872 | tf_op jit(solution)/shard_map/ppermute | solution.py:566
  68.9 13.3 %collective-permute-start.14 = (bf16[2048,128]{1,0:T(8,128)(2,1)S(1)}, bf16[2048,128]{1,0:T(8,128)(2,1)S(1)}, u32[]{:S(2)}, u32[]{:S(2)}) collective-permute-start(bf16[2048,128]{1,0:T(8,128)(2,1)S(1)} %get-tuple-element.93), channel_id=1, source_target_pairs={{0,1},{1,2},{2,3},{3,0},{4,5},{5,6},{6,7},{7,4},{8,9},{9,10},{10,1... | collective-permute-start | bytes 1572872 | tf_op jit(solution)/shard_map/ppermute | solution.py:566
  69.3 18.9 %collective-permute-start.16 = (bf16[2048,128]{1,0:T(8,128)(2,1)S(1)}, bf16[2048,128]{1,0:T(8,128)(2,1)S(1)}, u32[]{:S(2)}, u32[]{:S(2)}) collective-permute-start(bf16[2048,128]{1,0:T(8,128)(2,1)S(1)} %get-tuple-element.93), channel_id=1, source_target_pairs={{0,3},{1,0},{2,1},{3,2},{4,7},{5,4},{6,5},{7,6},{8,11},{9,8},{10,9... | collective-permute-start | bytes 1572872 | tf_op jit(solution)/shard_map/ppermute | solution.py:566
  86.8 13.9 %collective-permute-start.20 = (bf16[2048,128]{1,0:T(8,128)(2,1)S(1)}, bf16[2048,128]{1,0:T(8,128)(2,1)S(1)}, u32[]{:S(2)}, u32[]{:S(2)}) collective-permute-start(bf16[2048,128]{1,0:T(8,128)(2,1)S(1)} %get-tuple-element.98), channel_id=1, source_target_pairs={{0,3},{1,0},{2,1},{3,2},{4,7},{5,4},{6,5},{7,6},{8,11},{9,8},{10,9... | collective-permute-start | bytes 1572872 | tf_op jit(solution)/shard_map/ppermute | solution.py:566
  87.5 15.3 %collective-permute-start.18 = (bf16[2048,128]{1,0:T(8,128)(2,1)S(1)}, bf16[2048,128]{1,0:T(8,128)(2,1)S(1)}, u32[]{:S(2)}, u32[]{:S(2)}) collective-permute-start(bf16[2048,128]{1,0:T(8,128)(2,1)S(1)} %get-tuple-element.98), channel_id=1, source_target_pairs={{0,1},{1,2},{2,3},{3,0},{4,5},{5,6},{6,7},{7,4},{8,9},{9,10},{10,1... | collective-permute-start | bytes 1572872 | tf_op jit(solution)/shard_map/ppermute | solution.py:566
  88.3 18.9 %collective-permute-start.17 = (bf16[1024,128]{1,0:T(8,128)(2,1)S(1)}, bf16[1024,128]{1,0:T(8,128)(2,1)S(1)}, u32[]{:S(2)}, u32[]{:S(2)}) collective-permute-start(bf16[1024,128]{1,0:T(8,128)(2,1)S(1)} %slice.17), channel_id=1, source_target_pairs={{0,3},{1,0},{2,1},{3,2},{4,7},{5,4},{6,5},{7,6},{8,11},{9,8},{10,9... | collective-permute-start | bytes 786440 | tf_op jit(solution)/shard_map/ppermute | solution.py:566
  90.2 18.0 %collective-permute-start.15 = (bf16[1024,128]{1,0:T(8,128)(2,1)S(1)}, bf16[1024,128]{1,0:T(8,128)(2,1)S(1)}, u32[]{:S(2)}, u32[]{:S(2)}) collective-permute-start(bf16[1024,128]{1,0:T(8,128)(2,1)S(1)} %slice.16), channel_id=1, source_target_pairs={{0,1},{1,2},{2,3},{3,0},{4,5},{5,6},{6,7},{7,4},{8,9},{9,10},{10,1... | collective-permute-start | bytes 786440 | tf_op jit(solution)/shard_map/ppermute | solution.py:566
  100.7 10.8 %collective-permute-start.21 = (bf16[1024,128]{1,0:T(8,128)(2,1)S(1)}, bf16[1024,128]{1,0:T(8,128)(2,1)S(1)}, u32[]{:S(2)}, u32[]{:S(2)}) collective-permute-start(bf16[1024,128]{1,0:T(8,128)(2,1)S(1)} %slice.19), channel_id=1, source_target_pairs={{0,3},{1,0},{2,1},{3,2},{4,7},{5,4},{6,5},{7,6},{8,11},{9,8},{10,9... | collective-permute-start | bytes 786440 | tf_op jit(solution)/shard_map/ppermute | solution.py:566
  102.8 9.7 %collective-permute-start.19 = (bf16[1024,128]{1,0:T(8,128)(2,1)S(1)}, bf16[1024,128]{1,0:T(8,128)(2,1)S(1)}, u32[]{:S(2)}, u32[]{:S(2)}) collective-permute-start(bf16[1024,128]{1,0:T(8,128)(2,1)S(1)} %slice.18), channel_id=1, source_target_pairs={{0,1},{1,2},{2,3},{3,0},{4,5},{5,6},{6,7},{7,4},{8,9},{9,10},{10,1... | collective-permute-start | bytes 786440 | tf_op jit(solution)/shard_map/ppermute | solution.py:566
  113.7 10.2 %collective-permute-start.23 = (bf16[1024,128]{1,0:T(8,128)(2,1)S(1)}, bf16[1024,128]{1,0:T(8,128)(2,1)S(1)}, u32[]{:S(2)}, u32[]{:S(2)}) collective-permute-start(bf16[1024,128]{1,0:T(8,128)(2,1)S(1)} %bitcast.66), channel_id=1, source_target_pairs={{4,0},{8,4},{12,8},{16,12},{20,16},{24,20},{28,24},{32,28},{36,32}... | collective-permute-start | bytes 786440 | tf_op jit(solution)/shard_map/ppermute | solution.py:572
  131.4 11.2 %collective-permute-start.29 = (bf16[144,128]{1,0:T(8,128)(2,1)S(1)}, bf16[144,128]{1,0:T(8,128)(2,1)S(1)}, u32[]{:S(2)}, u32[]{:S(2)}) collective-permute-start(bf16[144,128]{1,0:T(8,128)(2,1)S(1)} %sum_group.3.rest_0_.refs_0_), channel_id=1, source_target_pairs={{0,96},{4,100},{8,104},{12,108},{16,112},{20,116},{24,120},{28,124... | collective-permute-start | bytes 110600 | tf_op jit(solution)/shard_map/ppermute | solution.py:601
  134.2 8.4 %collective-permute-start.28 = (bf16[144,128]{1,0:T(8,128)(2,1)S(1)}, bf16[144,128]{1,0:T(8,128)(2,1)S(1)}, u32[]{:S(2)}, u32[]{:S(2)}) collective-permute-start(bf16[144,128]{1,0:T(8,128)(2,1)S(1)} %sum_group.3.rest_0_.refs_0_), channel_id=1, source_target_pairs={{0,64},{4,68},{8,72},{12,76},{16,80},{20,84},{24,88},{28,92},{32,9... | collective-permute-start | bytes 110600 | tf_op jit(solution)/shard_map/ppermute | solution.py:601
  (26 other events, 184.1 us)

commit v7 on v6

--- a/solution.py
+++ b/solution.py
@@ -169,7 +169,7 @@
         ),
         in_specs=[SMEM] + [VMEM] * 5,
         out_specs=(VMEM,) * 7,
-        compiler_params=ROOMY,
+        compiler_params=PARAMS,
         name="prepare",
     )(position, *smalls, picked)
 

time: 160 us -> 158 us (0.988)
  Pallas kernels: 55.3 us -> 51.3 us
  waiting for transfers between devices: 41 us -> 44.3 us
    ppermute x4, starting transfers between devices: 14.7 us -> 20.2 us  [shift_slab(): return lax.ppermute(value, 'slab', pairs)]
    ppermute x6, starting transfers between devices: 10.9 us -> 7.11 us  [sum_slab(): lax.ppermute(value, 'slab', pairs)]
    pallas_call x1, Pallas kernels: 2.39 us -> 0.44 us  [prepare(): pl.pallas_call(functools.partial(prepare_kernel, own_blocks, here_blocks)...]
    ppermute x4, waiting for transfers between devices: 1.86 us -> 3.52 us  [shift_slab(): return lax.ppermute(value, 'slab', pairs)]
  transfers between devices with their start and end apart: 34 -> 34, of which waited for: 14 -> 15; matrix products, arithmetic and copies ran while one was open for 0% -> 0% of each run, Pallas kernels for 31% -> 28%
where the time goes in v7:
time: 158 us
  starting transfers between devices  58.9 us (37%)
  Pallas kernels  51.3 us (32%)
  waiting for transfers between devices  44.3 us (28%)
  local copies, waits for them, and re-layouts  1.91 us (1%)
  between operations  1.72 us (1%)
    ppermute x23, waiting for transfers between devices, shift_wsh(): lax.ppermute(value, 'wsh', [(i, (i + step) % parties) for i in range(part...  35.9 us
    ppermute x23, starting transfers between devices, shift_wsh(): lax.ppermute(value, 'wsh', [(i, (i + step) % parties) for i in range(part...  25.7 us
    ppermute x4, starting transfers between devices, shift_slab(): return lax.ppermute(value, 'slab', pairs)  20.2 us
    pallas_call x2, Pallas kernels, node_update(): pl.pallas_call(functools.partial(node_kernel, bool(before)), grid=(steps,...  9 us
    pallas_call x2, Pallas kernels, place_rows(): pl.pallas_call(functools.partial(place_kernel, k), out_shape=(jax.ShapeDt...  8.38 us
    pallas_call x3, Pallas kernels, forward_tiles(): pl.pallas_call(functools.partial(forward_kernel, ks), out_shape=(half,) *...  8.13 us
    ppermute x6, starting transfers between devices, sum_slab(): lax.ppermute(value, 'slab', pairs)  7.11 us
    pallas_call x3, Pallas kernels, backward_tiles(): pl.pallas_call(functools.partial(backward_kernel, ks, cuts, parts, bool(s...  6.65 us
  transfers between devices with their start and end apart: 34, of which 15 were waited for; matrix products, arithmetic and copies ran while one was open for 0% of the time, Pallas kernels for 28%

profile of v7, /device:TPU:1, one launch (start us, length us, event | category | flops | bytes accessed | tf_op | source)
XLA Modules:
  0.0 158.2 jit_solution(8684670454367070126)
XLA Ops:
  3.1 2.5 %collective-permute-start.2 = (bf16[144,128]{1,0:T(8,128)(2,1)}, bf16[144,128]{1,0:T(8,128)(2,1)S(1)}, u32[]{:S(2)}, u32[]{:S(2)}) collective-permute-start(bf16[144,128]{1,0:T(8,128)(2,1)} %get-tuple-element.64.s0_ref), channel_id=1, source_target_pairs={{0,1},{1,2},{2,3},{3,0},{4,5},{5,6},{6,7},{7,4},{8,9},{9,10},{10,1... | collective-permute-start | bytes 110600 | tf_op jit(solution)/shard_map/ppermute | solution.py:566
  5.6 3.3 %collective-permute-start.1 = (bf16[144,128]{1,0:T(8,128)(2,1)}, bf16[144,128]{1,0:T(8,128)(2,1)S(1)}, u32[]{:S(2)}, u32[]{:S(2)}) collective-permute-start(bf16[144,128]{1,0:T(8,128)(2,1)} %get-tuple-element.64.s0_ref), channel_id=1, source_target_pairs={{0,2},{1,3},{2,0},{3,1},{4,6},{5,7},{6,4},{7,5},{8,10},{9,11},{10,... | collective-permute-start | bytes 110600 | tf_op jit(solution)/shard_map/ppermute | solution.py:566
  10.8 6.3 %pick_rows.1.picked_ref = bf16[2048,128]{1,0:T(8,128)(2,1)} custom-call(s32[2,1024]{1,0:T(2,128)} %bitcast.38, s32[2]{0:T(128)} %bitcast.41, bf16[4096,128]{1,0:T(8,128)(2,1)} %feat_ref.11), custom_call_target="tpu_custom_call" | custom-call | tf_op jit(solution)/shard_map/pick_rows/pallas_call | solution.py:73
  20.7 5.7 %collective-permute-start.6 = (bf16[1024,128]{1,0:T(8,128)(2,1)S(1)}, bf16[1024,128]{1,0:T(8,128)(2,1)S(1)}, u32[]{:S(2)}, u32[]{:S(2)}) collective-permute-start(bf16[1024,128]{1,0:T(8,128)(2,1)S(1)} %get-tuple-element.70), channel_id=1, source_target_pairs={{0,4},{4,8},{8,12},{12,16},{16,20},{20,24},{24,28},{28,32},{32,36}... | collective-permute-start | bytes 786440 | tf_op jit(solution)/shard_map/ppermute | solution.py:572
  31.0 3.1 %collective-permute-done.7 = bf16[1024,128]{1,0:T(8,128)(2,1)S(1)} collective-permute-done((bf16[1024,128]{1,0:T(8,128)(2,1)S(1)}, bf16[1024,128]{1,0:T(8,128)(2,1)S(1)}, u32[]{:S(2)}, u32[]{:S(2)}) %collective-permute-start.7) | collective-permute-done | bytes 262176 | tf_op jit(solution)/shard_map/ppermute | solution.py:572
  35.9 2.7 %collective-permute-start.9 = (bf16[16,128,128]{2,1,0:T(8,128)(2,1)S(1)}, bf16[16,128,128]{2,1,0:T(8,128)(2,1)S(1)}, u32[]{:S(2)}, u32[]{:S(2)}) collective-permute-start(bf16[16,128,128]{2,1,0:T(8,128)(2,1)S(1)} %get-tuple-element.79), channel_id=1, source_target_pairs={{0,3},{1,0},{2,1},{3,2},{4,7},{5,4},{6,5},{7,6},{8,11},{9,8},{10,9... | collective-permute-start | bytes 1572872 | tf_op jit(solution)/shard_map/ppermute | solution.py:566
  38.6 2.8 %tile_lists.3 = (s32[8,144]{1,0:T(8,128)S(1)}, s32[8]{0:T(128)S(1)}) custom-call(s32[8,128]{1,0:T(8,128)S(1)} %get-tuple-element.65.code_ref, f32[8,128]{1,0:T(8,128)S(1)} %get-tuple-element.72.rest_0_), custom_call_target="tpu_custom_call" | custom-call | tf_op jit(solution)/shard_map/tile_lists/pallas_call | solution.py:222
  41.4 4.1 %forward_tiles.5 = (bf16[16,128,128]{2,1,0:T(8,128)(2,1)S(1)}, bf16[16,128,128]{2,1,0:T(8,128)(2,1)S(1)}, bf16[16,128,128]{2,1,0:T(8,128)(2,1)S(1)}, bf16[16,128,128]{2,1,0:T(8,128)(2,1)S(1)}, f32[8,128]{1,0:T(8,128)}) custom-call(s32[8,144]{1,0:T(8,128)S(1)} %get-tuple-element.73.list_ref, s32[8]{0:T(128)S(1)} %get-tuple-element.74.total_ref, ...), custom_call_target="tpu_custom_call" | custom-call | flops 2000000000 | bytes 8000000 | tf_op jit(solution)/shard_map/forward_tiles/pallas_call | solution.py:291
  45.5 3.2 %collective-permute-done.8.left_ref = bf16[16,128,128]{2,1,0:T(8,128)(2,1)S(1)} collective-permute-done((bf16[16,128,128]{2,1,0:T(8,128)(2,1)S(1)}, bf16[16,128,128]{2,1,0:T(8,128)(2,1)S(1)}, u32[]{:S(2)}, u32[]{:S(2)}) %collective-permute-start.8) | collective-permute-done | bytes 524320 | tf_op jit(solution)/shard_map/ppermute | solution.py:566
  55.2 5.6 %collective-permute-done.12 = bf16[16,128,128]{2,1,0:T(8,128)(2,1)S(1)} collective-permute-done((bf16[16,128,128]{2,1,0:T(8,128)(2,1)S(1)}, bf16[16,128,128]{2,1,0:T(8,128)(2,1)S(1)}, u32[]{:S(2)}, u32[]{:S(2)}) %collective-permute-start.12) | collective-permute-done | bytes 524320 | tf_op jit(solution)/shard_map/ppermute | solution.py:566
  60.8 2.3 %collective-permute-done.13 = bf16[16,128,128]{2,1,0:T(8,128)(2,1)S(1)} collective-permute-done((bf16[16,128,128]{2,1,0:T(8,128)(2,1)S(1)}, bf16[16,128,128]{2,1,0:T(8,128)(2,1)S(1)}, u32[]{:S(2)}, u32[]{:S(2)}) %collective-permute-start.13) | collective-permute-done | bytes 524320 | tf_op jit(solution)/shard_map/ppermute | solution.py:566
  63.1 4.4 %node_update.2 = (bf16[4096,128]{1,0:T(8,128)(2,1)}, bf16[4096,128]{1,0:T(8,128)(2,1)S(1)}, bf16[2048,128]{1,0:T(8,128)(2,1)S(1)}, f32[256,128]{1,0:T(8,128)S(1)...) custom-call(bf16[4096,128]{1,0:T(8,128)(2,1)S(1)} %copy-done.2, bf16[4096,128]{1,0:T(8,128)(2,1)S(1)} %copy-done.6, ...), custom_call_target="tpu_custom_call" | custom-call | flops 5000000000 | bytes 10000000 | tf_op jit(solution)/shard_map/node_update/pallas_call | solution.py:378
  70.2 4.2 %collective-permute-done.11 = bf16[16,128,128]{2,1,0:T(8,128)(2,1)S(1)} collective-permute-done((bf16[16,128,128]{2,1,0:T(8,128)(2,1)S(1)}, bf16[16,128,128]{2,1,0:T(8,128)(2,1)S(1)}, u32[]{:S(2)}, u32[]{:S(2)}) %collective-permute-start.11) | collective-permute-done | bytes 524320 | tf_op jit(solution)/shard_map/ppermute | solution.py:566
  74.3 6.4 %collective-permute-done.14.rest_5_ = bf16[2048,128]{1,0:T(8,128)(2,1)S(1)} collective-permute-done((bf16[2048,128]{1,0:T(8,128)(2,1)S(1)}, bf16[2048,128]{1,0:T(8,128)(2,1)S(1)}, u32[]{:S(2)}, u32[]{:S(2)}) %collective-permute-start.14) | collective-permute-done | bytes 524320 | tf_op jit(solution)/shard_map/ppermute | solution.py:566
  80.7 4.6 %node_update.3 = (bf16[4096,128]{1,0:T(8,128)(2,1)}, bf16[4096,128]{1,0:T(8,128)(2,1)S(1)}, bf16[2048,128]{1,0:T(8,128)(2,1)S(1)}, f32[256,128]{1,0:T(8,128)S(1)...) custom-call(bf16[4096,128]{1,0:T(8,128)(2,1)S(1)} %copy-done.2, ...), custom_call_target="tpu_custom_call", output_to_operand_aliasing={{0}: (8, {}), {1}: (9, {})} | custom-call | flops 5000000000 | bytes 10000000 | tf_op jit(solution)/shard_map/node_update/pallas_call | solution.py:378
  90.3 9.0 %collective-permute-done.20 = bf16[2048,128]{1,0:T(8,128)(2,1)S(1)} collective-permute-done((bf16[2048,128]{1,0:T(8,128)(2,1)S(1)}, bf16[2048,128]{1,0:T(8,128)(2,1)S(1)}, u32[]{:S(2)}, u32[]{:S(2)}) %collective-permute-start.20) | collective-permute-done | bytes 524320 | tf_op jit(solution)/shard_map/ppermute | solution.py:566
  101.0 4.1 %backward_tiles.3 = (f32[32,128,128]{2,1,0:T(8,128)S(1)}, f32[16,128,128]{2,1,0:T(8,128)S(1)}) custom-call(s32[8,144]{1,0:T(8,128)S(1)} %get-tuple-element.73.list_ref, s32[8]{0:T(128)S(1)} %get-tuple-element.74.total_ref, bf16[1024,128]{1,0:T(8,128)(2,1)S(1)} %copy-done.7, bf16[1024,128]{1,0:T(8,128)(2,1)S(1)} %collective-permute-done.3.rest_0_.rest_1_, ...), custom_call_target="tpu_custom_call" | custom-call | flops 6000000000 | bytes 4000000 | tf_op jit(solution)/shard_map/backward_tiles/pallas_call | solution.py:451
  106.4 2.8 %collective-permute-done.21 = bf16[1024,128]{1,0:T(8,128)(2,1)S(1)} collective-permute-done((bf16[1024,128]{1,0:T(8,128)(2,1)S(1)}, bf16[1024,128]{1,0:T(8,128)(2,1)S(1)}, u32[]{:S(2)}, u32[]{:S(2)}) %collective-permute-start.21) | collective-permute-done | bytes 262176 | tf_op jit(solution)/shard_map/ppermute | solution.py:566
  113.5 10.7 %collective-permute-start.22 = (bf16[1024,128]{1,0:T(8,128)(2,1)S(1)}, bf16[1024,128]{1,0:T(8,128)(2,1)S(1)}, u32[]{:S(2)}, u32[]{:S(2)}) collective-permute-start(bf16[1024,128]{1,0:T(8,128)(2,1)S(1)} %bitcast.65), channel_id=1, source_target_pairs={{0,4},{4,8},{8,12},{12,16},{16,20},{20,24},{24,28},{28,32},{32,36}... | collective-permute-start | bytes 786440 | tf_op jit(solution)/shard_map/ppermute | solution.py:572
  131.2 3.6 %place_rows.2 = (f32[4096,128]{1,0:T(8,128)S(1)}, f32[8,128]{1,0:T(8,128)S(1)}) custom-call(s32[2,1024]{1,0:T(2,128)S(1)} %bitcast.39, s32[2]{0:T(128)S(1)} %bitcast.43, f32[4096,128]{1,0:T(8,128)S(1)} %get-tuple-element.100.sum_ref, bf16[2048,128]{1,0:T(8,128)(2,1)S(1)} %get-tuple-element.109.dpre_ref, bf16[128,128]{1,0:T(8,128)(2,1)S(1)} %get-tuple-element.68.msg_ref), custom_call_target="tpu_custom_call" | custom-call | flops 4000000000 | bytes 7000000 | tf_op jit(solution)/shard_map/place_rows/pallas_call | solution.py:552
  136.9 4.8 %place_rows.3 = (bf16[4096,128]{1,0:T(8,128)(2,1)}, f32[8,128]{1,0:T(8,128)S(1)}) custom-call(s32[2,1024]{1,0:T(2,128)S(1)} %bitcast.40, s32[2]{0:T(128)S(1)} %bitcast.44, f32[4096,128]{1,0:T(8,128)S(1)} %get-tuple-element.110.sum_ref, bf16[2048,128]{1,0:T(8,128)(2,1)S(1)} %get-tuple-element.109.dpre_ref, bf16[128,128]{1,0:T(8,128)(2,1)S(1)} %get-tuple-element.68.msg_ref, ...), custom_call_target="tpu_custom_call" | custom-call | flops 4000000000 | bytes 7000000 | tf_op jit(solution)/shard_map/place_rows/pallas_call | solution.py:552
  141.7 4.4 %collective-permute-start.32 = (bf16[144,128]{1,0:T(8,128)(2,1)S(1)}, bf16[144,128]{1,0:T(8,128)(2,1)S(1)}, u32[]{:S(2)}, u32[]{:S(2)}) collective-permute-start(bf16[144,128]{1,0:T(8,128)(2,1)S(1)} %sum_group.4.refs_0_), channel_id=1, source_target_pairs={{0,24},{4,28},{8,0},{12,4},{16,8},{20,12},{24,16},{28,20},{32,56},... | collective-permute-start | bytes 110600 | tf_op jit(solution)/shard_map/ppermute | solution.py:601
  147.2 3.3 %collective-permute-done.31.refs_2_ = bf16[144,128]{1,0:T(8,128)(2,1)S(1)} collective-permute-done((bf16[144,128]{1,0:T(8,128)(2,1)S(1)}, bf16[144,128]{1,0:T(8,128)(2,1)S(1)}, u32[]{:S(2)}, u32[]{:S(2)}) %collective-permute-start.31) | collective-permute-done | bytes 36896 | tf_op jit(solution)/shard_map/ppermute | solution.py:601
  150.9 5.8 %collective-permute-start.33 = (bf16[144,128]{1,0:T(8,128)(2,1)S(1)}, bf16[144,128]{1,0:T(8,128)(2,1)S(1)}, u32[]{:S(2)}, u32[]{:S(2)}) collective-permute-start(bf16[144,128]{1,0:T(8,128)(2,1)S(1)} %sum_group.5.one_ref), channel_id=1, source_target_pairs={{0,4},{4,0},{8,12},{12,8},{16,20},{20,16},{24,28},{28,24},{32,36},... | collective-permute-start | bytes 110600 | tf_op jit(solution)/shard_map/ppermute | solution.py:605
  (88 shorter events, 46.8 us)
Async XLA Ops:
  3.1 14.0 %collective-permute-start.2 = (bf16[144,128]{1,0:T(8,128)(2,1)}, bf16[144,128]{1,0:T(8,128)(2,1)S(1)}, u32[]{:S(2)}, u32[]{:S(2)}) collective-permute-start(bf16[144,128]{1,0:T(8,128)(2,1)} %get-tuple-element.64.s0_ref), channel_id=1, source_target_pairs={{0,1},{1,2},{2,3},{3,0},{4,5},{5,6},{6,7},{7,4},{8,9},{9,10},{10,1... | collective-permute-start | bytes 110600 | tf_op jit(solution)/shard_map/ppermute | solution.py:566
  5.6 12.8 %collective-permute-start.1 = (bf16[144,128]{1,0:T(8,128)(2,1)}, bf16[144,128]{1,0:T(8,128)(2,1)S(1)}, u32[]{:S(2)}, u32[]{:S(2)}) collective-permute-start(bf16[144,128]{1,0:T(8,128)(2,1)} %get-tuple-element.64.s0_ref), channel_id=1, source_target_pairs={{0,2},{1,3},{2,0},{3,1},{4,6},{5,7},{6,4},{7,5},{8,10},{9,11},{10,... | collective-permute-start | bytes 110600 | tf_op jit(solution)/shard_map/ppermute | solution.py:566
  8.9 9.5 %collective-permute-start = (bf16[144,128]{1,0:T(8,128)(2,1)}, bf16[144,128]{1,0:T(8,128)(2,1)S(1)}, u32[]{:S(2)}, u32[]{:S(2)}) collective-permute-start(bf16[144,128]{1,0:T(8,128)(2,1)} %get-tuple-element.64.s0_ref), channel_id=1, source_target_pairs={{0,3},{1,0},{2,1},{3,2},{4,7},{5,4},{6,5},{7,6},{8,11},{9,8},{10,9... | collective-permute-start | bytes 110600 | tf_op jit(solution)/shard_map/ppermute | solution.py:566
  9.6 20.4 %collective-permute-start.5 = (bf16[1024,128]{1,0:T(8,128)(2,1)}, bf16[1024,128]{1,0:T(8,128)(2,1)S(1)}, u32[]{:S(2)}, u32[]{:S(2)}) collective-permute-start(bf16[1024,128]{1,0:T(8,128)(2,1)} %get-tuple-element.69.rest_0_), channel_id=1, source_target_pairs={{0,1},{1,2},{2,3},{3,0},{4,5},{5,6},{6,7},{7,4},{8,9},{9,10},{10,1... | collective-permute-start | bytes 786440 | tf_op jit(solution)/shard_map/ppermute | solution.py:566
  10.4 19.7 %collective-permute-start.4 = (bf16[1024,128]{1,0:T(8,128)(2,1)}, bf16[1024,128]{1,0:T(8,128)(2,1)S(1)}, u32[]{:S(2)}, u32[]{:S(2)}) collective-permute-start(bf16[1024,128]{1,0:T(8,128)(2,1)} %get-tuple-element.69.rest_0_), channel_id=1, source_target_pairs={{0,2},{1,3},{2,0},{3,1},{4,6},{5,7},{6,4},{7,5},{8,10},{9,11},{10,... | collective-permute-start | bytes 786440 | tf_op jit(solution)/shard_map/ppermute | solution.py:566
  17.2 12.9 %collective-permute-start.3 = (bf16[1024,128]{1,0:T(8,128)(2,1)}, bf16[1024,128]{1,0:T(8,128)(2,1)S(1)}, u32[]{:S(2)}, u32[]{:S(2)}) collective-permute-start(bf16[1024,128]{1,0:T(8,128)(2,1)} %get-tuple-element.69.rest_0_), channel_id=1, source_target_pairs={{0,3},{1,0},{2,1},{3,2},{4,7},{5,4},{6,5},{7,6},{8,11},{9,8},{10,9... | collective-permute-start | bytes 786440 | tf_op jit(solution)/shard_map/ppermute | solution.py:566
  20.7 10.3 %collective-permute-start.6 = (bf16[1024,128]{1,0:T(8,128)(2,1)S(1)}, bf16[1024,128]{1,0:T(8,128)(2,1)S(1)}, u32[]{:S(2)}, u32[]{:S(2)}) collective-permute-start(bf16[1024,128]{1,0:T(8,128)(2,1)S(1)} %get-tuple-element.70), channel_id=1, source_target_pairs={{0,4},{4,8},{8,12},{12,16},{16,20},{20,24},{24,28},{28,32},{32,36}... | collective-permute-start | bytes 786440 | tf_op jit(solution)/shard_map/ppermute | solution.py:572
  26.4 7.7 %collective-permute-start.7 = (bf16[1024,128]{1,0:T(8,128)(2,1)S(1)}, bf16[1024,128]{1,0:T(8,128)(2,1)S(1)}, u32[]{:S(2)}, u32[]{:S(2)}) collective-permute-start(bf16[1024,128]{1,0:T(8,128)(2,1)S(1)} %get-tuple-element.71), channel_id=1, source_target_pairs={{4,0},{8,4},{12,8},{16,12},{20,16},{24,20},{28,24},{32,28},{36,32}... | collective-permute-start | bytes 786440 | tf_op jit(solution)/shard_map/ppermute | solution.py:572
  35.9 12.9 %collective-permute-start.8 = (bf16[16,128,128]{2,1,0:T(8,128)(2,1)S(1)}, bf16[16,128,128]{2,1,0:T(8,128)(2,1)S(1)}, u32[]{:S(2)}, u32[]{:S(2)}) collective-permute-start(bf16[16,128,128]{2,1,0:T(8,128)(2,1)S(1)} %get-tuple-element.77), channel_id=1, source_target_pairs={{0,1},{1,2},{2,3},{3,0},{4,5},{5,6},{6,7},{7,4},{8,9},{9,10},{10,1... | collective-permute-start | bytes 1572872 | tf_op jit(solution)/shard_map/ppermute | solution.py:566
  35.9 12.8 %collective-permute-start.9 = (bf16[16,128,128]{2,1,0:T(8,128)(2,1)S(1)}, bf16[16,128,128]{2,1,0:T(8,128)(2,1)S(1)}, u32[]{:S(2)}, u32[]{:S(2)}) collective-permute-start(bf16[16,128,128]{2,1,0:T(8,128)(2,1)S(1)} %get-tuple-element.79), channel_id=1, source_target_pairs={{0,3},{1,0},{2,1},{3,2},{4,7},{5,4},{6,5},{7,6},{8,11},{9,8},{10,9... | collective-permute-start | bytes 1572872 | tf_op jit(solution)/shard_map/ppermute | solution.py:566
  45.5 15.2 %collective-permute-start.12 = (bf16[16,128,128]{2,1,0:T(8,128)(2,1)S(1)}, bf16[16,128,128]{2,1,0:T(8,128)(2,1)S(1)}, u32[]{:S(2)}, u32[]{:S(2)}) collective-permute-start(bf16[16,128,128]{2,1,0:T(8,128)(2,1)S(1)} %get-tuple-element.86), channel_id=1, source_target_pairs={{0,1},{1,2},{2,3},{3,0},{4,5},{5,6},{6,7},{7,4},{8,9},{9,10},{10,1... | collective-permute-start | bytes 1572872 | tf_op jit(solution)/shard_map/ppermute | solution.py:566
  49.0 14.1 %collective-permute-start.13 = (bf16[16,128,128]{2,1,0:T(8,128)(2,1)S(1)}, bf16[16,128,128]{2,1,0:T(8,128)(2,1)S(1)}, u32[]{:S(2)}, u32[]{:S(2)}) collective-permute-start(bf16[16,128,128]{2,1,0:T(8,128)(2,1)S(1)} %get-tuple-element.87), channel_id=1, source_target_pairs={{0,3},{1,0},{2,1},{3,2},{4,7},{5,4},{6,5},{7,6},{8,11},{9,8},{10,9... | collective-permute-start | bytes 1572872 | tf_op jit(solution)/shard_map/ppermute | solution.py:566
  50.3 24.0 %collective-permute-start.11 = (bf16[16,128,128]{2,1,0:T(8,128)(2,1)S(1)}, bf16[16,128,128]{2,1,0:T(8,128)(2,1)S(1)}, u32[]{:S(2)}, u32[]{:S(2)}) collective-permute-start(bf16[16,128,128]{2,1,0:T(8,128)(2,1)S(1)} %get-tuple-element.81), channel_id=1, source_target_pairs={{0,3},{1,0},{2,1},{3,2},{4,7},{5,4},{6,5},{7,6},{8,11},{9,8},{10,9... | collective-permute-start | bytes 1572872 | tf_op jit(solution)/shard_map/ppermute | solution.py:566
  54.2 20.1 %collective-permute-start.10 = (bf16[16,128,128]{2,1,0:T(8,128)(2,1)S(1)}, bf16[16,128,128]{2,1,0:T(8,128)(2,1)S(1)}, u32[]{:S(2)}, u32[]{:S(2)}) collective-permute-start(bf16[16,128,128]{2,1,0:T(8,128)(2,1)S(1)} %get-tuple-element.80), channel_id=1, source_target_pairs={{0,1},{1,2},{2,3},{3,0},{4,5},{5,6},{6,7},{7,4},{8,9},{9,10},{10,1... | collective-permute-start | bytes 1572872 | tf_op jit(solution)/shard_map/ppermute | solution.py:566
  67.5 13.2 %collective-permute-start.14 = (bf16[2048,128]{1,0:T(8,128)(2,1)S(1)}, bf16[2048,128]{1,0:T(8,128)(2,1)S(1)}, u32[]{:S(2)}, u32[]{:S(2)}) collective-permute-start(bf16[2048,128]{1,0:T(8,128)(2,1)S(1)} %get-tuple-element.93), channel_id=1, source_target_pairs={{0,1},{1,2},{2,3},{3,0},{4,5},{5,6},{6,7},{7,4},{8,9},{9,10},{10,1... | collective-permute-start | bytes 1572872 | tf_op jit(solution)/shard_map/ppermute | solution.py:566
  68.3 18.5 %collective-permute-start.16 = (bf16[2048,128]{1,0:T(8,128)(2,1)S(1)}, bf16[2048,128]{1,0:T(8,128)(2,1)S(1)}, u32[]{:S(2)}, u32[]{:S(2)}) collective-permute-start(bf16[2048,128]{1,0:T(8,128)(2,1)S(1)} %get-tuple-element.93), channel_id=1, source_target_pairs={{0,3},{1,0},{2,1},{3,2},{4,7},{5,4},{6,5},{7,6},{8,11},{9,8},{10,9... | collective-permute-start | bytes 1572872 | tf_op jit(solution)/shard_map/ppermute | solution.py:566
  85.3 14.0 %collective-permute-start.20 = (bf16[2048,128]{1,0:T(8,128)(2,1)S(1)}, bf16[2048,128]{1,0:T(8,128)(2,1)S(1)}, u32[]{:S(2)}, u32[]{:S(2)}) collective-permute-start(bf16[2048,128]{1,0:T(8,128)(2,1)S(1)} %get-tuple-element.98), channel_id=1, source_target_pairs={{0,3},{1,0},{2,1},{3,2},{4,7},{5,4},{6,5},{7,6},{8,11},{9,8},{10,9... | collective-permute-start | bytes 1572872 | tf_op jit(solution)/shard_map/ppermute | solution.py:566
  85.6 15.3 %collective-permute-start.18 = (bf16[2048,128]{1,0:T(8,128)(2,1)S(1)}, bf16[2048,128]{1,0:T(8,128)(2,1)S(1)}, u32[]{:S(2)}, u32[]{:S(2)}) collective-permute-start(bf16[2048,128]{1,0:T(8,128)(2,1)S(1)} %get-tuple-element.98), channel_id=1, source_target_pairs={{0,1},{1,2},{2,3},{3,0},{4,5},{5,6},{6,7},{7,4},{8,9},{9,10},{10,1... | collective-permute-start | bytes 1572872 | tf_op jit(solution)/shard_map/ppermute | solution.py:566
  86.8 18.2 %collective-permute-start.17 = (bf16[1024,128]{1,0:T(8,128)(2,1)S(1)}, bf16[1024,128]{1,0:T(8,128)(2,1)S(1)}, u32[]{:S(2)}, u32[]{:S(2)}) collective-permute-start(bf16[1024,128]{1,0:T(8,128)(2,1)S(1)} %slice.17), channel_id=1, source_target_pairs={{0,3},{1,0},{2,1},{3,2},{4,7},{5,4},{6,5},{7,6},{8,11},{9,8},{10,9... | collective-permute-start | bytes 786440 | tf_op jit(solution)/shard_map/ppermute | solution.py:566
  88.4 18.0 %collective-permute-start.15 = (bf16[1024,128]{1,0:T(8,128)(2,1)S(1)}, bf16[1024,128]{1,0:T(8,128)(2,1)S(1)}, u32[]{:S(2)}, u32[]{:S(2)}) collective-permute-start(bf16[1024,128]{1,0:T(8,128)(2,1)S(1)} %slice.16), channel_id=1, source_target_pairs={{0,1},{1,2},{2,3},{3,0},{4,5},{5,6},{6,7},{7,4},{8,9},{9,10},{10,1... | collective-permute-start | bytes 786440 | tf_op jit(solution)/shard_map/ppermute | solution.py:566
  99.3 9.9 %collective-permute-start.21 = (bf16[1024,128]{1,0:T(8,128)(2,1)S(1)}, bf16[1024,128]{1,0:T(8,128)(2,1)S(1)}, u32[]{:S(2)}, u32[]{:S(2)}) collective-permute-start(bf16[1024,128]{1,0:T(8,128)(2,1)S(1)} %slice.19), channel_id=1, source_target_pairs={{0,3},{1,0},{2,1},{3,2},{4,7},{5,4},{6,5},{7,6},{8,11},{9,8},{10,9... | collective-permute-start | bytes 786440 | tf_op jit(solution)/shard_map/ppermute | solution.py:566
  100.9 9.4 %collective-permute-start.19 = (bf16[1024,128]{1,0:T(8,128)(2,1)S(1)}, bf16[1024,128]{1,0:T(8,128)(2,1)S(1)}, u32[]{:S(2)}, u32[]{:S(2)}) collective-permute-start(bf16[1024,128]{1,0:T(8,128)(2,1)S(1)} %slice.18), channel_id=1, source_target_pairs={{0,1},{1,2},{2,3},{3,0},{4,5},{5,6},{6,7},{7,4},{8,9},{9,10},{10,1... | collective-permute-start | bytes 786440 | tf_op jit(solution)/shard_map/ppermute | solution.py:566
  111.6 15.5 %collective-permute-start.23 = (bf16[1024,128]{1,0:T(8,128)(2,1)S(1)}, bf16[1024,128]{1,0:T(8,128)(2,1)S(1)}, u32[]{:S(2)}, u32[]{:S(2)}) collective-permute-start(bf16[1024,128]{1,0:T(8,128)(2,1)S(1)} %bitcast.66), channel_id=1, source_target_pairs={{4,0},{8,4},{12,8},{16,12},{20,16},{24,20},{28,24},{32,28},{36,32}... | collective-permute-start | bytes 786440 | tf_op jit(solution)/shard_map/ppermute | solution.py:572
  113.5 14.0 %collective-permute-start.22 = (bf16[1024,128]{1,0:T(8,128)(2,1)S(1)}, bf16[1024,128]{1,0:T(8,128)(2,1)S(1)}, u32[]{:S(2)}, u32[]{:S(2)}) collective-permute-start(bf16[1024,128]{1,0:T(8,128)(2,1)S(1)} %bitcast.65), channel_id=1, source_target_pairs={{0,4},{4,8},{8,12},{12,16},{16,20},{20,24},{24,28},{28,32},{32,36}... | collective-permute-start | bytes 786440 | tf_op jit(solution)/shard_map/ppermute | solution.py:572
  (18 other events, 121.6 us)

commit v8 on v7

--- a/solution.py
+++ b/solution.py
@@ -51,7 +51,7 @@
 def pick_kernel(rows_ref, count_ref, feat_ref, out_ref, wide, picked):
     halo = rows_ref.shape[1]
     wide[...] = feat_ref[...].astype(F32)
-    group = 16
+    group = 32
     for k in range(2):
         count = count_ref[k]
 
@@ -535,7 +535,7 @@
     halo = rows_ref.shape[1]
     acc[...] = sum_ref[...]
     added[...] = contract_cols(dpre_ref[pl.ds(k * halo, halo), :], msg_ref[...])
-    group = 16
+    group = 32
 
     def body(step, carry):
         rows = [rows_ref[k, step * group + u] for u in range(group)]

time: 158 us -> 158 us (level)
  waiting for transfers between devices: 44.3 us -> 38.5 us
  starting transfers between devices: 58.9 us -> 61.8 us
    ppermute x23, starting transfers between devices: 25.7 us -> 31 us  [shift_wsh(): lax.ppermute(value, 'wsh', [(i, (i + step) % parties) for i in range(part...]
    ppermute x23, waiting for transfers between devices: 35.9 us -> 31.4 us  [shift_wsh(): lax.ppermute(value, 'wsh', [(i, (i + step) % parties) for i in range(part...]
    ppermute x4, starting transfers between devices: 20.2 us -> 18.4 us  [shift_slab(): return lax.ppermute(value, 'slab', pairs)]
    ppermute x6, starting transfers between devices: 7.11 us -> 5.47 us  [sum_slab(): lax.ppermute(value, 'slab', pairs)]
  transfers between devices with their start and end apart: 34 -> 34, of which waited for: 15 -> 13; matrix products, arithmetic and copies ran while one was open for 0% -> 0% of each run, Pallas kernels for 28% -> 28%
where the time goes in v8:
time: 158 us; the launch traced here: 157 us
  starting transfers between devices  61.8 us (39%)
  Pallas kernels  52.7 us (33%)
  waiting for transfers between devices  38.5 us (24%)
  local copies, waits for them, and re-layouts  1.91 us (1%)
  between operations  1.73 us (1%)
    ppermute x23, waiting for transfers between devices, shift_wsh(): lax.ppermute(value, 'wsh', [(i, (i + step) % parties) for i in range(part...  31.4 us
    ppermute x23, starting transfers between devices, shift_wsh(): lax.ppermute(value, 'wsh', [(i, (i + step) % parties) for i in range(part...  31 us
    ppermute x4, starting transfers between devices, shift_slab(): return lax.ppermute(value, 'slab', pairs)  18.4 us
    pallas_call x3, Pallas kernels, forward_tiles(): pl.pallas_call(functools.partial(forward_kernel, ks), out_shape=(half,) *...  9.32 us
    pallas_call x2, Pallas kernels, node_update(): pl.pallas_call(functools.partial(node_kernel, bool(before)), grid=(steps,...  9 us
    pallas_call x2, Pallas kernels, place_rows(): pl.pallas_call(functools.partial(place_kernel, k), out_shape=(jax.ShapeDt...  8.09 us
    pallas_call x3, Pallas kernels, backward_tiles(): pl.pallas_call(functools.partial(backward_kernel, ks, cuts, parts, bool(s...  7.64 us
    ppermute x1, starting transfers between devices, other_core(): lax.ppermute(value, 'slab', [(i, i ^ 1) for i in range(lax.axis_size('sla...  6.92 us
  transfers between devices with their start and end apart: 34, of which 13 were waited for; matrix products, arithmetic and copies ran while one was open for 0% of the time, Pallas kernels for 28%

profile of v8, /device:TPU:1, one launch (start us, length us, event | category | flops | bytes accessed | tf_op | source)
XLA Modules:
  0.0 156.7 jit_solution(5464901996870138565)
XLA Ops:
  3.1 2.5 %collective-permute-start.2 = (bf16[144,128]{1,0:T(8,128)(2,1)}, bf16[144,128]{1,0:T(8,128)(2,1)S(1)}, u32[]{:S(2)}, u32[]{:S(2)}) collective-permute-start(bf16[144,128]{1,0:T(8,128)(2,1)} %get-tuple-element.64.s0_ref), channel_id=1, source_target_pairs={{0,1},{1,2},{2,3},{3,0},{4,5},{5,6},{6,7},{7,4},{8,9},{9,10},{10,1... | collective-permute-start | bytes 110600 | tf_op jit(solution)/shard_map/ppermute | solution.py:566
  5.6 3.3 %collective-permute-start.1 = (bf16[144,128]{1,0:T(8,128)(2,1)}, bf16[144,128]{1,0:T(8,128)(2,1)S(1)}, u32[]{:S(2)}, u32[]{:S(2)}) collective-permute-start(bf16[144,128]{1,0:T(8,128)(2,1)} %get-tuple-element.64.s0_ref), channel_id=1, source_target_pairs={{0,2},{1,3},{2,0},{3,1},{4,6},{5,7},{6,4},{7,5},{8,10},{9,11},{10,... | collective-permute-start | bytes 110600 | tf_op jit(solution)/shard_map/ppermute | solution.py:566
  10.8 5.8 %pick_rows.1.picked_ref = bf16[2048,128]{1,0:T(8,128)(2,1)} custom-call(s32[2,1024]{1,0:T(2,128)} %bitcast.38, s32[2]{0:T(128)} %bitcast.41, bf16[4096,128]{1,0:T(8,128)(2,1)} %feat_ref.11), custom_call_target="tpu_custom_call" | custom-call | tf_op jit(solution)/shard_map/pick_rows/pallas_call | solution.py:73
  20.7 4.8 %collective-permute-start.6 = (bf16[1024,128]{1,0:T(8,128)(2,1)S(1)}, bf16[1024,128]{1,0:T(8,128)(2,1)S(1)}, u32[]{:S(2)}, u32[]{:S(2)}) collective-permute-start(bf16[1024,128]{1,0:T(8,128)(2,1)S(1)} %get-tuple-element.70), channel_id=1, source_target_pairs={{0,4},{4,8},{8,12},{12,16},{16,20},{20,24},{24,28},{28,32},{32,36}... | collective-permute-start | bytes 786440 | tf_op jit(solution)/shard_map/ppermute | solution.py:572
  30.6 2.5 %collective-permute-done.7 = bf16[1024,128]{1,0:T(8,128)(2,1)S(1)} collective-permute-done((bf16[1024,128]{1,0:T(8,128)(2,1)S(1)}, bf16[1024,128]{1,0:T(8,128)(2,1)S(1)}, u32[]{:S(2)}, u32[]{:S(2)}) %collective-permute-start.7) | collective-permute-done | bytes 262176 | tf_op jit(solution)/shard_map/ppermute | solution.py:572
  33.2 3.4 %forward_tiles.3 = (bf16[16,128,128]{2,1,0:T(8,128)(2,1)S(1)}, bf16[16,128,128]{2,1,0:T(8,128)(2,1)S(1)}, f32[8,128]{1,0:T(8,128)S(1)}) custom-call(s32[8,144]{1,0:T(8,128)S(1)} %get-tuple-element.66.list_ref, s32[8]{0:T(128)S(1)} %get-tuple-element.67.total_ref, bf16[32,128,128]{2,1,0:T(8,128)(2,1)S(1)} %bitcast.31, bf16[8,128,128]{2,1,0:T(8,128)(2,1)S(1)} %bitcast.51, ...), custom_call_target="tpu_custom_call" | custom-call | flops 1000000000 | bytes 4000000 | tf_op jit(solution)/shard_map/forward_tiles/pallas_call | solution.py:291
  36.6 2.7 %collective-permute-start.9 = (bf16[16,128,128]{2,1,0:T(8,128)(2,1)S(1)}, bf16[16,128,128]{2,1,0:T(8,128)(2,1)S(1)}, u32[]{:S(2)}, u32[]{:S(2)}) collective-permute-start(bf16[16,128,128]{2,1,0:T(8,128)(2,1)S(1)} %get-tuple-element.79), channel_id=1, source_target_pairs={{0,3},{1,0},{2,1},{3,2},{4,7},{5,4},{6,5},{7,6},{8,11},{9,8},{10,9... | collective-permute-start | bytes 1572872 | tf_op jit(solution)/shard_map/ppermute | solution.py:566
  39.3 2.4 %tile_lists.3 = (s32[8,144]{1,0:T(8,128)S(1)}, s32[8]{0:T(128)S(1)}) custom-call(s32[8,128]{1,0:T(8,128)S(1)} %get-tuple-element.65.code_ref, f32[8,128]{1,0:T(8,128)S(1)} %get-tuple-element.72.rest_0_), custom_call_target="tpu_custom_call" | custom-call | tf_op jit(solution)/shard_map/tile_lists/pallas_call | solution.py:222
  41.7 3.7 %forward_tiles.5 = (bf16[16,128,128]{2,1,0:T(8,128)(2,1)S(1)}, bf16[16,128,128]{2,1,0:T(8,128)(2,1)S(1)}, bf16[16,128,128]{2,1,0:T(8,128)(2,1)S(1)}, bf16[16,128,128]{2,1,0:T(8,128)(2,1)S(1)}, f32[8,128]{1,0:T(8,128)}) custom-call(s32[8,144]{1,0:T(8,128)S(1)} %get-tuple-element.73.list_ref, s32[8]{0:T(128)S(1)} %get-tuple-element.74.total_ref, ...), custom_call_target="tpu_custom_call" | custom-call | flops 2000000000 | bytes 8000000 | tf_op jit(solution)/shard_map/forward_tiles/pallas_call | solution.py:291
  47.1 3.5 %collective-permute-start.13 = (bf16[16,128,128]{2,1,0:T(8,128)(2,1)S(1)}, bf16[16,128,128]{2,1,0:T(8,128)(2,1)S(1)}, u32[]{:S(2)}, u32[]{:S(2)}) collective-permute-start(bf16[16,128,128]{2,1,0:T(8,128)(2,1)S(1)} %get-tuple-element.87), channel_id=1, source_target_pairs={{0,3},{1,0},{2,1},{3,2},{4,7},{5,4},{6,5},{7,6},{8,11},{9,8},{10,9... | collective-permute-start | bytes 1572872 | tf_op jit(solution)/shard_map/ppermute | solution.py:566
  54.7 5.9 %collective-permute-done.12 = bf16[16,128,128]{2,1,0:T(8,128)(2,1)S(1)} collective-permute-done((bf16[16,128,128]{2,1,0:T(8,128)(2,1)S(1)}, bf16[16,128,128]{2,1,0:T(8,128)(2,1)S(1)}, u32[]{:S(2)}, u32[]{:S(2)}) %collective-permute-start.12) | collective-permute-done | bytes 524320 | tf_op jit(solution)/shard_map/ppermute | solution.py:566
  62.4 4.4 %node_update.2 = (bf16[4096,128]{1,0:T(8,128)(2,1)}, bf16[4096,128]{1,0:T(8,128)(2,1)S(1)}, bf16[2048,128]{1,0:T(8,128)(2,1)S(1)}, f32[256,128]{1,0:T(8,128)S(1)...) custom-call(bf16[4096,128]{1,0:T(8,128)(2,1)S(1)} %copy-done.2, bf16[4096,128]{1,0:T(8,128)(2,1)S(1)} %copy-done.6, ...), custom_call_target="tpu_custom_call" | custom-call | flops 5000000000 | bytes 10000000 | tf_op jit(solution)/shard_map/node_update/pallas_call | solution.py:378
  66.8 3.5 %collective-permute-start.16 = (bf16[2048,128]{1,0:T(8,128)(2,1)S(1)}, bf16[2048,128]{1,0:T(8,128)(2,1)S(1)}, u32[]{:S(2)}, u32[]{:S(2)}) collective-permute-start(bf16[2048,128]{1,0:T(8,128)(2,1)S(1)} %get-tuple-element.93), channel_id=1, source_target_pairs={{0,3},{1,0},{2,1},{3,2},{4,7},{5,4},{6,5},{7,6},{8,11},{9,8},{10,9... | collective-permute-start | bytes 1572872 | tf_op jit(solution)/shard_map/ppermute | solution.py:566
  70.3 3.1 %collective-permute-done.11 = bf16[16,128,128]{2,1,0:T(8,128)(2,1)S(1)} collective-permute-done((bf16[16,128,128]{2,1,0:T(8,128)(2,1)S(1)}, bf16[16,128,128]{2,1,0:T(8,128)(2,1)S(1)}, u32[]{:S(2)}, u32[]{:S(2)}) %collective-permute-start.11) | collective-permute-done | bytes 524320 | tf_op jit(solution)/shard_map/ppermute | solution.py:566
  73.5 6.3 %collective-permute-done.14.rest_5_ = bf16[2048,128]{1,0:T(8,128)(2,1)S(1)} collective-permute-done((bf16[2048,128]{1,0:T(8,128)(2,1)S(1)}, bf16[2048,128]{1,0:T(8,128)(2,1)S(1)}, u32[]{:S(2)}, u32[]{:S(2)}) %collective-permute-start.14) | collective-permute-done | bytes 524320 | tf_op jit(solution)/shard_map/ppermute | solution.py:566
  79.8 4.6 %node_update.3 = (bf16[4096,128]{1,0:T(8,128)(2,1)}, bf16[4096,128]{1,0:T(8,128)(2,1)S(1)}, bf16[2048,128]{1,0:T(8,128)(2,1)S(1)}, f32[256,128]{1,0:T(8,128)S(1)...) custom-call(bf16[4096,128]{1,0:T(8,128)(2,1)S(1)} %copy-done.2, ...), custom_call_target="tpu_custom_call", output_to_operand_aliasing={{0}: (8, {}), {1}: (9, {})} | custom-call | flops 5000000000 | bytes 10000000 | tf_op jit(solution)/shard_map/node_update/pallas_call | solution.py:378
  85.9 2.4 %collective-permute-start.17 = (bf16[1024,128]{1,0:T(8,128)(2,1)S(1)}, bf16[1024,128]{1,0:T(8,128)(2,1)S(1)}, u32[]{:S(2)}, u32[]{:S(2)}) collective-permute-start(bf16[1024,128]{1,0:T(8,128)(2,1)S(1)} %slice.17), channel_id=1, source_target_pairs={{0,3},{1,0},{2,1},{3,2},{4,7},{5,4},{6,5},{7,6},{8,11},{9,8},{10,9... | collective-permute-start | bytes 786440 | tf_op jit(solution)/shard_map/ppermute | solution.py:566
  90.2 8.2 %collective-permute-done.20 = bf16[2048,128]{1,0:T(8,128)(2,1)S(1)} collective-permute-done((bf16[2048,128]{1,0:T(8,128)(2,1)S(1)}, bf16[2048,128]{1,0:T(8,128)(2,1)S(1)}, u32[]{:S(2)}, u32[]{:S(2)}) %collective-permute-start.20) | collective-permute-done | bytes 524320 | tf_op jit(solution)/shard_map/ppermute | solution.py:566
  100.9 3.7 %backward_tiles.3 = (f32[32,128,128]{2,1,0:T(8,128)S(1)}, f32[16,128,128]{2,1,0:T(8,128)S(1)}) custom-call(s32[8,144]{1,0:T(8,128)S(1)} %get-tuple-element.73.list_ref, s32[8]{0:T(128)S(1)} %get-tuple-element.74.total_ref, bf16[1024,128]{1,0:T(8,128)(2,1)S(1)} %copy-done.7, bf16[1024,128]{1,0:T(8,128)(2,1)S(1)} %collective-permute-done.3.rest_0_.rest_1_, ...), custom_call_target="tpu_custom_call" | custom-call | flops 6000000000 | bytes 4000000 | tf_op jit(solution)/shard_map/backward_tiles/pallas_call | solution.py:451
  113.5 9.8 %collective-permute-start.22 = (bf16[1024,128]{1,0:T(8,128)(2,1)S(1)}, bf16[1024,128]{1,0:T(8,128)(2,1)S(1)}, u32[]{:S(2)}, u32[]{:S(2)}) collective-permute-start(bf16[1024,128]{1,0:T(8,128)(2,1)S(1)} %bitcast.65), channel_id=1, source_target_pairs={{0,4},{4,8},{8,12},{12,16},{16,20},{20,24},{24,28},{28,32},{32,36}... | collective-permute-start | bytes 786440 | tf_op jit(solution)/shard_map/ppermute | solution.py:572
  130.8 3.0 %place_rows.2 = (f32[4096,128]{1,0:T(8,128)S(1)}, f32[8,128]{1,0:T(8,128)S(1)}) custom-call(s32[2,1024]{1,0:T(2,128)S(1)} %bitcast.39, s32[2]{0:T(128)S(1)} %bitcast.43, f32[4096,128]{1,0:T(8,128)S(1)} %get-tuple-element.100.sum_ref, bf16[2048,128]{1,0:T(8,128)(2,1)S(1)} %get-tuple-element.109.dpre_ref, bf16[128,128]{1,0:T(8,128)(2,1)S(1)} %get-tuple-element.68.msg_ref), custom_call_target="tpu_custom_call" | custom-call | flops 4000000000 | bytes 7000000 | tf_op jit(solution)/shard_map/place_rows/pallas_call | solution.py:552
  136.7 5.0 %place_rows.3 = (bf16[4096,128]{1,0:T(8,128)(2,1)}, f32[8,128]{1,0:T(8,128)S(1)}) custom-call(s32[2,1024]{1,0:T(2,128)S(1)} %bitcast.40, s32[2]{0:T(128)S(1)} %bitcast.44, f32[4096,128]{1,0:T(8,128)S(1)} %get-tuple-element.110.sum_ref, bf16[2048,128]{1,0:T(8,128)(2,1)S(1)} %get-tuple-element.109.dpre_ref, bf16[128,128]{1,0:T(8,128)(2,1)S(1)} %get-tuple-element.68.msg_ref, ...), custom_call_target="tpu_custom_call" | custom-call | flops 4000000000 | bytes 7000000 | tf_op jit(solution)/shard_map/place_rows/pallas_call | solution.py:552
  144.9 3.4 %collective-permute-done.31.refs_2_ = bf16[144,128]{1,0:T(8,128)(2,1)S(1)} collective-permute-done((bf16[144,128]{1,0:T(8,128)(2,1)S(1)}, bf16[144,128]{1,0:T(8,128)(2,1)S(1)}, u32[]{:S(2)}, u32[]{:S(2)}) %collective-permute-start.31) | collective-permute-done | bytes 36896 | tf_op jit(solution)/shard_map/ppermute | solution.py:601
  148.3 6.9 %collective-permute-start.33 = (bf16[144,128]{1,0:T(8,128)(2,1)S(1)}, bf16[144,128]{1,0:T(8,128)(2,1)S(1)}, u32[]{:S(2)}, u32[]{:S(2)}) collective-permute-start(bf16[144,128]{1,0:T(8,128)(2,1)S(1)} %sum_group.5.one_ref), channel_id=1, source_target_pairs={{0,4},{4,0},{8,12},{12,8},{16,20},{20,16},{24,28},{28,24},{32,36},... | collective-permute-start | bytes 110600 | tf_op jit(solution)/shard_map/ppermute | solution.py:605
  (88 shorter events, 50.2 us)
Async XLA Ops:
  3.1 13.5 %collective-permute-start.2 = (bf16[144,128]{1,0:T(8,128)(2,1)}, bf16[144,128]{1,0:T(8,128)(2,1)S(1)}, u32[]{:S(2)}, u32[]{:S(2)}) collective-permute-start(bf16[144,128]{1,0:T(8,128)(2,1)} %get-tuple-element.64.s0_ref), channel_id=1, source_target_pairs={{0,1},{1,2},{2,3},{3,0},{4,5},{5,6},{6,7},{7,4},{8,9},{9,10},{10,1... | collective-permute-start | bytes 110600 | tf_op jit(solution)/shard_map/ppermute | solution.py:566
  5.6 12.8 %collective-permute-start.1 = (bf16[144,128]{1,0:T(8,128)(2,1)}, bf16[144,128]{1,0:T(8,128)(2,1)S(1)}, u32[]{:S(2)}, u32[]{:S(2)}) collective-permute-start(bf16[144,128]{1,0:T(8,128)(2,1)} %get-tuple-element.64.s0_ref), channel_id=1, source_target_pairs={{0,2},{1,3},{2,0},{3,1},{4,6},{5,7},{6,4},{7,5},{8,10},{9,11},{10,... | collective-permute-start | bytes 110600 | tf_op jit(solution)/shard_map/ppermute | solution.py:566
  8.9 9.5 %collective-permute-start = (bf16[144,128]{1,0:T(8,128)(2,1)}, bf16[144,128]{1,0:T(8,128)(2,1)S(1)}, u32[]{:S(2)}, u32[]{:S(2)}) collective-permute-start(bf16[144,128]{1,0:T(8,128)(2,1)} %get-tuple-element.64.s0_ref), channel_id=1, source_target_pairs={{0,3},{1,0},{2,1},{3,2},{4,7},{5,4},{6,5},{7,6},{8,11},{9,8},{10,9... | collective-permute-start | bytes 110600 | tf_op jit(solution)/shard_map/ppermute | solution.py:566
  9.6 20.1 %collective-permute-start.5 = (bf16[1024,128]{1,0:T(8,128)(2,1)}, bf16[1024,128]{1,0:T(8,128)(2,1)S(1)}, u32[]{:S(2)}, u32[]{:S(2)}) collective-permute-start(bf16[1024,128]{1,0:T(8,128)(2,1)} %get-tuple-element.69.rest_0_), channel_id=1, source_target_pairs={{0,1},{1,2},{2,3},{3,0},{4,5},{5,6},{6,7},{7,4},{8,9},{9,10},{10,1... | collective-permute-start | bytes 786440 | tf_op jit(solution)/shard_map/ppermute | solution.py:566
  10.4 19.3 %collective-permute-start.4 = (bf16[1024,128]{1,0:T(8,128)(2,1)}, bf16[1024,128]{1,0:T(8,128)(2,1)S(1)}, u32[]{:S(2)}, u32[]{:S(2)}) collective-permute-start(bf16[1024,128]{1,0:T(8,128)(2,1)} %get-tuple-element.69.rest_0_), channel_id=1, source_target_pairs={{0,2},{1,3},{2,0},{3,1},{4,6},{5,7},{6,4},{7,5},{8,10},{9,11},{10,... | collective-permute-start | bytes 786440 | tf_op jit(solution)/shard_map/ppermute | solution.py:566
  16.6 13.1 %collective-permute-start.3 = (bf16[1024,128]{1,0:T(8,128)(2,1)}, bf16[1024,128]{1,0:T(8,128)(2,1)S(1)}, u32[]{:S(2)}, u32[]{:S(2)}) collective-permute-start(bf16[1024,128]{1,0:T(8,128)(2,1)} %get-tuple-element.69.rest_0_), channel_id=1, source_target_pairs={{0,3},{1,0},{2,1},{3,2},{4,7},{5,4},{6,5},{7,6},{8,11},{9,8},{10,9... | collective-permute-start | bytes 786440 | tf_op jit(solution)/shard_map/ppermute | solution.py:566
  20.7 10.0 %collective-permute-start.6 = (bf16[1024,128]{1,0:T(8,128)(2,1)S(1)}, bf16[1024,128]{1,0:T(8,128)(2,1)S(1)}, u32[]{:S(2)}, u32[]{:S(2)}) collective-permute-start(bf16[1024,128]{1,0:T(8,128)(2,1)S(1)} %get-tuple-element.70), channel_id=1, source_target_pairs={{0,4},{4,8},{8,12},{12,16},{16,20},{20,24},{24,28},{28,32},{32,36}... | collective-permute-start | bytes 786440 | tf_op jit(solution)/shard_map/ppermute | solution.py:572
  36.5 10.3 %collective-permute-start.8 = (bf16[16,128,128]{2,1,0:T(8,128)(2,1)S(1)}, bf16[16,128,128]{2,1,0:T(8,128)(2,1)S(1)}, u32[]{:S(2)}, u32[]{:S(2)}) collective-permute-start(bf16[16,128,128]{2,1,0:T(8,128)(2,1)S(1)} %get-tuple-element.77), channel_id=1, source_target_pairs={{0,1},{1,2},{2,3},{3,0},{4,5},{5,6},{6,7},{7,4},{8,9},{9,10},{10,1... | collective-permute-start | bytes 1572872 | tf_op jit(solution)/shard_map/ppermute | solution.py:566
  36.6 10.3 %collective-permute-start.9 = (bf16[16,128,128]{2,1,0:T(8,128)(2,1)S(1)}, bf16[16,128,128]{2,1,0:T(8,128)(2,1)S(1)}, u32[]{:S(2)}, u32[]{:S(2)}) collective-permute-start(bf16[16,128,128]{2,1,0:T(8,128)(2,1)S(1)} %get-tuple-element.79), channel_id=1, source_target_pairs={{0,3},{1,0},{2,1},{3,2},{4,7},{5,4},{6,5},{7,6},{8,11},{9,8},{10,9... | collective-permute-start | bytes 1572872 | tf_op jit(solution)/shard_map/ppermute | solution.py:566
  45.4 15.2 %collective-permute-start.12 = (bf16[16,128,128]{2,1,0:T(8,128)(2,1)S(1)}, bf16[16,128,128]{2,1,0:T(8,128)(2,1)S(1)}, u32[]{:S(2)}, u32[]{:S(2)}) collective-permute-start(bf16[16,128,128]{2,1,0:T(8,128)(2,1)S(1)} %get-tuple-element.86), channel_id=1, source_target_pairs={{0,1},{1,2},{2,3},{3,0},{4,5},{5,6},{6,7},{7,4},{8,9},{9,10},{10,1... | collective-permute-start | bytes 1572872 | tf_op jit(solution)/shard_map/ppermute | solution.py:566
  47.1 15.3 %collective-permute-start.13 = (bf16[16,128,128]{2,1,0:T(8,128)(2,1)S(1)}, bf16[16,128,128]{2,1,0:T(8,128)(2,1)S(1)}, u32[]{:S(2)}, u32[]{:S(2)}) collective-permute-start(bf16[16,128,128]{2,1,0:T(8,128)(2,1)S(1)} %get-tuple-element.87), channel_id=1, source_target_pairs={{0,3},{1,0},{2,1},{3,2},{4,7},{5,4},{6,5},{7,6},{8,11},{9,8},{10,9... | collective-permute-start | bytes 1572872 | tf_op jit(solution)/shard_map/ppermute | solution.py:566
  50.6 22.9 %collective-permute-start.11 = (bf16[16,128,128]{2,1,0:T(8,128)(2,1)S(1)}, bf16[16,128,128]{2,1,0:T(8,128)(2,1)S(1)}, u32[]{:S(2)}, u32[]{:S(2)}) collective-permute-start(bf16[16,128,128]{2,1,0:T(8,128)(2,1)S(1)} %get-tuple-element.81), channel_id=1, source_target_pairs={{0,3},{1,0},{2,1},{3,2},{4,7},{5,4},{6,5},{7,6},{8,11},{9,8},{10,9... | collective-permute-start | bytes 1572872 | tf_op jit(solution)/shard_map/ppermute | solution.py:566
  52.9 20.5 %collective-permute-start.10 = (bf16[16,128,128]{2,1,0:T(8,128)(2,1)S(1)}, bf16[16,128,128]{2,1,0:T(8,128)(2,1)S(1)}, u32[]{:S(2)}, u32[]{:S(2)}) collective-permute-start(bf16[16,128,128]{2,1,0:T(8,128)(2,1)S(1)} %get-tuple-element.80), channel_id=1, source_target_pairs={{0,1},{1,2},{2,3},{3,0},{4,5},{5,6},{6,7},{7,4},{8,9},{9,10},{10,1... | collective-permute-start | bytes 1572872 | tf_op jit(solution)/shard_map/ppermute | solution.py:566
  66.8 13.0 %collective-permute-start.14 = (bf16[2048,128]{1,0:T(8,128)(2,1)S(1)}, bf16[2048,128]{1,0:T(8,128)(2,1)S(1)}, u32[]{:S(2)}, u32[]{:S(2)}) collective-permute-start(bf16[2048,128]{1,0:T(8,128)(2,1)S(1)} %get-tuple-element.93), channel_id=1, source_target_pairs={{0,1},{1,2},{2,3},{3,0},{4,5},{5,6},{6,7},{7,4},{8,9},{9,10},{10,1... | collective-permute-start | bytes 1572872 | tf_op jit(solution)/shard_map/ppermute | solution.py:566
  66.8 19.1 %collective-permute-start.16 = (bf16[2048,128]{1,0:T(8,128)(2,1)S(1)}, bf16[2048,128]{1,0:T(8,128)(2,1)S(1)}, u32[]{:S(2)}, u32[]{:S(2)}) collective-permute-start(bf16[2048,128]{1,0:T(8,128)(2,1)S(1)} %get-tuple-element.93), channel_id=1, source_target_pairs={{0,3},{1,0},{2,1},{3,2},{4,7},{5,4},{6,5},{7,6},{8,11},{9,8},{10,9... | collective-permute-start | bytes 1572872 | tf_op jit(solution)/shard_map/ppermute | solution.py:566
  84.4 14.0 %collective-permute-start.20 = (bf16[2048,128]{1,0:T(8,128)(2,1)S(1)}, bf16[2048,128]{1,0:T(8,128)(2,1)S(1)}, u32[]{:S(2)}, u32[]{:S(2)}) collective-permute-start(bf16[2048,128]{1,0:T(8,128)(2,1)S(1)} %get-tuple-element.98), channel_id=1, source_target_pairs={{0,3},{1,0},{2,1},{3,2},{4,7},{5,4},{6,5},{7,6},{8,11},{9,8},{10,9... | collective-permute-start | bytes 1572872 | tf_op jit(solution)/shard_map/ppermute | solution.py:566
  85.5 15.3 %collective-permute-start.18 = (bf16[2048,128]{1,0:T(8,128)(2,1)S(1)}, bf16[2048,128]{1,0:T(8,128)(2,1)S(1)}, u32[]{:S(2)}, u32[]{:S(2)}) collective-permute-start(bf16[2048,128]{1,0:T(8,128)(2,1)S(1)} %get-tuple-element.98), channel_id=1, source_target_pairs={{0,1},{1,2},{2,3},{3,0},{4,5},{5,6},{6,7},{7,4},{8,9},{9,10},{10,1... | collective-permute-start | bytes 1572872 | tf_op jit(solution)/shard_map/ppermute | solution.py:566
  85.9 18.8 %collective-permute-start.17 = (bf16[1024,128]{1,0:T(8,128)(2,1)S(1)}, bf16[1024,128]{1,0:T(8,128)(2,1)S(1)}, u32[]{:S(2)}, u32[]{:S(2)}) collective-permute-start(bf16[1024,128]{1,0:T(8,128)(2,1)S(1)} %slice.17), channel_id=1, source_target_pairs={{0,3},{1,0},{2,1},{3,2},{4,7},{5,4},{6,5},{7,6},{8,11},{9,8},{10,9... | collective-permute-start | bytes 786440 | tf_op jit(solution)/shard_map/ppermute | solution.py:566
  88.3 18.0 %collective-permute-start.15 = (bf16[1024,128]{1,0:T(8,128)(2,1)S(1)}, bf16[1024,128]{1,0:T(8,128)(2,1)S(1)}, u32[]{:S(2)}, u32[]{:S(2)}) collective-permute-start(bf16[1024,128]{1,0:T(8,128)(2,1)S(1)} %slice.16), channel_id=1, source_target_pairs={{0,1},{1,2},{2,3},{3,0},{4,5},{5,6},{6,7},{7,4},{8,9},{9,10},{10,1... | collective-permute-start | bytes 786440 | tf_op jit(solution)/shard_map/ppermute | solution.py:566
  98.4 9.3 %collective-permute-start.21 = (bf16[1024,128]{1,0:T(8,128)(2,1)S(1)}, bf16[1024,128]{1,0:T(8,128)(2,1)S(1)}, u32[]{:S(2)}, u32[]{:S(2)}) collective-permute-start(bf16[1024,128]{1,0:T(8,128)(2,1)S(1)} %slice.19), channel_id=1, source_target_pairs={{0,3},{1,0},{2,1},{3,2},{4,7},{5,4},{6,5},{7,6},{8,11},{9,8},{10,9... | collective-permute-start | bytes 786440 | tf_op jit(solution)/shard_map/ppermute | solution.py:566
  100.8 9.2 %collective-permute-start.19 = (bf16[1024,128]{1,0:T(8,128)(2,1)S(1)}, bf16[1024,128]{1,0:T(8,128)(2,1)S(1)}, u32[]{:S(2)}, u32[]{:S(2)}) collective-permute-start(bf16[1024,128]{1,0:T(8,128)(2,1)S(1)} %slice.18), channel_id=1, source_target_pairs={{0,1},{1,2},{2,3},{3,0},{4,5},{5,6},{6,7},{7,4},{8,9},{9,10},{10,1... | collective-permute-start | bytes 786440 | tf_op jit(solution)/shard_map/ppermute | solution.py:566
  111.5 15.6 %collective-permute-start.23 = (bf16[1024,128]{1,0:T(8,128)(2,1)S(1)}, bf16[1024,128]{1,0:T(8,128)(2,1)S(1)}, u32[]{:S(2)}, u32[]{:S(2)}) collective-permute-start(bf16[1024,128]{1,0:T(8,128)(2,1)S(1)} %bitcast.66), channel_id=1, source_target_pairs={{4,0},{8,4},{12,8},{16,12},{20,16},{24,20},{28,24},{32,28},{36,32}... | collective-permute-start | bytes 786440 | tf_op jit(solution)/shard_map/ppermute | solution.py:572
  113.5 13.7 %collective-permute-start.22 = (bf16[1024,128]{1,0:T(8,128)(2,1)S(1)}, bf16[1024,128]{1,0:T(8,128)(2,1)S(1)}, u32[]{:S(2)}, u32[]{:S(2)}) collective-permute-start(bf16[1024,128]{1,0:T(8,128)(2,1)S(1)} %bitcast.65), channel_id=1, source_target_pairs={{0,4},{4,8},{8,12},{12,16},{16,20},{20,24},{24,28},{28,32},{32,36}... | collective-permute-start | bytes 786440 | tf_op jit(solution)/shard_map/ppermute | solution.py:572
  134.0 7.8 %collective-permute-start.29 = (bf16[144,128]{1,0:T(8,128)(2,1)S(1)}, bf16[144,128]{1,0:T(8,128)(2,1)S(1)}, u32[]{:S(2)}, u32[]{:S(2)}) collective-permute-start(bf16[144,128]{1,0:T(8,128)(2,1)S(1)} %sum_group.3.rest_0_.refs_0_), channel_id=1, source_target_pairs={{0,96},{4,100},{8,104},{12,108},{16,112},{20,116},{24,120},{28,124... | collective-permute-start | bytes 110600 | tf_op jit(solution)/shard_map/ppermute | solution.py:601
  (18 other events, 120.6 us)
